TPU v7x, 32 devices: a whole 2x2x4 slice. The times are simulated.
32 devices in a mesh: inline: 8 (over y, x, core), crosslin: 4 (over z).
Axes of the slice: x: 2, y: 2, z: 4, core: 2. Of those that a mesh axis runs over, the one named last changes fastest.
Arguments:
- traces: float32 [4096, 4, 1024], P(('inline', 'crosslin')), may hold values from -6 to 6
- destination: int32 [4096, 1], P(('inline', 'crosslin')), may hold values from 0 to 31; in each aligned block of 128 rows (0 to 127, 128 to 255, ...) at most 8 rows name the same one
- bin_index: int32 [4096, 4], P(('inline', 'crosslin')), may hold values from 0 to 1023
- dip_inline: int32 [256, 128], P('inline', 'crosslin'), may hold values from -2 to 2
- dip_cross: int32 [256, 128], P('inline', 'crosslin'), may hold values from -2 to 2
Outputs:
- smoothed: float32 [256, 128, 1024], P('inline', 'crosslin')
Inputs may be any that keep to these rules, and one draw needn't show every extreme that they name: `destination`: at most 8 of one device's blocks name the same tile, and that many are reached.
All inputs are finite; a program needn't handle non-finite values.
Results may differ from a plain program's by a relative error of at most 0.00009.
Values sent between devices are 32-bit elements; how exact they have to be, the bound alone decides.
No kernel may reach another device: no remote copies, remote signals or barrier semaphores. Data moves between devices by JAX's collectives and lax.ppermute only.
A program may use at most 64 MiB of HBM per device.

v0:
```python
import jax
import jax.numpy as jnp
from jax import lax
from jax.sharding import PartitionSpec as P

HALF = 7
DMAX = 2


def padded_2(cells, sides, width):
    for axis, dim in sides:
        count = lax.axis_size(axis)
        ends = count - 1
        head = lax.slice_in_dim(cells, 0, width, axis=dim)
        tail = lax.slice_in_dim(cells, cells.shape[dim] - width, cells.shape[dim], axis=dim)
        cells = jnp.concatenate(
            [
                lax.ppermute(tail, axis, [(i, (i + 1) % count) for i in range(ends)]),
                cells,
                lax.ppermute(head, axis, [((i + 1) % count, i) for i in range(ends)]),
            ],
            axis=dim,
        )
    return cells


def steer(padded, dip_index, along_dim):
    margin = HALF * DMAX
    samples = padded.shape[-1] - 2 * margin
    extent = padded.shape[along_dim] - 2 * HALF
    result = jnp.zeros(dip_index.shape + (samples,), jnp.float32)
    for dip_value in range(-DMAX, DMAX + 1):
        running = jnp.zeros(dip_index.shape + (samples,), jnp.float32)
        for offset in range(-HALF, HALF + 1):
            weight = (HALF + 1 - abs(offset)) / float((HALF + 1) ** 2)
            shifted = lax.slice_in_dim(
                padded, HALF + offset, HALF + offset + extent, axis=along_dim
            )
            begin = margin + dip_value * offset
            shifted = shifted[..., begin : begin + samples]
            running = running + weight * shifted
        result = jnp.where((dip_index == dip_value)[..., None], running, result)
    return result


def pad_time(gridded):
    margin = HALF * DMAX
    return jnp.pad(gridded, ((0, 0), (0, 0), (margin, margin)))


def smooth_inline(gridded, dip_index):
    padded = padded_2(pad_time(gridded), (("inline", 0),), HALF)
    return steer(padded, dip_index, 0)


def smooth_cross(gridded, dip_index):
    padded = padded_2(pad_time(gridded), (("crosslin", 1),), HALF)
    return steer(padded, dip_index, 1)


def on_device(traces, destination, bin_index, dip_inline, dip_cross):
    held_blocks, block_rows, samples = traces.shape
    rows_inline = lax.axis_size("inline")
    cols_cross = lax.axis_size("crosslin")
    devices = rows_inline * cols_cross
    capacity = 2 * held_blocks // devices
    tile_rows, tile_cols = dip_inline.shape
    bin_total = tile_rows * tile_cols
    target = destination[:, 0]
    positions = jnp.arange(held_blocks, dtype=jnp.int32)
    earlier = (target[:, None] == target[None, :]) & (positions[None, :] < positions[:, None])
    ranking = jnp.sum(earlier.astype(jnp.int32), axis=1)
    slot_index = target * capacity + ranking
    slot_range = jnp.arange(devices * capacity, dtype=jnp.int32)
    matches = slot_range[:, None] == slot_index[None, :]
    source = jnp.sum(jnp.where(matches, positions[None, :], 0), axis=1)
    filled = jnp.any(matches, axis=1)
    outgoing = jnp.where(filled[:, None, None], traces[source], 0.0)
    outgoing_bins = jnp.where(filled[:, None], bin_index[source], bin_total)
    outgoing = outgoing.reshape(devices, capacity, block_rows, samples)
    outgoing_bins = outgoing_bins.reshape(devices, capacity, block_rows)
    arrived, arrived_bins = (
        lax.all_to_all(outgoing, ("inline", "crosslin"), split_axis=0, concat_axis=0, tiled=True),
        lax.all_to_all(
            outgoing_bins, ("inline", "crosslin"), split_axis=0, concat_axis=0, tiled=True
        ),
    )
    arrived_rows = arrived.reshape(-1, samples)
    arrived_bins = arrived_bins.reshape(-1)
    member = (jnp.arange(bin_total, dtype=jnp.int32)[:, None] == arrived_bins[None, :]).astype(
        jnp.float32
    )
    summed = jnp.dot(
        member, arrived_rows, precision=lax.Precision.HIGHEST, preferred_element_type=jnp.float32
    )
    fold_count = jnp.sum(member, axis=1)
    stacked = (summed / jnp.maximum(fold_count, 1.0)[:, None]).reshape(
        tile_rows, tile_cols, samples
    )
    first_pass = smooth_inline(stacked, dip_inline)
    second_pass = smooth_cross(first_pass, dip_cross)
    return smooth_inline(second_pass, dip_inline)


def solution(mesh):
    return jax.shard_map(
        on_device,
        mesh=mesh,
        in_specs=(
            P(("inline", "crosslin"), None, None),
            P(("inline", "crosslin"), None),
            P(("inline", "crosslin"), None),
            P("inline", "crosslin"),
            P("inline", "crosslin"),
        ),
        out_specs=P("inline", "crosslin", None),
        check_vma=False,
    )
```

profile of v0, /device:TPU:11, one launch (start us, length us, event | category | flops | bytes accessed | tf_op | source)
XLA Modules:
  0.0 832.1 jit_solution(6084094000723593945)
XLA Ops:
  0.0 1.0 convert_reduce_fusion.1
  1.0 0.7 multiply_add_fusion
  1.7 0.1 select_reduce_fusion
  1.8 0.1 fusion.641
  1.9 0.8 copy.31
  2.7 0.7 gather_fusion
  3.4 0.2 copy.32
  3.7 0.1 broadcast_in_dim.134
  3.8 0.7 broadcast_select_fusion.1
  4.5 6.3 all-to-all-start
  10.8 4.8 gather_fusion.1
  15.6 4.1 broadcast_select_fusion
  19.8 5.9 all-to-all-start.1
  25.7 0.3 copy.33
  25.9 0.1 eq.85
  26.0 0.5 convert_reduce_fusion
  26.5 91.7 %all-to-all-done.1 = f32[32,8,4,1024]{3,2,1,0:T(4,128)} async-done(((f32[32,8,4,1024]{3,2,1,0:T(4,128)}), f32[32,8,4,1024]{3,2,1,0:T(4,128)}, u32[]{:S(2)}, u32[]{:S(2)}) %all-to-all-start.1) | async-done | bytes 4194336 | tf_op jit(solution)/shard_map/all_to_all | solution.py:83
  118.2 5.3 reshape.55
  123.5 9.7 %broadcast_divide_fusion = f32[1024,1024]{1,0:T(8,128)S(1)} fusion(f32[1024]{0:T(1024)S(1)} %broadcast_maximum_fusion, f32[1024,1024]{1,0:T(8,128)} %reshape.55, s32[1024]{0:T(1024)S(1)} %eq.85), kind=kOutput, calls=%fused_computation.1058 | convolution fusion | flops 12886999040 | bytes 8396800 | tf_op jit(solution)/shard_map/dot_general | solution.py:93
  133.2 0.0 copy-start.4
  133.3 0.6 pad_slice_fusion.413
  133.9 3.8 collective-permute-start
  137.7 2.1 collective-permute-start.1
  139.8 3.4 pad.10
  143.2 13.3 %collective-permute-done = f32[7,32,1052]{2,1,0:T(8,128)S(1)} collective-permute-done((f32[7,32,1052]{2,1,0:T(8,128)S(1)}, f32[7,32,1052]{2,1,0:T(8,128)S(1)}, u32[]{:S(2)}, u32[]{:S(2)}) %collective-permute-start) | collective-permute-done | bytes 942624 | tf_op jit(solution)/shard_map/ppermute | solution.py:18
  156.6 6.2 collective-permute-done.1
  162.8 177.3 %fusion.219 = f32[32,32,1024]{2,1,0:T(8,128)} fusion(f32[32,32,1052]{2,1,0:T(8,128)} %pad.10, f32[7,32,1052]{2,1,0:T(8,128)S(1)} %collective-permute-done.1, f32[7,32,1052]{2,1,0:T(8,128)S(1)} %collective-permute-done, f32[32,32,1024]{2,1,0:T(8,128)} %bitcast.10, pred[32,32]{1,0:T(8,128)(4,1)S(1)} %get-tuple-element.19, ...), kind=kLoop, calls=%fused_computation.629 | loop fusion | flops 226492416 | bytes 14587904 | tf_op jit(solution)/shard_map/jit(_where)/select_n | solution.py:42
  340.1 0.0 copy-start.6
  340.1 0.0 copy-start.2
  340.1 2.4 pad_slice_fusion.411
  342.5 0.2 copy.34
  342.7 1.9 collective-permute-start.2
  344.6 0.2 copy.36
  344.8 3.4 collective-permute-start.3
  348.3 3.4 pad.11
  351.7 16.0 %collective-permute-done.2 = f32[32,7,1052]{2,0,1:T(8,128)S(1)} collective-permute-done((f32[32,7,1052]{2,0,1:T(8,128)S(1)}, f32[32,7,1052]{2,0,1:T(8,128)S(1)}, u32[]{:S(2)}, u32[]{:S(2)}) %collective-permute-start.2) | collective-permute-done | bytes 942624 | tf_op jit(solution)/shard_map/ppermute | solution.py:18
  367.8 0.6 copy.35
  368.4 2.1 collective-permute-done.3
  370.5 0.6 copy.37
  371.1 251.4 %fusion.430 = f32[32,32,1024]{2,1,0:T(8,128)} fusion(f32[32,32,1052]{2,1,0:T(8,128)} %pad.11, f32[32,7,1052]{2,1,0:T(8,128)S(1)} %copy.37, f32[32,7,1052]{2,1,0:T(8,128)S(1)} %copy.35, f32[32,32,1024]{2,1,0:T(8,128)} %fusion.219, pred[32,32]{1,0:T(8,128)(4,1)S(1)} %get-tuple-element.14, pred[32,32]{1,0:T(8,128)(4,1)S(1)} %get-tuple-element.15, ...), kind=kLoop, calls=%fused_computation.840 | loop fusion | flops 226492416 | bytes 14587904 | tf_op jit(solution)/shard_map/jit(_where)/select_n | solution.py:42
  622.6 0.0 copy-start.3
  622.6 2.2 pad_slice_fusion.409
  624.8 1.9 collective-permute-start.4
  626.7 2.4 collective-permute-start.5
  629.1 0.0 copy-start.1
  629.1 3.4 pad.12
  632.6 12.9 %collective-permute-done.4 = f32[7,32,1052]{2,1,0:T(8,128)S(1)} collective-permute-done((f32[7,32,1052]{2,1,0:T(8,128)S(1)}, f32[7,32,1052]{2,1,0:T(8,128)S(1)}, u32[]{:S(2)}, u32[]{:S(2)}) %collective-permute-start.4) | collective-permute-done | bytes 942624 | tf_op jit(solution)/shard_map/ppermute | solution.py:18
  645.5 186.1 %fusion.8 = f32[32,32,1024]{2,1,0:T(8,128)} fusion(f32[32,32,1052]{2,1,0:T(8,128)} %pad.12, f32[7,32,1052]{2,1,0:T(8,128)} %collective-permute-done.5, f32[7,32,1052]{2,1,0:T(8,128)S(1)} %collective-permute-done.4, f32[32,32,1024]{2,1,0:T(8,128)} %fusion.430, pred[32,32]{1,0:T(8,128)(4,1)S(1)} %get-tuple-element.19, ...), kind=kLoop, calls=%fused_computation.418 | loop fusion | flops 226492416 | bytes 14587904 | tf_op jit(solution)/shard_map/jit(_where)/select_n | solution.py:42
  (16 shorter events, 0.1 us)
Async XLA Ops:
  0.0 10.8 %copy-start = (f32[128,4,1024]{2,1,0:T(4,128)S(1)}, f32[128,4,1024]{2,1,0:T(4,128)}, u32[]{:S(2)}) copy-start(f32[128,4,1024]{2,1,0:T(4,128)} %param.5) | copy-start | bytes 6291460
  4.5 15.3 %all-to-all-start = ((s32[32,8,4]{1,2,0:T(4,128)}), s32[32,8,4]{1,2,0:T(4,128)S(1)}, u32[]{:S(2)}, u32[]{:S(2)}) async-start(s32[32,8,4]{1,2,0:T(4,128)} %broadcast_select_fusion.1), calls=%async_computation | async-start | bytes 131072 | tf_op jit(solution)/shard_map/all_to_all | solution.py:84
  19.8 98.5 %all-to-all-start.1 = ((f32[32,8,4,1024]{3,2,1,0:T(4,128)}), f32[32,8,4,1024]{3,2,1,0:T(4,128)}, u32[]{:S(2)}, u32[]{:S(2)}) async-start(f32[32,8,4,1024]{3,2,1,0:T(4,128)} %broadcast_select_fusion), calls=%async_computation.1 | async-start | bytes 8388608 | tf_op jit(solution)/shard_map/all_to_all | solution.py:83
  133.2 10.0 %copy-start.4 = (f32[1024,1024]{1,0:T(8,128)}, f32[1024,1024]{1,0:T(8,128)S(1)}, u32[]{:S(2)}) copy-start(f32[1024,1024]{1,0:T(8,128)S(1)} %broadcast_divide_fusion) | copy-start | bytes 12582916
  133.3 6.5 copy-start.5
  133.9 22.7 %collective-permute-start = (f32[7,32,1052]{2,1,0:T(8,128)S(1)}, f32[7,32,1052]{2,1,0:T(8,128)S(1)}, u32[]{:S(2)}, u32[]{:S(2)}) collective-permute-start(f32[7,32,1052]{2,1,0:T(8,128)S(1)} %get-tuple-element.9), channel_id=1, source_target_pairs={{0,4},{4,8},{8,12},{12,16},{16,20},{20,24},{24,28},{1,5},{5,9},{9,... | collective-permute-start | bytes 2827784 | tf_op jit(solution)/shard_map/ppermute | solution.py:18
  137.7 25.1 %collective-permute-start.1 = (f32[7,32,1052]{2,1,0:T(8,128)S(1)}, f32[7,32,1052]{2,1,0:T(8,128)S(1)}, u32[]{:S(2)}, u32[]{:S(2)}) collective-permute-start(f32[7,32,1052]{2,1,0:T(8,128)S(1)} %get-tuple-element.10), channel_id=1, source_target_pairs={{4,0},{8,4},{12,8},{16,12},{20,16},{24,20},{28,24},{5,1},{9,5},{13... | collective-permute-start | bytes 2827784 | tf_op jit(solution)/shard_map/ppermute | solution.py:20
  340.1 8.2 copy-start.6
  340.1 8.2 copy-start.2
  342.7 25.1 %collective-permute-start.2 = (f32[32,7,1052]{2,0,1:T(8,128)S(1)}, f32[32,7,1052]{2,0,1:T(8,128)S(1)}, u32[]{:S(2)}, u32[]{:S(2)}) collective-permute-start(f32[32,7,1052]{2,0,1:T(8,128)S(1)} %copy.34), channel_id=1, source_target_pairs={{0,1},{1,2},{2,3},{4,5},{5,6},{6,7},{8,9},{9,10},{10,11},{12,13},{... | collective-permute-start | bytes 2827784 | tf_op jit(solution)/shard_map/ppermute | solution.py:18
  344.8 25.7 %collective-permute-start.3 = (f32[32,7,1052]{2,0,1:T(8,128)S(1)}, f32[32,7,1052]{2,0,1:T(8,128)S(1)}, u32[]{:S(2)}, u32[]{:S(2)}) collective-permute-start(f32[32,7,1052]{2,0,1:T(8,128)S(1)} %copy.36), channel_id=1, source_target_pairs={{1,0},{2,1},{3,2},{5,4},{6,5},{7,6},{9,8},{10,9},{11,10},{13,12},{... | collective-permute-start | bytes 2827784 | tf_op jit(solution)/shard_map/ppermute | solution.py:20
  622.6 6.6 copy-start.3
  624.8 20.7 %collective-permute-start.4 = (f32[7,32,1052]{2,1,0:T(8,128)S(1)}, f32[7,32,1052]{2,1,0:T(8,128)S(1)}, u32[]{:S(2)}, u32[]{:S(2)}) collective-permute-start(f32[7,32,1052]{2,1,0:T(8,128)S(1)} %get-tuple-element.5), channel_id=1, source_target_pairs={{0,4},{4,8},{8,12},{12,16},{16,20},{20,24},{24,28},{1,5},{5,9},{9,... | collective-permute-start | bytes 2827784 | tf_op jit(solution)/shard_map/ppermute | solution.py:18
  626.7 18.8 %collective-permute-start.5 = (f32[7,32,1052]{2,1,0:T(8,128)S(1)}, f32[7,32,1052]{2,1,0:T(8,128)}, u32[]{:S(2)}, u32[]{:S(2)}) collective-permute-start(f32[7,32,1052]{2,1,0:T(8,128)S(1)} %get-tuple-element.6), channel_id=1, source_target_pairs={{4,0},{8,4},{12,8},{16,12},{20,16},{24,20},{28,24},{5,1},{9,5},{13... | collective-permute-start | bytes 2827784 | tf_op jit(solution)/shard_map/ppermute | solution.py:20
  629.1 202.5 %copy-start.1 = (f32[128,4,1024]{2,1,0:T(4,128)S(1)}, f32[128,4,1024]{2,1,0:T(4,128)}, u32[]{:S(2)}) copy-start(f32[128,4,1024]{2,1,0:T(4,128)} %param.5) | copy-start | bytes 6291460
where the time goes:
time: 847 us; the launch traced here: 832 us
  other arithmetic  622 us (73%)
  waiting for transfers between devices  142 us (17%)
  local copies, waits for them, and re-layouts  29.4 us (3%)
  starting transfers between devices  27.8 us (3%)
  matrix products  9.71 us (1%)
    select_n x3, other arithmetic, steer(): result = jnp.where((dip_index == dip_value)[..., None], running, result)  615 us
    all_to_all x1, waiting for transfers between devices, on_device(): lax.all_to_all(outgoing, ('inline', 'crosslin'), split_axis=0, concat_axi...  91.7 us
    ppermute x3, waiting for transfers between devices, padded_2(): lax.ppermute(tail, axis, [(i, (i + 1) % count) for i in range(ends)])  42.3 us
  transfers between devices with their start and end apart: 8, of which 6 were waited for; matrix products, arithmetic and copies ran while one was open for 3% of the time, Pallas kernels for 0%

commit v1 on v0

v1 whole, which is shorter than its diff:
```python
import functools

import jax
import jax.numpy as jnp
from jax import lax
from jax.experimental import pallas as pl
from jax.experimental.pallas import tpu as pltpu
from jax.sharding import PartitionSpec as P

HALF = 7
LANES = 128
SUB = 8


def weight(offset):
    return (HALF + 1 - abs(offset)) / float((HALF + 1) ** 2)


def take_lanes(cells, index):
    return jnp.take_along_axis(cells, index, axis=1, mode="promise_in_bounds")


def steer_kernel(dip_ref, low_ref, own_ref, high_ref, out_ref, rows_ref, *, swap):
    tiles, extent = own_ref.shape[:2]
    rows_ref[:, 0:HALF] = low_ref[...]
    rows_ref[:, HALF : HALF + extent] = own_ref[...]
    rows_ref[:, HALF + extent :] = high_ref[...]
    lane = lax.broadcasted_iota(jnp.int32, (SUB, LANES), 1)
    nothing = jnp.zeros((SUB, LANES), jnp.float32)

    def one_row(row, _):
        dip = dip_ref[row]
        upward = dip > 0
        totals = [weight(0) * rows_ref[t, row + HALF] for t in range(tiles)]
        for offset in range(1, HALF + 1):
            moved = dip * offset
            pair = []
            for side, shift in ((1, moved), (-1, -moved)):
                index = (lane + shift) & (LANES - 1)
                outside = (lane < shift) | (lane >= LANES + shift)
                row_tiles = [rows_ref[t, row + HALF + side * offset] for t in range(tiles)]
                shifted = []
                for t in range(tiles):
                    before = row_tiles[t - 1] if t > 0 else nothing
                    after = row_tiles[t + 1] if t + 1 < tiles else nothing
                    if side > 0:
                        beside = jnp.where(upward, after, before)
                    else:
                        beside = jnp.where(upward, before, after)
                    merged = jnp.where(outside, beside, row_tiles[t])
                    shifted.append(take_lanes(merged, index))
                pair.append(shifted)
            for t in range(tiles):
                totals[t] = totals[t] + weight(offset) * (pair[0][t] + pair[1][t])
        for t in range(tiles):
            if swap:
                out_ref[t, pl.ds(row, SUB, stride=extent), :] = totals[t]
            else:
                out_ref[row, :, pl.ds(t * LANES, LANES)] = totals[t]
        return 0

    lax.fori_loop(0, extent, one_row, 0)


def steer(low, own, high, dip, swap):
    tiles, extent, across, _ = own.shape
    dip_lanes = jnp.broadcast_to(dip[:, :, None], (extent, across, LANES))
    if swap:
        out_shape = jax.ShapeDtypeStruct((tiles, across * extent, LANES), jnp.float32)
        out_spec = pl.BlockSpec((tiles, SUB * extent, LANES), lambda i: (0, i, 0))
    else:
        out_shape = jax.ShapeDtypeStruct((extent, across, tiles * LANES), jnp.float32)
        out_spec = pl.BlockSpec((extent, SUB, tiles * LANES), lambda i: (0, i, 0))
    result = pl.pallas_call(
        functools.partial(steer_kernel, swap=swap),
        grid=(across // SUB,),
        in_specs=[
            pl.BlockSpec((extent, SUB, LANES), lambda i: (0, i, 0)),
            pl.BlockSpec((tiles, HALF, SUB, LANES), lambda i: (0, 0, i, 0)),
            pl.BlockSpec((tiles, extent, SUB, LANES), lambda i: (0, 0, i, 0)),
            pl.BlockSpec((tiles, HALF, SUB, LANES), lambda i: (0, 0, i, 0)),
        ],
        out_specs=out_spec,
        out_shape=out_shape,
        scratch_shapes=[pltpu.VMEM((tiles, extent + 2 * HALF, SUB, LANES), jnp.float32)],
        compiler_params=pltpu.CompilerParams(vmem_limit_bytes=32 * 2**20),
        cost_estimate=pl.CostEstimate(
            flops=60 * extent * across * tiles * LANES,
            bytes_accessed=8 * extent * across * tiles * LANES,
            transcendentals=0,
        ),
    )(dip_lanes, low, own, high)
    if swap:
        result = result.reshape(tiles, across, extent, LANES)
    return result


def ends(cells, axis):
    count = lax.axis_size(axis)
    tail = cells[:, cells.shape[1] - HALF :]
    head = cells[:, :HALF]
    low = lax.ppermute(tail, axis, [(i, i + 1) for i in range(count - 1)])
    high = lax.ppermute(head, axis, [(i + 1, i) for i in range(count - 1)])
    return low, high


def on_device(traces, destination, bin_index, dip_inline, dip_cross):
    held_blocks, block_rows, samples = traces.shape
    rows_inline = lax.axis_size("inline")
    cols_cross = lax.axis_size("crosslin")
    devices = rows_inline * cols_cross
    capacity = 2 * held_blocks // devices
    tile_rows, tile_cols = dip_inline.shape
    bin_total = tile_rows * tile_cols
    target = destination[:, 0]
    positions = jnp.arange(held_blocks, dtype=jnp.int32)
    earlier = (target[:, None] == target[None, :]) & (positions[None, :] < positions[:, None])
    ranking = jnp.sum(earlier.astype(jnp.int32), axis=1)
    slot_index = target * capacity + ranking
    slot_range = jnp.arange(devices * capacity, dtype=jnp.int32)
    matches = slot_range[:, None] == slot_index[None, :]
    source = jnp.sum(jnp.where(matches, positions[None, :], 0), axis=1)
    filled = jnp.any(matches, axis=1)
    outgoing = jnp.where(filled[:, None, None], traces[source], 0.0)
    outgoing_bins = jnp.where(filled[:, None], bin_index[source], bin_total)
    outgoing = outgoing.reshape(devices, capacity, block_rows, samples)
    outgoing_bins = outgoing_bins.reshape(devices, capacity, block_rows)
    arrived, arrived_bins = (
        lax.all_to_all(outgoing, ("inline", "crosslin"), split_axis=0, concat_axis=0, tiled=True),
        lax.all_to_all(
            outgoing_bins, ("inline", "crosslin"), split_axis=0, concat_axis=0, tiled=True
        ),
    )
    arrived_rows = arrived.reshape(-1, samples)
    arrived_bins = arrived_bins.reshape(-1)
    member = (jnp.arange(bin_total, dtype=jnp.int32)[:, None] == arrived_bins[None, :]).astype(
        jnp.float32
    )
    summed = jnp.dot(
        member, arrived_rows, precision=lax.Precision.HIGHEST, preferred_element_type=jnp.float32
    )
    fold_count = jnp.sum(member, axis=1)
    stacked = (summed / jnp.maximum(fold_count, 1.0)[:, None]).reshape(
        tile_rows, tile_cols, samples
    )
    stacked = jnp.moveaxis(stacked.reshape(tile_rows, tile_cols, -1, LANES), 2, 0)
    low, high = ends(stacked, "inline")
    first_pass = steer(low, stacked, high, dip_inline, True)
    low, high = ends(first_pass, "crosslin")
    second_pass = steer(low, first_pass, high, dip_cross.T, True)
    low, high = ends(second_pass, "inline")
    return steer(low, second_pass, high, dip_inline, False)


def solution(mesh):
    return jax.shard_map(
        on_device,
        mesh=mesh,
        in_specs=(
            P(("inline", "crosslin"), None, None),
            P(("inline", "crosslin"), None),
            P(("inline", "crosslin"), None),
            P("inline", "crosslin"),
            P("inline", "crosslin"),
        ),
        out_specs=P("inline", "crosslin", None),
        check_vma=False,
    )
```

time: 847 us -> 317 us (0.37); the launches traced: 832 us -> 315 us
  other arithmetic: 622 us -> 7.2 us
  Pallas kernels: 0 us -> 99.7 us
    select_n x3 -> x0, other arithmetic: 615 us -> none  [steer(): result = jnp.where((dip_index == dip_value)[..., None], running, result)]
    pallas_call x0 -> x3, Pallas kernels: none -> 99.7 us  [steer(): pl.pallas_call(functools.partial(steer_kernel, swap=swap), grid=(across /...]
    pad x3 -> x0, local copies, waits for them, and re-layouts: 10.3 us -> none  [pad_time(): return jnp.pad(gridded, ((0, 0), (0, 0), (margin, margin)))]
where the time goes in v1:
time: 317 us; the launch traced here: 315 us
  waiting for transfers between devices  145 us (46%)
  Pallas kernels  99.7 us (31%)
  starting transfers between devices  32.6 us (10%)
  local copies, waits for them, and re-layouts  21.3 us (7%)
  matrix products  9.72 us (3%)
  other arithmetic  7.2 us (2%)
    pallas_call x3, Pallas kernels, steer(): pl.pallas_call(functools.partial(steer_kernel, swap=swap), grid=(across /...  99.7 us
    all_to_all x1, waiting for transfers between devices, on_device(): lax.all_to_all(outgoing, ('inline', 'crosslin'), split_axis=0, concat_axi...  91.7 us
    ppermute x3, waiting for transfers between devices, ends(): high = lax.ppermute(head, axis, [(i + 1, i) for i in range(count - 1)])  48.4 us
    ppermute x3, starting transfers between devices, ends(): low = lax.ppermute(tail, axis, [(i, i + 1) for i in range(count - 1)])  10.8 us
    dot_general x1, matrix products, on_device(): jnp.dot(member, arrived_rows, precision=lax.Precision.HIGHEST, preferred_...  9.72 us
    ppermute x3, starting transfers between devices, ends(): high = lax.ppermute(head, axis, [(i + 1, i) for i in range(count - 1)])  9.54 us
  transfers between devices with their start and end apart: 8, of which 6 were waited for; matrix products, arithmetic and copies ran while one was open for 3% of the time, Pallas kernels for 0%

profile of v1, /device:TPU:11, one launch (start us, length us, event | category | flops | bytes accessed | tf_op | source)
XLA Modules:
  0.0 315.2 jit_solution(9344440630921487914)
XLA Ops:
  0.0 0.0 copy-start
  0.0 1.0 convert_reduce_fusion.1
  1.0 0.7 multiply_add_fusion
  1.7 0.1 fusion.2
  1.8 0.1 select_reduce_fusion
  1.9 0.1 broadcast_in_dim.44
  2.0 0.8 copy.17
  2.8 0.7 gather_fusion
  3.5 0.3 copy.18
  3.8 0.7 broadcast_select_fusion.1
  4.5 6.3 %all-to-all-start = ((s32[32,8,4]{1,2,0:T(4,128)}), s32[32,8,4]{1,2,0:T(4,128)S(1)}, u32[]{:S(2)}, u32[]{:S(2)}) async-start(s32[32,8,4]{1,2,0:T(4,128)} %broadcast_select_fusion.1), calls=%async_computation | async-start | bytes 131072 | tf_op jit(solution)/shard_map/all_to_all | solution.py:130
  10.8 4.8 %gather_fusion.1 = f32[256,4,1024]{2,1,0:T(4,128)} fusion(f32[128,4,1024]{2,1,0:T(4,128)S(1)} %copy-done, s32[1024]{0:T(1024)S(1)} %pad_clamp_fusion), kind=kCustom, calls=%fused_computation.1 | custom fusion | bytes 8389632 | tf_op jit(solution)/shard_map/gather | solution.py:124
  15.6 4.1 %broadcast_select_fusion = f32[32,8,4,1024]{3,2,1,0:T(4,128)} fusion(f32[32,8,4,1024]{3,2,1,0:T(4,128)} %bitcast.24, pred[32,8]{1,0:T(8,128)(4,1)S(1)} %broadcast_in_dim.44), kind=kLoop, calls=%fused_computation.7 | loop fusion | flops 1048576 | bytes 8388864 | tf_op jit(solution)/shard_map/jit(_where)/select_n | solution.py:124
  19.8 0.0 all-to-all-done
  19.8 5.9 %all-to-all-start.1 = ((f32[32,8,4,1024]{3,2,1,0:T(4,128)}), f32[32,8,4,1024]{3,2,1,0:T(4,128)}, u32[]{:S(2)}, u32[]{:S(2)}) async-start(f32[32,8,4,1024]{3,2,1,0:T(4,128)} %broadcast_select_fusion), calls=%async_computation.1 | async-start | bytes 8388608 | tf_op jit(solution)/shard_map/all_to_all | solution.py:129
  25.7 0.3 copy.19
  25.9 0.1 eq.48
  26.0 0.5 convert_reduce_fusion
  26.5 91.7 %all-to-all-done.1 = f32[32,8,4,1024]{3,2,1,0:T(4,128)} async-done(((f32[32,8,4,1024]{3,2,1,0:T(4,128)}), f32[32,8,4,1024]{3,2,1,0:T(4,128)}, u32[]{:S(2)}, u32[]{:S(2)}) %all-to-all-start.1) | async-done | bytes 4194336 | tf_op jit(solution)/shard_map/all_to_all | solution.py:129
  118.2 5.3 %reshape.50 = f32[1024,1024]{1,0:T(8,128)} reshape(f32[32,8,4,1024]{3,2,1,0:T(4,128)} %all-to-all-done.1) | data formatting | bytes 8388608 | tf_op jit(solution)/shard_map/reshape | solution.py:134
  123.5 9.7 %divide_bitcast_fusion = f32[128,8,8,128]{3,1,2,0:T(8,128)S(1)} fusion(f32[1024]{0:T(1024)S(1)} %broadcast_maximum_fusion, f32[1024,1024]{1,0:T(8,128)} %reshape.50, s32[1024]{0:T(1024)S(1)} %eq.48), kind=kOutput, calls=%fused_computation.3 | convolution fusion | flops 12886999040 | bytes 8396800 | tf_op jit(solution)/shard_map/dot_general | solution.py:139
  133.2 1.0 copy.21
  134.3 0.0 copy-start.3
  134.3 0.8 copy.23
  135.1 0.2 fusion.6
  135.3 3.6 %collective-permute-start.1 = (f32[8,7,32,128]{3,2,1,0:T(8,128)S(1)}, f32[8,7,32,128]{3,2,1,0:T(8,128)S(1)}, u32[]{:S(2)}, u32[]{:S(2)}) collective-permute-start(f32[8,7,32,128]{3,2,1,0:T(8,128)S(1)} %get-tuple-element.9), channel_id=1, source_target_pairs={{4,0},{8,4},{12,8},{16,12},{20,16},{24,20},{28,24},{5,1},{9,5},{13... | collective-permute-start | bytes 2752520 | tf_op jit(solution)/shard_map/ppermute | solution.py:103
  138.9 3.1 collective-permute-start
  141.9 15.3 %collective-permute-done.1.high_ref = f32[8,7,32,128]{3,2,1,0:T(8,128)S(1)} collective-permute-done((f32[8,7,32,128]{3,2,1,0:T(8,128)S(1)}, f32[8,7,32,128]{3,2,1,0:T(8,128)S(1)}, u32[]{:S(2)}, u32[]{:S(2)}) %collective-permute-start.1) | collective-permute-done | bytes 917536 | tf_op jit(solution)/shard_map/ppermute | solution.py:103
  157.3 2.4 collective-permute-done.low_ref
  159.7 0.2 broadcast_in_dim.42.dip_ref
  159.9 33.6 %shard_map.55 = f32[8,1024,128]{2,1,0:T(8,128)S(1)} custom-call(s32[32,32,128]{2,1,0:T(8,128)S(1)} %broadcast_in_dim.42.dip_ref, f32[8,7,32,128]{3,2,1,0:T(8,128)S(1)} %collective-permute-done.low_ref, f32[8,32,32,128]{3,2,1,0:T(8,128)S(1)} %bitcast.18, f32[8,7,32,128]{3,2,1,0:T(8,128)S(1)} %collective-permute-done.1.high_ref), custom_call_target="tpu_custom_call" | custom-call | flops 62914560 | bytes 8388608 | tf_op jit(solution)/shard_map/pallas_call | solution.py:74
  193.4 1.4 fusion.5
  194.9 2.0 copy-done.1
  196.9 4.0 %collective-permute-start.3 = (f32[8,7,32,128]{3,2,1,0:T(8,128)}, f32[8,7,32,128]{3,2,1,0:T(8,128)S(1)}, u32[]{:S(2)}, u32[]{:S(2)}) collective-permute-start(f32[8,7,32,128]{3,2,1,0:T(8,128)} %get-tuple-element.7), channel_id=1, source_target_pairs={{1,0},{2,1},{3,2},{5,4},{6,5},{7,6},{9,8},{10,9},{11,10},{13,12},{... | collective-permute-start | bytes 2752520 | tf_op jit(solution)/shard_map/ppermute | solution.py:103
  200.9 1.9 collective-permute-start.2
  202.8 0.8 copy.16
  203.6 15.9 %collective-permute-done.3.high_ref = f32[8,7,32,128]{3,2,1,0:T(8,128)S(1)} collective-permute-done((f32[8,7,32,128]{3,2,1,0:T(8,128)}, f32[8,7,32,128]{3,2,1,0:T(8,128)S(1)}, u32[]{:S(2)}, u32[]{:S(2)}) %collective-permute-start.3) | collective-permute-done | bytes 917536 | tf_op jit(solution)/shard_map/ppermute | solution.py:103
  219.6 2.0 collective-permute-done.2.low_ref
  221.6 0.2 broadcast_in_dim.43.dip_ref
  221.8 0.0 copy-start.2
  221.8 2.2 copy-done.2
  224.0 34.0 %shard_map.56 = f32[8,1024,128]{2,1,0:T(8,128)S(1)} custom-call(s32[32,32,128]{2,1,0:T(8,128)S(1)} %broadcast_in_dim.43.dip_ref, f32[8,7,32,128]{3,2,1,0:T(8,128)} %collective-permute-done.2.low_ref, f32[8,32,32,128]{3,2,1,0:T(8,128)S(1)} %bitcast.20, f32[8,7,32,128]{3,2,1,0:T(8,128)S(1)} %collective-permute-done.3.high_ref), custom_call_target="tpu_custom_call" | custom-call | flops 62914560 | bytes 8388608 | tf_op jit(solution)/shard_map/pallas_call | solution.py:74
  258.0 0.2 fusion.4
  258.2 1.9 collective-permute-start.5
  260.1 5.8 %collective-permute-start.4 = (f32[8,7,32,128]{3,2,1,0:T(8,128)S(1)}, f32[8,7,32,128]{3,2,1,0:T(8,128)S(1)}, u32[]{:S(2)}, u32[]{:S(2)}) collective-permute-start(f32[8,7,32,128]{3,2,1,0:T(8,128)S(1)} %get-tuple-element.6), channel_id=1, source_target_pairs={{0,4},{4,8},{8,12},{12,16},{16,20},{20,24},{24,28},{1,5},{5,9},{9,... | collective-permute-start | bytes 2752520 | tf_op jit(solution)/shard_map/ppermute | solution.py:102
  265.9 17.2 %collective-permute-done.5.high_ref = f32[8,7,32,128]{3,2,1,0:T(8,128)S(1)} collective-permute-done((f32[8,7,32,128]{3,2,1,0:T(8,128)S(1)}, f32[8,7,32,128]{3,2,1,0:T(8,128)S(1)}, u32[]{:S(2)}, u32[]{:S(2)}) %collective-permute-start.5) | collective-permute-done | bytes 917536 | tf_op jit(solution)/shard_map/ppermute | solution.py:103
  283.1 0.0 collective-permute-done.4.low_ref
  283.1 32.1 %shard_map.57 = f32[32,32,1024]{2,1,0:T(8,128)} custom-call(s32[32,32,128]{2,1,0:T(8,128)S(1)} %broadcast_in_dim.42.dip_ref, f32[8,7,32,128]{3,2,1,0:T(8,128)S(1)} %collective-permute-done.4.low_ref, f32[8,32,32,128]{3,2,1,0:T(8,128)S(1)} %bitcast.22, f32[8,7,32,128]{3,2,1,0:T(8,128)S(1)} %collective-permute-done.5.high_ref), custom_call_target="tpu_custom_call" | custom-call | flops 62914560 | bytes 8388608 | tf_op jit(solution)/shard_map/pallas_call | solution.py:74
  (6 shorter events, 0.0 us)
Async XLA Ops:
  0.0 10.8 %copy-start = (f32[128,4,1024]{2,1,0:T(4,128)S(1)}, f32[128,4,1024]{2,1,0:T(4,128)}, u32[]{:S(2)}) copy-start(f32[128,4,1024]{2,1,0:T(4,128)} %param.5) | copy-start | bytes 6291460
  4.5 15.3 %all-to-all-start = ((s32[32,8,4]{1,2,0:T(4,128)}), s32[32,8,4]{1,2,0:T(4,128)S(1)}, u32[]{:S(2)}, u32[]{:S(2)}) async-start(s32[32,8,4]{1,2,0:T(4,128)} %broadcast_select_fusion.1), calls=%async_computation | async-start | bytes 131072 | tf_op jit(solution)/shard_map/all_to_all | solution.py:130
  19.8 98.5 %all-to-all-start.1 = ((f32[32,8,4,1024]{3,2,1,0:T(4,128)}), f32[32,8,4,1024]{3,2,1,0:T(4,128)}, u32[]{:S(2)}, u32[]{:S(2)}) async-start(f32[32,8,4,1024]{3,2,1,0:T(4,128)} %broadcast_select_fusion), calls=%async_computation.1 | async-start | bytes 8388608 | tf_op jit(solution)/shard_map/all_to_all | solution.py:129
  134.3 25.4 %copy-start.3 = (s32[32,32]{1,0:T(8,128)S(1)}, s32[32,32]{1,0:T(8,128)}, u32[]{:S(2)}) copy-start(s32[32,32]{1,0:T(8,128)} %param.8) | copy-start | bytes 12292
  135.3 22.0 %collective-permute-start.1 = (f32[8,7,32,128]{3,2,1,0:T(8,128)S(1)}, f32[8,7,32,128]{3,2,1,0:T(8,128)S(1)}, u32[]{:S(2)}, u32[]{:S(2)}) collective-permute-start(f32[8,7,32,128]{3,2,1,0:T(8,128)S(1)} %get-tuple-element.9), channel_id=1, source_target_pairs={{4,0},{8,4},{12,8},{16,12},{20,16},{24,20},{28,24},{5,1},{9,5},{13... | collective-permute-start | bytes 2752520 | tf_op jit(solution)/shard_map/ppermute | solution.py:103
  138.9 20.8 %collective-permute-start = (f32[8,7,32,128]{3,2,1,0:T(8,128)S(1)}, f32[8,7,32,128]{3,2,1,0:T(8,128)S(1)}, u32[]{:S(2)}, u32[]{:S(2)}) collective-permute-start(f32[8,7,32,128]{3,2,1,0:T(8,128)S(1)} %get-tuple-element.10), channel_id=1, source_target_pairs={{0,4},{4,8},{8,12},{12,16},{16,20},{20,24},{24,28},{1,5},{5,9},{9,... | collective-permute-start | bytes 2752520 | tf_op jit(solution)/shard_map/ppermute | solution.py:102
  194.9 2.0 copy-start.1
  196.9 22.7 %collective-permute-start.3 = (f32[8,7,32,128]{3,2,1,0:T(8,128)}, f32[8,7,32,128]{3,2,1,0:T(8,128)S(1)}, u32[]{:S(2)}, u32[]{:S(2)}) collective-permute-start(f32[8,7,32,128]{3,2,1,0:T(8,128)} %get-tuple-element.7), channel_id=1, source_target_pairs={{1,0},{2,1},{3,2},{5,4},{6,5},{7,6},{9,8},{10,9},{11,10},{13,12},{... | collective-permute-start | bytes 2752520 | tf_op jit(solution)/shard_map/ppermute | solution.py:103
  200.9 20.7 %collective-permute-start.2 = (f32[8,7,32,128]{3,2,1,0:T(8,128)}, f32[8,7,32,128]{3,2,1,0:T(8,128)}, u32[]{:S(2)}, u32[]{:S(2)}) collective-permute-start(f32[8,7,32,128]{3,2,1,0:T(8,128)} %get-tuple-element.8), channel_id=1, source_target_pairs={{0,1},{1,2},{2,3},{4,5},{5,6},{6,7},{8,9},{9,10},{10,11},{12,13},{... | collective-permute-start | bytes 2752520 | tf_op jit(solution)/shard_map/ppermute | solution.py:102
  221.8 2.2 copy-start.2
  258.2 24.9 %collective-permute-start.5 = (f32[8,7,32,128]{3,2,1,0:T(8,128)S(1)}, f32[8,7,32,128]{3,2,1,0:T(8,128)S(1)}, u32[]{:S(2)}, u32[]{:S(2)}) collective-permute-start(f32[8,7,32,128]{3,2,1,0:T(8,128)S(1)} %get-tuple-element.5), channel_id=1, source_target_pairs={{4,0},{8,4},{12,8},{16,12},{20,16},{24,20},{28,24},{5,1},{9,5},{13... | collective-permute-start | bytes 2752520 | tf_op jit(solution)/shard_map/ppermute | solution.py:103
  260.1 23.0 %collective-permute-start.4 = (f32[8,7,32,128]{3,2,1,0:T(8,128)S(1)}, f32[8,7,32,128]{3,2,1,0:T(8,128)S(1)}, u32[]{:S(2)}, u32[]{:S(2)}) collective-permute-start(f32[8,7,32,128]{3,2,1,0:T(8,128)S(1)} %get-tuple-element.6), channel_id=1, source_target_pairs={{0,4},{4,8},{8,12},{12,16},{16,20},{20,24},{24,28},{1,5},{5,9},{9,... | collective-permute-start | bytes 2752520 | tf_op jit(solution)/shard_map/ppermute | solution.py:102

commit v2 on v0

v2 whole, which is shorter than its diff:
```python
import functools

import jax
import jax.numpy as jnp
from jax import lax
from jax.experimental import pallas as pl
from jax.experimental.pallas import tpu as pltpu
from jax.sharding import PartitionSpec as P

HALF = 7
DMAX = 2
LANES = 128
PHASES = 8
LINES = 8
REACH = -(-HALF * DMAX // PHASES)
SPAN = (2 * REACH + 1) * PHASES
BOTH = ("inline", "crosslin")


def weight(offset):
    return (HALF + 1 - abs(offset)) / float((HALF + 1) ** 2)


def fill_interleave(table_ref, time_dim):
    size = table_ref.shape[0]
    time = lax.broadcasted_iota(jnp.int32, (size, size), time_dim)
    place = lax.broadcasted_iota(jnp.int32, (size, size), 1 - time_dim)
    hit = time == (place & (LANES - 1)) * PHASES + place // LANES
    table_ref[...] = jnp.where(hit, 1.0, 0.0).astype(jnp.bfloat16)


def move_samples(rows, table_ref):
    upper = rows.astype(jnp.bfloat16)
    rest = (rows - upper.astype(jnp.float32)).astype(jnp.bfloat16)
    table = table_ref[...]
    moved = jnp.dot(upper, table, preferred_element_type=jnp.float32)
    return moved + jnp.dot(rest, table, preferred_element_type=jnp.float32)


def pack_kernel(target_ref, traces_ref, out_ref, table_ref, tiles_ref, used_ref, sem, *, capacity):
    held, block_rows, samples = traces_ref.shape
    devices = used_ref.shape[0]
    block_span = block_rows * PHASES
    group = 32
    fill_interleave(table_ref, 0)

    def clear(device, _):
        used_ref[device] = 0
        return 0

    lax.fori_loop(0, devices, clear, 0)

    def one_group(g, _):
        rows = traces_ref[pl.ds(g * group, group)].reshape(group * block_rows, samples)
        moved = move_samples(rows, table_ref)
        for eight in range(group * block_rows // 8):
            for phase in range(PHASES):
                tiles_ref[
                    pl.ds(g * group * block_span + eight * 8 * PHASES + phase, 8, stride=PHASES), :
                ] = moved[eight * 8 : eight * 8 + 8, phase * LANES : (phase + 1) * LANES]

        def send_block(i, _):
            block = g * group + i
            device = target_ref[block]
            rank = used_ref[device]
            used_ref[device] = rank + 1
            pltpu.make_async_copy(
                tiles_ref.at[pl.ds(block * block_span, block_span), :],
                out_ref.at[device * capacity + rank],
                sem,
            ).start()
            return 0

        lax.fori_loop(0, group, send_block, 0)
        return 0

    lax.fori_loop(0, held // group, one_group, 0)
    pltpu.make_async_copy(tiles_ref, tiles_ref, sem).wait()


def pack(traces, target, devices, capacity):
    held, block_rows, samples = traces.shape
    return pl.pallas_call(
        functools.partial(pack_kernel, capacity=capacity),
        in_specs=[
            pl.BlockSpec(memory_space=pltpu.SMEM),
            pl.BlockSpec(memory_space=pltpu.VMEM),
        ],
        out_specs=pl.BlockSpec(memory_space=pl.ANY),
        out_shape=jax.ShapeDtypeStruct(
            (devices * capacity, block_rows * PHASES, LANES), jnp.float32
        ),
        scratch_shapes=[
            pltpu.VMEM((samples, samples), jnp.bfloat16),
            pltpu.VMEM((held * block_rows * PHASES, LANES), jnp.float32),
            pltpu.SMEM((devices,), jnp.int32),
            pltpu.SemaphoreType.DMA,
        ],
        compiler_params=pltpu.CompilerParams(vmem_limit_bytes=32 * 2**20),
    )(target, traces)


def bin_kernel(bins_ref, scale_ref, blocks_ref, out_ref, even_ref, odd_ref):
    step = pl.program_id(0)
    slots, block_span, _ = blocks_ref.shape
    block_rows = block_span // PHASES
    bin_total = out_ref.shape[0]
    unroll = 8

    @pl.when(step == 0)
    def _():
        def clear(i, _):
            for j in range(unroll):
                even_ref[i * unroll + j] = jnp.zeros((PHASES, LANES), jnp.float32)
                odd_ref[i * unroll + j] = jnp.zeros((PHASES, LANES), jnp.float32)
            return 0

        lax.fori_loop(0, bin_total // unroll, clear, 0)

    def add_slot(slot, _):
        first = (step * slots + slot) * block_rows
        for j in range(block_rows):
            total_ref = odd_ref if j % 2 else even_ref
            place = bins_ref[first + j]
            total_ref[place] += blocks_ref[slot, j * PHASES : (j + 1) * PHASES]
        return 0

    lax.fori_loop(0, slots, add_slot, 0)

    @pl.when(step == pl.num_programs(0) - 1)
    def _():
        def finish(i, _):
            for j in range(unroll):
                place = i * unroll + j
                out_ref[place] = (even_ref[place] + odd_ref[place]) * scale_ref[place]
            return 0

        lax.fori_loop(0, bin_total // unroll, finish, 0)


def stack_bins(blocks, bins, scale):
    slots, block_span, _ = blocks.shape
    bin_total = scale.shape[0]
    steps = 8
    return pl.pallas_call(
        bin_kernel,
        grid=(steps,),
        in_specs=[
            pl.BlockSpec(memory_space=pltpu.SMEM),
            pl.BlockSpec(memory_space=pltpu.SMEM),
            pl.BlockSpec((slots // steps, block_span, LANES), lambda i: (i, 0, 0)),
        ],
        out_specs=pl.BlockSpec((bin_total, PHASES, LANES), lambda i: (0, 0, 0)),
        out_shape=jax.ShapeDtypeStruct((bin_total, PHASES, LANES), jnp.float32),
        scratch_shapes=[
            pltpu.VMEM((bin_total + 8, PHASES, LANES), jnp.float32),
            pltpu.VMEM((bin_total + 8, PHASES, LANES), jnp.float32),
        ],
        compiler_params=pltpu.CompilerParams(vmem_limit_bytes=40 * 2**20),
    )(bins, scale, blocks)


def steer_line(dip_of, cell_of, put, extent, spread_ref):
    lane = lax.broadcasted_iota(jnp.int32, (PHASES, LANES), 1)
    for place in range(extent + 2 * HALF):
        cell = cell_of(place)
        for reach in range(-REACH, REACH + 1):
            moved = cell
            if reach:
                moved = pltpu.roll(cell, (-reach) % LANES, axis=1)
                inside = lane < LANES - reach if reach > 0 else lane >= -reach
                moved = jnp.where(inside, moved, 0.0)
            spread_ref[pl.ds(place * SPAN + (reach + REACH) * PHASES, PHASES), :] = moved
    for place in range(extent):
        dip = dip_of(place)
        centre = (place + HALF) * SPAN + REACH * PHASES

        def tap(offset):
            return spread_ref[pl.ds(centre + offset * SPAN + dip * offset, PHASES), :]

        total = weight(0) * tap(0)
        for offset in range(1, HALF + 1):
            total = total + weight(offset) * (tap(offset) + tap(-offset))
        put(place, total)


def steer_kernel(dip_ref, low_ref, own_ref, high_ref, out_ref, spread_a, spread_b, *more, along):
    extent = own_ref.shape[along]
    start = pl.program_id(0) * LINES
    final = len(more) > 0
    if final:
        staged_ref, table_ref = more

        @pl.when(pl.program_id(0) == 0)
        def _():
            fill_interleave(table_ref, 1)

    def at(place, line):
        return (place, line) if along == 0 else (line, place)

    def one_line(line, spread_ref):
        def cell_of(place):
            if place < HALF:
                return low_ref[at(place, line)]
            if place < HALF + extent:
                return own_ref[at(place - HALF, line)]
            return high_ref[at(place - HALF - extent, line)]

        def put(place, value):
            if final:
                staged_ref[pl.ds((place * LINES + line) * PHASES, PHASES), :] = value
            else:
                out_ref[at(place, line)] = value

        steer_line(lambda place: dip_ref[at(place, start + line)], cell_of, put, extent, spread_ref)

    def two_lines(i, _):
        one_line(2 * i, spread_a)
        one_line(2 * i + 1, spread_b)
        return 0

    lax.fori_loop(0, LINES // 2, two_lines, 0)
    if final:
        rows = jnp.concatenate(
            [
                jnp.concatenate(
                    [
                        staged_ref[pl.ds(place * LINES * PHASES + phase, LINES, stride=PHASES), :]
                        for phase in range(PHASES)
                    ],
                    axis=1,
                )
                for place in range(extent)
            ],
            axis=0,
        )
        out_ref[...] = move_samples(rows, table_ref).reshape(out_ref.shape)


def steer(low, own, high, dip, along, final=False):
    rows, cols = own.shape[:2]
    extent = own.shape[along]
    samples = PHASES * LANES

    def block(count):
        if along == 0:
            return pl.BlockSpec((count, LINES, PHASES, LANES), lambda i: (0, i, 0, 0))
        return pl.BlockSpec((LINES, count, PHASES, LANES), lambda i: (i, 0, 0, 0))

    spread = pltpu.VMEM(((extent + 2 * HALF) * SPAN, LANES), jnp.float32)
    scratch = [spread, spread]
    out_shape, out_spec = jax.ShapeDtypeStruct(own.shape, jnp.float32), block(extent)
    if final:
        out_shape = jax.ShapeDtypeStruct((rows, cols, samples), jnp.float32)
        out_spec = pl.BlockSpec((rows, LINES, samples), lambda i: (0, i, 0))
        scratch += [
            pltpu.VMEM((extent * LINES * PHASES, LANES), jnp.float32),
            pltpu.VMEM((samples, samples), jnp.bfloat16),
        ]
    return pl.pallas_call(
        functools.partial(steer_kernel, along=along),
        grid=(own.shape[1 - along] // LINES,),
        in_specs=[
            pl.BlockSpec(memory_space=pltpu.SMEM),
            block(HALF),
            block(extent),
            block(HALF),
        ],
        out_specs=out_spec,
        out_shape=out_shape,
        scratch_shapes=scratch,
        compiler_params=pltpu.CompilerParams(vmem_limit_bytes=40 * 2**20),
        cost_estimate=pl.CostEstimate(
            flops=30 * rows * cols * samples,
            bytes_accessed=8 * rows * cols * samples,
            transcendentals=0,
        ),
    )(dip, low, own, high)


def ends(cells, axis, along):
    count = lax.axis_size(axis)
    size = cells.shape[along]
    tail = lax.slice_in_dim(cells, size - HALF, size, axis=along)
    head = lax.slice_in_dim(cells, 0, HALF, axis=along)
    low = lax.ppermute(tail, axis, [(i, i + 1) for i in range(count - 1)])
    high = lax.ppermute(head, axis, [(i + 1, i) for i in range(count - 1)])
    return low, high


def arrived_bins(destination, bin_index, devices, capacity, bin_total):
    held = destination.shape[0]
    mine = lax.axis_index("inline") * lax.axis_size("crosslin") + lax.axis_index("crosslin")
    listed = lax.all_gather(jnp.concatenate([destination, bin_index], axis=1), BOTH, axis=0, tiled=True)
    listed = listed.reshape(devices, held, -1)
    hit = listed[:, :, 0] == mine
    rank = jnp.cumsum(hit.astype(jnp.int32), axis=1) - 1
    slots = jnp.arange(capacity, dtype=jnp.int32)
    chosen = hit[:, None, :] & (rank[:, None, :] == slots[None, :, None])
    bins = jnp.sum(jnp.where(chosen[..., None], listed[:, None, :, 1:], 0), axis=2)
    bins = jnp.where(jnp.any(chosen, axis=2)[..., None], bins, bin_total).reshape(-1)
    fold = jnp.sum(
        (jnp.arange(bin_total, dtype=jnp.int32)[:, None] == bins[None, :]).astype(jnp.float32), axis=1
    )
    return bins, 1.0 / jnp.maximum(fold, 1.0)


def on_device(traces, destination, bin_index, dip_inline, dip_cross):
    held = traces.shape[0]
    devices = lax.axis_size("inline") * lax.axis_size("crosslin")
    capacity = 2 * held // devices
    tile_rows, tile_cols = dip_inline.shape
    bins, scale = arrived_bins(destination, bin_index, devices, capacity, tile_rows * tile_cols)
    outgoing = pack(traces, destination.reshape(-1), devices, capacity)
    arrived = lax.all_to_all(outgoing, BOTH, split_axis=0, concat_axis=0, tiled=True)
    stacked = stack_bins(arrived, bins, scale).reshape(tile_rows, tile_cols, PHASES, LANES)
    low, high = ends(stacked, "inline", 0)
    first_pass = steer(low, stacked, high, dip_inline, 0)
    low, high = ends(first_pass, "crosslin", 1)
    second_pass = steer(low, first_pass, high, dip_cross, 1)
    low, high = ends(second_pass, "inline", 0)
    return steer(low, second_pass, high, dip_inline, 0, final=True)


def solution(mesh):
    return jax.shard_map(
        on_device,
        mesh=mesh,
        in_specs=(
            P(BOTH, None, None),
            P(BOTH, None),
            P(BOTH, None),
            P("inline", "crosslin"),
            P("inline", "crosslin"),
        ),
        out_specs=P("inline", "crosslin", None),
        check_vma=False,
    )
```

time: 847 us -> 312 us (0.37); the launches traced: 832 us -> 310 us
  other arithmetic: 622 us -> 3.76 us
  blocking collectives: 0 us -> 145 us
  waiting for transfers between devices: 142 us -> 50.9 us
  Pallas kernels: 0 us -> 75.3 us
  local copies, waits for them, and re-layouts: 29.4 us -> 5.1 us
  matrix products: 9.71 us -> 0 us
    select_n x6 -> x1, other arithmetic: 620 us -> 0.03 us  [arrived_bins(): jnp.where(jnp.any(chosen, axis=2)[..., None], bins, bin_total).reshape(-1)]
    all_gather x0 -> x1, blocking collectives: none -> 145 us  [arrived_bins(): lax.all_gather(jnp.concatenate([destination, bin_index], axis=1), BOTH, a...]
    all_to_all x2 -> x1, waiting for transfers between devices: 91.7 us -> 0.01 us  [on_device(): lax.all_to_all(outgoing, BOTH, split_axis=0, concat_axis=0, tiled=True)]
    pallas_call x0 -> x5, Pallas kernels: none -> 75.3 us  [the longest x3 58.3 us: steer(): pl.pallas_call(functools.partial(steer_kernel, along=along), grid=(own.sh...]
    pad x3 -> x0, local copies, waits for them, and re-layouts: 10.3 us -> none  [pad_time(): return jnp.pad(gridded, ((0, 0), (0, 0), (margin, margin)))]
    dot_general x1 -> x0, matrix products: 9.71 us -> none  [on_device(): jnp.dot(member, arrived_rows, precision=lax.Precision.HIGHEST, preferred_...]
  transfers between devices with their start and end apart: 8 -> 7, of which waited for: 6 -> 4; matrix products, arithmetic and copies ran while one was open for 3% -> 1% of each run, Pallas kernels for 0% -> 0%
where the time goes in v2:
time: 312 us; the launch traced here: 310 us
  blocking collectives  145 us (46%)
  Pallas kernels  75.3 us (24%)
  waiting for transfers between devices  50.9 us (16%)
  starting transfers between devices  29 us (9%)
  local copies, waits for them, and re-layouts  5.1 us (2%)
  other arithmetic  3.76 us (1%)
    all_gather x1, blocking collectives, arrived_bins(): lax.all_gather(jnp.concatenate([destination, bin_index], axis=1), BOTH, a...  145 us
    pallas_call x3, Pallas kernels, steer(): pl.pallas_call(functools.partial(steer_kernel, along=along), grid=(own.sh...  58.3 us
    ppermute x3, waiting for transfers between devices, ends(): high = lax.ppermute(head, axis, [(i + 1, i) for i in range(count - 1)])  31 us
    ppermute x3, waiting for transfers between devices, ends(): low = lax.ppermute(tail, axis, [(i, i + 1) for i in range(count - 1)])  19.8 us
    ppermute x3, starting transfers between devices, ends(): low = lax.ppermute(tail, axis, [(i, i + 1) for i in range(count - 1)])  13.5 us
    ppermute x3, starting transfers between devices, ends(): high = lax.ppermute(head, axis, [(i + 1, i) for i in range(count - 1)])  9.14 us
    pallas_call x1, Pallas kernels, stack_bins(): pl.pallas_call(bin_kernel, grid=(steps,), in_specs=[pl.BlockSpec(memory_s...  8.48 us
    pallas_call x1, Pallas kernels, pack(): pl.pallas_call(functools.partial(pack_kernel, capacity=capacity), in_spec...  8.44 us
  transfers between devices with their start and end apart: 7, of which 4 were waited for; matrix products, arithmetic and copies ran while one was open for 1% of the time, Pallas kernels for 0%

profile of v2, /device:TPU:11, one launch (start us, length us, event | category | flops | bytes accessed | tf_op | source)
XLA Modules:
  0.0 309.5 jit_solution(5126340410293891893)
XLA Ops:
  0.0 0.0 copy-start.1
  0.0 1.6 copy-done.1
  1.6 0.0 copy-start.4
  1.6 0.7 copy-done.4
  2.2 8.4 %shard_map.55 = f32[256,32,128]{2,1,0:T(8,128)S(1)} custom-call(s32[128]{0:T(128)S(1)} %bitcast.14, f32[128,4,1024]{2,1,0:T(4,128)S(1)} %copy-done.1), custom_call_target="tpu_custom_call" | custom-call | tf_op jit(solution)/shard_map/pallas_call | solution.py:83
  10.7 0.0 copy-start
  10.7 2.0 copy-done
  12.7 0.0 copy-start.5
  12.7 0.0 copy-start.6
  12.7 6.4 %all-to-all-start = ((f32[256,32,128]{2,1,0:T(8,128)}), f32[256,32,128]{2,1,0:T(8,128)}, u32[]{:S(2)}, u32[]{:S(2)}) async-start(f32[256,32,128]{2,1,0:T(8,128)} %copy-done), calls=%async_computation | async-start | bytes 8388608 | tf_op jit(solution)/shard_map/all_to_all | solution.py:315
  19.1 0.0 copy-done.5
  19.1 0.0 copy-done.6
  19.1 145.3 %all_gather.3 = s32[4096,5]{0,1:T(8,128)S(1)} all-gather(s32[128,5]{0,1:T(8,128)S(1)} %pad_add_fusion), channel_id=1, replica_groups=mesh['inline'=8,'crosslin'=4] {'inline','crosslin'}, dimensions={0}, use_global_device_ids=true | all-gather | bytes 84480 | tf_op jit(solution)/shard_map/all_gather | solution.py:294
  164.6 0.3 reduce_window_sum.11
  164.9 0.6 fusion.2
  165.5 2.3 select_reduce_fusion
  167.8 0.3 copy.9
  168.1 0.1 select_n.18.bins_ref
  168.2 0.5 convert_reduce_fusion
  168.7 0.0 copy-start.2
  168.7 0.0 all-to-all-done.blocks_ref
  168.8 8.5 %shard_map.56 = f32[1024,8,128]{2,1,0:T(8,128)S(1)} custom-call(s32[1024]{0:T(1024)S(1)} %select_n.18.bins_ref, f32[1024]{0:T(1024)S(1)} %maximum_divide_fusion.scale_ref, f32[256,32,128]{2,1,0:T(8,128)} %all-to-all-done.blocks_ref), custom_call_target="tpu_custom_call" | custom-call | tf_op jit(solution)/shard_map/pallas_call | solution.py:145
  177.2 0.1 fusion.7
  177.4 7.0 %collective-permute-start = (f32[7,32,8,128]{3,2,1,0:T(8,128)S(1)}, f32[7,32,8,128]{3,2,1,0:T(8,128)S(1)}, u32[]{:S(2)}, u32[]{:S(2)}) collective-permute-start(f32[7,32,8,128]{3,2,1,0:T(8,128)S(1)} %bitcast.16), channel_id=1, source_target_pairs={{0,4},{4,8},{8,12},{12,16},{16,20},{20,24},{24,28},{1,5},{5,9},{9,... | collective-permute-start | bytes 2752520 | tf_op jit(solution)/shard_map/ppermute | solution.py:286
  184.4 1.9 collective-permute-start.1
  186.3 15.7 %collective-permute-done.low_ref = f32[7,32,8,128]{3,2,1,0:T(8,128)S(1)} collective-permute-done((f32[7,32,8,128]{3,2,1,0:T(8,128)S(1)}, f32[7,32,8,128]{3,2,1,0:T(8,128)S(1)}, u32[]{:S(2)}, u32[]{:S(2)}) %collective-permute-start) | collective-permute-done | bytes 917536 | tf_op jit(solution)/shard_map/ppermute | solution.py:286
  202.1 0.0 collective-permute-done.1.high_ref
  202.1 0.0 copy-done.2
  202.1 0.0 copy-start.3
  202.1 17.4 %shard_map.57.own_ref = f32[32,32,8,128]{3,2,1,0:T(8,128)S(1)} custom-call(s32[32,32]{1,0:T(8,128)S(1)} %copy-done.2, f32[7,32,8,128]{3,2,1,0:T(8,128)S(1)} %collective-permute-done.low_ref, f32[32,32,8,128]{3,2,1,0:T(8,128)S(1)} %bitcast.13, f32[7,32,8,128]{3,2,1,0:T(8,128)S(1)} %collective-permute-done.1.high_ref), custom_call_target="tpu_custom_call" | custom-call | flops 31457280 | bytes 8388608 | tf_op jit(solution)/shard_map/pallas_call | solution.py:260
  219.5 0.1 fusion.6
  219.7 5.3 %collective-permute-start.3 = (f32[32,7,8,128]{3,2,1,0:T(8,128)S(1)}, f32[32,7,8,128]{3,2,1,0:T(8,128)S(1)}, u32[]{:S(2)}, u32[]{:S(2)}) collective-permute-start(f32[32,7,8,128]{3,2,1,0:T(8,128)S(1)} %get-tuple-element.9), channel_id=1, source_target_pairs={{1,0},{2,1},{3,2},{5,4},{6,5},{7,6},{9,8},{10,9},{11,10},{13,12},{... | collective-permute-start | bytes 2752520 | tf_op jit(solution)/shard_map/ppermute | solution.py:287
  225.0 1.9 collective-permute-start.2
  226.9 15.3 %collective-permute-done.3.high_ref = f32[32,7,8,128]{3,2,1,0:T(8,128)S(1)} collective-permute-done((f32[32,7,8,128]{3,2,1,0:T(8,128)S(1)}, f32[32,7,8,128]{3,2,1,0:T(8,128)S(1)}, u32[]{:S(2)}, u32[]{:S(2)}) %collective-permute-start.3) | collective-permute-done | bytes 917536 | tf_op jit(solution)/shard_map/ppermute | solution.py:287
  242.2 4.1 %collective-permute-done.2.low_ref = f32[32,7,8,128]{3,2,1,0:T(8,128)S(1)} collective-permute-done((f32[32,7,8,128]{3,2,1,0:T(8,128)S(1)}, f32[32,7,8,128]{3,2,1,0:T(8,128)S(1)}, u32[]{:S(2)}, u32[]{:S(2)}) %collective-permute-start.2) | collective-permute-done | bytes 917536 | tf_op jit(solution)/shard_map/ppermute | solution.py:286
  246.3 0.0 copy-done.3
  246.3 17.3 %shard_map.58.own_ref = f32[32,32,8,128]{3,2,1,0:T(8,128)S(1)} custom-call(s32[32,32]{1,0:T(8,128)S(1)} %copy-done.3, f32[32,7,8,128]{3,2,1,0:T(8,128)S(1)} %collective-permute-done.2.low_ref, f32[32,32,8,128]{3,2,1,0:T(8,128)S(1)} %shard_map.57.own_ref, f32[32,7,8,128]{3,2,1,0:T(8,128)S(1)} %collective-permute-done.3.high_ref), custom_call_target="tpu_custom_call" | custom-call | flops 31457280 | bytes 8388608 | tf_op jit(solution)/shard_map/pallas_call | solution.py:260
  263.6 0.1 fusion.5
  263.8 1.9 collective-permute-start.5
  265.7 4.5 %collective-permute-start.4 = (f32[7,32,8,128]{3,2,1,0:T(8,128)S(1)}, f32[7,32,8,128]{3,2,1,0:T(8,128)S(1)}, u32[]{:S(2)}, u32[]{:S(2)}) collective-permute-start(f32[7,32,8,128]{3,2,1,0:T(8,128)S(1)} %get-tuple-element.8), channel_id=1, source_target_pairs={{0,4},{4,8},{8,12},{12,16},{16,20},{20,24},{24,28},{1,5},{5,9},{9,... | collective-permute-start | bytes 2752520 | tf_op jit(solution)/shard_map/ppermute | solution.py:286
  270.2 15.7 %collective-permute-done.5.high_ref = f32[7,32,8,128]{3,2,1,0:T(8,128)S(1)} collective-permute-done((f32[7,32,8,128]{3,2,1,0:T(8,128)S(1)}, f32[7,32,8,128]{3,2,1,0:T(8,128)S(1)}, u32[]{:S(2)}, u32[]{:S(2)}) %collective-permute-start.5) | collective-permute-done | bytes 917536 | tf_op jit(solution)/shard_map/ppermute | solution.py:287
  285.9 0.0 collective-permute-done.4.low_ref
  285.9 23.6 %shard_map.59 = f32[32,32,1024]{2,1,0:T(8,128)} custom-call(s32[32,32]{1,0:T(8,128)S(1)} %copy-done.2, f32[7,32,8,128]{3,2,1,0:T(8,128)S(1)} %collective-permute-done.4.low_ref, f32[32,32,8,128]{3,2,1,0:T(8,128)S(1)} %shard_map.58.own_ref, f32[7,32,8,128]{3,2,1,0:T(8,128)S(1)} %collective-permute-done.5.high_ref), custom_call_target="tpu_custom_call" | custom-call | flops 31457280 | bytes 8388608 | tf_op jit(solution)/shard_map/pallas_call | solution.py:260
  (8 shorter events, 0.1 us)
Async XLA Ops:
  0.0 1.6 copy-start.1
  1.6 0.7 copy-start.4
  10.7 2.0 copy-start
  12.7 6.4 %copy-start.5 = (s32[128,1]{0,1:T(1,128)S(1)}, s32[128,1]{0,1:T(1,128)}, u32[]{:S(2)}) copy-start(s32[128,1]{0,1:T(1,128)} %param.6) | copy-start | bytes 1540
  12.7 6.4 %copy-start.6 = (s32[128,4]{0,1:T(4,128)S(1)}, s32[128,4]{0,1:T(4,128)}, u32[]{:S(2)}) copy-start(s32[128,4]{0,1:T(4,128)} %param.7) | copy-start | bytes 6148
  12.7 156.0 %all-to-all-start = ((f32[256,32,128]{2,1,0:T(8,128)}), f32[256,32,128]{2,1,0:T(8,128)}, u32[]{:S(2)}, u32[]{:S(2)}) async-start(f32[256,32,128]{2,1,0:T(8,128)} %copy-done), calls=%async_computation | async-start | bytes 8388608 | tf_op jit(solution)/shard_map/all_to_all | solution.py:315
  168.7 33.3 %copy-start.2 = (s32[32,32]{1,0:T(8,128)S(1)}, s32[32,32]{1,0:T(8,128)}, u32[]{:S(2)}) copy-start(s32[32,32]{1,0:T(8,128)} %dip_ref.5) | copy-start | bytes 12292
  177.4 24.7 %collective-permute-start = (f32[7,32,8,128]{3,2,1,0:T(8,128)S(1)}, f32[7,32,8,128]{3,2,1,0:T(8,128)S(1)}, u32[]{:S(2)}, u32[]{:S(2)}) collective-permute-start(f32[7,32,8,128]{3,2,1,0:T(8,128)S(1)} %bitcast.16), channel_id=1, source_target_pairs={{0,4},{4,8},{8,12},{12,16},{16,20},{20,24},{24,28},{1,5},{5,9},{9,... | collective-permute-start | bytes 2752520 | tf_op jit(solution)/shard_map/ppermute | solution.py:286
  184.4 17.7 %collective-permute-start.1 = (f32[7,32,8,128]{3,2,1,0:T(8,128)S(1)}, f32[7,32,8,128]{3,2,1,0:T(8,128)S(1)}, u32[]{:S(2)}, u32[]{:S(2)}) collective-permute-start(f32[7,32,8,128]{3,2,1,0:T(8,128)S(1)} %bitcast.15), channel_id=1, source_target_pairs={{4,0},{8,4},{12,8},{16,12},{20,16},{24,20},{28,24},{5,1},{9,5},{13... | collective-permute-start | bytes 2752520 | tf_op jit(solution)/shard_map/ppermute | solution.py:287
  202.1 44.2 %copy-start.3 = (s32[32,32]{1,0:T(8,128)S(1)}, s32[32,32]{1,0:T(8,128)}, u32[]{:S(2)}) copy-start(s32[32,32]{1,0:T(8,128)} %dip_ref.4) | copy-start | bytes 12292
  219.7 22.6 %collective-permute-start.3 = (f32[32,7,8,128]{3,2,1,0:T(8,128)S(1)}, f32[32,7,8,128]{3,2,1,0:T(8,128)S(1)}, u32[]{:S(2)}, u32[]{:S(2)}) collective-permute-start(f32[32,7,8,128]{3,2,1,0:T(8,128)S(1)} %get-tuple-element.9), channel_id=1, source_target_pairs={{1,0},{2,1},{3,2},{5,4},{6,5},{7,6},{9,8},{10,9},{11,10},{13,12},{... | collective-permute-start | bytes 2752520 | tf_op jit(solution)/shard_map/ppermute | solution.py:287
  225.0 21.3 %collective-permute-start.2 = (f32[32,7,8,128]{3,2,1,0:T(8,128)S(1)}, f32[32,7,8,128]{3,2,1,0:T(8,128)S(1)}, u32[]{:S(2)}, u32[]{:S(2)}) collective-permute-start(f32[32,7,8,128]{3,2,1,0:T(8,128)S(1)} %get-tuple-element.10), channel_id=1, source_target_pairs={{0,1},{1,2},{2,3},{4,5},{5,6},{6,7},{8,9},{9,10},{10,11},{12,13},{... | collective-permute-start | bytes 2752520 | tf_op jit(solution)/shard_map/ppermute | solution.py:286
  263.8 22.2 %collective-permute-start.5 = (f32[7,32,8,128]{3,2,1,0:T(8,128)S(1)}, f32[7,32,8,128]{3,2,1,0:T(8,128)S(1)}, u32[]{:S(2)}, u32[]{:S(2)}) collective-permute-start(f32[7,32,8,128]{3,2,1,0:T(8,128)S(1)} %get-tuple-element.7), channel_id=1, source_target_pairs={{4,0},{8,4},{12,8},{16,12},{20,16},{24,20},{28,24},{5,1},{9,5},{13... | collective-permute-start | bytes 2752520 | tf_op jit(solution)/shard_map/ppermute | solution.py:287
  265.7 20.3 %collective-permute-start.4 = (f32[7,32,8,128]{3,2,1,0:T(8,128)S(1)}, f32[7,32,8,128]{3,2,1,0:T(8,128)S(1)}, u32[]{:S(2)}, u32[]{:S(2)}) collective-permute-start(f32[7,32,8,128]{3,2,1,0:T(8,128)S(1)} %get-tuple-element.8), channel_id=1, source_target_pairs={{0,4},{4,8},{8,12},{12,16},{16,20},{20,24},{24,28},{1,5},{5,9},{9,... | collective-permute-start | bytes 2752520 | tf_op jit(solution)/shard_map/ppermute | solution.py:286

commit v3 on v2

v3 whole, which is shorter than its diff:
```python
import functools

import jax
import jax.numpy as jnp
from jax import lax
from jax.experimental import pallas as pl
from jax.experimental.pallas import tpu as pltpu
from jax.sharding import PartitionSpec as P

HALF = 7
DMAX = 2
LANES = 128
PHASES = 8
LINES = 8
PARTS = 2
REACH = -(-HALF * DMAX // PHASES)
SPAN = (2 * REACH + 1) * PHASES
BOTH = ("inline", "crosslin")
MIB = 2**20


def weight(offset):
    return (HALF + 1 - abs(offset)) / float((HALF + 1) ** 2)


def fill_interleave(table_ref, time_dim):
    size = table_ref.shape[0]
    time = lax.broadcasted_iota(jnp.int32, (size, size), time_dim)
    place = lax.broadcasted_iota(jnp.int32, (size, size), 1 - time_dim)
    hit = time == (place & (LANES - 1)) * PHASES + place // LANES
    table_ref[...] = jnp.where(hit, 1.0, 0.0).astype(jnp.bfloat16)


def move_samples(rows, table_ref):
    count = rows.shape[0]
    upper = rows.astype(jnp.bfloat16)
    rest = (rows - upper.astype(jnp.float32)).astype(jnp.bfloat16)
    both = jnp.concatenate([upper, rest], axis=0)
    moved = jnp.dot(both, table_ref[...], preferred_element_type=jnp.float32)
    return moved[:count] + moved[count:]


def pack_kernel(target_ref, lists_ref, traces_ref, out_ref, table_ref, tiles_ref, used_ref, sem, *more, part, capacity):
    held, block_rows, samples = traces_ref.shape
    share = block_rows // PARTS
    devices = used_ref.shape[0]
    span = share * PHASES
    fill_interleave(table_ref, 0)
    rows = traces_ref[:, part * share : (part + 1) * share, :].reshape(held * share, samples)
    moved = move_samples(rows, table_ref)
    for eight in range(held * share // 8):
        for phase in range(PHASES):
            tiles_ref[pl.ds(eight * 8 * PHASES + phase, 8, stride=PHASES), :] = moved[
                eight * 8 : eight * 8 + 8, phase * LANES : (phase + 1) * LANES
            ]

    def clear(device, _):
        used_ref[device] = 0
        return 0

    lax.fori_loop(0, devices, clear, 0)
    if more:
        listed_ref, listed_sem = more
        room = listed_ref.shape[1]
        listed_ref[...] = jnp.full(listed_ref.shape, -1.0, jnp.float32)

    def send_block(block, _):
        device = target_ref[block]
        rank = used_ref[device]
        used_ref[device] = rank + 1
        pltpu.make_async_copy(
            tiles_ref.at[pl.ds(pl.multiple_of(block * span, 8), span), :],
            out_ref.at[device, pl.ds(pl.multiple_of(rank * span, 8), span), :],
            sem,
        ).start()
        if more:
            listed_ref[device, pl.ds(rank, 1), :] = lists_ref[pl.ds(block, 1), :]
        return 0

    lax.fori_loop(0, held, send_block, 0, unroll=4)
    if more:
        copy = pltpu.make_async_copy(
            listed_ref, out_ref.at[:, capacity * span : capacity * span + room, :], listed_sem
        )
        copy.start()
        copy.wait()
    pltpu.make_async_copy(tiles_ref, tiles_ref, sem).wait()


def pack(traces, target, lists, devices, capacity, part):
    held, block_rows, samples = traces.shape
    span = block_rows // PARTS * PHASES
    room = -(-capacity // 8) * 8
    scratch = [
        pltpu.VMEM((samples, samples), jnp.bfloat16),
        pltpu.VMEM((held * span, LANES), jnp.float32),
        pltpu.SMEM((devices,), jnp.int32),
        pltpu.SemaphoreType.DMA,
    ]
    rows = capacity * span
    if part == 0:
        scratch += [pltpu.VMEM((devices, room, LANES), jnp.float32), pltpu.SemaphoreType.DMA]
        rows += room
    return pl.pallas_call(
        functools.partial(pack_kernel, part=part, capacity=capacity),
        in_specs=[
            pl.BlockSpec(memory_space=pltpu.SMEM),
            pl.BlockSpec(memory_space=pltpu.VMEM),
            pl.BlockSpec(memory_space=pltpu.VMEM),
        ],
        out_specs=pl.BlockSpec(memory_space=pl.ANY),
        out_shape=jax.ShapeDtypeStruct((devices, rows, LANES), jnp.float32),
        scratch_shapes=scratch,
        compiler_params=pltpu.CompilerParams(vmem_limit_bytes=32 * MIB),
        cost_estimate=pl.CostEstimate(
            flops=4 * samples * samples * held, bytes_accessed=4 * MIB, transcendentals=0
        ),
    )(target, lists, traces)


def bin_kernel(bins_ref, scale_ref, blocks_ref, *refs, part, capacity, last):
    if last:
        before_ref, out_ref, even_ref, odd_ref = refs
    else:
        out_ref, even_ref, odd_ref = refs
    step = pl.program_id(0)
    senders = blocks_ref.shape[0]
    bin_total = out_ref.shape[0]
    block_rows = bins_ref.shape[0] // (senders * pl.num_programs(0) * capacity)
    share = block_rows // PARTS
    unroll = 8

    @pl.when(step == 0)
    def _():
        def clear(i, _):
            for j in range(unroll):
                even_ref[i * unroll + j] = jnp.zeros((PHASES, LANES), jnp.float32)
                odd_ref[i * unroll + j] = jnp.zeros((PHASES, LANES), jnp.float32)
            return 0

        lax.fori_loop(0, bin_total // unroll, clear, 0)

    def add_sender(sender, _):
        first = (step * senders + sender) * (capacity * block_rows) + part * share
        for rank in range(capacity):
            for j in range(share):
                total_ref = odd_ref if j % 2 else even_ref
                place = bins_ref[first + rank * block_rows + j]
                row = (rank * share + j) * PHASES
                total_ref[place] += blocks_ref[sender, row : row + PHASES, :]
        return 0

    lax.fori_loop(0, senders, add_sender, 0)

    @pl.when(step == pl.num_programs(0) - 1)
    def _():
        def finish(i, _):
            for j in range(unroll):
                place = i * unroll + j
                total = even_ref[place] + odd_ref[place]
                if last:
                    total = (total + before_ref[place]) * scale_ref[place]
                out_ref[place] = total
            return 0

        lax.fori_loop(0, bin_total // unroll, finish, 0)


def stack_bins(blocks, bins, scale, capacity, part, before):
    devices, rows, _ = blocks.shape
    bin_total = scale.shape[0]
    steps = 8
    last = part == PARTS - 1
    whole = pl.BlockSpec((bin_total, PHASES, LANES), lambda i: (0, 0, 0))
    return pl.pallas_call(
        functools.partial(bin_kernel, part=part, capacity=capacity, last=last),
        grid=(steps,),
        in_specs=[
            pl.BlockSpec(memory_space=pltpu.SMEM),
            pl.BlockSpec(memory_space=pltpu.SMEM),
            pl.BlockSpec((devices // steps, rows, LANES), lambda i: (i, 0, 0)),
        ]
        + [whole] * last,
        out_specs=whole,
        out_shape=jax.ShapeDtypeStruct((bin_total, PHASES, LANES), jnp.float32),
        scratch_shapes=[
            pltpu.VMEM((bin_total + 8, PHASES, LANES), jnp.float32),
            pltpu.VMEM((bin_total + 8, PHASES, LANES), jnp.float32),
        ],
        compiler_params=pltpu.CompilerParams(vmem_limit_bytes=40 * MIB),
        cost_estimate=pl.CostEstimate(
            flops=8 * MIB, bytes_accessed=12 * MIB, transcendentals=0
        ),
    )(bins, scale, blocks, *([before] if last else []))


def steer_line(dip_of, cell_of, put, extent, spread_ref):
    lane = lax.broadcasted_iota(jnp.int32, (PHASES, LANES), 1)
    for place in range(extent + 2 * HALF):
        cell = cell_of(place)
        for reach in range(-REACH, REACH + 1):
            moved = cell
            if reach:
                moved = pltpu.roll(cell, (-reach) % LANES, axis=1)
                inside = lane < LANES - reach if reach > 0 else lane >= -reach
                moved = jnp.where(inside, moved, 0.0)
            spread_ref[pl.ds(place * SPAN + (reach + REACH) * PHASES, PHASES), :] = moved
    for place in range(extent):
        centre = (place + HALF) * SPAN + REACH * PHASES
        pace = dip_of(place) + SPAN
        above = below = centre
        total = weight(0) * spread_ref[pl.ds(centre, PHASES), :]
        for offset in range(1, HALF + 1):
            above = above + pace
            below = below - pace
            both = spread_ref[pl.ds(above, PHASES), :] + spread_ref[pl.ds(below, PHASES), :]
            total = total + weight(offset) * both
        put(place, total)


def steer_kernel(dip_ref, *refs, along, places, block_of, final):
    inputs = 1 + max(index for index, _ in places)
    pieces, refs = refs[:inputs], refs[inputs:]
    if final is not None:
        if final > 0:
            refs = refs[1:]
        out_ref, spread_a, spread_b, staged_ref, table_ref = refs

        @pl.when(pl.program_id(0) == 0)
        def _():
            fill_interleave(table_ref, 1)

    else:
        out_ref, spread_a, spread_b = refs
    extent = len(places) - 2 * HALF
    start = block_of(pl.program_id(0)) * LINES

    def at(place, line):
        return (place, line) if along == 0 else (line, place)

    def one_line(line, spread_ref):
        def cell_of(place):
            index, local = places[place]
            return pieces[index][at(local, line)]

        def put(place, value):
            if final is not None:
                staged_ref[pl.ds((place * LINES + line) * PHASES, PHASES), :] = value
            else:
                out_ref[at(place, line)] = value

        steer_line(lambda place: dip_ref[at(place, start + line)], cell_of, put, extent, spread_ref)

    def two_lines(i, _):
        one_line(2 * i, spread_a)
        one_line(2 * i + 1, spread_b)
        return 0

    lax.fori_loop(0, LINES // 2, two_lines, 0)
    if final is not None:
        rows = jnp.concatenate(
            [
                jnp.concatenate(
                    [
                        staged_ref[pl.ds(place * LINES * PHASES + phase, LINES, stride=PHASES), :]
                        for phase in range(PHASES)
                    ],
                    axis=1,
                )
                for place in range(extent)
            ],
            axis=0,
        )
        out_ref[...] = move_samples(rows, table_ref).reshape(out_ref.shape)


def steer(pieces, order, dip, along, steps, block_of, final=None, before=None):
    extent = dip.shape[along]
    lines = dip.shape[1 - along]
    samples = PHASES * LANES
    places = [(index, first + i) for index, first, count in order for i in range(count)]

    def spec(array, whole):
        chosen = block_of if whole else lambda i: i
        if along == 0:
            return pl.BlockSpec((array.shape[0], LINES, PHASES, LANES), lambda i: (0, chosen(i), 0, 0))
        return pl.BlockSpec((LINES, array.shape[1], PHASES, LANES), lambda i: (chosen(i), 0, 0, 0))

    in_specs = [pl.BlockSpec(memory_space=pltpu.SMEM)] + [spec(*piece) for piece in pieces]
    operands = [dip] + [array for array, _ in pieces]
    spread = pltpu.VMEM((len(places) * SPAN, LANES), jnp.float32)
    scratch = [spread, spread]
    aliases = {}
    if final is not None:
        out_shape = jax.ShapeDtypeStruct((extent, lines, samples), jnp.float32)
        out_spec = pl.BlockSpec((extent, LINES, samples), lambda i: (0, block_of(i), 0))
        scratch += [
            pltpu.VMEM((extent * LINES * PHASES, LANES), jnp.float32),
            pltpu.VMEM((samples, samples), jnp.bfloat16),
        ]
        if final > 0:
            aliases = {len(operands): 0}
            in_specs.append(pl.BlockSpec(memory_space=pl.ANY))
            operands.append(before)
    else:
        shape = (extent, steps * LINES) if along == 0 else (steps * LINES, extent)
        out_shape = jax.ShapeDtypeStruct(shape + (PHASES, LANES), jnp.float32)
        out_spec = spec(out_shape, False)
    return pl.pallas_call(
        functools.partial(steer_kernel, along=along, places=places, block_of=block_of, final=final),
        grid=(steps,),
        in_specs=in_specs,
        out_specs=out_spec,
        out_shape=out_shape,
        scratch_shapes=scratch,
        input_output_aliases=aliases,
        compiler_params=pltpu.CompilerParams(vmem_limit_bytes=40 * MIB),
        cost_estimate=pl.CostEstimate(
            flops=30 * extent * steps * LINES * samples,
            bytes_accessed=16 * extent * steps * LINES * samples,
            transcendentals=0,
        ),
    )(*operands)


def swap_ends(head, tail, axis):
    count = lax.axis_size(axis)
    low = lax.ppermute(tail, axis, [(i, i + 1) for i in range(count - 1)])
    high = lax.ppermute(head, axis, [(i + 1, i) for i in range(count - 1)])
    return low, high


def outer_of(cells, dim):
    size = cells.shape[dim]
    return jnp.concatenate(
        [lax.slice_in_dim(cells, 0, LINES, axis=dim), lax.slice_in_dim(cells, size - LINES, size, axis=dim)],
        axis=dim,
    )


def inner_of(cells, dim):
    return lax.slice_in_dim(cells, LINES, cells.shape[dim] - LINES, axis=dim)


def smooth(stacked, dip_inline, dip_cross):
    rows, cols = dip_inline.shape
    row_blocks, col_blocks = rows // LINES, cols // LINES
    steps_in = lambda blocks: blocks - 2
    inner = lambda i: i + 1
    outer = lambda blocks: lambda i: i * (blocks - 1)

    head, tail = stacked[:HALF], stacked[rows - HALF :]
    order = [(0, 0, HALF), (1, 0, rows), (2, 0, HALF)]
    firsts = []
    for pick, steps, block_of in (
        (outer_of, 2, outer(col_blocks)),
        (inner_of, col_blocks - 2, inner),
    ):
        low, high = swap_ends(pick(head, 1), pick(tail, 1), "inline")
        firsts.append(
            steer([(low, False), (stacked, True), (high, False)], order, dip_inline, 0, steps, block_of)
        )
    border, middle = firsts

    head, tail = border[:, :HALF], border[:, 2 * LINES - HALF :]
    order = [(0, 0, HALF), (1, 0, LINES), (2, 0, cols - 2 * LINES), (1, LINES, LINES), (3, 0, HALF)]
    seconds = []
    for pick, steps, block_of in (
        (outer_of, 2, outer(row_blocks)),
        (inner_of, row_blocks - 2, inner),
    ):
        low, high = swap_ends(pick(head, 0), pick(tail, 0), "crosslin")
        seconds.append(
            steer(
                [(low, False), (border, True), (middle, True), (high, False)],
                order, dip_cross, 1, steps, block_of,
            )
        )
    border, middle = seconds

    head, tail = border[:HALF], border[2 * LINES - HALF :]
    order = [(0, 0, HALF), (1, 0, LINES), (2, 0, rows - 2 * LINES), (1, LINES, LINES), (3, 0, HALF)]
    half = col_blocks // 2
    result = None
    for group in range(2):
        begin, steps = (0, half) if group == 0 else (half, col_blocks - half)
        pick = lambda cells: cells[:, begin * LINES : (begin + steps) * LINES]
        low, high = swap_ends(pick(head), pick(tail), "inline")
        result = steer(
            [(low, False), (border, True), (middle, True), (high, False)],
            order, dip_inline, 0, steps, functools.partial(lambda begin, i: i + begin, begin),
            final=group, before=result,
        )
    return result


def on_device(traces, destination, bin_index, dip_inline, dip_cross):
    held, block_rows, _ = traces.shape
    devices = lax.axis_size("inline") * lax.axis_size("crosslin")
    capacity = 2 * held // devices
    tile_rows, tile_cols = dip_inline.shape
    bin_total = tile_rows * tile_cols
    target = destination.reshape(-1)
    lists = jnp.pad(bin_index.astype(jnp.float32), ((0, 0), (0, LANES - block_rows)))
    arrived = [
        lax.all_to_all(
            pack(traces, target, lists, devices, capacity, part), BOTH, split_axis=0, concat_axis=0, tiled=True
        )
        for part in range(PARTS)
    ]
    room = capacity * block_rows // PARTS * PHASES
    listed = arrived[0][:, room : room + capacity, :block_rows].astype(jnp.int32)
    bins = jnp.where(listed < 0, bin_total, listed).reshape(-1)
    fold = jnp.sum(
        (jnp.arange(bin_total, dtype=jnp.int32)[:, None] == bins[None, :]).astype(jnp.float32), axis=1
    )
    scale = 1.0 / jnp.maximum(fold, 1.0)
    total = None
    for part in range(PARTS):
        total = stack_bins(arrived[part], bins, scale, capacity, part, total)
    return smooth(total.reshape(tile_rows, tile_cols, PHASES, LANES), dip_inline, dip_cross)


def solution(mesh):
    return jax.shard_map(
        on_device,
        mesh=mesh,
        in_specs=(
            P(BOTH, None, None),
            P(BOTH, None),
            P(BOTH, None),
            P("inline", "crosslin"),
            P("inline", "crosslin"),
        ),
        out_specs=P("inline", "crosslin", None),
        check_vma=False,
    )
```

time: 312 us -> 237 us (0.76)
  blocking collectives: 145 us -> 0 us
  waiting for transfers between devices: 50.9 us -> 87.7 us
  starting transfers between devices: 29 us -> 49.3 us
  Pallas kernels: 75.3 us -> 86.3 us
  local copies, waits for them, and re-layouts: 5.1 us -> 11.4 us
    all_gather x1 -> x0, blocking collectives: 145 us -> none  [arrived_bins(): lax.all_gather(jnp.concatenate([destination, bin_index], axis=1), BOTH, a...]
    all_to_all x1 -> x2, waiting for transfers between devices: 0.01 us -> 83.8 us  [on_device(): lax.all_to_all(pack(traces, target, lists, devices, capacity, part), BOTH...]
    ppermute x6 -> x12, waiting for transfers between devices: 50.9 us -> 3.85 us  [the longest x6 3.79 us: swap_ends(): low = lax.ppermute(tail, axis, [(i, i + 1) for i in range(count - 1)])]
    ppermute x6 -> x12, starting transfers between devices: 22.6 us -> 38.5 us  [the longest x6 25.7 us: swap_ends(): low = lax.ppermute(tail, axis, [(i, i + 1) for i in range(count - 1)])]
    pallas_call x5 -> x10, Pallas kernels: 75.3 us -> 86.3 us  [the longest x6 66.1 us: steer(): pl.pallas_call(functools.partial(steer_kernel, along=along, places=places...]
    unnamed x15 -> x20, local copies, waits for them, and re-layouts: 4.29 us -> 10.7 us
    all_to_all x1 -> x2, starting transfers between devices: 6.38 us -> 10.7 us  [on_device(): lax.all_to_all(pack(traces, target, lists, devices, capacity, part), BOTH...]
  transfers between devices with their start and end apart: 7 -> 14, of which waited for: 4 -> 3; matrix products, arithmetic and copies ran while one was open for 1% -> 0% of each run, Pallas kernels for 0% -> 26%
where the time goes in v3:
time: 237 us; the launch traced here: 236 us
  waiting for transfers between devices  87.7 us (37%)
  Pallas kernels  86.3 us (36%)
  starting transfers between devices  49.3 us (21%)
  local copies, waits for them, and re-layouts  11.4 us (5%)
    all_to_all x2, waiting for transfers between devices, on_device(): lax.all_to_all(pack(traces, target, lists, devices, capacity, part), BOTH...  83.8 us
    pallas_call x6, Pallas kernels, steer(): pl.pallas_call(functools.partial(steer_kernel, along=along, places=places...  66.1 us
    ppermute x6, starting transfers between devices, swap_ends(): low = lax.ppermute(tail, axis, [(i, i + 1) for i in range(count - 1)])  25.7 us
    ppermute x6, starting transfers between devices, swap_ends(): high = lax.ppermute(head, axis, [(i + 1, i) for i in range(count - 1)])  12.9 us
    all_to_all x2, starting transfers between devices, on_device(): lax.all_to_all(pack(traces, target, lists, devices, capacity, part), BOTH...  10.7 us
    unnamed x20, local copies, waits for them, and re-layouts  10.7 us
    pallas_call x2, Pallas kernels, stack_bins(): pl.pallas_call(functools.partial(bin_kernel, part=part, capacity=capacity...  10.4 us
    pallas_call x2, Pallas kernels, pack(): pl.pallas_call(functools.partial(pack_kernel, part=part, capacity=capacit...  9.72 us
  transfers between devices with their start and end apart: 14, of which 3 were waited for; matrix products, arithmetic and copies ran while one was open for 0% of the time, Pallas kernels for 26%

profile of v3, /device:TPU:11, one launch (start us, length us, event | category | flops | bytes accessed | tf_op | source)
XLA Modules:
  0.0 236.4 jit_solution(795121363373403552)
XLA Ops:
  0.0 0.7 convert_element_type.11
  0.7 0.1 copy.10
  0.8 0.0 copy-start.3
  0.8 1.6 copy-done.3
  2.4 0.7 copy-done.8
  3.1 4.9 %shard_map.55 = f32[32,136,128]{2,1,0:T(8,128)S(1)} custom-call(s32[128]{0:T(128)S(1)} %bitcast.6, f32[128,128]{1,0:T(8,128)S(1)} %pad.4.lists_ref, f32[128,4,1024]{2,1,0:T(4,128)S(1)} %copy-done.3), custom_call_target="tpu_custom_call" | custom-call | flops 536870912 | bytes 4194304 | tf_op jit(solution)/shard_map/pallas_call | solution.py:104
  8.0 0.0 copy-start.2
  8.0 1.4 copy-done.2
  9.3 6.3 %all-to-all-start = ((f32[32,136,128]{2,1,0:T(8,128)}), f32[32,136,128]{2,1,0:T(8,128)S(1)}, u32[]{:S(2)}, u32[]{:S(2)}) async-start(f32[32,136,128]{2,1,0:T(8,128)} %copy-done.2), calls=%async_computation | async-start | bytes 4456448 | tf_op jit(solution)/shard_map/all_to_all | solution.py:406
  15.7 0.0 copy-start.4
  15.7 1.6 copy-done.4
  17.3 4.8 %shard_map.56 = f32[32,128,128]{2,1,0:T(8,128)S(1)} custom-call(s32[128]{0:T(128)S(1)} %bitcast.7, f32[128,128]{1,0:T(8,128)S(1)} %pad.4.lists_ref, f32[128,4,1024]{2,1,0:T(4,128)S(1)} %copy-done.4), custom_call_target="tpu_custom_call" | custom-call | flops 536870912 | bytes 4194304 | tf_op jit(solution)/shard_map/pallas_call | solution.py:104
  22.1 1.3 copy-done.5
  23.4 42.6 %all-to-all-done.blocks_ref = f32[32,136,128]{2,1,0:T(8,128)S(1)} async-done(((f32[32,136,128]{2,1,0:T(8,128)}), f32[32,136,128]{2,1,0:T(8,128)S(1)}, u32[]{:S(2)}, u32[]{:S(2)}) %all-to-all-start) | async-done | bytes 2228256 | tf_op jit(solution)/shard_map/all_to_all | solution.py:406
  66.0 4.4 %all-to-all-start.1 = ((f32[32,128,128]{2,1,0:T(8,128)}), f32[32,128,128]{2,1,0:T(8,128)}, u32[]{:S(2)}, u32[]{:S(2)}) async-start(f32[32,128,128]{2,1,0:T(8,128)} %copy-done.5), calls=%async_computation.1 | async-start | bytes 4194304 | tf_op jit(solution)/shard_map/all_to_all | solution.py:406
  70.4 0.1 reshape.13.bins_ref
  70.6 0.5 convert_reduce_fusion
  71.1 3.6 %shard_map.57.refs_0_ = f32[1024,8,128]{2,1,0:T(8,128)S(1)} custom-call(s32[1024]{0:T(1024)S(1)} %reshape.13.bins_ref, f32[1024]{0:T(1024)S(1)} %maximum_divide_fusion.scale_ref, f32[32,136,128]{2,1,0:T(8,128)S(1)} %all-to-all-done.blocks_ref), custom_call_target="tpu_custom_call" | custom-call | flops 8388608 | bytes 12582912 | tf_op jit(solution)/shard_map/pallas_call | solution.py:175
  74.7 0.0 copy-start
  74.7 2.0 copy-done
  76.7 41.3 %all-to-all-done.1.blocks_ref = f32[32,128,128]{2,1,0:T(8,128)} async-done(((f32[32,128,128]{2,1,0:T(8,128)}), f32[32,128,128]{2,1,0:T(8,128)}, u32[]{:S(2)}, u32[]{:S(2)}) %all-to-all-start.1) | async-done | bytes 2097184 | tf_op jit(solution)/shard_map/all_to_all | solution.py:406
  117.9 2.2 copy-done.1
  120.1 6.8 %shard_map.58 = f32[1024,8,128]{2,1,0:T(8,128)S(1)} custom-call(s32[1024]{0:T(1024)S(1)} %reshape.13.bins_ref, f32[1024]{0:T(1024)S(1)} %maximum_divide_fusion.scale_ref, f32[32,128,128]{2,1,0:T(8,128)} %all-to-all-done.1.blocks_ref, f32[1024,8,128]{2,1,0:T(8,128)S(1)} %copy-done.1), custom_call_target="tpu_custom_call" | custom-call | flops 8388608 | bytes 12582912 | tf_op jit(solution)/shard_map/pallas_call | solution.py:175
  127.0 0.1 fusion
  127.1 0.0 copy-start.6
  127.2 2.6 %collective-permute-start.1 = (f32[7,16,8,128]{3,2,1,0:T(8,128)S(1)}, f32[7,16,8,128]{3,2,1,0:T(8,128)S(1)}, u32[]{:S(2)}, u32[]{:S(2)}) collective-permute-start(f32[7,16,8,128]{3,2,1,0:T(8,128)S(1)} %pad_maximum_fusion.1), channel_id=1, source_target_pairs={{4,0},{8,4},{12,8},{16,12},{20,16},{24,20},{28,24},{5,1},{9,5},{13... | collective-permute-start | bytes 1376264 | tf_op jit(solution)/shard_map/ppermute | solution.py:329
  129.9 3.8 %collective-permute-start = (f32[7,16,8,128]{3,2,1,0:T(8,128)S(1)}, f32[7,16,8,128]{3,2,1,0:T(8,128)S(1)}, u32[]{:S(2)}, u32[]{:S(2)}) collective-permute-start(f32[7,16,8,128]{3,2,1,0:T(8,128)S(1)} %pad_maximum_fusion), channel_id=1, source_target_pairs={{0,4},{4,8},{8,12},{12,16},{16,20},{20,24},{24,28},{1,5},{5,9},{9,... | collective-permute-start | bytes 1376264 | tf_op jit(solution)/shard_map/ppermute | solution.py:328
  133.8 1.9 collective-permute-start.4
  135.7 4.5 %collective-permute-start.3 = (f32[7,16,8,128]{3,2,1,0:T(8,128)S(1)}, f32[7,16,8,128]{3,2,1,0:T(8,128)S(1)}, u32[]{:S(2)}, u32[]{:S(2)}) collective-permute-start(f32[7,16,8,128]{3,2,1,0:T(8,128)S(1)} %slice.107), channel_id=1, source_target_pairs={{0,4},{4,8},{8,12},{12,16},{16,20},{20,24},{24,28},{1,5},{5,9},{9,... | collective-permute-start | bytes 1376264 | tf_op jit(solution)/shard_map/ppermute | solution.py:328
  140.3 0.0 collective-permute-done.1.refs_2_
  140.3 3.8 %collective-permute-done.refs_0_ = f32[7,16,8,128]{3,2,1,0:T(8,128)S(1)} collective-permute-done((f32[7,16,8,128]{3,2,1,0:T(8,128)S(1)}, f32[7,16,8,128]{3,2,1,0:T(8,128)S(1)}, u32[]{:S(2)}, u32[]{:S(2)}) %collective-permute-start) | collective-permute-done | bytes 458784 | tf_op jit(solution)/shard_map/ppermute | solution.py:328
  144.1 9.7 %shard_map.59.refs_1_ = f32[32,16,8,128]{3,2,1,0:T(8,128)S(1)} custom-call(s32[32,32]{1,0:T(8,128)S(1)} %copy-done.6, f32[7,16,8,128]{3,2,1,0:T(8,128)S(1)} %collective-permute-done.refs_0_, f32[32,32,8,128]{3,2,1,0:T(8,128)S(1)} %bitcast.4, f32[7,16,8,128]{3,2,1,0:T(8,128)S(1)} %collective-permute-done.1.refs_2_), custom_call_target="tpu_custom_call" | custom-call | flops 15728640 | bytes 8388608 | tf_op jit(solution)/shard_map/pallas_call | solution.py:309
  153.9 0.1 fusion.3
  154.0 2.7 %collective-permute-start.2 = (f32[16,7,8,128]{3,2,1,0:T(8,128)S(1)}, f32[16,7,8,128]{3,2,1,0:T(8,128)S(1)}, u32[]{:S(2)}, u32[]{:S(2)}) collective-permute-start(f32[16,7,8,128]{3,2,1,0:T(8,128)S(1)} %pad_maximum_fusion.2), channel_id=1, source_target_pairs={{0,1},{1,2},{2,3},{4,5},{5,6},{6,7},{8,9},{9,10},{10,11},{12,13},{... | collective-permute-start | bytes 1376264 | tf_op jit(solution)/shard_map/ppermute | solution.py:328
  156.8 2.6 %collective-permute-start.5 = (f32[16,7,8,128]{3,2,1,0:T(8,128)S(1)}, f32[16,7,8,128]{3,2,1,0:T(8,128)S(1)}, u32[]{:S(2)}, u32[]{:S(2)}) collective-permute-start(f32[16,7,8,128]{3,2,1,0:T(8,128)S(1)} %pad_maximum_fusion.3), channel_id=1, source_target_pairs={{1,0},{2,1},{3,2},{5,4},{6,5},{7,6},{9,8},{10,9},{11,10},{13,12},{... | collective-permute-start | bytes 1376264 | tf_op jit(solution)/shard_map/ppermute | solution.py:329
  159.3 0.1 fusion.2
  159.4 1.9 collective-permute-start.8
  161.4 3.4 %collective-permute-start.7 = (f32[16,7,8,128]{3,2,1,0:T(8,128)S(1)}, f32[16,7,8,128]{3,2,1,0:T(8,128)S(1)}, u32[]{:S(2)}, u32[]{:S(2)}) collective-permute-start(f32[16,7,8,128]{3,2,1,0:T(8,128)S(1)} %get-tuple-element.12), channel_id=1, source_target_pairs={{0,1},{1,2},{2,3},{4,5},{5,6},{6,7},{8,9},{9,10},{10,11},{12,13},{... | collective-permute-start | bytes 1376264 | tf_op jit(solution)/shard_map/ppermute | solution.py:328
  164.7 9.8 %shard_map.60.refs_2_ = f32[32,16,8,128]{3,2,1,0:T(8,128)S(1)} custom-call(s32[32,32]{1,0:T(8,128)S(1)} %copy-done.6, f32[7,16,8,128]{3,2,1,0:T(8,128)S(1)} %collective-permute-done.3.refs_0_, f32[32,32,8,128]{3,2,1,0:T(8,128)S(1)} %bitcast.5, f32[7,16,8,128]{3,2,1,0:T(8,128)S(1)} %collective-permute-done.4.refs_2_), custom_call_target="tpu_custom_call" | custom-call | flops 15728640 | bytes 8388608 | tf_op jit(solution)/shard_map/pallas_call | solution.py:309
  174.5 9.9 %shard_map.61.refs_1_ = f32[16,32,8,128]{3,2,1,0:T(8,128)S(1)} custom-call(s32[32,32]{1,0:T(8,128)S(1)} %copy-done.7, f32[16,7,8,128]{3,2,1,0:T(8,128)S(1)} %collective-permute-done.2.refs_0_, f32[32,16,8,128]{3,2,1,0:T(8,128)S(1)} %shard_map.59.refs_1_, f32[32,16,8,128]{3,2,1,0:T(8,128)S(1)} %shard_map.60.refs_2_, ...), custom_call_target="tpu_custom_call" | custom-call | flops 15728640 | bytes 8388608 | tf_op jit(solution)/shard_map/pallas_call | solution.py:309
  184.4 0.1 fusion.1
  184.5 1.9 collective-permute-start.11
  186.5 6.4 %collective-permute-start.10 = (f32[7,16,8,128]{3,2,1,0:T(8,128)S(1)}, f32[7,16,8,128]{3,2,1,0:T(8,128)S(1)}, u32[]{:S(2)}, u32[]{:S(2)}) collective-permute-start(f32[7,16,8,128]{3,2,1,0:T(8,128)S(1)} %get-tuple-element.8), channel_id=1, source_target_pairs={{0,4},{4,8},{8,12},{12,16},{16,20},{20,24},{24,28},{1,5},{5,9},{9,... | collective-permute-start | bytes 1376264 | tf_op jit(solution)/shard_map/ppermute | solution.py:328
  192.9 1.9 collective-permute-start.9
  194.8 4.7 %collective-permute-start.6 = (f32[7,16,8,128]{3,2,1,0:T(8,128)S(1)}, f32[7,16,8,128]{3,2,1,0:T(8,128)S(1)}, u32[]{:S(2)}, u32[]{:S(2)}) collective-permute-start(f32[7,16,8,128]{3,2,1,0:T(8,128)S(1)} %get-tuple-element.10), channel_id=1, source_target_pairs={{0,4},{4,8},{8,12},{12,16},{16,20},{20,24},{24,28},{1,5},{5,9},{9,... | collective-permute-start | bytes 1376264 | tf_op jit(solution)/shard_map/ppermute | solution.py:328
  199.6 9.8 %shard_map.62.refs_2_ = f32[16,32,8,128]{3,2,1,0:T(8,128)S(1)} custom-call(s32[32,32]{1,0:T(8,128)S(1)} %copy-done.7, f32[16,7,8,128]{3,2,1,0:T(8,128)S(1)} %collective-permute-done.7.refs_0_, f32[32,16,8,128]{3,2,1,0:T(8,128)S(1)} %shard_map.59.refs_1_, f32[32,16,8,128]{3,2,1,0:T(8,128)S(1)} %shard_map.60.refs_2_, ...), custom_call_target="tpu_custom_call" | custom-call | flops 15728640 | bytes 8388608 | tf_op jit(solution)/shard_map/pallas_call | solution.py:309
  209.4 13.5 %shard_map.63.refs_4_ = f32[32,32,1024]{2,1,0:T(8,128)} custom-call(s32[32,32]{1,0:T(8,128)S(1)} %copy-done.6, f32[7,16,8,128]{3,2,1,0:T(8,128)S(1)} %collective-permute-done.10.refs_0_, f32[16,32,8,128]{3,2,1,0:T(8,128)S(1)} %shard_map.61.refs_1_, f32[16,32,8,128]{3,2,1,0:T(8,128)S(1)} %shard_map.62.refs_2_, ...), custom_call_target="tpu_custom_call" | custom-call | flops 15728640 | bytes 8388608 | tf_op jit(solution)/shard_map/pallas_call | solution.py:309
  222.9 13.5 %shard_map.64 = f32[32,32,1024]{2,1,0:T(8,128)} custom-call(s32[32,32]{1,0:T(8,128)S(1)} %copy-done.6, f32[7,16,8,128]{3,2,1,0:T(8,128)S(1)} %collective-permute-done.6.refs_0_, f32[16,32,8,128]{3,2,1,0:T(8,128)S(1)} %shard_map.61.refs_1_, f32[16,32,8,128]{3,2,1,0:T(8,128)S(1)} %shard_map.62.refs_2_, ...), custom_call_target="tpu_custom_call", output_to_operand_aliasing={{}: (5, {})} | custom-call | flops 15728640 | bytes 8388608 | tf_op jit(solution)/shard_map/pallas_call | solution.py:309
  (29 shorter events, 0.3 us)
Async XLA Ops:
  0.8 1.6 copy-start.3
  2.4 0.7 copy-start.8
  8.0 1.4 copy-start.2
  9.3 6.4 %copy-start.9 = (s32[128,1]{0,1:T(1,128)S(1)}, s32[128,1]{0,1:T(1,128)}, u32[]{:S(2)}) copy-start(s32[128,1]{0,1:T(1,128)} %param.6) | copy-start | bytes 1540
  9.3 56.7 %all-to-all-start = ((f32[32,136,128]{2,1,0:T(8,128)}), f32[32,136,128]{2,1,0:T(8,128)S(1)}, u32[]{:S(2)}, u32[]{:S(2)}) async-start(f32[32,136,128]{2,1,0:T(8,128)} %copy-done.2), calls=%async_computation | async-start | bytes 4456448 | tf_op jit(solution)/shard_map/all_to_all | solution.py:406
  15.7 1.6 copy-start.4
  22.1 1.3 copy-start.5
  66.0 51.9 %all-to-all-start.1 = ((f32[32,128,128]{2,1,0:T(8,128)}), f32[32,128,128]{2,1,0:T(8,128)}, u32[]{:S(2)}, u32[]{:S(2)}) async-start(f32[32,128,128]{2,1,0:T(8,128)} %copy-done.5), calls=%async_computation.1 | async-start | bytes 4194304 | tf_op jit(solution)/shard_map/all_to_all | solution.py:406
  74.7 2.0 copy-start
  117.9 2.2 copy-start.1
  127.1 17.0 %copy-start.6 = (s32[32,32]{1,0:T(8,128)S(1)}, s32[32,32]{1,0:T(8,128)}, u32[]{:S(2)}) copy-start(s32[32,32]{1,0:T(8,128)} %dip_ref.11) | copy-start | bytes 12292
  127.2 13.1 %collective-permute-start.1 = (f32[7,16,8,128]{3,2,1,0:T(8,128)S(1)}, f32[7,16,8,128]{3,2,1,0:T(8,128)S(1)}, u32[]{:S(2)}, u32[]{:S(2)}) collective-permute-start(f32[7,16,8,128]{3,2,1,0:T(8,128)S(1)} %pad_maximum_fusion.1), channel_id=1, source_target_pairs={{4,0},{8,4},{12,8},{16,12},{20,16},{24,20},{28,24},{5,1},{9,5},{13... | collective-permute-start | bytes 1376264 | tf_op jit(solution)/shard_map/ppermute | solution.py:329
  129.9 14.2 %collective-permute-start = (f32[7,16,8,128]{3,2,1,0:T(8,128)S(1)}, f32[7,16,8,128]{3,2,1,0:T(8,128)S(1)}, u32[]{:S(2)}, u32[]{:S(2)}) collective-permute-start(f32[7,16,8,128]{3,2,1,0:T(8,128)S(1)} %pad_maximum_fusion), channel_id=1, source_target_pairs={{0,4},{4,8},{8,12},{12,16},{16,20},{20,24},{24,28},{1,5},{5,9},{9,... | collective-permute-start | bytes 1376264 | tf_op jit(solution)/shard_map/ppermute | solution.py:328
  133.8 27.5 %collective-permute-start.4 = (f32[7,16,8,128]{3,2,1,0:T(8,128)S(1)}, f32[7,16,8,128]{3,2,1,0:T(8,128)S(1)}, u32[]{:S(2)}, u32[]{:S(2)}) collective-permute-start(f32[7,16,8,128]{3,2,1,0:T(8,128)S(1)} %slice.108), channel_id=1, source_target_pairs={{4,0},{8,4},{12,8},{16,12},{20,16},{24,20},{28,24},{5,1},{9,5},{13... | collective-permute-start | bytes 1376264 | tf_op jit(solution)/shard_map/ppermute | solution.py:329
  135.7 29.0 %collective-permute-start.3 = (f32[7,16,8,128]{3,2,1,0:T(8,128)S(1)}, f32[7,16,8,128]{3,2,1,0:T(8,128)S(1)}, u32[]{:S(2)}, u32[]{:S(2)}) collective-permute-start(f32[7,16,8,128]{3,2,1,0:T(8,128)S(1)} %slice.107), channel_id=1, source_target_pairs={{0,4},{4,8},{8,12},{12,16},{16,20},{20,24},{24,28},{1,5},{5,9},{9,... | collective-permute-start | bytes 1376264 | tf_op jit(solution)/shard_map/ppermute | solution.py:328
  154.0 20.5 %collective-permute-start.2 = (f32[16,7,8,128]{3,2,1,0:T(8,128)S(1)}, f32[16,7,8,128]{3,2,1,0:T(8,128)S(1)}, u32[]{:S(2)}, u32[]{:S(2)}) collective-permute-start(f32[16,7,8,128]{3,2,1,0:T(8,128)S(1)} %pad_maximum_fusion.2), channel_id=1, source_target_pairs={{0,1},{1,2},{2,3},{4,5},{5,6},{6,7},{8,9},{9,10},{10,11},{12,13},{... | collective-permute-start | bytes 1376264 | tf_op jit(solution)/shard_map/ppermute | solution.py:328
  156.8 17.7 %collective-permute-start.5 = (f32[16,7,8,128]{3,2,1,0:T(8,128)S(1)}, f32[16,7,8,128]{3,2,1,0:T(8,128)S(1)}, u32[]{:S(2)}, u32[]{:S(2)}) collective-permute-start(f32[16,7,8,128]{3,2,1,0:T(8,128)S(1)} %pad_maximum_fusion.3), channel_id=1, source_target_pairs={{1,0},{2,1},{3,2},{5,4},{6,5},{7,6},{9,8},{10,9},{11,10},{13,12},{... | collective-permute-start | bytes 1376264 | tf_op jit(solution)/shard_map/ppermute | solution.py:329
  159.4 35.4 %collective-permute-start.8 = (f32[16,7,8,128]{3,2,1,0:T(8,128)S(1)}, f32[16,7,8,128]{3,2,1,0:T(8,128)S(1)}, u32[]{:S(2)}, u32[]{:S(2)}) collective-permute-start(f32[16,7,8,128]{3,2,1,0:T(8,128)S(1)} %get-tuple-element.11), channel_id=1, source_target_pairs={{1,0},{2,1},{3,2},{5,4},{6,5},{7,6},{9,8},{10,9},{11,10},{13,12},{... | collective-permute-start | bytes 1376264 | tf_op jit(solution)/shard_map/ppermute | solution.py:329
  161.3 13.2 %copy-start.7 = (s32[32,32]{1,0:T(8,128)S(1)}, s32[32,32]{1,0:T(8,128)}, u32[]{:S(2)}) copy-start(s32[32,32]{1,0:T(8,128)} %dip_ref.9) | copy-start | bytes 12292
  161.4 38.2 %collective-permute-start.7 = (f32[16,7,8,128]{3,2,1,0:T(8,128)S(1)}, f32[16,7,8,128]{3,2,1,0:T(8,128)S(1)}, u32[]{:S(2)}, u32[]{:S(2)}) collective-permute-start(f32[16,7,8,128]{3,2,1,0:T(8,128)S(1)} %get-tuple-element.12), channel_id=1, source_target_pairs={{0,1},{1,2},{2,3},{4,5},{5,6},{6,7},{8,9},{9,10},{10,11},{12,13},{... | collective-permute-start | bytes 1376264 | tf_op jit(solution)/shard_map/ppermute | solution.py:328
  184.5 24.9 %collective-permute-start.11 = (f32[7,16,8,128]{3,2,1,0:T(8,128)S(1)}, f32[7,16,8,128]{3,2,1,0:T(8,128)S(1)}, u32[]{:S(2)}, u32[]{:S(2)}) collective-permute-start(f32[7,16,8,128]{3,2,1,0:T(8,128)S(1)} %get-tuple-element.7), channel_id=1, source_target_pairs={{4,0},{8,4},{12,8},{16,12},{20,16},{24,20},{28,24},{5,1},{9,5},{13... | collective-permute-start | bytes 1376264 | tf_op jit(solution)/shard_map/ppermute | solution.py:329
  186.5 23.0 %collective-permute-start.10 = (f32[7,16,8,128]{3,2,1,0:T(8,128)S(1)}, f32[7,16,8,128]{3,2,1,0:T(8,128)S(1)}, u32[]{:S(2)}, u32[]{:S(2)}) collective-permute-start(f32[7,16,8,128]{3,2,1,0:T(8,128)S(1)} %get-tuple-element.8), channel_id=1, source_target_pairs={{0,4},{4,8},{8,12},{12,16},{16,20},{20,24},{24,28},{1,5},{5,9},{9,... | collective-permute-start | bytes 1376264 | tf_op jit(solution)/shard_map/ppermute | solution.py:328
  192.9 30.0 %collective-permute-start.9 = (f32[7,16,8,128]{3,2,1,0:T(8,128)S(1)}, f32[7,16,8,128]{3,2,1,0:T(8,128)S(1)}, u32[]{:S(2)}, u32[]{:S(2)}) collective-permute-start(f32[7,16,8,128]{3,2,1,0:T(8,128)S(1)} %get-tuple-element.9), channel_id=1, source_target_pairs={{4,0},{8,4},{12,8},{16,12},{20,16},{24,20},{28,24},{5,1},{9,5},{13... | collective-permute-start | bytes 1376264 | tf_op jit(solution)/shard_map/ppermute | solution.py:329
  194.8 28.1 %collective-permute-start.6 = (f32[7,16,8,128]{3,2,1,0:T(8,128)S(1)}, f32[7,16,8,128]{3,2,1,0:T(8,128)S(1)}, u32[]{:S(2)}, u32[]{:S(2)}) collective-permute-start(f32[7,16,8,128]{3,2,1,0:T(8,128)S(1)} %get-tuple-element.10), channel_id=1, source_target_pairs={{0,4},{4,8},{8,12},{12,16},{16,20},{20,24},{24,28},{1,5},{5,9},{9,... | collective-permute-start | bytes 1376264 | tf_op jit(solution)/shard_map/ppermute | solution.py:328

commit v4 on v3

--- a/solution.py
+++ b/solution.py
@@ -14,7 +14,8 @@
 LINES = 8
 PARTS = 2
 REACH = -(-HALF * DMAX // PHASES)
-SPAN = (2 * REACH + 1) * PHASES
+PAIR = 2 * PHASES
+GROUP = 16
 BOTH = ("inline", "crosslin")
 MIB = 2**20
 
@@ -194,51 +195,86 @@
     )(bins, scale, blocks, *([before] if last else []))
 
 
-def steer_line(dip_of, cell_of, put, extent, spread_ref):
+def steer_line(dip_ref, line, cell_of, put, extent, halves_ref, taps_refs, spots_ref, weights_ref):
+    for pair in range((extent + 2 * HALF) // 2):
+        cells = jnp.concatenate([cell_of(2 * pair), cell_of(2 * pair + 1)], axis=0)
+        upper = cells.astype(jnp.bfloat16)
+        halves_ref[pair * PAIR : (pair + 1) * PAIR, :LANES] = upper
+        rest = (cells - upper.astype(jnp.float32)).astype(jnp.bfloat16)
+        halves_ref[pair * PAIR : (pair + 1) * PAIR, LANES:] = rest
+    row = lax.broadcasted_iota(jnp.int32, (PAIR, LANES), 0)
+    column = lax.broadcasted_iota(jnp.int32, (PAIR, LANES), 1)
+    phase_gap = ((row & (PHASES - 1)) - (column & (PHASES - 1))).astype(jnp.float32).astype(jnp.bfloat16)
     lane = lax.broadcasted_iota(jnp.int32, (PHASES, LANES), 1)
-    for place in range(extent + 2 * HALF):
-        cell = cell_of(place)
-        for reach in range(-REACH, REACH + 1):
-            moved = cell
-            if reach:
-                moved = pltpu.roll(cell, (-reach) % LANES, axis=1)
-                inside = lane < LANES - reach if reach > 0 else lane >= -reach
-                moved = jnp.where(inside, moved, 0.0)
-            spread_ref[pl.ds(place * SPAN + (reach + REACH) * PHASES, PHASES), :] = moved
-    for place in range(extent):
-        centre = (place + HALF) * SPAN + REACH * PHASES
-        pace = dip_of(place) + SPAN
-        above = below = centre
-        total = weight(0) * spread_ref[pl.ds(centre, PHASES), :]
-        for offset in range(1, HALF + 1):
-            above = above + pace
-            below = below - pace
-            both = spread_ref[pl.ds(above, PHASES), :] + spread_ref[pl.ds(below, PHASES), :]
-            total = total + weight(offset) * both
-        put(place, total)
-
-
-def steer_kernel(dip_ref, *refs, along, places, block_of, final):
+    none = jnp.zeros((PAIR, LANES), jnp.bfloat16)
+    reaches = range(-REACH, REACH + 1)
+    for group in range(extent // GROUP):
+        taps_ref = taps_refs[group % 2]
+        for pair in range(GROUP // 2):
+            first = (group * GROUP // 2 + pair) * PAIR
+            dip = dip_ref[line, first : first + PAIR, :]
+            for half in range(2):
+                block = pl.ds((pair * 2 + half) * PAIR, PAIR)
+                move = phase_gap + dip * spots_ref[block, :]
+                weights = weights_ref[block, :]
+                for reach in reaches:
+                    begin = (pair * len(reaches) + reach + REACH) * PAIR
+                    taps_ref[begin : begin + PAIR, half * LANES : (half + 1) * LANES] = jnp.where(
+                        move == jnp.bfloat16(reach * PHASES), weights, none
+                    )
+        start = group * GROUP * PHASES
+        both = jnp.dot(
+            taps_ref[...], halves_ref[start : start + 2 * LANES, :], preferred_element_type=jnp.float32
+        )
+        for pair in range(GROUP // 2):
+            for member in range(2):
+                total = None
+                for reach in reaches:
+                    begin = (pair * len(reaches) + reach + REACH) * PAIR + member * PHASES
+                    part = both[begin : begin + PHASES, :LANES] + both[begin : begin + PHASES, LANES:]
+                    if reach:
+                        part = pltpu.roll(part, (-reach) % LANES, axis=1)
+                        inside = lane < LANES - reach if reach > 0 else lane >= -reach
+                        part = jnp.where(inside, part, 0.0)
+                    total = part if total is None else total + part
+                put(group * GROUP + 2 * pair + member, total)
+
+
+def fill_weights(spots_ref, weights_ref):
+    row = lax.broadcasted_iota(jnp.int32, (PAIR, LANES), 0)
+    column = lax.broadcasted_iota(jnp.int32, (PAIR, LANES), 1)
+    for pair in range(GROUP // 2):
+        for half in range(2):
+            block = pl.ds((pair * 2 + half) * PAIR, PAIR)
+            spot = half * PAIR + column // PHASES - HALF - 2 * pair - row // PHASES
+            share = jnp.maximum(HALF + 1 - jnp.abs(spot), 0).astype(jnp.float32) / (HALF + 1) ** 2
+            spots_ref[block, :] = jnp.clip(spot, -HALF - 1, HALF + 1).astype(jnp.float32).astype(jnp.bfloat16)
+            weights_ref[block, :] = share.astype(jnp.bfloat16)
+
+
+def steer_kernel(dip_ref, *refs, along, places, final):
     inputs = 1 + max(index for index, _ in places)
     pieces, refs = refs[:inputs], refs[inputs:]
+    if final is not None and final > 0:
+        refs = refs[1:]
+    out_ref, halves_a, halves_b, taps_a, taps_b, spots_ref, weights_ref, *more = refs
     if final is not None:
-        if final > 0:
-            refs = refs[1:]
-        out_ref, spread_a, spread_b, staged_ref, table_ref = refs
-
-        @pl.when(pl.program_id(0) == 0)
-        def _():
+        staged_ref, table_ref = more
+    extent = len(places) - 2 * HALF
+
+    @pl.when(pl.program_id(0) == 0)
+    def _():
+        fill_weights(spots_ref, weights_ref)
+        for halves_ref in (halves_a, halves_b):
+            filled = len(places) * PHASES
+            halves_ref[filled:, :] = jnp.zeros((halves_ref.shape[0] - filled, 2 * LANES), jnp.bfloat16)
+        if final is not None:
             fill_interleave(table_ref, 1)
-
-    else:
-        out_ref, spread_a, spread_b = refs
-    extent = len(places) - 2 * HALF
-    start = block_of(pl.program_id(0)) * LINES
 
     def at(place, line):
         return (place, line) if along == 0 else (line, place)
 
-    def one_line(line, spread_ref):
+    def one_line(line, halves_ref):
         def cell_of(place):
             index, local = places[place]
             return pieces[index][at(local, line)]
@@ -249,11 +285,13 @@
             else:
                 out_ref[at(place, line)] = value
 
-        steer_line(lambda place: dip_ref[at(place, start + line)], cell_of, put, extent, spread_ref)
+        steer_line(
+            dip_ref, line, cell_of, put, extent, halves_ref, (taps_a, taps_b), spots_ref, weights_ref
+        )
 
     def two_lines(i, _):
-        one_line(2 * i, spread_a)
-        one_line(2 * i + 1, spread_b)
+        one_line(2 * i, halves_a)
+        one_line(2 * i + 1, halves_b)
         return 0
 
     lax.fori_loop(0, LINES // 2, two_lines, 0)
@@ -275,8 +313,7 @@
 
 
 def steer(pieces, order, dip, along, steps, block_of, final=None, before=None):
-    extent = dip.shape[along]
-    lines = dip.shape[1 - along]
+    lines, extent = dip.shape[0], dip.shape[1] // PHASES
     samples = PHASES * LANES
     places = [(index, first + i) for index, first, count in order for i in range(count)]
 
@@ -286,10 +323,13 @@
             return pl.BlockSpec((array.shape[0], LINES, PHASES, LANES), lambda i: (0, chosen(i), 0, 0))
         return pl.BlockSpec((LINES, array.shape[1], PHASES, LANES), lambda i: (chosen(i), 0, 0, 0))
 
-    in_specs = [pl.BlockSpec(memory_space=pltpu.SMEM)] + [spec(*piece) for piece in pieces]
+    in_specs = [pl.BlockSpec((LINES, extent * PHASES, LANES), lambda i: (block_of(i), 0, 0))]
+    in_specs += [spec(*piece) for piece in pieces]
     operands = [dip] + [array for array, _ in pieces]
-    spread = pltpu.VMEM((len(places) * SPAN, LANES), jnp.float32)
-    scratch = [spread, spread]
+    halves = pltpu.VMEM((extent * PHASES + LANES, 2 * LANES), jnp.bfloat16)
+    taps = pltpu.VMEM((GROUP * (2 * REACH + 1) * PHASES, 2 * LANES), jnp.bfloat16)
+    constant = pltpu.VMEM((GROUP * PAIR, LANES), jnp.bfloat16)
+    scratch = [halves, halves, taps, taps, constant, constant]
     aliases = {}
     if final is not None:
         out_shape = jax.ShapeDtypeStruct((extent, lines, samples), jnp.float32)
@@ -307,7 +347,7 @@
         out_shape = jax.ShapeDtypeStruct(shape + (PHASES, LANES), jnp.float32)
         out_spec = spec(out_shape, False)
     return pl.pallas_call(
-        functools.partial(steer_kernel, along=along, places=places, block_of=block_of, final=final),
+        functools.partial(steer_kernel, along=along, places=places, final=final),
         grid=(steps,),
         in_specs=in_specs,
         out_specs=out_spec,
@@ -342,8 +382,15 @@
     return lax.slice_in_dim(cells, LINES, cells.shape[dim] - LINES, axis=dim)
 
 
+def dip_tiles(dip):
+    lines, extent = dip.shape
+    tiles = jnp.broadcast_to(dip.astype(jnp.bfloat16)[:, :, None, None], (lines, extent, PHASES, LANES))
+    return tiles.reshape(lines, extent * PHASES, LANES)
+
+
 def smooth(stacked, dip_inline, dip_cross):
     rows, cols = dip_inline.shape
+    dip_inline, dip_cross = dip_tiles(dip_inline.T), dip_tiles(dip_cross)
     row_blocks, col_blocks = rows // LINES, cols // LINES
     steps_in = lambda blocks: blocks - 2
     inner = lambda i: i + 1

time: 237 us -> 234 us (0.987)
  Pallas kernels: 86.3 us -> 69.5 us
  local copies, waits for them, and re-layouts: 11.4 us -> 25 us
  waiting for transfers between devices: 87.7 us -> 84 us
  other arithmetic: 1.34 us -> 4.59 us
    pallas_call x6, Pallas kernels: 66.1 us -> 49.4 us  [steer(): pl.pallas_call(functools.partial(steer_kernel, along=along, places=places...]
    unnamed x20 -> x34, local copies, waits for them, and re-layouts: 10.7 us -> 19 us
    ppermute x6, waiting for transfers between devices: 3.79 us -> 0.19 us  [swap_ends(): low = lax.ppermute(tail, axis, [(i, i + 1) for i in range(count - 1)])]
    concatenate x4, other arithmetic: 0.13 us -> 3.37 us  [outer_of(): jnp.concatenate([lax.slice_in_dim(cells, 0, LINES, axis=dim), lax.slice_i...]
    broadcast_in_dim x0 -> x6, local copies, waits for them, and re-layouts: none -> 2.63 us  [dip_tiles(): jnp.broadcast_to(dip.astype(jnp.bfloat16)[:, :, None, None], (lines, exte...]
    slice x3, local copies, waits for them, and re-layouts: 0.13 us -> 2.64 us  [inner_of(): return lax.slice_in_dim(cells, LINES, cells.shape[dim] - LINES, axis=dim)]
  transfers between devices with their start and end apart: 14 -> 14, of which waited for: 3 -> 3; matrix products, arithmetic and copies ran while one was open for 0% -> 4% of each run, Pallas kernels for 26% -> 20%
where the time goes in v4:
time: 234 us; the launch traced here: 233 us
  waiting for transfers between devices  84 us (36%)
  Pallas kernels  69.5 us (30%)
  starting transfers between devices  49.8 us (21%)
  local copies, waits for them, and re-layouts  25 us (11%)
  other arithmetic  4.59 us (2%)
    all_to_all x2, waiting for transfers between devices, on_device(): lax.all_to_all(pack(traces, target, lists, devices, capacity, part), BOTH...  83.8 us
    pallas_call x6, Pallas kernels, steer(): pl.pallas_call(functools.partial(steer_kernel, along=along, places=places...  49.4 us
    ppermute x6, starting transfers between devices, swap_ends(): low = lax.ppermute(tail, axis, [(i, i + 1) for i in range(count - 1)])  25.5 us
    unnamed x34, local copies, waits for them, and re-layouts  19 us
    ppermute x6, starting transfers between devices, swap_ends(): high = lax.ppermute(head, axis, [(i + 1, i) for i in range(count - 1)])  13.6 us
    all_to_all x2, starting transfers between devices, on_device(): lax.all_to_all(pack(traces, target, lists, devices, capacity, part), BOTH...  10.8 us
    pallas_call x2, Pallas kernels, stack_bins(): pl.pallas_call(functools.partial(bin_kernel, part=part, capacity=capacity...  10.4 us
    pallas_call x2, Pallas kernels, pack(): pl.pallas_call(functools.partial(pack_kernel, part=part, capacity=capacit...  9.73 us
  transfers between devices with their start and end apart: 14, of which 3 were waited for; matrix products, arithmetic and copies ran while one was open for 4% of the time, Pallas kernels for 20%

profile of v4, /device:TPU:11, one launch (start us, length us, event | category | flops | bytes accessed | tf_op | source)
XLA Modules:
  0.0 233.4 jit_solution(16179705388758945726)
XLA Ops:
  0.0 0.7 convert_element_type.23
  0.8 1.6 copy-done.8
  2.4 0.7 copy-done.13
  3.1 4.9 %shard_map.55 = f32[32,136,128]{2,1,0:T(8,128)S(1)} custom-call(s32[128]{0:T(128)S(1)} %bitcast.12, f32[128,128]{1,0:T(8,128)S(1)} %pad.4.lists_ref, f32[128,4,1024]{2,1,0:T(4,128)S(1)} %copy-done.8), custom_call_target="tpu_custom_call" | custom-call | flops 536870912 | bytes 4194304 | tf_op jit(solution)/shard_map/pallas_call | solution.py:105
  8.0 1.4 copy-done.7
  9.3 6.3 %all-to-all-start = ((f32[32,136,128]{2,1,0:T(8,128)}), f32[32,136,128]{2,1,0:T(8,128)S(1)}, u32[]{:S(2)}, u32[]{:S(2)}) async-start(f32[32,136,128]{2,1,0:T(8,128)} %copy-done.7), calls=%async_computation | async-start | bytes 4456448 | tf_op jit(solution)/shard_map/all_to_all | solution.py:453
  15.7 1.6 copy-done.9
  17.3 4.8 %shard_map.56 = f32[32,128,128]{2,1,0:T(8,128)S(1)} custom-call(s32[128]{0:T(128)S(1)} %bitcast.13, f32[128,128]{1,0:T(8,128)S(1)} %pad.4.lists_ref, f32[128,4,1024]{2,1,0:T(4,128)S(1)} %copy-done.9), custom_call_target="tpu_custom_call" | custom-call | flops 536870912 | bytes 4194304 | tf_op jit(solution)/shard_map/pallas_call | solution.py:105
  22.1 1.3 copy-done.10
  23.5 42.5 %all-to-all-done.blocks_ref = f32[32,136,128]{2,1,0:T(8,128)S(1)} async-done(((f32[32,136,128]{2,1,0:T(8,128)}), f32[32,136,128]{2,1,0:T(8,128)S(1)}, u32[]{:S(2)}, u32[]{:S(2)}) %all-to-all-start) | async-done | bytes 2228256 | tf_op jit(solution)/shard_map/all_to_all | solution.py:453
  66.0 4.4 %all-to-all-start.1 = ((f32[32,128,128]{2,1,0:T(8,128)}), f32[32,128,128]{2,1,0:T(8,128)}, u32[]{:S(2)}, u32[]{:S(2)}) async-start(f32[32,128,128]{2,1,0:T(8,128)} %copy-done.10), calls=%async_computation.1 | async-start | bytes 4194304 | tf_op jit(solution)/shard_map/all_to_all | solution.py:453
  71.1 3.6 %shard_map.57.refs_0_ = f32[1024,8,128]{2,1,0:T(8,128)S(1)} custom-call(s32[1024]{0:T(1024)S(1)} %reshape.19.bins_ref, f32[1024]{0:T(1024)S(1)} %maximum_divide_fusion.scale_ref, f32[32,136,128]{2,1,0:T(8,128)S(1)} %all-to-all-done.blocks_ref), custom_call_target="tpu_custom_call" | custom-call | flops 8388608 | bytes 12582912 | tf_op jit(solution)/shard_map/pallas_call | solution.py:176
  74.7 2.0 copy-done.5
  76.7 41.3 %all-to-all-done.1.blocks_ref = f32[32,128,128]{2,1,0:T(8,128)} async-done(((f32[32,128,128]{2,1,0:T(8,128)}), f32[32,128,128]{2,1,0:T(8,128)}, u32[]{:S(2)}, u32[]{:S(2)}) %all-to-all-start.1) | async-done | bytes 2097184 | tf_op jit(solution)/shard_map/all_to_all | solution.py:453
  117.9 2.2 copy-done.6
  120.1 6.8 %shard_map.58 = f32[1024,8,128]{2,1,0:T(8,128)S(1)} custom-call(s32[1024]{0:T(1024)S(1)} %reshape.19.bins_ref, f32[1024]{0:T(1024)S(1)} %maximum_divide_fusion.scale_ref, f32[32,128,128]{2,1,0:T(8,128)} %all-to-all-done.1.blocks_ref, f32[1024,8,128]{2,1,0:T(8,128)S(1)} %copy-done.6), custom_call_target="tpu_custom_call" | custom-call | flops 8388608 | bytes 12582912 | tf_op jit(solution)/shard_map/pallas_call | solution.py:176
  127.2 1.8 copy-done
  129.0 0.8 pad_maximum_fusion.1
  129.8 2.5 %collective-permute-start.1 = (f32[7,16,8,128]{3,2,1,0:T(8,128)}, f32[7,16,8,128]{3,2,1,0:T(8,128)S(1)}, u32[]{:S(2)}, u32[]{:S(2)}) collective-permute-start(f32[7,16,8,128]{3,2,1,0:T(8,128)} %pad_maximum_fusion.1), channel_id=1, source_target_pairs={{4,0},{8,4},{12,8},{16,12},{20,16},{24,20},{28,24},{5,1},{9,5},{13... | collective-permute-start | bytes 1376264 | tf_op jit(solution)/shard_map/ppermute | solution.py:369
  132.3 0.8 pad_maximum_fusion
  133.1 4.0 %collective-permute-start = (f32[7,16,8,128]{3,2,1,0:T(8,128)}, f32[7,16,8,128]{3,2,1,0:T(8,128)S(1)}, u32[]{:S(2)}, u32[]{:S(2)}) collective-permute-start(f32[7,16,8,128]{3,2,1,0:T(8,128)} %pad_maximum_fusion), channel_id=1, source_target_pairs={{0,4},{4,8},{8,12},{12,16},{16,20},{20,24},{24,28},{1,5},{5,9},{9,... | collective-permute-start | bytes 1376264 | tf_op jit(solution)/shard_map/ppermute | solution.py:368
  137.3 0.8 slice.107
  138.1 0.8 slice.108
  138.9 1.9 collective-permute-start.4
  140.9 4.5 %collective-permute-start.3 = (f32[7,16,8,128]{3,2,1,0:T(8,128)}, f32[7,16,8,128]{3,2,1,0:T(8,128)S(1)}, u32[]{:S(2)}, u32[]{:S(2)}) collective-permute-start(f32[7,16,8,128]{3,2,1,0:T(8,128)} %slice.107), channel_id=1, source_target_pairs={{0,4},{4,8},{8,12},{12,16},{16,20},{20,24},{24,28},{1,5},{5,9},{9,... | collective-permute-start | bytes 1376264 | tf_op jit(solution)/shard_map/ppermute | solution.py:368
  145.6 0.8 copy-done.11
  146.4 1.2 broadcast_in_dim.27.dip_ref
  147.6 2.2 copy-done.1
  149.8 1.0 copy-done.12
  150.8 6.9 %shard_map.59.refs_1_ = f32[32,16,8,128]{3,2,1,0:T(8,128)S(1)} custom-call(bf16[32,256,128]{2,1,0:T(8,128)(2,1)S(1)} %broadcast_in_dim.27.dip_ref, f32[7,16,8,128]{3,2,1,0:T(8,128)S(1)} %copy-done.12, f32[32,32,8,128]{3,2,1,0:T(8,128)S(1)} %bitcast.10, f32[7,16,8,128]{3,2,1,0:T(8,128)S(1)} %collective-permute-done.1.refs_2_), custom_call_target="tpu_custom_call" | custom-call | flops 15728640 | bytes 8388608 | tf_op jit(solution)/shard_map/pallas_call | solution.py:349
  157.8 0.9 pad_maximum_fusion.2
  158.8 2.6 %collective-permute-start.2 = (f32[16,7,8,128]{3,2,1,0:T(8,128)}, f32[16,7,8,128]{3,2,1,0:T(8,128)}, u32[]{:S(2)}, u32[]{:S(2)}) collective-permute-start(f32[16,7,8,128]{3,2,1,0:T(8,128)} %pad_maximum_fusion.2), channel_id=1, source_target_pairs={{0,1},{1,2},{2,3},{4,5},{5,6},{6,7},{8,9},{9,10},{10,11},{12,13},{... | collective-permute-start | bytes 1376264 | tf_op jit(solution)/shard_map/ppermute | solution.py:368
  161.4 0.8 pad_maximum_fusion.3
  162.2 3.5 %collective-permute-start.5 = (f32[16,7,8,128]{3,2,1,0:T(8,128)}, f32[16,7,8,128]{3,2,1,0:T(8,128)}, u32[]{:S(2)}, u32[]{:S(2)}) collective-permute-start(f32[16,7,8,128]{3,2,1,0:T(8,128)} %pad_maximum_fusion.3), channel_id=1, source_target_pairs={{1,0},{2,1},{3,2},{5,4},{6,5},{7,6},{9,8},{10,9},{11,10},{13,12},{... | collective-permute-start | bytes 1376264 | tf_op jit(solution)/shard_map/ppermute | solution.py:369
  165.6 1.0 fusion.2
  166.6 1.9 collective-permute-start.8
  168.6 3.4 %collective-permute-start.7 = (f32[16,7,8,128]{3,2,1,0:T(8,128)}, f32[16,7,8,128]{3,2,1,0:T(8,128)S(1)}, u32[]{:S(2)}, u32[]{:S(2)}) collective-permute-start(f32[16,7,8,128]{3,2,1,0:T(8,128)} %get-tuple-element.12), channel_id=1, source_target_pairs={{0,1},{1,2},{2,3},{4,5},{5,6},{6,7},{8,9},{9,10},{10,11},{12,13},{... | collective-permute-start | bytes 1376264 | tf_op jit(solution)/shard_map/ppermute | solution.py:368
  172.0 2.2 copy-done.2
  174.2 6.9 %shard_map.60.refs_2_ = f32[32,16,8,128]{3,2,1,0:T(8,128)S(1)} custom-call(bf16[32,256,128]{2,1,0:T(8,128)(2,1)S(1)} %broadcast_in_dim.27.dip_ref, f32[7,16,8,128]{3,2,1,0:T(8,128)S(1)} %collective-permute-done.3.refs_0_, f32[32,32,8,128]{3,2,1,0:T(8,128)S(1)} %bitcast.11, f32[7,16,8,128]{3,2,1,0:T(8,128)S(1)} %collective-permute-done.4.refs_2_), custom_call_target="tpu_custom_call" | custom-call | flops 15728640 | bytes 8388608 | tf_op jit(solution)/shard_map/pallas_call | solution.py:349
  181.2 1.2 broadcast_in_dim.30.dip_ref
  182.8 7.6 %shard_map.61.refs_1_ = f32[16,32,8,128]{3,2,1,0:T(8,128)S(1)} custom-call(bf16[32,256,128]{2,1,0:T(8,128)(2,1)S(1)} %broadcast_in_dim.30.dip_ref, f32[16,7,8,128]{3,2,1,0:T(8,128)} %collective-permute-done.2.refs_0_, f32[32,16,8,128]{3,2,1,0:T(8,128)S(1)} %copy-done.4, f32[32,16,8,128]{3,2,1,0:T(8,128)S(1)} %shard_map.60.refs_2_, ...), custom_call_target="tpu_custom_call" | custom-call | flops 15728640 | bytes 8388608 | tf_op jit(solution)/shard_map/pallas_call | solution.py:349
  190.6 1.9 collective-permute-start.11
  192.5 6.3 %collective-permute-start.10 = (f32[7,16,8,128]{3,2,1,0:T(8,128)S(1)}, f32[7,16,8,128]{3,2,1,0:T(8,128)S(1)}, u32[]{:S(2)}, u32[]{:S(2)}) collective-permute-start(f32[7,16,8,128]{3,2,1,0:T(8,128)S(1)} %get-tuple-element.8), channel_id=1, source_target_pairs={{0,4},{4,8},{8,12},{12,16},{16,20},{20,24},{24,28},{1,5},{5,9},{9,... | collective-permute-start | bytes 1376264 | tf_op jit(solution)/shard_map/ppermute | solution.py:368
  198.8 1.9 collective-permute-start.9
  200.8 4.7 %collective-permute-start.6 = (f32[7,16,8,128]{3,2,1,0:T(8,128)S(1)}, f32[7,16,8,128]{3,2,1,0:T(8,128)S(1)}, u32[]{:S(2)}, u32[]{:S(2)}) collective-permute-start(f32[7,16,8,128]{3,2,1,0:T(8,128)S(1)} %get-tuple-element.10), channel_id=1, source_target_pairs={{0,4},{4,8},{8,12},{12,16},{16,20},{20,24},{24,28},{1,5},{5,9},{9,... | collective-permute-start | bytes 1376264 | tf_op jit(solution)/shard_map/ppermute | solution.py:368
  205.5 6.6 %shard_map.62.refs_2_ = f32[16,32,8,128]{3,2,1,0:T(8,128)S(1)} custom-call(bf16[32,256,128]{2,1,0:T(8,128)(2,1)S(1)} %broadcast_in_dim.30.dip_ref, f32[16,7,8,128]{3,2,1,0:T(8,128)S(1)} %collective-permute-done.7.refs_0_, f32[32,16,8,128]{3,2,1,0:T(8,128)S(1)} %copy-done.4, f32[32,16,8,128]{3,2,1,0:T(8,128)S(1)} %shard_map.60.refs_2_, ...), custom_call_target="tpu_custom_call" | custom-call | flops 15728640 | bytes 8388608 | tf_op jit(solution)/shard_map/pallas_call | solution.py:349
  212.1 10.7 %shard_map.63.refs_4_ = f32[32,32,1024]{2,1,0:T(8,128)} custom-call(bf16[32,256,128]{2,1,0:T(8,128)(2,1)S(1)} %broadcast_in_dim.27.dip_ref, f32[7,16,8,128]{3,2,1,0:T(8,128)S(1)} %collective-permute-done.10.refs_0_, f32[16,32,8,128]{3,2,1,0:T(8,128)S(1)} %shard_map.61.refs_1_, f32[16,32,8,128]{3,2,1,0:T(8,128)S(1)} %shard_map.62.refs_2_, ...), custom_call_target="tpu_custom_call" | custom-call | flops 15728640 | bytes 8388608 | tf_op jit(solution)/shard_map/pallas_call | solution.py:349
  222.8 10.7 %shard_map.64 = f32[32,32,1024]{2,1,0:T(8,128)} custom-call(bf16[32,256,128]{2,1,0:T(8,128)(2,1)S(1)} %broadcast_in_dim.27.dip_ref, f32[7,16,8,128]{3,2,1,0:T(8,128)S(1)} %collective-permute-done.6.refs_0_, f32[16,32,8,128]{3,2,1,0:T(8,128)S(1)} %shard_map.61.refs_1_, f32[16,32,8,128]{3,2,1,0:T(8,128)S(1)} %shard_map.62.refs_2_, ...), custom_call_target="tpu_custom_call", output_to_operand_aliasing={{}: (5, {})} | custom-call | flops 15728640 | bytes 8388608 | tf_op jit(solution)/shard_map/pallas_call | solution.py:349
  (52 shorter events, 2.0 us)
Async XLA Ops:
  0.8 1.6 copy-start.8
  2.4 0.7 copy-start.13
  8.0 1.4 copy-start.7
  9.3 6.4 %copy-start.14 = (s32[128,1]{0,1:T(1,128)S(1)}, s32[128,1]{0,1:T(1,128)}, u32[]{:S(2)}) copy-start(s32[128,1]{0,1:T(1,128)} %param.6) | copy-start | bytes 1540
  9.3 56.7 %all-to-all-start = ((f32[32,136,128]{2,1,0:T(8,128)}), f32[32,136,128]{2,1,0:T(8,128)S(1)}, u32[]{:S(2)}, u32[]{:S(2)}) async-start(f32[32,136,128]{2,1,0:T(8,128)} %copy-done.7), calls=%async_computation | async-start | bytes 4456448 | tf_op jit(solution)/shard_map/all_to_all | solution.py:453
  15.7 1.6 copy-start.9
  22.1 1.3 copy-start.10
  66.0 51.9 %all-to-all-start.1 = ((f32[32,128,128]{2,1,0:T(8,128)}), f32[32,128,128]{2,1,0:T(8,128)}, u32[]{:S(2)}, u32[]{:S(2)}) async-start(f32[32,128,128]{2,1,0:T(8,128)} %copy-done.10), calls=%async_computation.1 | async-start | bytes 4194304 | tf_op jit(solution)/shard_map/all_to_all | solution.py:453
  74.7 2.0 copy-start.5
  117.9 2.2 copy-start.6
  127.0 2.0 copy-start
  127.1 10.0 %copy-start.15 = (s32[32,32]{1,0:T(8,128)S(1)}, s32[32,32]{1,0:T(8,128)}, u32[]{:S(2)}) copy-start(s32[32,32]{1,0:T(8,128)} %param.9) | copy-start | bytes 12292
  127.1 10.1 %copy-start.16 = (s32[32,32]{1,0:T(8,128)S(1)}, s32[32,32]{1,0:T(8,128)}, u32[]{:S(2)}) copy-start(s32[32,32]{1,0:T(8,128)} %param.8) | copy-start | bytes 12292
  129.8 15.6 %collective-permute-start.1 = (f32[7,16,8,128]{3,2,1,0:T(8,128)}, f32[7,16,8,128]{3,2,1,0:T(8,128)S(1)}, u32[]{:S(2)}, u32[]{:S(2)}) collective-permute-start(f32[7,16,8,128]{3,2,1,0:T(8,128)} %pad_maximum_fusion.1), channel_id=1, source_target_pairs={{4,0},{8,4},{12,8},{16,12},{20,16},{24,20},{28,24},{5,1},{9,5},{13... | collective-permute-start | bytes 1376264 | tf_op jit(solution)/shard_map/ppermute | solution.py:369
  133.1 12.5 %collective-permute-start = (f32[7,16,8,128]{3,2,1,0:T(8,128)}, f32[7,16,8,128]{3,2,1,0:T(8,128)S(1)}, u32[]{:S(2)}, u32[]{:S(2)}) collective-permute-start(f32[7,16,8,128]{3,2,1,0:T(8,128)} %pad_maximum_fusion), channel_id=1, source_target_pairs={{0,4},{4,8},{8,12},{12,16},{16,20},{20,24},{24,28},{1,5},{5,9},{9,... | collective-permute-start | bytes 1376264 | tf_op jit(solution)/shard_map/ppermute | solution.py:368
  138.9 29.7 %collective-permute-start.4 = (f32[7,16,8,128]{3,2,1,0:T(8,128)}, f32[7,16,8,128]{3,2,1,0:T(8,128)S(1)}, u32[]{:S(2)}, u32[]{:S(2)}) collective-permute-start(f32[7,16,8,128]{3,2,1,0:T(8,128)} %slice.108), channel_id=1, source_target_pairs={{4,0},{8,4},{12,8},{16,12},{20,16},{24,20},{28,24},{5,1},{9,5},{13... | collective-permute-start | bytes 1376264 | tf_op jit(solution)/shard_map/ppermute | solution.py:369
  140.9 31.2 %collective-permute-start.3 = (f32[7,16,8,128]{3,2,1,0:T(8,128)}, f32[7,16,8,128]{3,2,1,0:T(8,128)S(1)}, u32[]{:S(2)}, u32[]{:S(2)}) collective-permute-start(f32[7,16,8,128]{3,2,1,0:T(8,128)} %slice.107), channel_id=1, source_target_pairs={{0,4},{4,8},{8,12},{12,16},{16,20},{20,24},{24,28},{1,5},{5,9},{9,... | collective-permute-start | bytes 1376264 | tf_op jit(solution)/shard_map/ppermute | solution.py:368
  145.6 0.8 copy-start.11
  147.6 2.2 copy-start.1
  149.8 1.0 copy-start.12
  157.8 8.9 %copy-start.3 = (f32[32,16,8,128]{3,2,1,0:T(8,128)}, f32[32,16,8,128]{3,2,1,0:T(8,128)S(1)}, u32[]{:S(2)}) copy-start(f32[32,16,8,128]{3,2,1,0:T(8,128)S(1)} %shard_map.59.refs_1_) | copy-start | bytes 6291460
  158.8 22.4 %collective-permute-start.2 = (f32[16,7,8,128]{3,2,1,0:T(8,128)}, f32[16,7,8,128]{3,2,1,0:T(8,128)}, u32[]{:S(2)}, u32[]{:S(2)}) collective-permute-start(f32[16,7,8,128]{3,2,1,0:T(8,128)} %pad_maximum_fusion.2), channel_id=1, source_target_pairs={{0,1},{1,2},{2,3},{4,5},{5,6},{6,7},{8,9},{9,10},{10,11},{12,13},{... | collective-permute-start | bytes 1376264 | tf_op jit(solution)/shard_map/ppermute | solution.py:368
  162.2 19.0 %collective-permute-start.5 = (f32[16,7,8,128]{3,2,1,0:T(8,128)}, f32[16,7,8,128]{3,2,1,0:T(8,128)}, u32[]{:S(2)}, u32[]{:S(2)}) collective-permute-start(f32[16,7,8,128]{3,2,1,0:T(8,128)} %pad_maximum_fusion.3), channel_id=1, source_target_pairs={{1,0},{2,1},{3,2},{5,4},{6,5},{7,6},{9,8},{10,9},{11,10},{13,12},{... | collective-permute-start | bytes 1376264 | tf_op jit(solution)/shard_map/ppermute | solution.py:369
  166.6 34.1 %collective-permute-start.8 = (f32[16,7,8,128]{3,2,1,0:T(8,128)}, f32[16,7,8,128]{3,2,1,0:T(8,128)S(1)}, u32[]{:S(2)}, u32[]{:S(2)}) collective-permute-start(f32[16,7,8,128]{3,2,1,0:T(8,128)} %get-tuple-element.11), channel_id=1, source_target_pairs={{1,0},{2,1},{3,2},{5,4},{6,5},{7,6},{9,8},{10,9},{11,10},{13,12},{... | collective-permute-start | bytes 1376264 | tf_op jit(solution)/shard_map/ppermute | solution.py:369
  168.6 36.8 %collective-permute-start.7 = (f32[16,7,8,128]{3,2,1,0:T(8,128)}, f32[16,7,8,128]{3,2,1,0:T(8,128)S(1)}, u32[]{:S(2)}, u32[]{:S(2)}) collective-permute-start(f32[16,7,8,128]{3,2,1,0:T(8,128)} %get-tuple-element.12), channel_id=1, source_target_pairs={{0,1},{1,2},{2,3},{4,5},{5,6},{6,7},{8,9},{9,10},{10,11},{12,13},{... | collective-permute-start | bytes 1376264 | tf_op jit(solution)/shard_map/ppermute | solution.py:368
  172.0 2.2 copy-start.2
  181.2 1.6 copy-start.4
  190.6 21.5 %collective-permute-start.11 = (f32[7,16,8,128]{3,2,1,0:T(8,128)S(1)}, f32[7,16,8,128]{3,2,1,0:T(8,128)S(1)}, u32[]{:S(2)}, u32[]{:S(2)}) collective-permute-start(f32[7,16,8,128]{3,2,1,0:T(8,128)S(1)} %get-tuple-element.7), channel_id=1, source_target_pairs={{4,0},{8,4},{12,8},{16,12},{20,16},{24,20},{28,24},{5,1},{9,5},{13... | collective-permute-start | bytes 1376264 | tf_op jit(solution)/shard_map/ppermute | solution.py:369
  192.5 19.6 %collective-permute-start.10 = (f32[7,16,8,128]{3,2,1,0:T(8,128)S(1)}, f32[7,16,8,128]{3,2,1,0:T(8,128)S(1)}, u32[]{:S(2)}, u32[]{:S(2)}) collective-permute-start(f32[7,16,8,128]{3,2,1,0:T(8,128)S(1)} %get-tuple-element.8), channel_id=1, source_target_pairs={{0,4},{4,8},{8,12},{12,16},{16,20},{20,24},{24,28},{1,5},{5,9},{9,... | collective-permute-start | bytes 1376264 | tf_op jit(solution)/shard_map/ppermute | solution.py:368
  198.8 23.9 %collective-permute-start.9 = (f32[7,16,8,128]{3,2,1,0:T(8,128)S(1)}, f32[7,16,8,128]{3,2,1,0:T(8,128)S(1)}, u32[]{:S(2)}, u32[]{:S(2)}) collective-permute-start(f32[7,16,8,128]{3,2,1,0:T(8,128)S(1)} %get-tuple-element.9), channel_id=1, source_target_pairs={{4,0},{8,4},{12,8},{16,12},{20,16},{24,20},{28,24},{5,1},{9,5},{13... | collective-permute-start | bytes 1376264 | tf_op jit(solution)/shard_map/ppermute | solution.py:369
  200.8 22.0 %collective-permute-start.6 = (f32[7,16,8,128]{3,2,1,0:T(8,128)S(1)}, f32[7,16,8,128]{3,2,1,0:T(8,128)S(1)}, u32[]{:S(2)}, u32[]{:S(2)}) collective-permute-start(f32[7,16,8,128]{3,2,1,0:T(8,128)S(1)} %get-tuple-element.10), channel_id=1, source_target_pairs={{0,4},{4,8},{8,12},{12,16},{16,20},{20,24},{24,28},{1,5},{5,9},{9,... | collective-permute-start | bytes 1376264 | tf_op jit(solution)/shard_map/ppermute | solution.py:368

commit v5 on v0

v5 whole, which is shorter than its diff:
```python
import functools

import jax
import jax.numpy as jnp
import numpy as np
from jax import lax
from jax.experimental import pallas as pl
from jax.experimental.pallas import tpu as pltpu
from jax.sharding import PartitionSpec as P

HALF = 7
DMAX = 2
LANES = 128
PHASES = 8
PAIR = 2 * PHASES
WIDE = 2 * LANES
BORDER = 8
REACH = -(-HALF * DMAX // PHASES)
REACHES = range(-REACH, REACH + 1)
BOTH = ("inline", "crosslin")
MIB = 2**20
VMEM = pl.BlockSpec(memory_space=pltpu.VMEM)
SMEM = pl.BlockSpec(memory_space=pltpu.SMEM)
ANY = pl.BlockSpec(memory_space=pl.ANY)
HBM = pl.BlockSpec(memory_space=pltpu.HBM)
F32, BF16, I32 = jnp.float32, jnp.bfloat16, jnp.int32


def interleave_table(samples):
    table = np.zeros((samples, samples), np.float32)
    time = np.arange(samples)
    table[time, time % PHASES * LANES + time // PHASES] = 1.0
    return table


def move_samples(rows, table):
    count = rows.shape[0]
    upper = rows.astype(BF16)
    rest = (rows - upper.astype(F32)).astype(BF16)
    both = jnp.concatenate([upper, rest], axis=0)
    moved = jnp.dot(both, table, preferred_element_type=F32)
    return moved[:count] + moved[count:]


def pack_kernel(target_ref, bins_ref, traces_ref, table_ref, out_ref, tiles_ref, used_ref, listed_ref, sem, listed_sem, *, capacity):
    held, block_rows, samples = traces_ref.shape
    devices, room, _ = listed_ref.shape
    span = block_rows * PHASES
    groups = 2
    lane = lax.broadcasted_iota(I32, (1, LANES), 1)
    listed_ref[...] = jnp.full(listed_ref.shape, -1.0, F32)

    def clear(device, _):
        used_ref[device] = 0
        return 0

    lax.fori_loop(0, devices, clear, 0)

    def send_block(block, _):
        device = target_ref[block]
        rank = used_ref[device]
        used_ref[device] = rank + 1
        pltpu.make_async_copy(
            tiles_ref.at[pl.ds(pl.multiple_of(block * span, 8), span), :],
            out_ref.at[device, pl.ds(pl.multiple_of(rank * span, 8), span), :],
            sem,
        ).start()
        row = jnp.zeros((1, LANES), I32)
        for j in range(block_rows):
            row = jnp.where(lane == j, bins_ref[j, block], row)
        listed_ref[device, pl.ds(rank, 1), :] = row.astype(F32)
        return 0

    for group in range(groups):
        count = held // groups
        rows = traces_ref[group * count : (group + 1) * count].reshape(count * block_rows, samples)
        moved = move_samples(rows, table_ref[...])
        for eight in range(count * block_rows // 8):
            for phase in range(PHASES):
                first = (group * count * block_rows + eight * 8) * PHASES + phase
                tiles_ref[pl.ds(first, 8, stride=PHASES), :] = moved[
                    eight * 8 : eight * 8 + 8, phase * LANES : (phase + 1) * LANES
                ]
        lax.fori_loop(group * count, (group + 1) * count, send_block, 0, unroll=4)
    copy = pltpu.make_async_copy(
        listed_ref, out_ref.at[:, capacity * span : capacity * span + room, :], listed_sem
    )
    copy.start()
    copy.wait()
    pltpu.make_async_copy(tiles_ref, tiles_ref, sem).wait()


def pack(traces, target, bins, table, devices, capacity):
    held, block_rows, samples = traces.shape
    span = block_rows * PHASES
    room = -(-capacity // 8) * 8
    return pl.pallas_call(
        functools.partial(pack_kernel, capacity=capacity),
        in_specs=[SMEM, SMEM, VMEM, VMEM],
        out_specs=HBM,
        out_shape=jax.ShapeDtypeStruct((devices, capacity * span + room, LANES), F32),
        scratch_shapes=[
            pltpu.VMEM((held * span, LANES), F32),
            pltpu.SMEM((devices,), I32),
            pltpu.VMEM((devices, room, LANES), F32),
            pltpu.SemaphoreType.DMA,
            pltpu.SemaphoreType.DMA,
        ],
        compiler_params=pltpu.CompilerParams(vmem_limit_bytes=20 * MIB),
    )(target, bins, traces, table)


def bin_kernel(blocks_ref, out_ref, head_ref, tail_ref, even_ref, odd_ref, listed_ref, places_ref, fold_ref, sems, *, capacity, edge):
    devices, rows, _ = blocks_ref.shape
    room = listed_ref.shape[1]
    bin_total = out_ref.shape[0]
    block_rows = (rows - room) // (capacity * PHASES)
    unroll = 8
    listed = blocks_ref[:, rows - room :, :]
    listed_ref[...] = jnp.where(listed < 0, float(bin_total), listed).astype(I32)
    copy = pltpu.make_async_copy(listed_ref, places_ref, sems.at[0])
    copy.start()
    nothing = jnp.zeros((PHASES, LANES), F32)

    def clear(i, _):
        for j in range(unroll):
            even_ref[i * unroll + j] = nothing
            odd_ref[i * unroll + j] = nothing
            fold_ref[i * unroll + j] = 0
        return 0

    lax.fori_loop(0, bin_total // unroll, clear, 0)
    fold_ref[bin_total] = 0
    copy.wait()

    def add_sender(sender, _):
        for rank in range(capacity):
            for j in range(block_rows):
                total_ref = odd_ref if j % 2 else even_ref
                place = places_ref[sender, rank, j]
                row = (rank * block_rows + j) * PHASES
                total_ref[place] += blocks_ref[sender, row : row + PHASES, :]
                fold_ref[place] = fold_ref[place] + 1
        return 0

    lax.fori_loop(0, devices, add_sender, 0)

    def finish(i, _):
        for j in range(unroll):
            place = i * unroll + j
            fold = jnp.full((PHASES, LANES), jnp.maximum(fold_ref[place], 1).astype(F32))
            out_ref[place] = (even_ref[place] + odd_ref[place]) / fold
        return 0

    lax.fori_loop(0, edge // unroll, finish, 0)
    head_copy = pltpu.make_async_copy(out_ref.at[pl.ds(0, edge)], head_ref, sems.at[1])
    head_copy.start()
    lax.fori_loop((bin_total - edge) // unroll, bin_total // unroll, finish, 0)
    tail_copy = pltpu.make_async_copy(out_ref.at[pl.ds(bin_total - edge, edge)], tail_ref, sems.at[2])
    tail_copy.start()
    lax.fori_loop(edge // unroll, (bin_total - edge) // unroll, finish, 0)
    head_copy.wait()
    tail_copy.wait()


def stack_bins(blocks, tile_rows, tile_cols, capacity):
    devices = blocks.shape[0]
    bin_total = tile_rows * tile_cols
    edge = HALF * tile_cols
    room = -(-capacity // 8) * 8
    stacked, head, tail = pl.pallas_call(
        functools.partial(bin_kernel, capacity=capacity, edge=edge),
        in_specs=[VMEM],
        out_specs=[VMEM, HBM, HBM],
        out_shape=[
            jax.ShapeDtypeStruct((bin_total, PHASES, LANES), F32),
            jax.ShapeDtypeStruct((edge, PHASES, LANES), F32),
            jax.ShapeDtypeStruct((edge, PHASES, LANES), F32),
        ],
        scratch_shapes=[
            pltpu.VMEM((bin_total + 8, PHASES, LANES), F32),
            pltpu.VMEM((bin_total + 8, PHASES, LANES), F32),
            pltpu.VMEM((devices, room, LANES), I32),
            pltpu.SMEM((devices, room, LANES), I32),
            pltpu.SMEM((bin_total + 8,), I32),
            pltpu.SemaphoreType.DMA((3,)),
        ],
        compiler_params=pltpu.CompilerParams(vmem_limit_bytes=20 * MIB),
    )(blocks)
    shape = (tile_cols, PHASES, LANES)
    return stacked.reshape((tile_rows,) + shape), head.reshape((HALF,) + shape), tail.reshape((HALF,) + shape)


def fill_weights(spots_ref, weights_ref):
    row = lax.broadcasted_iota(I32, (PAIR, LANES), 0)
    column = lax.broadcasted_iota(I32, (PAIR, LANES), 1)
    for pair in range(spots_ref.shape[0] // (2 * PAIR)):
        for half in range(2):
            block = pl.ds((pair * 2 + half) * PAIR, PAIR)
            spot = half * PAIR + column // PHASES - HALF - 2 * pair - row // PHASES
            share = jnp.maximum(HALF + 1 - jnp.abs(spot), 0).astype(F32) / (HALF + 1) ** 2
            spots_ref[block, :] = jnp.clip(spot, -HALF - 1, HALF + 1).astype(F32).astype(BF16)
            weights_ref[block, :] = share.astype(BF16)


def steer_window(dip_of, cells, first, count, put, halves_ref, spots_ref, weights_ref):
    for pair in range(len(cells) // 2):
        both = jnp.concatenate([cells[2 * pair](), cells[2 * pair + 1]()], axis=0)
        upper = both.astype(BF16)
        halves_ref[pair * PAIR : (pair + 1) * PAIR, :LANES] = upper
        rest = (both - upper.astype(F32)).astype(BF16)
        halves_ref[pair * PAIR : (pair + 1) * PAIR, LANES:] = rest
    row = lax.broadcasted_iota(I32, (PAIR, LANES), 0)
    column = lax.broadcasted_iota(I32, (PAIR, LANES), 1)
    phase_gap = ((row & (PHASES - 1)) - (column & (PHASES - 1))).astype(F32).astype(BF16)
    lane = lax.broadcasted_iota(I32, (PHASES, LANES), 1)
    none = jnp.zeros((PAIR, LANES), BF16)
    taps = []
    for pair in range(count // 2):
        dip = dip_of(first // 2 + pair)
        moves, weights = [], []
        for half in range(2):
            block = pl.ds((pair * 2 + half) * PAIR, PAIR)
            moves.append(phase_gap + dip * spots_ref[block, :])
            weights.append(weights_ref[block, :])
        for reach in REACHES:
            taps.append(
                jnp.concatenate(
                    [jnp.where(moves[h] == jnp.bfloat16(reach * PHASES), weights[h], none) for h in range(2)],
                    axis=1,
                )
            )
    sums = jnp.dot(jnp.concatenate(taps, axis=0), halves_ref[...], preferred_element_type=F32)
    for pair in range(count // 2):
        for member in range(2):
            total = None
            for reach in REACHES:
                begin = (pair * len(REACHES) + reach + REACH) * PAIR + member * PHASES
                part = sums[begin : begin + PHASES, :LANES] + sums[begin : begin + PHASES, LANES:]
                if reach:
                    part = pltpu.roll(part, (-reach) % LANES, axis=1)
                    inside = lane < LANES - reach if reach > 0 else lane >= -reach
                    part = jnp.where(inside, part, 0.0)
                total = part if total is None else total + part
            put(first + 2 * pair + member, total)


def steer_kernel(dip_ref, *refs, along, whole, lines, line_of, windows, local_of, edges, final, chained, pieces_count):
    pieces, refs = refs[:pieces_count], refs[pieces_count:]
    if final:
        table_ref, refs = refs[0], refs[1:]
    if chained:
        refs = refs[1:]
    out_ref, refs = refs[0], refs[1:]
    edge_refs, refs = refs[: len(edges)], refs[len(edges) :]
    spots_ref, weights_ref, sems, *refs = refs
    halves = refs[: 2 * len(windows)]
    if final:
        staged_ref, result_ref = refs[2 * len(windows) :]
    fill_weights(spots_ref, weights_ref)
    for i, halves_ref in enumerate(halves):
        filled = len(windows[i % len(windows)][2]) * PHASES
        if filled < WIDE:
            halves_ref[filled:, :] = jnp.zeros((WIDE - filled, WIDE), BF16)

    def at(place, line):
        return (place, line) if along == 0 else (line, place)

    def one_line(line, parity):
        full = line_of(line)

        def cell(index, local):
            return lambda: pieces[index][at(local, full if whole[index] else line)]

        def put(place, value):
            if final:
                staged_ref[pl.ds((local_of(place) * final + line % final) * PHASES, PHASES), :] = value
            else:
                out_ref[at(local_of(place), line)] = value

        for i, (first, count, places) in enumerate(windows):
            steer_window(
                lambda pair: dip_ref[full, pair * PAIR : (pair + 1) * PAIR, :],
                [cell(*place) for place in places],
                first, count, put, halves[parity * len(windows) + i], spots_ref, weights_ref,
            )

    def two_lines(i, _):
        one_line(2 * i, 0)
        one_line(2 * i + 1, 1)
        return 0

    if not final:
        lax.fori_loop(0, lines // 2, two_lines, 0)
        copies = [
            pltpu.make_async_copy(out_ref.at[pick], edge_ref, sems.at[i])
            for i, (pick, edge_ref) in enumerate(zip(edges, edge_refs))
        ]
        for copy in copies:
            copy.start()
        for copy in copies:
            copy.wait()
        return

    outputs = sum(count for _, count, _ in windows)

    def copies_of(batch, slot):
        return [
            pltpu.make_async_copy(
                result_ref.at[slot, pl.ds(local_of(first), count)],
                out_ref.at[pl.ds(first, count), pl.ds(pl.multiple_of(batch * final, 8), final), :],
                sems.at[slot * len(windows) + i],
            )
            for i, (first, count, _) in enumerate(windows)
        ]

    for batch in range(lines // final):
        lax.fori_loop(batch * final // 2, (batch + 1) * final // 2, two_lines, 0)
        rows = jnp.concatenate(
            [
                jnp.concatenate(
                    [
                        staged_ref[pl.ds(eight * 8 * PHASES + phase, 8, stride=PHASES), :]
                        for phase in range(PHASES)
                    ],
                    axis=1,
                )
                for eight in range(outputs * final // 8)
            ],
            axis=0,
        )
        slot = batch % 2
        if batch >= 2:
            for copy in copies_of(batch - 2, slot):
                copy.wait()
        result_ref[slot] = move_samples(rows, table_ref[...]).reshape(result_ref.shape[1:])
        for copy in copies_of(batch, slot):
            copy.start()
    for batch in range(max(0, lines // final - 2), lines // final):
        for copy in copies_of(batch, batch % 2):
            copy.wait()


def steer(dip, pieces, along, lines, line_of, windows, local_of, edges=(), table=None, before=None):
    samples = PHASES * LANES
    outputs = sum(count for _, count, _ in windows)
    final = 16 if table is not None else 0
    operands = [dip] + [array for array, _ in pieces]
    in_specs = [VMEM] * len(operands)
    aliases = {}
    if final:
        operands.append(table)
        in_specs.append(VMEM)
        if before is not None:
            aliases = {len(operands): 0}
            operands.append(before)
            in_specs.append(HBM)
        extent = dip.shape[1] // PHASES
        out_shape = [jax.ShapeDtypeStruct((extent, lines, samples), F32)]
        out_specs = [HBM]
    else:
        shape = (outputs, lines) if along == 0 else (lines, outputs)
        out_shape = [jax.ShapeDtypeStruct(shape + (PHASES, LANES), F32)]
        out_specs = [VMEM]
        for pick in edges:
            size = [len(range(*s.indices(n))) for s, n in zip(pick, shape)]
            out_shape.append(jax.ShapeDtypeStruct(tuple(size) + (PHASES, LANES), F32))
            out_specs.append(HBM)
    most = max(count for _, count, _ in windows)
    constant = pltpu.VMEM((most * PAIR, LANES), BF16)
    scratch = [constant, constant, pltpu.SemaphoreType.DMA((2 * len(windows) if final else max(1, len(edges)),))]
    scratch += [pltpu.VMEM((WIDE, WIDE), BF16)] * (2 * len(windows))
    if final:
        scratch += [
            pltpu.VMEM((outputs * final * PHASES, LANES), F32),
            pltpu.VMEM((2, outputs, final, samples), F32),
        ]
    return pl.pallas_call(
        functools.partial(
            steer_kernel,
            along=along, whole=[whole for _, whole in pieces], lines=lines, line_of=line_of, windows=windows,
            local_of=local_of, edges=edges, final=final, chained=before is not None, pieces_count=len(pieces),
        ),
        in_specs=in_specs,
        out_specs=out_specs,
        out_shape=out_shape,
        scratch_shapes=scratch,
        input_output_aliases=aliases,
        compiler_params=pltpu.CompilerParams(vmem_limit_bytes=16 * MIB),
        cost_estimate=pl.CostEstimate(
            flops=2400 * outputs * lines * samples,
            bytes_accessed=8 * outputs * lines * samples,
            transcendentals=0,
        ),
    )(*operands)


def swap_ends(head, tail, axis):
    count = lax.axis_size(axis)
    low = lax.ppermute(tail, axis, [(i, i + 1) for i in range(count - 1)])
    high = lax.ppermute(head, axis, [(i + 1, i) for i in range(count - 1)])
    return low, high


def dip_tiles(dip):
    lines, extent = dip.shape
    tiles = jnp.broadcast_to(dip.astype(BF16)[:, :, None, None], (lines, extent, PHASES, LANES))
    return tiles.reshape(lines, extent * PHASES, LANES)


def span_of(index, first, count):
    return [(index, first + i) for i in range(count)]


def smooth(stacked, head, tail, along_rows, along_cols, table):
    rows, cols = stacked.shape[:2]
    mid_rows, mid_cols = rows - 2 * BORDER, cols - 2 * BORDER
    same = lambda line: line
    inner = lambda line: line + BORDER
    outer_col = lambda line: line + jnp.where(line < BORDER, 0, mid_cols)
    outer_row = lambda line: line + jnp.where(line < BORDER, 0, mid_rows)
    mid_place = lambda place: place - BORDER
    outer_place = lambda place: place if place < BORDER else place - mid_rows
    every = slice(None)
    lead, last = slice(0, HALF), slice(2 * BORDER - HALF, 2 * BORDER)

    def mid_windows(places):
        return [(BORDER + i, 16, places[i : i + 16 + 2 * HALF]) for i in range(0, mid_rows, 16)]

    low, high = swap_ends(head, tail, "inline")
    middle, head_mid, tail_mid = steer(
        along_rows, [(stacked, True)], 0, cols, same,
        mid_windows(span_of(0, BORDER - HALF, mid_rows + 2 * HALF)), mid_place,
        edges=[(every, lead), (every, slice(cols - HALF, cols))],
    )
    low_mid, high_mid = swap_ends(head_mid, tail_mid, "crosslin")
    pieces = [(low, True), (stacked, True), (high, True)]
    windows = [
        (0, BORDER, span_of(0, 0, HALF) + span_of(1, 0, BORDER + HALF)),
        (rows - BORDER, BORDER, span_of(1, rows - BORDER - HALF, BORDER + HALF) + span_of(2, 0, HALF)),
    ]
    corners, head_out, tail_out = steer(
        along_rows, pieces, 0, 2 * BORDER, outer_col, windows, outer_place, edges=[(every, lead), (every, last)]
    )
    low_out, high_out = swap_ends(head_out, tail_out, "crosslin")
    (flanks,) = steer(along_rows, pieces, 0, mid_cols, inner, windows, outer_place)

    def cross_windows(places):
        return [(i, 16, places[i : i + 16 + 2 * HALF]) for i in range(0, cols, 16)]

    places = span_of(0, 0, HALF) + span_of(1, 0, cols) + span_of(2, 0, HALF)
    (middle_second,) = steer(
        along_cols, [(low_mid, False), (middle, False), (high_mid, False)], 1, mid_rows, inner,
        cross_windows(places), same,
    )
    places = (
        span_of(0, 0, HALF) + span_of(1, 0, BORDER) + span_of(2, 0, mid_cols) + span_of(1, BORDER, BORDER) + span_of(3, 0, HALF)
    )
    border_second, head, tail = steer(
        along_cols, [(low_out, False), (corners, False), (flanks, False), (high_out, False)], 1, 2 * BORDER,
        outer_row, cross_windows(places), same, edges=[(lead, every), (last, every)],
    )

    low, high = swap_ends(head, tail, "inline")
    places = span_of(0, BORDER - HALF, HALF) + span_of(1, 0, mid_rows) + span_of(0, BORDER, HALF)
    (result,) = steer(
        along_rows, [(border_second, True), (middle_second, True)], 0, cols, same, mid_windows(places), mid_place,
        table=table,
    )
    windows = [
        (0, BORDER, span_of(0, 0, HALF) + span_of(1, 0, BORDER) + span_of(2, 0, HALF)),
        (rows - BORDER, BORDER, span_of(2, mid_rows - HALF, HALF) + span_of(1, BORDER, BORDER) + span_of(3, 0, HALF)),
    ]
    (result,) = steer(
        along_rows, [(low, True), (border_second, True), (middle_second, True), (high, True)], 0, cols, same,
        windows, outer_place, table=table, before=result,
    )
    return result


def on_device(traces, destination, bin_index, dip_inline, dip_cross):
    held, block_rows, samples = traces.shape
    devices = lax.axis_size("inline") * lax.axis_size("crosslin")
    capacity = 2 * held // devices
    tile_rows, tile_cols = dip_inline.shape
    table = interleave_table(samples)
    outgoing = pack(traces, destination.reshape(-1), bin_index.T, jnp.asarray(table, BF16), devices, capacity)
    arrived = lax.all_to_all(outgoing, BOTH, split_axis=0, concat_axis=0, tiled=True)
    back, along_rows, along_cols = jnp.asarray(table.T, BF16), dip_tiles(dip_inline.T), dip_tiles(dip_cross)
    arrived, along_rows, along_cols = lax.optimization_barrier((arrived, along_rows, along_cols))
    stacked, head, tail = stack_bins(arrived, tile_rows, tile_cols, capacity)
    return smooth(stacked, head, tail, along_rows, along_cols, back)


def solution(mesh):
    return jax.shard_map(
        on_device,
        mesh=mesh,
        in_specs=(
            P(BOTH, None, None),
            P(BOTH, None),
            P(BOTH, None),
            P("inline", "crosslin"),
            P("inline", "crosslin"),
        ),
        out_specs=P("inline", "crosslin", None),
        check_vma=False,
    )
```

time: 847 us -> 239 us (0.28); the launches traced: 832 us -> 235 us
  other arithmetic: 622 us -> 0.01 us
  Pallas kernels: 0 us -> 67.3 us
  local copies, waits for them, and re-layouts: 29.4 us -> 9.3 us
  waiting for transfers between devices: 142 us -> 131 us
  matrix products: 9.71 us -> 0 us
    select_n x6 -> x0, other arithmetic: 620 us -> none  [the longest x3 615 us: steer(): result = jnp.where((dip_index == dip_value)[..., None], running, result)]
    pallas_call x0 -> x9, Pallas kernels: none -> 67.3 us  [the longest x7 46.8 us: steer(): pl.pallas_call(functools.partial(steer_kernel, along=along, whole=[whole...]
    ppermute x6 -> x8, waiting for transfers between devices: 50.6 us -> 36.1 us  [the longest x4 25.5 us: swap_ends(): low = lax.ppermute(tail, axis, [(i, i + 1) for i in range(count - 1)])]
    pad x3 -> x0, local copies, waits for them, and re-layouts: 10.3 us -> none  [pad_time(): return jnp.pad(gridded, ((0, 0), (0, 0), (margin, margin)))]
    dot_general x1 -> x0, matrix products: 9.71 us -> none  [on_device(): jnp.dot(member, arrived_rows, precision=lax.Precision.HIGHEST, preferred_...]
    ppermute x6 -> x8, starting transfers between devices: 15.6 us -> 20.8 us  [the longest x4 11.3 us: swap_ends(): high = lax.ppermute(head, axis, [(i + 1, i) for i in range(count - 1)])]
    all_to_all x2 -> x1, waiting for transfers between devices: 91.7 us -> 95.1 us  [on_device(): lax.all_to_all(outgoing, BOTH, split_axis=0, concat_axis=0, tiled=True)]
  transfers between devices with their start and end apart: 8 -> 9, of which waited for: 6 -> 7; matrix products, arithmetic and copies ran while one was open for 3% -> 0% of each run, Pallas kernels for 0% -> 11%
where the time goes in v5:
time: 239 us; the launch traced here: 235 us
  waiting for transfers between devices  131 us (55%)
  Pallas kernels  67.3 us (28%)
  starting transfers between devices  27.2 us (11%)
  local copies, waits for them, and re-layouts  9.3 us (4%)
    all_to_all x1, waiting for transfers between devices, on_device(): lax.all_to_all(outgoing, BOTH, split_axis=0, concat_axis=0, tiled=True)  95.1 us
    pallas_call x7, Pallas kernels, steer(): pl.pallas_call(functools.partial(steer_kernel, along=along, whole=[whole...  46.8 us
    ppermute x4, waiting for transfers between devices, swap_ends(): low = lax.ppermute(tail, axis, [(i, i + 1) for i in range(count - 1)])  25.5 us
    pallas_call x1, Pallas kernels, stack_bins(): pl.pallas_call(functools.partial(bin_kernel, capacity=capacity, edge=edge...  12.8 us
    ppermute x4, starting transfers between devices, swap_ends(): high = lax.ppermute(head, axis, [(i + 1, i) for i in range(count - 1)])  11.3 us
    ppermute x4, waiting for transfers between devices, swap_ends(): high = lax.ppermute(head, axis, [(i + 1, i) for i in range(count - 1)])  10.6 us
    ppermute x4, starting transfers between devices, swap_ends(): low = lax.ppermute(tail, axis, [(i, i + 1) for i in range(count - 1)])  9.55 us
    pallas_call x1, Pallas kernels, pack(): pl.pallas_call(functools.partial(pack_kernel, capacity=capacity), in_spec...  7.72 us
  transfers between devices with their start and end apart: 9, of which 7 were waited for; matrix products, arithmetic and copies ran while one was open for 0% of the time, Pallas kernels for 11%

profile of v5, /device:TPU:11, one launch (start us, length us, event | category | flops | bytes accessed | tf_op | source)
XLA Modules:
  0.0 235.4 jit_solution(1526694739922221810)
XLA Ops:
  0.0 0.0 copy-start.2
  0.0 1.6 copy-done.2
  1.6 0.0 copy-start.3
  1.6 1.6 copy-done.3
  3.2 0.0 copy-start.4
  3.2 0.7 copy-done.4
  3.9 0.0 copy-start.5
  3.9 0.7 copy-done.5
  4.5 7.7 %shard_map.73 = f32[32,264,128]{2,1,0:T(8,128)S(1)} custom-call(s32[128]{0:T(128)S(1)} %bitcast.15, s32[4,128]{1,0:T(4,128)S(1)} %bitcast.14, f32[128,4,1024]{2,1,0:T(4,128)S(1)} %copy-done.2, bf16[1024,1024]{1,0:T(8,128)(2,1)S(1)} %copy-done.3), custom_call_target="tpu_custom_call" | custom-call | tf_op jit(solution)/shard_map/pallas_call | solution.py:97
  12.3 0.0 copy-start
  12.3 2.1 copy-done
  14.3 0.0 copy-start.6
  14.3 0.0 copy-start.7
  14.3 6.4 %all-to-all-start = ((f32[32,264,128]{2,1,0:T(8,128)}), f32[32,264,128]{2,1,0:T(8,128)}, u32[]{:S(2)}, u32[]{:S(2)}) async-start(f32[32,264,128]{2,1,0:T(8,128)} %copy-done), calls=%async_computation | async-start | bytes 8650752 | tf_op jit(solution)/shard_map/all_to_all | solution.py:488
  20.7 0.0 copy-done.6
  20.7 0.1 copy.11
  20.8 0.1 copy.12
  20.9 0.0 copy-done.7
  21.0 0.1 copy.10
  21.0 95.1 %all-to-all-done.blocks_ref = f32[32,264,128]{2,1,0:T(8,128)} async-done(((f32[32,264,128]{2,1,0:T(8,128)}), f32[32,264,128]{2,1,0:T(8,128)}, u32[]{:S(2)}, u32[]{:S(2)}) %all-to-all-start) | async-done | bytes 4325408 | tf_op jit(solution)/shard_map/all_to_all | solution.py:488
  116.1 1.2 broadcast_in_dim.22.dip_ref
  117.3 1.2 broadcast_in_dim.25.dip_ref
  118.6 12.8 %shard_map.74 = (f32[1024,8,128]{2,1,0:T(8,128)S(1)}, f32[224,8,128]{2,1,0:T(8,128)S(1)}, f32[224,8,128]{2,1,0:T(8,128)S(1)}) custom-call(f32[32,264,128]{2,1,0:T(8,128)} %all-to-all-done.blocks_ref), custom_call_target="tpu_custom_call" | custom-call | tf_op jit(solution)/shard_map/pallas_call | solution.py:171
  131.4 3.8 %collective-permute-start = (f32[7,32,8,128]{3,2,1,0:T(8,128)S(1)}, f32[7,32,8,128]{3,2,1,0:T(8,128)S(1)}, u32[]{:S(2)}, u32[]{:S(2)}) collective-permute-start(f32[7,32,8,128]{3,2,1,0:T(8,128)S(1)} %bitcast.17), channel_id=1, source_target_pairs={{0,4},{4,8},{8,12},{12,16},{16,20},{20,24},{24,28},{1,5},{5,9},{9,... | collective-permute-start | bytes 2752520 | tf_op jit(solution)/shard_map/ppermute | solution.py:400
  135.2 1.9 collective-permute-start.1
  137.2 14.5 %collective-permute-done.refs_0_ = f32[7,32,8,128]{3,2,1,0:T(8,128)S(1)} collective-permute-done((f32[7,32,8,128]{3,2,1,0:T(8,128)S(1)}, f32[7,32,8,128]{3,2,1,0:T(8,128)S(1)}, u32[]{:S(2)}, u32[]{:S(2)}) %collective-permute-start) | collective-permute-done | bytes 917536 | tf_op jit(solution)/shard_map/ppermute | solution.py:400
  151.6 6.3 %collective-permute-done.1.refs_2_ = f32[7,32,8,128]{3,2,1,0:T(8,128)S(1)} collective-permute-done((f32[7,32,8,128]{3,2,1,0:T(8,128)S(1)}, f32[7,32,8,128]{3,2,1,0:T(8,128)S(1)}, u32[]{:S(2)}, u32[]{:S(2)}) %collective-permute-start.1) | collective-permute-done | bytes 917536 | tf_op jit(solution)/shard_map/ppermute | solution.py:401
  158.0 3.7 %shard_map.75 = (f32[16,16,8,128]{3,2,1,0:T(8,128)S(1)}, f32[16,7,8,128]{3,2,1,0:T(8,128)S(1)}, f32[16,7,8,128]{3,2,1,0:T(8,128)S(1)}) custom-call(bf16[32,256,128]{2,1,0:T(8,128)(2,1)S(1)} %broadcast_in_dim.22.dip_ref, f32[7,32,8,128]{3,2,1,0:T(8,128)S(1)} %collective-permute-done.refs_0_, f32[32,32,8,128]{3,2,1,0:T(8,128)S(1)} %bitcast.11, ...), custom_call_target="tpu_custom_call" | custom-call | flops 629145600 | bytes 2097152 | tf_op jit(solution)/shard_map/pallas_call | solution.py:378
  161.7 1.9 collective-permute-start.2
  163.6 3.4 %collective-permute-start.3 = (f32[16,7,8,128]{3,2,1,0:T(8,128)S(1)}, f32[16,7,8,128]{3,2,1,0:T(8,128)S(1)}, u32[]{:S(2)}, u32[]{:S(2)}) collective-permute-start(f32[16,7,8,128]{3,2,1,0:T(8,128)S(1)} %get-tuple-element.28), channel_id=1, source_target_pairs={{1,0},{2,1},{3,2},{5,4},{6,5},{7,6},{9,8},{10,9},{11,10},{13,12},{... | collective-permute-start | bytes 1376264 | tf_op jit(solution)/shard_map/ppermute | solution.py:401
  167.0 3.6 %shard_map.76.refs_2_ = f32[16,16,8,128]{3,2,1,0:T(8,128)S(1)} custom-call(bf16[32,256,128]{2,1,0:T(8,128)(2,1)S(1)} %broadcast_in_dim.22.dip_ref, f32[7,32,8,128]{3,2,1,0:T(8,128)S(1)} %collective-permute-done.refs_0_, f32[32,32,8,128]{3,2,1,0:T(8,128)S(1)} %bitcast.12, f32[7,32,8,128]{3,2,1,0:T(8,128)S(1)} %collective-permute-done.1.refs_2_), custom_call_target="tpu_custom_call" | custom-call | flops 629145600 | bytes 2097152 | tf_op jit(solution)/shard_map/pallas_call | solution.py:378
  170.6 3.8 %collective-permute-done.2.refs_0_ = f32[16,7,8,128]{3,2,1,0:T(8,128)S(1)} collective-permute-done((f32[16,7,8,128]{3,2,1,0:T(8,128)S(1)}, f32[16,7,8,128]{3,2,1,0:T(8,128)S(1)}, u32[]{:S(2)}, u32[]{:S(2)}) %collective-permute-start.2) | collective-permute-done | bytes 458784 | tf_op jit(solution)/shard_map/ppermute | solution.py:400
  174.4 2.6 %collective-permute-done.3.refs_3_ = f32[16,7,8,128]{3,2,1,0:T(8,128)S(1)} collective-permute-done((f32[16,7,8,128]{3,2,1,0:T(8,128)S(1)}, f32[16,7,8,128]{3,2,1,0:T(8,128)S(1)}, u32[]{:S(2)}, u32[]{:S(2)}) %collective-permute-start.3) | collective-permute-done | bytes 458784 | tf_op jit(solution)/shard_map/ppermute | solution.py:401
  177.0 5.6 %shard_map.77 = (f32[16,32,8,128]{3,2,1,0:T(8,128)S(1)}, f32[7,32,8,128]{3,2,1,0:T(8,128)S(1)}, f32[7,32,8,128]{3,2,1,0:T(8,128)S(1)}) custom-call(bf16[32,256,128]{2,1,0:T(8,128)(2,1)S(1)} %broadcast_in_dim.25.dip_ref, f32[16,7,8,128]{3,2,1,0:T(8,128)S(1)} %collective-permute-done.2.refs_0_, f32[16,16,8,128]{3,2,1,0:T(8,128)S(1)} %get-tuple-element.27.refs_1_, ...), custom_call_target="tpu_custom_call" | custom-call | flops 1258291200 | bytes 4194304 | tf_op jit(solution)/shard_map/pallas_call | solution.py:378
  182.6 1.9 collective-permute-start.4
  184.6 2.4 %collective-permute-start.7 = (f32[7,32,8,128]{3,2,1,0:T(8,128)S(1)}, f32[7,32,8,128]{3,2,1,0:T(8,128)S(1)}, u32[]{:S(2)}, u32[]{:S(2)}) collective-permute-start(f32[7,32,8,128]{3,2,1,0:T(8,128)S(1)} %get-tuple-element.34), channel_id=1, source_target_pairs={{4,0},{8,4},{12,8},{16,12},{20,16},{24,20},{28,24},{5,1},{9,5},{13... | collective-permute-start | bytes 2752520 | tf_op jit(solution)/shard_map/ppermute | solution.py:401
  187.0 7.3 %shard_map.78 = (f32[16,32,8,128]{3,2,1,0:T(8,128)S(1)}, f32[16,7,8,128]{3,2,1,0:T(8,128)S(1)}, f32[16,7,8,128]{3,2,1,0:T(8,128)S(1)}) custom-call(bf16[32,256,128]{2,1,0:T(8,128)(2,1)S(1)} %broadcast_in_dim.22.dip_ref, f32[32,32,8,128]{3,2,1,0:T(8,128)S(1)} %bitcast.13), custom_call_target="tpu_custom_call" | custom-call | flops 1258291200 | bytes 4194304 | tf_op jit(solution)/shard_map/pallas_call | solution.py:378
  194.3 1.9 collective-permute-start.5
  196.2 3.6 %collective-permute-start.6 = (f32[16,7,8,128]{3,2,1,0:T(8,128)S(1)}, f32[16,7,8,128]{3,2,1,0:T(8,128)S(1)}, u32[]{:S(2)}, u32[]{:S(2)}) collective-permute-start(f32[16,7,8,128]{3,2,1,0:T(8,128)S(1)} %get-tuple-element.33), channel_id=1, source_target_pairs={{1,0},{2,1},{3,2},{5,4},{6,5},{7,6},{9,8},{10,9},{11,10},{13,12},{... | collective-permute-start | bytes 1376264 | tf_op jit(solution)/shard_map/ppermute | solution.py:401
  199.8 7.2 %collective-permute-done.5.refs_0_ = f32[16,7,8,128]{3,2,1,0:T(8,128)S(1)} collective-permute-done((f32[16,7,8,128]{3,2,1,0:T(8,128)S(1)}, f32[16,7,8,128]{3,2,1,0:T(8,128)S(1)}, u32[]{:S(2)}, u32[]{:S(2)}) %collective-permute-start.5) | collective-permute-done | bytes 458784 | tf_op jit(solution)/shard_map/ppermute | solution.py:400
  207.0 1.7 collective-permute-done.6.refs_2_
  208.7 0.0 copy-start.1
  208.7 5.2 %shard_map.79.refs_1_.refs_2_ = f32[16,32,8,128]{3,2,1,0:T(8,128)S(1)} custom-call(bf16[32,256,128]{2,1,0:T(8,128)(2,1)S(1)} %broadcast_in_dim.25.dip_ref, f32[16,7,8,128]{3,2,1,0:T(8,128)S(1)} %collective-permute-done.5.refs_0_, f32[16,32,8,128]{3,2,1,0:T(8,128)S(1)} %get-tuple-element.32.refs_1_, f32[16,7,8,128]{3,2,1,0:T(8,128)S(1)} %collective-permute-done.6.refs_2_), custom_call_target="tpu_custom_call" | custom-call | flops 1258291200 | bytes 4194304 | tf_op jit(solution)/shard_map/pallas_call | solution.py:378
  213.9 0.0 copy-done.1
  213.9 10.7 %shard_map.80.refs_5_ = f32[32,32,1024]{2,1,0:T(8,128)} custom-call(bf16[32,256,128]{2,1,0:T(8,128)(2,1)S(1)} %broadcast_in_dim.22.dip_ref, f32[16,32,8,128]{3,2,1,0:T(8,128)S(1)} %get-tuple-element.30.refs_0_.refs_1_, f32[16,32,8,128]{3,2,1,0:T(8,128)S(1)} %shard_map.79.refs_1_.refs_2_, bf16[1024,1024]{1,0:T(8,128)(2,1)S(1)} %copy-done.1), custom_call_target="tpu_custom_call" | custom-call | flops 1258291200 | bytes 4194304 | tf_op jit(solution)/shard_map/pallas_call | solution.py:378
  224.6 0.0 collective-permute-done.4.refs_0_
  224.6 0.0 collective-permute-done.7.refs_3_
  224.6 10.6 %shard_map.81 = f32[32,32,1024]{2,1,0:T(8,128)} custom-call(bf16[32,256,128]{2,1,0:T(8,128)(2,1)S(1)} %broadcast_in_dim.22.dip_ref, f32[7,32,8,128]{3,2,1,0:T(8,128)S(1)} %collective-permute-done.4.refs_0_, f32[16,32,8,128]{3,2,1,0:T(8,128)S(1)} %get-tuple-element.30.refs_0_.refs_1_, ...), custom_call_target="tpu_custom_call", output_to_operand_aliasing={{}: (6, {})} | custom-call | flops 1258291200 | bytes 4194304 | tf_op jit(solution)/shard_map/pallas_call | solution.py:378
  (4 shorter events, 0.0 us)
Async XLA Ops:
  0.0 1.6 copy-start.2
  1.6 1.6 copy-start.3
  3.2 0.7 copy-start.4
  3.9 0.7 copy-start.5
  12.3 2.1 copy-start
  14.3 6.4 %copy-start.6 = (s32[32,32]{1,0:T(8,128)S(1)}, s32[32,32]{1,0:T(8,128)}, u32[]{:S(2)}) copy-start(s32[32,32]{1,0:T(8,128)} %param.11) | copy-start | bytes 12292
  14.3 6.6 %copy-start.7 = (s32[32,32]{1,0:T(8,128)S(1)}, s32[32,32]{1,0:T(8,128)}, u32[]{:S(2)}) copy-start(s32[32,32]{1,0:T(8,128)} %param.10) | copy-start | bytes 12292
  14.3 101.8 %all-to-all-start = ((f32[32,264,128]{2,1,0:T(8,128)}), f32[32,264,128]{2,1,0:T(8,128)}, u32[]{:S(2)}, u32[]{:S(2)}) async-start(f32[32,264,128]{2,1,0:T(8,128)} %copy-done), calls=%async_computation | async-start | bytes 8650752 | tf_op jit(solution)/shard_map/all_to_all | solution.py:488
  131.4 20.2 %collective-permute-start = (f32[7,32,8,128]{3,2,1,0:T(8,128)S(1)}, f32[7,32,8,128]{3,2,1,0:T(8,128)S(1)}, u32[]{:S(2)}, u32[]{:S(2)}) collective-permute-start(f32[7,32,8,128]{3,2,1,0:T(8,128)S(1)} %bitcast.17), channel_id=1, source_target_pairs={{0,4},{4,8},{8,12},{12,16},{16,20},{20,24},{24,28},{1,5},{5,9},{9,... | collective-permute-start | bytes 2752520 | tf_op jit(solution)/shard_map/ppermute | solution.py:400
  135.2 22.7 %collective-permute-start.1 = (f32[7,32,8,128]{3,2,1,0:T(8,128)S(1)}, f32[7,32,8,128]{3,2,1,0:T(8,128)S(1)}, u32[]{:S(2)}, u32[]{:S(2)}) collective-permute-start(f32[7,32,8,128]{3,2,1,0:T(8,128)S(1)} %bitcast.16), channel_id=1, source_target_pairs={{4,0},{8,4},{12,8},{16,12},{20,16},{24,20},{28,24},{5,1},{9,5},{13... | collective-permute-start | bytes 2752520 | tf_op jit(solution)/shard_map/ppermute | solution.py:401
  161.7 12.7 %collective-permute-start.2 = (f32[16,7,8,128]{3,2,1,0:T(8,128)S(1)}, f32[16,7,8,128]{3,2,1,0:T(8,128)S(1)}, u32[]{:S(2)}, u32[]{:S(2)}) collective-permute-start(f32[16,7,8,128]{3,2,1,0:T(8,128)S(1)} %get-tuple-element.26), channel_id=1, source_target_pairs={{0,1},{1,2},{2,3},{4,5},{5,6},{6,7},{8,9},{9,10},{10,11},{12,13},{... | collective-permute-start | bytes 1376264 | tf_op jit(solution)/shard_map/ppermute | solution.py:400
  163.6 13.4 %collective-permute-start.3 = (f32[16,7,8,128]{3,2,1,0:T(8,128)S(1)}, f32[16,7,8,128]{3,2,1,0:T(8,128)S(1)}, u32[]{:S(2)}, u32[]{:S(2)}) collective-permute-start(f32[16,7,8,128]{3,2,1,0:T(8,128)S(1)} %get-tuple-element.28), channel_id=1, source_target_pairs={{1,0},{2,1},{3,2},{5,4},{6,5},{7,6},{9,8},{10,9},{11,10},{13,12},{... | collective-permute-start | bytes 1376264 | tf_op jit(solution)/shard_map/ppermute | solution.py:401
  182.6 42.0 %collective-permute-start.4 = (f32[7,32,8,128]{3,2,1,0:T(8,128)S(1)}, f32[7,32,8,128]{3,2,1,0:T(8,128)S(1)}, u32[]{:S(2)}, u32[]{:S(2)}) collective-permute-start(f32[7,32,8,128]{3,2,1,0:T(8,128)S(1)} %get-tuple-element.29), channel_id=1, source_target_pairs={{0,4},{4,8},{8,12},{12,16},{16,20},{20,24},{24,28},{1,5},{5,9},{9,... | collective-permute-start | bytes 2752520 | tf_op jit(solution)/shard_map/ppermute | solution.py:400
  184.6 40.1 %collective-permute-start.7 = (f32[7,32,8,128]{3,2,1,0:T(8,128)S(1)}, f32[7,32,8,128]{3,2,1,0:T(8,128)S(1)}, u32[]{:S(2)}, u32[]{:S(2)}) collective-permute-start(f32[7,32,8,128]{3,2,1,0:T(8,128)S(1)} %get-tuple-element.34), channel_id=1, source_target_pairs={{4,0},{8,4},{12,8},{16,12},{20,16},{24,20},{28,24},{5,1},{9,5},{13... | collective-permute-start | bytes 2752520 | tf_op jit(solution)/shard_map/ppermute | solution.py:401
  194.3 12.7 %collective-permute-start.5 = (f32[16,7,8,128]{3,2,1,0:T(8,128)S(1)}, f32[16,7,8,128]{3,2,1,0:T(8,128)S(1)}, u32[]{:S(2)}, u32[]{:S(2)}) collective-permute-start(f32[16,7,8,128]{3,2,1,0:T(8,128)S(1)} %get-tuple-element.31), channel_id=1, source_target_pairs={{0,1},{1,2},{2,3},{4,5},{5,6},{6,7},{8,9},{9,10},{10,11},{12,13},{... | collective-permute-start | bytes 1376264 | tf_op jit(solution)/shard_map/ppermute | solution.py:400
  196.2 12.5 %collective-permute-start.6 = (f32[16,7,8,128]{3,2,1,0:T(8,128)S(1)}, f32[16,7,8,128]{3,2,1,0:T(8,128)S(1)}, u32[]{:S(2)}, u32[]{:S(2)}) collective-permute-start(f32[16,7,8,128]{3,2,1,0:T(8,128)S(1)} %get-tuple-element.33), channel_id=1, source_target_pairs={{1,0},{2,1},{3,2},{5,4},{6,5},{7,6},{9,8},{10,9},{11,10},{13,12},{... | collective-permute-start | bytes 1376264 | tf_op jit(solution)/shard_map/ppermute | solution.py:401
  208.7 5.2 %copy-start.1 = (bf16[1024,1024]{1,0:T(8,128)(2,1)S(1)}, bf16[1024,1024]{1,0:T(8,128)(2,1)}, u32[]{:S(2)}) copy-start(bf16[1024,1024]{1,0:T(8,128)(2,1)} %constant.5.clone.refs_2_.refs_4_) | copy-start | bytes 6291460

commit v6 on v5

--- a/solution.py
+++ b/solution.py
@@ -42,11 +42,28 @@
     return moved[:count] + moved[count:]
 
 
-def pack_kernel(target_ref, bins_ref, traces_ref, table_ref, out_ref, tiles_ref, used_ref, listed_ref, sem, listed_sem, *, capacity):
+def fill_interleave(table_ref):
+    size = table_ref.shape[0]
+    time = lax.broadcasted_iota(I32, (size, LANES), 0)
+    lane = lax.broadcasted_iota(I32, (size, LANES), 1)
+    gap = time - lane * PHASES
+    for phase in range(PHASES):
+        table_ref[:, phase * LANES : (phase + 1) * LANES] = jnp.where(gap == phase, 1.0, 0.0).astype(BF16)
+
+
+def pack_kernel(target_ref, bins_ref, traces_ref, out_ref, held_ref, table_ref, tiles_ref, used_ref, listed_ref, in_sems, sem, listed_sem, *, capacity):
     held, block_rows, samples = traces_ref.shape
     devices, room, _ = listed_ref.shape
     span = block_rows * PHASES
-    groups = 2
+    groups = held_ref.shape[0]
+    count = held // groups
+    loads = [
+        pltpu.make_async_copy(traces_ref.at[pl.ds(group * count, count)], held_ref.at[group], in_sems.at[group])
+        for group in range(groups)
+    ]
+    for load in loads:
+        load.start()
+    fill_interleave(table_ref)
     lane = lax.broadcasted_iota(I32, (1, LANES), 1)
     listed_ref[...] = jnp.full(listed_ref.shape, -1.0, F32)
 
@@ -72,8 +89,8 @@
         return 0
 
     for group in range(groups):
-        count = held // groups
-        rows = traces_ref[group * count : (group + 1) * count].reshape(count * block_rows, samples)
+        loads[group].wait()
+        rows = held_ref[group].reshape(count * block_rows, samples)
         moved = move_samples(rows, table_ref[...])
         for eight in range(count * block_rows // 8):
             for phase in range(PHASES):
@@ -90,87 +107,94 @@
     pltpu.make_async_copy(tiles_ref, tiles_ref, sem).wait()
 
 
-def pack(traces, target, bins, table, devices, capacity):
+def pack(traces, target, bins, devices, capacity):
     held, block_rows, samples = traces.shape
     span = block_rows * PHASES
     room = -(-capacity // 8) * 8
+    groups = 2
     return pl.pallas_call(
         functools.partial(pack_kernel, capacity=capacity),
-        in_specs=[SMEM, SMEM, VMEM, VMEM],
+        in_specs=[SMEM, SMEM, HBM],
         out_specs=HBM,
         out_shape=jax.ShapeDtypeStruct((devices, capacity * span + room, LANES), F32),
         scratch_shapes=[
+            pltpu.VMEM((groups, held // groups, block_rows, samples), F32),
+            pltpu.VMEM((samples, samples), BF16),
             pltpu.VMEM((held * span, LANES), F32),
             pltpu.SMEM((devices,), I32),
             pltpu.VMEM((devices, room, LANES), F32),
+            pltpu.SemaphoreType.DMA((groups,)),
             pltpu.SemaphoreType.DMA,
             pltpu.SemaphoreType.DMA,
         ],
-        compiler_params=pltpu.CompilerParams(vmem_limit_bytes=20 * MIB),
-    )(target, bins, traces, table)
-
-
-def bin_kernel(blocks_ref, out_ref, head_ref, tail_ref, even_ref, odd_ref, listed_ref, places_ref, fold_ref, sems, *, capacity, edge):
-    devices, rows, _ = blocks_ref.shape
-    room = listed_ref.shape[1]
+        compiler_params=pltpu.CompilerParams(vmem_limit_bytes=60 * MIB),
+    )(target, bins, traces)
+
+
+def bin_kernel(bins_ref, scale_ref, blocks_ref, out_ref, head_ref, tail_ref, held_ref, even_ref, odd_ref, sems, in_sems, *, capacity, block_rows, edge):
+    parts = held_ref.shape[0]
+    senders = blocks_ref.shape[0] // parts
     bin_total = out_ref.shape[0]
-    block_rows = (rows - room) // (capacity * PHASES)
+    rows = held_ref.shape[2]
     unroll = 8
-    listed = blocks_ref[:, rows - room :, :]
-    listed_ref[...] = jnp.where(listed < 0, float(bin_total), listed).astype(I32)
-    copy = pltpu.make_async_copy(listed_ref, places_ref, sems.at[0])
-    copy.start()
+    loads = [
+        pltpu.make_async_copy(
+            blocks_ref.at[pl.ds(part * senders, senders), pl.ds(0, rows), :], held_ref.at[part], in_sems.at[part]
+        )
+        for part in range(parts)
+    ]
+    for load in loads:
+        load.start()
     nothing = jnp.zeros((PHASES, LANES), F32)
 
     def clear(i, _):
         for j in range(unroll):
             even_ref[i * unroll + j] = nothing
             odd_ref[i * unroll + j] = nothing
-            fold_ref[i * unroll + j] = 0
         return 0
 
     lax.fori_loop(0, bin_total // unroll, clear, 0)
-    fold_ref[bin_total] = 0
-    copy.wait()
-
-    def add_sender(sender, _):
-        for rank in range(capacity):
-            for j in range(block_rows):
-                total_ref = odd_ref if j % 2 else even_ref
-                place = places_ref[sender, rank, j]
-                row = (rank * block_rows + j) * PHASES
-                total_ref[place] += blocks_ref[sender, row : row + PHASES, :]
-                fold_ref[place] = fold_ref[place] + 1
-        return 0
-
-    lax.fori_loop(0, devices, add_sender, 0)
+    for part in range(parts):
+        loads[part].wait()
+
+        def add_sender(sender, _):
+            first = (part * senders + sender) * (capacity * block_rows)
+            for i in range(capacity * block_rows):
+                total_ref = odd_ref if i % 2 else even_ref
+                total_ref[bins_ref[first + i]] += held_ref[part, sender, i * PHASES : (i + 1) * PHASES]
+            return 0
+
+        lax.fori_loop(0, senders, add_sender, 0)
 
     def finish(i, _):
         for j in range(unroll):
             place = i * unroll + j
-            fold = jnp.full((PHASES, LANES), jnp.maximum(fold_ref[place], 1).astype(F32))
-            out_ref[place] = (even_ref[place] + odd_ref[place]) / fold
+            out_ref[place] = (even_ref[place] + odd_ref[place]) * scale_ref[place]
         return 0
 
     lax.fori_loop(0, edge // unroll, finish, 0)
-    head_copy = pltpu.make_async_copy(out_ref.at[pl.ds(0, edge)], head_ref, sems.at[1])
+    head_copy = pltpu.make_async_copy(out_ref.at[pl.ds(0, edge)], head_ref, sems.at[0])
     head_copy.start()
     lax.fori_loop((bin_total - edge) // unroll, bin_total // unroll, finish, 0)
-    tail_copy = pltpu.make_async_copy(out_ref.at[pl.ds(bin_total - edge, edge)], tail_ref, sems.at[2])
+    tail_copy = pltpu.make_async_copy(out_ref.at[pl.ds(bin_total - edge, edge)], tail_ref, sems.at[1])
     tail_copy.start()
     lax.fori_loop(edge // unroll, (bin_total - edge) // unroll, finish, 0)
     head_copy.wait()
     tail_copy.wait()
 
 
-def stack_bins(blocks, tile_rows, tile_cols, capacity):
+def stack_bins(blocks, tile_rows, tile_cols, capacity, block_rows):
     devices = blocks.shape[0]
     bin_total = tile_rows * tile_cols
     edge = HALF * tile_cols
-    room = -(-capacity // 8) * 8
+    rows = capacity * block_rows * PHASES
+    listed = blocks[:, rows : rows + capacity, :block_rows].astype(I32)
+    bins = jnp.where(listed < 0, bin_total, listed).reshape(-1)
+    fold = jnp.sum((jnp.arange(bin_total, dtype=I32)[:, None] == bins[None, :]).astype(F32), axis=1)
+    parts = 4
     stacked, head, tail = pl.pallas_call(
-        functools.partial(bin_kernel, capacity=capacity, edge=edge),
-        in_specs=[VMEM],
+        functools.partial(bin_kernel, capacity=capacity, block_rows=block_rows, edge=edge),
+        in_specs=[SMEM, SMEM, ANY],
         out_specs=[VMEM, HBM, HBM],
         out_shape=[
             jax.ShapeDtypeStruct((bin_total, PHASES, LANES), F32),
@@ -178,15 +202,14 @@
             jax.ShapeDtypeStruct((edge, PHASES, LANES), F32),
         ],
         scratch_shapes=[
+            pltpu.VMEM((parts, devices // parts, rows, LANES), F32),
             pltpu.VMEM((bin_total + 8, PHASES, LANES), F32),
             pltpu.VMEM((bin_total + 8, PHASES, LANES), F32),
-            pltpu.VMEM((devices, room, LANES), I32),
-            pltpu.SMEM((devices, room, LANES), I32),
-            pltpu.SMEM((bin_total + 8,), I32),
-            pltpu.SemaphoreType.DMA((3,)),
+            pltpu.SemaphoreType.DMA((2,)),
+            pltpu.SemaphoreType.DMA((parts,)),
         ],
         compiler_params=pltpu.CompilerParams(vmem_limit_bytes=20 * MIB),
-    )(blocks)
+    )(bins, 1.0 / jnp.maximum(fold, 1.0), blocks)
     shape = (tile_cols, PHASES, LANES)
     return stacked.reshape((tile_rows,) + shape), head.reshape((HALF,) + shape), tail.reshape((HALF,) + shape)
 
@@ -217,7 +240,9 @@
     none = jnp.zeros((PAIR, LANES), BF16)
     taps = []
     for pair in range(count // 2):
-        dip = dip_of(first // 2 + pair)
+        dip = jnp.concatenate(
+            [jnp.full((PHASES, LANES), dip_of(first + 2 * pair + i).astype(F32)) for i in range(2)], axis=0
+        ).astype(BF16)
         moves, weights = [], []
         for half in range(2):
             block = pl.ds((pair * 2 + half) * PAIR, PAIR)
@@ -245,18 +270,17 @@
             put(first + 2 * pair + member, total)
 
 
-def steer_kernel(dip_ref, *refs, along, whole, lines, line_of, windows, local_of, edges, final, chained, pieces_count):
+def steer_kernel(dip_ref, *refs, along, whole, lines, line_of, windows, local_of, edges, final, chained, pieces_count, abreast):
     pieces, refs = refs[:pieces_count], refs[pieces_count:]
     if final:
         table_ref, refs = refs[0], refs[1:]
-    if chained:
-        refs = refs[1:]
+    refs = refs[chained:]
     out_ref, refs = refs[0], refs[1:]
     edge_refs, refs = refs[: len(edges)], refs[len(edges) :]
     spots_ref, weights_ref, sems, *refs = refs
-    halves = refs[: 2 * len(windows)]
+    halves = refs[: abreast * len(windows)]
     if final:
-        staged_ref, result_ref = refs[2 * len(windows) :]
+        staged_ref, result_ref = refs[abreast * len(windows) :]
     fill_weights(spots_ref, weights_ref)
     for i, halves_ref in enumerate(halves):
         filled = len(windows[i % len(windows)][2]) * PHASES
@@ -280,18 +304,18 @@
 
         for i, (first, count, places) in enumerate(windows):
             steer_window(
-                lambda pair: dip_ref[full, pair * PAIR : (pair + 1) * PAIR, :],
+                lambda place: dip_ref[at(place, full)],
                 [cell(*place) for place in places],
                 first, count, put, halves[parity * len(windows) + i], spots_ref, weights_ref,
             )
 
-    def two_lines(i, _):
-        one_line(2 * i, 0)
-        one_line(2 * i + 1, 1)
+    def some_lines(i, _):
+        for j in range(abreast):
+            one_line(abreast * i + j, j)
         return 0
 
     if not final:
-        lax.fori_loop(0, lines // 2, two_lines, 0)
+        lax.fori_loop(0, lines // abreast, some_lines, 0)
         copies = [
             pltpu.make_async_copy(out_ref.at[pick], edge_ref, sems.at[i])
             for i, (pick, edge_ref) in enumerate(zip(edges, edge_refs))
@@ -315,7 +339,7 @@
         ]
 
     for batch in range(lines // final):
-        lax.fori_loop(batch * final // 2, (batch + 1) * final // 2, two_lines, 0)
+        lax.fori_loop(batch * final // abreast, (batch + 1) * final // abreast, some_lines, 0)
         rows = jnp.concatenate(
             [
                 jnp.concatenate(
@@ -341,12 +365,13 @@
             copy.wait()
 
 
-def steer(dip, pieces, along, lines, line_of, windows, local_of, edges=(), table=None, before=None):
+def steer(dip, pieces, along, lines, line_of, windows, local_of, edges=(), table=None, before=None, after=None):
+    abreast = 2 if along else 4
     samples = PHASES * LANES
     outputs = sum(count for _, count, _ in windows)
     final = 16 if table is not None else 0
     operands = [dip] + [array for array, _ in pieces]
-    in_specs = [VMEM] * len(operands)
+    in_specs = [SMEM] + [VMEM] * len(pieces)
     aliases = {}
     if final:
         operands.append(table)
@@ -355,8 +380,7 @@
             aliases = {len(operands): 0}
             operands.append(before)
             in_specs.append(HBM)
-        extent = dip.shape[1] // PHASES
-        out_shape = [jax.ShapeDtypeStruct((extent, lines, samples), F32)]
+        out_shape = [jax.ShapeDtypeStruct((dip.shape[0], lines, samples), F32)]
         out_specs = [HBM]
     else:
         shape = (outputs, lines) if along == 0 else (lines, outputs)
@@ -366,10 +390,13 @@
             size = [len(range(*s.indices(n))) for s, n in zip(pick, shape)]
             out_shape.append(jax.ShapeDtypeStruct(tuple(size) + (PHASES, LANES), F32))
             out_specs.append(HBM)
+    if after is not None:
+        operands.append(after)
+        in_specs.append(ANY)
     most = max(count for _, count, _ in windows)
     constant = pltpu.VMEM((most * PAIR, LANES), BF16)
     scratch = [constant, constant, pltpu.SemaphoreType.DMA((2 * len(windows) if final else max(1, len(edges)),))]
-    scratch += [pltpu.VMEM((WIDE, WIDE), BF16)] * (2 * len(windows))
+    scratch += [pltpu.VMEM((WIDE, WIDE), BF16)] * (abreast * len(windows))
     if final:
         scratch += [
             pltpu.VMEM((outputs * final * PHASES, LANES), F32),
@@ -379,7 +406,7 @@
         functools.partial(
             steer_kernel,
             along=along, whole=[whole for _, whole in pieces], lines=lines, line_of=line_of, windows=windows,
-            local_of=local_of, edges=edges, final=final, chained=before is not None, pieces_count=len(pieces),
+            local_of=local_of, edges=edges, final=final, chained=len(operands) - len(pieces) - 1 - bool(final), pieces_count=len(pieces), abreast=abreast,
         ),
         in_specs=in_specs,
         out_specs=out_specs,
@@ -402,12 +429,6 @@
     return low, high
 
 
-def dip_tiles(dip):
-    lines, extent = dip.shape
-    tiles = jnp.broadcast_to(dip.astype(BF16)[:, :, None, None], (lines, extent, PHASES, LANES))
-    return tiles.reshape(lines, extent * PHASES, LANES)
-
-
 def span_of(index, first, count):
     return [(index, first + i) for i in range(count)]
 
@@ -440,10 +461,11 @@
         (rows - BORDER, BORDER, span_of(1, rows - BORDER - HALF, BORDER + HALF) + span_of(2, 0, HALF)),
     ]
     corners, head_out, tail_out = steer(
-        along_rows, pieces, 0, 2 * BORDER, outer_col, windows, outer_place, edges=[(every, lead), (every, last)]
+        along_rows, pieces, 0, 2 * BORDER, outer_col, windows, outer_place, edges=[(every, lead), (every, last)],
+        after=middle,
     )
     low_out, high_out = swap_ends(head_out, tail_out, "crosslin")
-    (flanks,) = steer(along_rows, pieces, 0, mid_cols, inner, windows, outer_place)
+    (flanks,) = steer(along_rows, pieces, 0, mid_cols, inner, windows, outer_place, after=corners)
 
     def cross_windows(places):
         return [(i, 16, places[i : i + 16 + 2 * HALF]) for i in range(0, cols, 16)]
@@ -451,14 +473,14 @@
     places = span_of(0, 0, HALF) + span_of(1, 0, cols) + span_of(2, 0, HALF)
     (middle_second,) = steer(
         along_cols, [(low_mid, False), (middle, False), (high_mid, False)], 1, mid_rows, inner,
-        cross_windows(places), same,
+        cross_windows(places), same, after=flanks,
     )
     places = (
         span_of(0, 0, HALF) + span_of(1, 0, BORDER) + span_of(2, 0, mid_cols) + span_of(1, BORDER, BORDER) + span_of(3, 0, HALF)
     )
     border_second, head, tail = steer(
         along_cols, [(low_out, False), (corners, False), (flanks, False), (high_out, False)], 1, 2 * BORDER,
-        outer_row, cross_windows(places), same, edges=[(lead, every), (last, every)],
+        outer_row, cross_windows(places), same, edges=[(lead, every), (last, every)], after=middle_second,
     )
 
     low, high = swap_ends(head, tail, "inline")
@@ -483,13 +505,11 @@
     devices = lax.axis_size("inline") * lax.axis_size("crosslin")
     capacity = 2 * held // devices
     tile_rows, tile_cols = dip_inline.shape
-    table = interleave_table(samples)
-    outgoing = pack(traces, destination.reshape(-1), bin_index.T, jnp.asarray(table, BF16), devices, capacity)
+    outgoing = pack(traces, destination.reshape(-1), bin_index.T, devices, capacity)
     arrived = lax.all_to_all(outgoing, BOTH, split_axis=0, concat_axis=0, tiled=True)
-    back, along_rows, along_cols = jnp.asarray(table.T, BF16), dip_tiles(dip_inline.T), dip_tiles(dip_cross)
-    arrived, along_rows, along_cols = lax.optimization_barrier((arrived, along_rows, along_cols))
-    stacked, head, tail = stack_bins(arrived, tile_rows, tile_cols, capacity)
-    return smooth(stacked, head, tail, along_rows, along_cols, back)
+    stacked, head, tail = stack_bins(arrived, tile_rows, tile_cols, capacity, block_rows)
+    back = jnp.asarray(interleave_table(samples).T, BF16)
+    return smooth(stacked, head, tail, dip_inline, dip_cross, back)
 
 
 def solution(mesh):

time: 239 us -> 206 us (0.86)
  the two profiles are of different devices: /device:TPU:11 before, /device:TPU:1 now
where the time goes in v6:
time: 206 us; the launch traced here: 205 us
  blocking collectives  105 us (51%)
  Pallas kernels  56.7 us (28%)
  starting transfers between devices  19.8 us (10%)
  waiting for transfers between devices  18.1 us (9%)
  local copies, waits for them, and re-layouts  4.32 us (2%)
    all_to_all x1, blocking collectives, on_device(): lax.all_to_all(outgoing, BOTH, split_axis=0, concat_axis=0, tiled=True)  105 us
    pallas_call x7, Pallas kernels, steer(): pl.pallas_call(functools.partial(steer_kernel, along=along, whole=[whole...  43.8 us
    ppermute x4, waiting for transfers between devices, swap_ends(): high = lax.ppermute(head, axis, [(i + 1, i) for i in range(count - 1)])  18 us
    ppermute x4, starting transfers between devices, swap_ends(): low = lax.ppermute(tail, axis, [(i, i + 1) for i in range(count - 1)])  13.2 us
    ppermute x4, starting transfers between devices, swap_ends(): high = lax.ppermute(head, axis, [(i + 1, i) for i in range(count - 1)])  6.63 us
    pallas_call x1, Pallas kernels, stack_bins(): pl.pallas_call(functools.partial(bin_kernel, capacity=capacity, block_row...  6.57 us
    pallas_call x1, Pallas kernels, pack(): pl.pallas_call(functools.partial(pack_kernel, capacity=capacity), in_spec...  6.37 us
    unnamed x10, local copies, waits for them, and re-layouts  4.21 us
  transfers between devices with their start and end apart: 8, of which 2 were waited for; matrix products, arithmetic and copies ran while one was open for 0% of the time, Pallas kernels for 14%

profile of v6, /device:TPU:1, one launch (start us, length us, event | category | flops | bytes accessed | tf_op | source)
XLA Modules:
  0.0 204.6 jit_solution(7076801086850373485)
XLA Ops:
  0.0 6.4 %shard_map.64 = f32[32,264,128]{2,1,0:T(8,128)} custom-call(s32[128]{0:T(128)} %bitcast.11, s32[4,128]{1,0:T(4,128)} %bitcast.10, f32[128,4,1024]{2,1,0:T(4,128)} %traces_ref.1), custom_call_target="tpu_custom_call" | custom-call | tf_op jit(solution)/shard_map/pallas_call | solution.py:115
  6.4 104.8 %all_to_all.5.blocks_ref = f32[32,264,128]{2,1,0:T(8,128)S(1)} all-to-all(f32[32,264,128]{2,1,0:T(8,128)} %shard_map.64), channel_id=1, replica_groups=mesh['inline'=8,'crosslin'=4] {'inline','crosslin'}, dimensions={0} | all-to-all | bytes 8650752 | tf_op jit(solution)/shard_map/all_to_all | solution.py:509
  111.1 0.0 copy-start.3
  111.2 0.0 copy-start
  111.2 2.0 copy-done
  113.1 0.1 reshape.17.bins_ref
  113.3 0.5 convert_reduce_fusion
  113.8 0.0 copy-start.1
  113.8 2.2 %copy-done.1 = f32[32,264,128]{2,1,0:T(8,128)S(1)} copy-done((f32[32,264,128]{2,1,0:T(8,128)S(1)}, f32[32,264,128]{2,1,0:T(8,128)}, u32[]{:S(2)}) %copy-start.1) | copy-done | bytes 4325400
  116.0 6.6 %shard_map.65 = (f32[1024,8,128]{2,1,0:T(8,128)S(1)}, f32[224,8,128]{2,1,0:T(8,128)S(1)}, f32[224,8,128]{2,1,0:T(8,128)S(1)}) custom-call(s32[1024]{0:T(1024)S(1)} %reshape.17.bins_ref, f32[1024]{0:T(1024)S(1)} %maximum_divide_fusion.scale_ref, f32[32,264,128]{2,1,0:T(8,128)S(1)} %copy-done.1), custom_call_target="tpu_custom_call" | custom-call | tf_op jit(solution)/shard_map/pallas_call | solution.py:195
  122.6 2.4 %collective-permute-start = (f32[7,32,8,128]{3,2,1,0:T(8,128)S(1)}, f32[7,32,8,128]{3,2,1,0:T(8,128)S(1)}, u32[]{:S(2)}, u32[]{:S(2)}) collective-permute-start(f32[7,32,8,128]{3,2,1,0:T(8,128)S(1)} %bitcast.9), channel_id=1, source_target_pairs={{0,4},{4,8},{8,12},{12,16},{16,20},{20,24},{24,28},{1,5},{5,9},{9,... | collective-permute-start | bytes 2752520 | tf_op jit(solution)/shard_map/ppermute | solution.py:427
  125.0 1.9 collective-permute-start.1
  127.0 0.0 copy-done.3
  127.0 6.0 %shard_map.66 = (f32[16,32,8,128]{3,2,1,0:T(8,128)S(1)}, f32[16,7,8,128]{3,2,1,0:T(8,128)S(1)}, f32[16,7,8,128]{3,2,1,0:T(8,128)S(1)}) custom-call(s32[32,32]{1,0:T(8,128)S(1)} %copy-done.3, f32[32,32,8,128]{3,2,1,0:T(8,128)S(1)} %bitcast.5), custom_call_target="tpu_custom_call" | custom-call | flops 1258291200 | bytes 4194304 | tf_op jit(solution)/shard_map/pallas_call | solution.py:405
  133.0 2.6 %collective-permute-start.4 = (f32[16,7,8,128]{3,2,1,0:T(8,128)S(1)}, f32[16,7,8,128]{3,2,1,0:T(8,128)S(1)}, u32[]{:S(2)}, u32[]{:S(2)}) collective-permute-start(f32[16,7,8,128]{3,2,1,0:T(8,128)S(1)} %get-tuple-element.24), channel_id=1, source_target_pairs={{0,1},{1,2},{2,3},{4,5},{5,6},{6,7},{8,9},{9,10},{10,11},{12,13},{... | collective-permute-start | bytes 1376264 | tf_op jit(solution)/shard_map/ppermute | solution.py:427
  135.7 1.3 collective-permute-start.5
  137.0 0.0 collective-permute-done.refs_0_
  137.0 10.1 %collective-permute-done.1.refs_2_ = f32[7,32,8,128]{3,2,1,0:T(8,128)S(1)} collective-permute-done((f32[7,32,8,128]{3,2,1,0:T(8,128)S(1)}, f32[7,32,8,128]{3,2,1,0:T(8,128)S(1)}, u32[]{:S(2)}, u32[]{:S(2)}) %collective-permute-start.1) | collective-permute-done | bytes 917536 | tf_op jit(solution)/shard_map/ppermute | solution.py:428
  147.1 3.4 %shard_map.67 = (f32[16,16,8,128]{3,2,1,0:T(8,128)S(1)}, f32[16,7,8,128]{3,2,1,0:T(8,128)S(1)}, f32[16,7,8,128]{3,2,1,0:T(8,128)S(1)}) custom-call(s32[32,32]{1,0:T(8,128)S(1)} %copy-done.3, f32[7,32,8,128]{3,2,1,0:T(8,128)S(1)} %collective-permute-done.refs_0_, f32[32,32,8,128]{3,2,1,0:T(8,128)S(1)} %bitcast.6, ...), custom_call_target="tpu_custom_call" | custom-call | flops 629145600 | bytes 2097152 | tf_op jit(solution)/shard_map/pallas_call | solution.py:405
  150.5 0.0 copy-start.4
  150.5 2.6 %collective-permute-start.2 = (f32[16,7,8,128]{3,2,1,0:T(8,128)S(1)}, f32[16,7,8,128]{3,2,1,0:T(8,128)S(1)}, u32[]{:S(2)}, u32[]{:S(2)}) collective-permute-start(f32[16,7,8,128]{3,2,1,0:T(8,128)S(1)} %get-tuple-element.21), channel_id=1, source_target_pairs={{0,1},{1,2},{2,3},{4,5},{5,6},{6,7},{8,9},{9,10},{10,11},{12,13},{... | collective-permute-start | bytes 1376264 | tf_op jit(solution)/shard_map/ppermute | solution.py:427
  153.1 1.3 collective-permute-start.3
  154.4 3.3 %shard_map.68.refs_3_.refs_2_ = f32[16,16,8,128]{3,2,1,0:T(8,128)S(1)} custom-call(s32[32,32]{1,0:T(8,128)S(1)} %copy-done.3, f32[7,32,8,128]{3,2,1,0:T(8,128)S(1)} %collective-permute-done.refs_0_, f32[32,32,8,128]{3,2,1,0:T(8,128)S(1)} %bitcast.7, f32[7,32,8,128]{3,2,1,0:T(8,128)S(1)} %collective-permute-done.1.refs_2_, ...), custom_call_target="tpu_custom_call" | custom-call | flops 629145600 | bytes 2097152 | tf_op jit(solution)/shard_map/pallas_call | solution.py:405
  157.7 0.0 copy-start.2
  157.7 0.0 collective-permute-done.4.refs_0_
  157.7 0.0 collective-permute-done.5.refs_2_
  157.7 0.0 copy-done.4
  157.8 6.0 %shard_map.69.refs_4_.refs_1_.refs_2_ = f32[16,32,8,128]{3,2,1,0:T(8,128)S(1)} custom-call(s32[32,32]{1,0:T(8,128)S(1)} %copy-done.4, f32[16,7,8,128]{3,2,1,0:T(8,128)S(1)} %collective-permute-done.4.refs_0_, f32[16,32,8,128]{3,2,1,0:T(8,128)S(1)} %get-tuple-element.20.refs_3_.refs_1_, f32[16,7,8,128]{3,2,1,0:T(8,128)S(1)} %collective-permute-done.5.refs_2_, ...), custom_call_target="tpu_custom_call" | custom-call | flops 1258291200 | bytes 4194304 | tf_op jit(solution)/shard_map/pallas_call | solution.py:405
  163.7 0.0 collective-permute-done.2.refs_0_
  163.7 0.0 collective-permute-done.3.refs_3_
  163.7 6.4 %shard_map.70 = (f32[16,32,8,128]{3,2,1,0:T(8,128)S(1)}, f32[7,32,8,128]{3,2,1,0:T(8,128)S(1)}, f32[7,32,8,128]{3,2,1,0:T(8,128)S(1)}) custom-call(s32[32,32]{1,0:T(8,128)S(1)} %copy-done.4, f32[16,7,8,128]{3,2,1,0:T(8,128)S(1)} %collective-permute-done.2.refs_0_, f32[16,16,8,128]{3,2,1,0:T(8,128)S(1)} %get-tuple-element.22.refs_3_.refs_1_, ...), custom_call_target="tpu_custom_call" | custom-call | flops 1258291200 | bytes 4194304 | tf_op jit(solution)/shard_map/pallas_call | solution.py:405
  170.1 5.6 %collective-permute-start.6 = (f32[7,32,8,128]{3,2,1,0:T(8,128)S(1)}, f32[7,32,8,128]{3,2,1,0:T(8,128)S(1)}, u32[]{:S(2)}, u32[]{:S(2)}) collective-permute-start(f32[7,32,8,128]{3,2,1,0:T(8,128)S(1)} %get-tuple-element.26), channel_id=1, source_target_pairs={{0,4},{4,8},{8,12},{12,16},{16,20},{20,24},{24,28},{1,5},{5,9},{9,... | collective-permute-start | bytes 2752520 | tf_op jit(solution)/shard_map/ppermute | solution.py:427
  175.7 2.1 %collective-permute-start.7 = (f32[7,32,8,128]{3,2,1,0:T(8,128)S(1)}, f32[7,32,8,128]{3,2,1,0:T(8,128)S(1)}, u32[]{:S(2)}, u32[]{:S(2)}) collective-permute-start(f32[7,32,8,128]{3,2,1,0:T(8,128)S(1)} %get-tuple-element.28), channel_id=1, source_target_pairs={{4,0},{8,4},{12,8},{16,12},{20,16},{24,20},{28,24},{5,1},{9,5},{13... | collective-permute-start | bytes 2752520 | tf_op jit(solution)/shard_map/ppermute | solution.py:428
  177.8 0.0 copy-done.2
  177.8 9.5 %shard_map.71.refs_5_ = f32[32,32,1024]{2,1,0:T(8,128)} custom-call(s32[32,32]{1,0:T(8,128)S(1)} %copy-done.3, f32[16,32,8,128]{3,2,1,0:T(8,128)S(1)} %get-tuple-element.27.refs_0_.refs_1_, f32[16,32,8,128]{3,2,1,0:T(8,128)S(1)} %shard_map.69.refs_4_.refs_1_.refs_2_, bf16[1024,1024]{1,0:T(8,128)(2,1)S(1)} %copy-done.2), custom_call_target="tpu_custom_call" | custom-call | flops 1258291200 | bytes 4194304 | tf_op jit(solution)/shard_map/pallas_call | solution.py:405
  187.3 0.0 collective-permute-done.6.refs_0_
  187.3 7.9 %collective-permute-done.7.refs_3_ = f32[7,32,8,128]{3,2,1,0:T(8,128)S(1)} collective-permute-done((f32[7,32,8,128]{3,2,1,0:T(8,128)S(1)}, f32[7,32,8,128]{3,2,1,0:T(8,128)S(1)}, u32[]{:S(2)}, u32[]{:S(2)}) %collective-permute-start.7) | collective-permute-done | bytes 917536 | tf_op jit(solution)/shard_map/ppermute | solution.py:428
  195.2 9.2 %shard_map.72 = f32[32,32,1024]{2,1,0:T(8,128)} custom-call(s32[32,32]{1,0:T(8,128)S(1)} %copy-done.3, f32[7,32,8,128]{3,2,1,0:T(8,128)S(1)} %collective-permute-done.6.refs_0_, f32[16,32,8,128]{3,2,1,0:T(8,128)S(1)} %get-tuple-element.27.refs_0_.refs_1_, f32[16,32,8,128]{3,2,1,0:T(8,128)S(1)} %shard_map.69.refs_4_.refs_1_.refs_2_, ...), custom_call_target="tpu_custom_call", output_to_operand_aliasing={{}: (6, {})} | custom-call | flops 1258291200 | bytes 4194304 | tf_op jit(solution)/shard_map/pallas_call | solution.py:405
  (2 shorter events, 0.0 us)
Async XLA Ops:
  111.1 15.8 %copy-start.3 = (s32[32,32]{1,0:T(8,128)S(1)}, s32[32,32]{1,0:T(8,128)}, u32[]{:S(2)}) copy-start(s32[32,32]{1,0:T(8,128)} %dip_ref.13) | copy-start | bytes 12292
  111.2 2.0 copy-start
  113.8 2.2 %copy-start.1 = (f32[32,264,128]{2,1,0:T(8,128)S(1)}, f32[32,264,128]{2,1,0:T(8,128)}, u32[]{:S(2)}) copy-start(f32[32,264,128]{2,1,0:T(8,128)} %copy-done) | copy-start | bytes 12976132
  122.6 14.4 %collective-permute-start = (f32[7,32,8,128]{3,2,1,0:T(8,128)S(1)}, f32[7,32,8,128]{3,2,1,0:T(8,128)S(1)}, u32[]{:S(2)}, u32[]{:S(2)}) collective-permute-start(f32[7,32,8,128]{3,2,1,0:T(8,128)S(1)} %bitcast.9), channel_id=1, source_target_pairs={{0,4},{4,8},{8,12},{12,16},{16,20},{20,24},{24,28},{1,5},{5,9},{9,... | collective-permute-start | bytes 2752520 | tf_op jit(solution)/shard_map/ppermute | solution.py:427
  125.0 22.0 %collective-permute-start.1 = (f32[7,32,8,128]{3,2,1,0:T(8,128)S(1)}, f32[7,32,8,128]{3,2,1,0:T(8,128)S(1)}, u32[]{:S(2)}, u32[]{:S(2)}) collective-permute-start(f32[7,32,8,128]{3,2,1,0:T(8,128)S(1)} %bitcast.8), channel_id=1, source_target_pairs={{4,0},{8,4},{12,8},{16,12},{20,16},{24,20},{28,24},{5,1},{9,5},{13... | collective-permute-start | bytes 2752520 | tf_op jit(solution)/shard_map/ppermute | solution.py:428
  133.0 24.7 %collective-permute-start.4 = (f32[16,7,8,128]{3,2,1,0:T(8,128)S(1)}, f32[16,7,8,128]{3,2,1,0:T(8,128)S(1)}, u32[]{:S(2)}, u32[]{:S(2)}) collective-permute-start(f32[16,7,8,128]{3,2,1,0:T(8,128)S(1)} %get-tuple-element.24), channel_id=1, source_target_pairs={{0,1},{1,2},{2,3},{4,5},{5,6},{6,7},{8,9},{9,10},{10,11},{12,13},{... | collective-permute-start | bytes 1376264 | tf_op jit(solution)/shard_map/ppermute | solution.py:427
  135.7 22.1 %collective-permute-start.5 = (f32[16,7,8,128]{3,2,1,0:T(8,128)S(1)}, f32[16,7,8,128]{3,2,1,0:T(8,128)S(1)}, u32[]{:S(2)}, u32[]{:S(2)}) collective-permute-start(f32[16,7,8,128]{3,2,1,0:T(8,128)S(1)} %get-tuple-element.25), channel_id=1, source_target_pairs={{1,0},{2,1},{3,2},{5,4},{6,5},{7,6},{9,8},{10,9},{11,10},{13,12},{... | collective-permute-start | bytes 1376264 | tf_op jit(solution)/shard_map/ppermute | solution.py:428
  150.5 7.3 %copy-start.4 = (s32[32,32]{1,0:T(8,128)S(1)}, s32[32,32]{1,0:T(8,128)}, u32[]{:S(2)}) copy-start(s32[32,32]{1,0:T(8,128)} %dip_ref.11) | copy-start | bytes 12292
  150.5 13.2 %collective-permute-start.2 = (f32[16,7,8,128]{3,2,1,0:T(8,128)S(1)}, f32[16,7,8,128]{3,2,1,0:T(8,128)S(1)}, u32[]{:S(2)}, u32[]{:S(2)}) collective-permute-start(f32[16,7,8,128]{3,2,1,0:T(8,128)S(1)} %get-tuple-element.21), channel_id=1, source_target_pairs={{0,1},{1,2},{2,3},{4,5},{5,6},{6,7},{8,9},{9,10},{10,11},{12,13},{... | collective-permute-start | bytes 1376264 | tf_op jit(solution)/shard_map/ppermute | solution.py:427
  153.1 10.6 %collective-permute-start.3 = (f32[16,7,8,128]{3,2,1,0:T(8,128)S(1)}, f32[16,7,8,128]{3,2,1,0:T(8,128)S(1)}, u32[]{:S(2)}, u32[]{:S(2)}) collective-permute-start(f32[16,7,8,128]{3,2,1,0:T(8,128)S(1)} %get-tuple-element.23), channel_id=1, source_target_pairs={{1,0},{2,1},{3,2},{5,4},{6,5},{7,6},{9,8},{10,9},{11,10},{13,12},{... | collective-permute-start | bytes 1376264 | tf_op jit(solution)/shard_map/ppermute | solution.py:428
  157.7 20.1 %copy-start.2 = (bf16[1024,1024]{1,0:T(8,128)(2,1)S(1)}, bf16[1024,1024]{1,0:T(8,128)(2,1)}, u32[]{:S(2)}) copy-start(bf16[1024,1024]{1,0:T(8,128)(2,1)} %constant.10.clone.refs_2_.refs_4_) | copy-start | bytes 6291460
  170.1 17.1 %collective-permute-start.6 = (f32[7,32,8,128]{3,2,1,0:T(8,128)S(1)}, f32[7,32,8,128]{3,2,1,0:T(8,128)S(1)}, u32[]{:S(2)}, u32[]{:S(2)}) collective-permute-start(f32[7,32,8,128]{3,2,1,0:T(8,128)S(1)} %get-tuple-element.26), channel_id=1, source_target_pairs={{0,4},{4,8},{8,12},{12,16},{16,20},{20,24},{24,28},{1,5},{5,9},{9,... | collective-permute-start | bytes 2752520 | tf_op jit(solution)/shard_map/ppermute | solution.py:427
  175.7 19.5 %collective-permute-start.7 = (f32[7,32,8,128]{3,2,1,0:T(8,128)S(1)}, f32[7,32,8,128]{3,2,1,0:T(8,128)S(1)}, u32[]{:S(2)}, u32[]{:S(2)}) collective-permute-start(f32[7,32,8,128]{3,2,1,0:T(8,128)S(1)} %get-tuple-element.28), channel_id=1, source_target_pairs={{4,0},{8,4},{12,8},{16,12},{20,16},{24,20},{28,24},{5,1},{9,5},{13... | collective-permute-start | bytes 2752520 | tf_op jit(solution)/shard_map/ppermute | solution.py:428

commit v7 on v6

--- a/solution.py
+++ b/solution.py
@@ -14,6 +14,8 @@
 PHASES = 8
 PAIR = 2 * PHASES
 WIDE = 2 * LANES
+WINDOW = 16
+DIPS = 2 * DMAX + 1
 BORDER = 8
 REACH = -(-HALF * DMAX // PHASES)
 REACHES = range(-REACH, REACH + 1)
@@ -131,20 +133,9 @@
     )(target, bins, traces)
 
 
-def bin_kernel(bins_ref, scale_ref, blocks_ref, out_ref, head_ref, tail_ref, held_ref, even_ref, odd_ref, sems, in_sems, *, capacity, block_rows, edge):
-    parts = held_ref.shape[0]
-    senders = blocks_ref.shape[0] // parts
+def bin_kernel(bins_ref, scale_ref, blocks_ref, out_ref, head_ref, tail_ref, even_ref, odd_ref, sems, *, capacity, block_rows, edge):
     bin_total = out_ref.shape[0]
-    rows = held_ref.shape[2]
     unroll = 8
-    loads = [
-        pltpu.make_async_copy(
-            blocks_ref.at[pl.ds(part * senders, senders), pl.ds(0, rows), :], held_ref.at[part], in_sems.at[part]
-        )
-        for part in range(parts)
-    ]
-    for load in loads:
-        load.start()
     nothing = jnp.zeros((PHASES, LANES), F32)
 
     def clear(i, _):
@@ -154,17 +145,15 @@
         return 0
 
     lax.fori_loop(0, bin_total // unroll, clear, 0)
-    for part in range(parts):
-        loads[part].wait()
-
-        def add_sender(sender, _):
-            first = (part * senders + sender) * (capacity * block_rows)
-            for i in range(capacity * block_rows):
-                total_ref = odd_ref if i % 2 else even_ref
-                total_ref[bins_ref[first + i]] += held_ref[part, sender, i * PHASES : (i + 1) * PHASES]
-            return 0
-
-        lax.fori_loop(0, senders, add_sender, 0)
+
+    def add_sender(sender, _):
+        first = sender * (capacity * block_rows)
+        for i in range(capacity * block_rows):
+            total_ref = odd_ref if i % 2 else even_ref
+            total_ref[bins_ref[first + i]] += blocks_ref[sender, i * PHASES : (i + 1) * PHASES]
+        return 0
+
+    lax.fori_loop(0, blocks_ref.shape[0], add_sender, 0)
 
     def finish(i, _):
         for j in range(unroll):
@@ -184,17 +173,15 @@
 
 
 def stack_bins(blocks, tile_rows, tile_cols, capacity, block_rows):
-    devices = blocks.shape[0]
     bin_total = tile_rows * tile_cols
     edge = HALF * tile_cols
     rows = capacity * block_rows * PHASES
     listed = blocks[:, rows : rows + capacity, :block_rows].astype(I32)
     bins = jnp.where(listed < 0, bin_total, listed).reshape(-1)
     fold = jnp.sum((jnp.arange(bin_total, dtype=I32)[:, None] == bins[None, :]).astype(F32), axis=1)
-    parts = 4
     stacked, head, tail = pl.pallas_call(
         functools.partial(bin_kernel, capacity=capacity, block_rows=block_rows, edge=edge),
-        in_specs=[SMEM, SMEM, ANY],
+        in_specs=[SMEM, SMEM, VMEM],
         out_specs=[VMEM, HBM, HBM],
         out_shape=[
             jax.ShapeDtypeStruct((bin_total, PHASES, LANES), F32),
@@ -202,59 +189,44 @@
             jax.ShapeDtypeStruct((edge, PHASES, LANES), F32),
         ],
         scratch_shapes=[
-            pltpu.VMEM((parts, devices // parts, rows, LANES), F32),
             pltpu.VMEM((bin_total + 8, PHASES, LANES), F32),
             pltpu.VMEM((bin_total + 8, PHASES, LANES), F32),
             pltpu.SemaphoreType.DMA((2,)),
-            pltpu.SemaphoreType.DMA((parts,)),
         ],
-        compiler_params=pltpu.CompilerParams(vmem_limit_bytes=20 * MIB),
+        compiler_params=pltpu.CompilerParams(vmem_limit_bytes=14 * MIB),
     )(bins, 1.0 / jnp.maximum(fold, 1.0), blocks)
     shape = (tile_cols, PHASES, LANES)
     return stacked.reshape((tile_rows,) + shape), head.reshape((HALF,) + shape), tail.reshape((HALF,) + shape)
 
 
-def fill_weights(spots_ref, weights_ref):
-    row = lax.broadcasted_iota(I32, (PAIR, LANES), 0)
-    column = lax.broadcasted_iota(I32, (PAIR, LANES), 1)
-    for pair in range(spots_ref.shape[0] // (2 * PAIR)):
-        for half in range(2):
-            block = pl.ds((pair * 2 + half) * PAIR, PAIR)
-            spot = half * PAIR + column // PHASES - HALF - 2 * pair - row // PHASES
-            share = jnp.maximum(HALF + 1 - jnp.abs(spot), 0).astype(F32) / (HALF + 1) ** 2
-            spots_ref[block, :] = jnp.clip(spot, -HALF - 1, HALF + 1).astype(F32).astype(BF16)
-            weights_ref[block, :] = share.astype(BF16)
-
-
-def steer_window(dip_of, cells, first, count, put, halves_ref, spots_ref, weights_ref):
+def tap_tables():
+    dips = np.arange(-DMAX, DMAX + 1)
+    pair, dip, reach, member, phase, place, old = np.ogrid[
+        : WINDOW // 2, -DMAX : DMAX + 1, -REACH : REACH + 1, :2, :PHASES, : WIDE // PHASES, :PHASES
+    ]
+    offset = place - HALF - 2 * pair - member
+    hit = phase + dip * offset - old == reach * PHASES
+    taps = np.where(hit, np.maximum(HALF + 1 - np.abs(offset), 0), 0) / float((HALF + 1) ** 2)
+    count = len(dips)
+    both = np.zeros((WINDOW // 2, count, count, len(REACHES), 2, PHASES, WIDE), np.float32)
+    taps = taps.reshape(WINDOW // 2, count, len(REACHES), 2, PHASES, WIDE)
+    both[:, :, :, :, 0] = taps[:, :, None, :, 0]
+    both[:, :, :, :, 1] = taps[:, None, :, :, 1]
+    return both.reshape(-1, len(REACHES) * PAIR, WIDE)
+
+
+def steer_window(dip_of, cells, first, count, put, halves_ref, taps_ref):
     for pair in range(len(cells) // 2):
         both = jnp.concatenate([cells[2 * pair](), cells[2 * pair + 1]()], axis=0)
         upper = both.astype(BF16)
         halves_ref[pair * PAIR : (pair + 1) * PAIR, :LANES] = upper
         rest = (both - upper.astype(F32)).astype(BF16)
         halves_ref[pair * PAIR : (pair + 1) * PAIR, LANES:] = rest
-    row = lax.broadcasted_iota(I32, (PAIR, LANES), 0)
-    column = lax.broadcasted_iota(I32, (PAIR, LANES), 1)
-    phase_gap = ((row & (PHASES - 1)) - (column & (PHASES - 1))).astype(F32).astype(BF16)
     lane = lax.broadcasted_iota(I32, (PHASES, LANES), 1)
-    none = jnp.zeros((PAIR, LANES), BF16)
     taps = []
     for pair in range(count // 2):
-        dip = jnp.concatenate(
-            [jnp.full((PHASES, LANES), dip_of(first + 2 * pair + i).astype(F32)) for i in range(2)], axis=0
-        ).astype(BF16)
-        moves, weights = [], []
-        for half in range(2):
-            block = pl.ds((pair * 2 + half) * PAIR, PAIR)
-            moves.append(phase_gap + dip * spots_ref[block, :])
-            weights.append(weights_ref[block, :])
-        for reach in REACHES:
-            taps.append(
-                jnp.concatenate(
-                    [jnp.where(moves[h] == jnp.bfloat16(reach * PHASES), weights[h], none) for h in range(2)],
-                    axis=1,
-                )
-            )
+        chosen = (pair * DIPS + dip_of(first + 2 * pair) + DMAX) * DIPS + dip_of(first + 2 * pair + 1) + DMAX
+        taps.append(taps_ref[chosen])
     sums = jnp.dot(jnp.concatenate(taps, axis=0), halves_ref[...], preferred_element_type=F32)
     for pair in range(count // 2):
         for member in range(2):
@@ -270,18 +242,17 @@
             put(first + 2 * pair + member, total)
 
 
-def steer_kernel(dip_ref, *refs, along, whole, lines, line_of, windows, local_of, edges, final, chained, pieces_count, abreast):
+def steer_kernel(dip_ref, taps_ref, *refs, along, whole, lines, line_of, windows, local_of, edges, final, chained, pieces_count, abreast):
     pieces, refs = refs[:pieces_count], refs[pieces_count:]
     if final:
         table_ref, refs = refs[0], refs[1:]
     refs = refs[chained:]
     out_ref, refs = refs[0], refs[1:]
     edge_refs, refs = refs[: len(edges)], refs[len(edges) :]
-    spots_ref, weights_ref, sems, *refs = refs
+    sems, *refs = refs
     halves = refs[: abreast * len(windows)]
     if final:
         staged_ref, result_ref = refs[abreast * len(windows) :]
-    fill_weights(spots_ref, weights_ref)
     for i, halves_ref in enumerate(halves):
         filled = len(windows[i % len(windows)][2]) * PHASES
         if filled < WIDE:
@@ -306,7 +277,7 @@
             steer_window(
                 lambda place: dip_ref[at(place, full)],
                 [cell(*place) for place in places],
-                first, count, put, halves[parity * len(windows) + i], spots_ref, weights_ref,
+                first, count, put, halves[parity * len(windows) + i], taps_ref,
             )
 
     def some_lines(i, _):
@@ -365,13 +336,13 @@
             copy.wait()
 
 
-def steer(dip, pieces, along, lines, line_of, windows, local_of, edges=(), table=None, before=None, after=None):
+def steer(dip, taps, pieces, along, lines, line_of, windows, local_of, edges=(), table=None, before=None, after=None):
     abreast = 2 if along else 4
     samples = PHASES * LANES
     outputs = sum(count for _, count, _ in windows)
     final = 16 if table is not None else 0
-    operands = [dip] + [array for array, _ in pieces]
-    in_specs = [SMEM] + [VMEM] * len(pieces)
+    operands = [dip, taps] + [array for array, _ in pieces]
+    in_specs = [SMEM, VMEM] + [VMEM] * len(pieces)
     aliases = {}
     if final:
         operands.append(table)
@@ -393,9 +364,7 @@
     if after is not None:
         operands.append(after)
         in_specs.append(ANY)
-    most = max(count for _, count, _ in windows)
-    constant = pltpu.VMEM((most * PAIR, LANES), BF16)
-    scratch = [constant, constant, pltpu.SemaphoreType.DMA((2 * len(windows) if final else max(1, len(edges)),))]
+    scratch = [pltpu.SemaphoreType.DMA((2 * len(windows) if final else max(1, len(edges)),))]
     scratch += [pltpu.VMEM((WIDE, WIDE), BF16)] * (abreast * len(windows))
     if final:
         scratch += [
@@ -406,7 +375,7 @@
         functools.partial(
             steer_kernel,
             along=along, whole=[whole for _, whole in pieces], lines=lines, line_of=line_of, windows=windows,
-            local_of=local_of, edges=edges, final=final, chained=len(operands) - len(pieces) - 1 - bool(final), pieces_count=len(pieces), abreast=abreast,
+            local_of=local_of, edges=edges, final=final, chained=len(operands) - len(pieces) - 2 - bool(final), pieces_count=len(pieces), abreast=abreast,
         ),
         in_specs=in_specs,
         out_specs=out_specs,
@@ -433,7 +402,7 @@
     return [(index, first + i) for i in range(count)]
 
 
-def smooth(stacked, head, tail, along_rows, along_cols, table):
+def smooth(stacked, head, tail, along_rows, along_cols, taps, table):
     rows, cols = stacked.shape[:2]
     mid_rows, mid_cols = rows - 2 * BORDER, cols - 2 * BORDER
     same = lambda line: line
@@ -446,11 +415,11 @@
     lead, last = slice(0, HALF), slice(2 * BORDER - HALF, 2 * BORDER)
 
     def mid_windows(places):
-        return [(BORDER + i, 16, places[i : i + 16 + 2 * HALF]) for i in range(0, mid_rows, 16)]
+        return [(BORDER + i, WINDOW, places[i : i + WINDOW + 2 * HALF]) for i in range(0, mid_rows, WINDOW)]
 
     low, high = swap_ends(head, tail, "inline")
     middle, head_mid, tail_mid = steer(
-        along_rows, [(stacked, True)], 0, cols, same,
+        along_rows, taps, [(stacked, True)], 0, cols, same,
         mid_windows(span_of(0, BORDER - HALF, mid_rows + 2 * HALF)), mid_place,
         edges=[(every, lead), (every, slice(cols - HALF, cols))],
     )
@@ -461,32 +430,32 @@
         (rows - BORDER, BORDER, span_of(1, rows - BORDER - HALF, BORDER + HALF) + span_of(2, 0, HALF)),
     ]
     corners, head_out, tail_out = steer(
-        along_rows, pieces, 0, 2 * BORDER, outer_col, windows, outer_place, edges=[(every, lead), (every, last)],
+        along_rows, taps, pieces, 0, 2 * BORDER, outer_col, windows, outer_place, edges=[(every, lead), (every, last)],
         after=middle,
     )
     low_out, high_out = swap_ends(head_out, tail_out, "crosslin")
-    (flanks,) = steer(along_rows, pieces, 0, mid_cols, inner, windows, outer_place, after=corners)
+    (flanks,) = steer(along_rows, taps, pieces, 0, mid_cols, inner, windows, outer_place, after=corners)
 
     def cross_windows(places):
-        return [(i, 16, places[i : i + 16 + 2 * HALF]) for i in range(0, cols, 16)]
+        return [(i, WINDOW, places[i : i + WINDOW + 2 * HALF]) for i in range(0, cols, WINDOW)]
 
     places = span_of(0, 0, HALF) + span_of(1, 0, cols) + span_of(2, 0, HALF)
     (middle_second,) = steer(
-        along_cols, [(low_mid, False), (middle, False), (high_mid, False)], 1, mid_rows, inner,
+        along_cols, taps, [(low_mid, False), (middle, False), (high_mid, False)], 1, mid_rows, inner,
         cross_windows(places), same, after=flanks,
     )
     places = (
         span_of(0, 0, HALF) + span_of(1, 0, BORDER) + span_of(2, 0, mid_cols) + span_of(1, BORDER, BORDER) + span_of(3, 0, HALF)
     )
     border_second, head, tail = steer(
-        along_cols, [(low_out, False), (corners, False), (flanks, False), (high_out, False)], 1, 2 * BORDER,
+        along_cols, taps, [(low_out, False), (corners, False), (flanks, False), (high_out, False)], 1, 2 * BORDER,
         outer_row, cross_windows(places), same, edges=[(lead, every), (last, every)], after=middle_second,
     )
 
     low, high = swap_ends(head, tail, "inline")
     places = span_of(0, BORDER - HALF, HALF) + span_of(1, 0, mid_rows) + span_of(0, BORDER, HALF)
     (result,) = steer(
-        along_rows, [(border_second, True), (middle_second, True)], 0, cols, same, mid_windows(places), mid_place,
+        along_rows, taps, [(border_second, True), (middle_second, True)], 0, cols, same, mid_windows(places), mid_place,
         table=table,
     )
     windows = [
@@ -494,7 +463,7 @@
         (rows - BORDER, BORDER, span_of(2, mid_rows - HALF, HALF) + span_of(1, BORDER, BORDER) + span_of(3, 0, HALF)),
     ]
     (result,) = steer(
-        along_rows, [(low, True), (border_second, True), (middle_second, True), (high, True)], 0, cols, same,
+        along_rows, taps, [(low, True), (border_second, True), (middle_second, True), (high, True)], 0, cols, same,
         windows, outer_place, table=table, before=result,
     )
     return result
@@ -509,7 +478,7 @@
     arrived = lax.all_to_all(outgoing, BOTH, split_axis=0, concat_axis=0, tiled=True)
     stacked, head, tail = stack_bins(arrived, tile_rows, tile_cols, capacity, block_rows)
     back = jnp.asarray(interleave_table(samples).T, BF16)
-    return smooth(stacked, head, tail, dip_inline, dip_cross, back)
+    return smooth(stacked, head, tail, dip_inline, dip_cross, jnp.asarray(tap_tables(), BF16), back)
 
 
 def solution(mesh):

time: 206 us -> 205 us (level)
  local copies, waits for them, and re-layouts: 4.32 us -> 7.68 us
  waiting for transfers between devices: 18.1 us -> 15.8 us
    unnamed x10 -> x16, local copies, waits for them, and re-layouts: 4.21 us -> 7.56 us
    ppermute x4, waiting for transfers between devices: 18 us -> 15.8 us  [swap_ends(): high = lax.ppermute(head, axis, [(i + 1, i) for i in range(count - 1)])]
where the time goes in v7:
time: 205 us
  blocking collectives  105 us (51%)
  Pallas kernels  56.1 us (27%)
  starting transfers between devices  19.5 us (10%)
  waiting for transfers between devices  15.8 us (8%)
  local copies, waits for them, and re-layouts  7.68 us (4%)
    all_to_all x1, blocking collectives, on_device(): lax.all_to_all(outgoing, BOTH, split_axis=0, concat_axis=0, tiled=True)  105 us
    pallas_call x7, Pallas kernels, steer(): pl.pallas_call(functools.partial(steer_kernel, along=along, whole=[whole...  43.8 us
    ppermute x4, waiting for transfers between devices, swap_ends(): high = lax.ppermute(head, axis, [(i + 1, i) for i in range(count - 1)])  15.8 us
    ppermute x4, starting transfers between devices, swap_ends(): low = lax.ppermute(tail, axis, [(i, i + 1) for i in range(count - 1)])  12.9 us
    unnamed x16, local copies, waits for them, and re-layouts  7.56 us
    ppermute x4, starting transfers between devices, swap_ends(): high = lax.ppermute(head, axis, [(i + 1, i) for i in range(count - 1)])  6.61 us
    pallas_call x1, Pallas kernels, pack(): pl.pallas_call(functools.partial(pack_kernel, capacity=capacity), in_spec...  6.35 us
    pallas_call x1, Pallas kernels, stack_bins(): pl.pallas_call(functools.partial(bin_kernel, capacity=capacity, block_row...  5.99 us
  transfers between devices with their start and end apart: 8, of which 2 were waited for; matrix products, arithmetic and copies ran while one was open for 0% of the time, Pallas kernels for 14%

profile of v7, /device:TPU:1, one launch (start us, length us, event | category | flops | bytes accessed | tf_op | source)
XLA Modules:
  0.0 204.8 jit_solution(2894162954527789823)
XLA Ops:
  0.0 6.4 %shard_map.73 = f32[32,264,128]{2,1,0:T(8,128)} custom-call(s32[128]{0:T(128)} %bitcast.13, s32[4,128]{1,0:T(4,128)} %bitcast.12, f32[128,4,1024]{2,1,0:T(4,128)} %traces_ref.1), custom_call_target="tpu_custom_call" | custom-call | tf_op jit(solution)/shard_map/pallas_call | solution.py:117
  6.4 104.7 %all_to_all.5.blocks_ref = f32[32,264,128]{2,1,0:T(8,128)S(1)} all-to-all(f32[32,264,128]{2,1,0:T(8,128)} %shard_map.73), channel_id=1, replica_groups=mesh['inline'=8,'crosslin'=4] {'inline','crosslin'}, dimensions={0} | all-to-all | bytes 8650752 | tf_op jit(solution)/shard_map/all_to_all | solution.py:478
  111.1 0.0 copy-start.4
  111.1 0.0 copy-start.1
  111.1 2.0 copy-done.1
  113.1 0.1 reshape.17.bins_ref
  113.2 0.5 convert_reduce_fusion
  113.8 0.0 copy-start.2
  113.8 2.2 %copy-done.2 = f32[32,264,128]{2,1,0:T(8,128)S(1)} copy-done((f32[32,264,128]{2,1,0:T(8,128)S(1)}, f32[32,264,128]{2,1,0:T(8,128)}, u32[]{:S(2)}) %copy-start.2) | copy-done | bytes 4325400
  116.0 6.0 %shard_map.74 = (f32[1024,8,128]{2,1,0:T(8,128)S(1)}, f32[224,8,128]{2,1,0:T(8,128)S(1)}, f32[224,8,128]{2,1,0:T(8,128)S(1)}) custom-call(s32[1024]{0:T(1024)S(1)} %reshape.17.bins_ref, f32[1024]{0:T(1024)S(1)} %maximum_divide_fusion.scale_ref, f32[32,264,128]{2,1,0:T(8,128)S(1)} %copy-done.2), custom_call_target="tpu_custom_call" | custom-call | tf_op jit(solution)/shard_map/pallas_call | solution.py:182
  122.0 2.7 %collective-permute-start = (f32[7,32,8,128]{3,2,1,0:T(8,128)S(1)}, f32[7,32,8,128]{3,2,1,0:T(8,128)S(1)}, u32[]{:S(2)}, u32[]{:S(2)}) collective-permute-start(f32[7,32,8,128]{3,2,1,0:T(8,128)S(1)} %bitcast.11), channel_id=1, source_target_pairs={{0,4},{4,8},{8,12},{12,16},{16,20},{20,24},{24,28},{1,5},{5,9},{9,... | collective-permute-start | bytes 2752520 | tf_op jit(solution)/shard_map/ppermute | solution.py:396
  124.7 1.9 collective-permute-start.1
  126.6 0.0 copy-done.4
  126.6 0.0 copy-start
  126.6 3.3 %copy-done = bf16[200,80,256]{2,1,0:T(8,128)(2,1)S(1)} copy-done((bf16[200,80,256]{2,1,0:T(8,128)(2,1)S(1)}, bf16[200,80,256]{2,1,0:T(8,128)(2,1)}, u32[]{:S(2)}) %copy-start) | copy-done | bytes 8192024
  130.0 6.0 %shard_map.75 = (f32[16,32,8,128]{3,2,1,0:T(8,128)S(1)}, f32[16,7,8,128]{3,2,1,0:T(8,128)S(1)}, f32[16,7,8,128]{3,2,1,0:T(8,128)S(1)}) custom-call(s32[32,32]{1,0:T(8,128)S(1)} %copy-done.4, bf16[200,80,256]{2,1,0:T(8,128)(2,1)S(1)} %copy-done, f32[32,32,8,128]{3,2,1,0:T(8,128)S(1)} %bitcast.7), custom_call_target="tpu_custom_call" | custom-call | flops 1258291200 | bytes 4194304 | tf_op jit(solution)/shard_map/pallas_call | solution.py:374
  136.0 2.4 %collective-permute-start.4 = (f32[16,7,8,128]{3,2,1,0:T(8,128)S(1)}, f32[16,7,8,128]{3,2,1,0:T(8,128)S(1)}, u32[]{:S(2)}, u32[]{:S(2)}) collective-permute-start(f32[16,7,8,128]{3,2,1,0:T(8,128)S(1)} %get-tuple-element.24), channel_id=1, source_target_pairs={{0,1},{1,2},{2,3},{4,5},{5,6},{6,7},{8,9},{9,10},{10,11},{12,13},{... | collective-permute-start | bytes 1376264 | tf_op jit(solution)/shard_map/ppermute | solution.py:396
  138.4 1.3 collective-permute-start.5
  139.7 0.0 collective-permute-done.refs_0_
  139.8 6.8 %collective-permute-done.1.refs_2_ = f32[7,32,8,128]{3,2,1,0:T(8,128)S(1)} collective-permute-done((f32[7,32,8,128]{3,2,1,0:T(8,128)S(1)}, f32[7,32,8,128]{3,2,1,0:T(8,128)S(1)}, u32[]{:S(2)}, u32[]{:S(2)}) %collective-permute-start.1) | collective-permute-done | bytes 917536 | tf_op jit(solution)/shard_map/ppermute | solution.py:397
  146.6 3.4 %shard_map.76 = (f32[16,16,8,128]{3,2,1,0:T(8,128)S(1)}, f32[16,7,8,128]{3,2,1,0:T(8,128)S(1)}, f32[16,7,8,128]{3,2,1,0:T(8,128)S(1)}) custom-call(s32[32,32]{1,0:T(8,128)S(1)} %copy-done.4, bf16[200,80,256]{2,1,0:T(8,128)(2,1)S(1)} %copy-done, f32[7,32,8,128]{3,2,1,0:T(8,128)S(1)} %collective-permute-done.refs_0_, f32[32,32,8,128]{3,2,1,0:T(8,128)S(1)} %bitcast.8, ...), custom_call_target="tpu_custom_call" | custom-call | flops 629145600 | bytes 2097152 | tf_op jit(solution)/shard_map/pallas_call | solution.py:374
  150.0 1.9 collective-permute-start.2
  152.0 1.3 collective-permute-start.3
  153.3 0.0 slice-start
  153.3 0.0 slice-start.1
  153.3 0.0 copy-start.5
  153.3 3.3 %shard_map.77.refs_3_.refs_2_ = f32[16,16,8,128]{3,2,1,0:T(8,128)S(1)} custom-call(s32[32,32]{1,0:T(8,128)S(1)} %copy-done.4, bf16[200,80,256]{2,1,0:T(8,128)(2,1)S(1)} %copy-done, f32[7,32,8,128]{3,2,1,0:T(8,128)S(1)} %collective-permute-done.refs_0_, f32[32,32,8,128]{3,2,1,0:T(8,128)S(1)} %bitcast.9, f32[7,32,8,128]{3,2,1,0:T(8,128)S(1)} %collective-permute-done.1.refs_2_, ...), custom_call_target="tpu_custom_call" | custom-call | flops 629145600 | bytes 2097152 | tf_op jit(solution)/shard_map/pallas_call | solution.py:374
  156.6 0.0 collective-permute-done.4.refs_0_
  156.6 0.0 collective-permute-done.5.refs_2_
  156.7 0.0 slice-done
  156.7 0.0 slice-done.1
  156.7 0.0 copy-done.5
  156.7 5.9 %shard_map.78.refs_4_.refs_1_.refs_2_ = f32[16,32,8,128]{3,2,1,0:T(8,128)S(1)} custom-call(s32[32,32]{1,0:T(8,128)S(1)} %copy-done.5, bf16[200,80,256]{2,1,0:T(8,128)(2,1)S(1)} %bitcast.6, f32[16,7,8,128]{3,2,1,0:T(8,128)S(1)} %collective-permute-done.4.refs_0_, f32[16,32,8,128]{3,2,1,0:T(8,128)S(1)} %get-tuple-element.20.refs_3_.refs_1_, ...), custom_call_target="tpu_custom_call" | custom-call | flops 1258291200 | bytes 4194304 | tf_op jit(solution)/shard_map/pallas_call | solution.py:374
  162.6 0.0 copy-start.3
  162.6 0.0 collective-permute-done.2.refs_0_
  162.6 0.0 collective-permute-done.3.refs_3_
  162.6 6.4 %shard_map.79 = (f32[16,32,8,128]{3,2,1,0:T(8,128)S(1)}, f32[7,32,8,128]{3,2,1,0:T(8,128)S(1)}, f32[7,32,8,128]{3,2,1,0:T(8,128)S(1)}) custom-call(s32[32,32]{1,0:T(8,128)S(1)} %copy-done.5, bf16[200,80,256]{2,1,0:T(8,128)(2,1)S(1)} %bitcast.6, f32[16,7,8,128]{3,2,1,0:T(8,128)S(1)} %collective-permute-done.2.refs_0_, ...), custom_call_target="tpu_custom_call" | custom-call | flops 1258291200 | bytes 4194304 | tf_op jit(solution)/shard_map/pallas_call | solution.py:374
  169.0 5.8 %collective-permute-start.6 = (f32[7,32,8,128]{3,2,1,0:T(8,128)S(1)}, f32[7,32,8,128]{3,2,1,0:T(8,128)S(1)}, u32[]{:S(2)}, u32[]{:S(2)}) collective-permute-start(f32[7,32,8,128]{3,2,1,0:T(8,128)S(1)} %get-tuple-element.26), channel_id=1, source_target_pairs={{0,4},{4,8},{8,12},{12,16},{16,20},{20,24},{24,28},{1,5},{5,9},{9,... | collective-permute-start | bytes 2752520 | tf_op jit(solution)/shard_map/ppermute | solution.py:396
  174.8 2.1 %collective-permute-start.7 = (f32[7,32,8,128]{3,2,1,0:T(8,128)S(1)}, f32[7,32,8,128]{3,2,1,0:T(8,128)S(1)}, u32[]{:S(2)}, u32[]{:S(2)}) collective-permute-start(f32[7,32,8,128]{3,2,1,0:T(8,128)S(1)} %get-tuple-element.28), channel_id=1, source_target_pairs={{4,0},{8,4},{12,8},{16,12},{20,16},{24,20},{28,24},{5,1},{9,5},{13... | collective-permute-start | bytes 2752520 | tf_op jit(solution)/shard_map/ppermute | solution.py:397
  176.9 0.0 copy-done.3
  176.9 9.4 %shard_map.80.refs_5_ = f32[32,32,1024]{2,1,0:T(8,128)} custom-call(s32[32,32]{1,0:T(8,128)S(1)} %copy-done.4, bf16[200,80,256]{2,1,0:T(8,128)(2,1)S(1)} %bitcast.6, f32[16,32,8,128]{3,2,1,0:T(8,128)S(1)} %get-tuple-element.27.refs_0_.refs_1_, f32[16,32,8,128]{3,2,1,0:T(8,128)S(1)} %shard_map.78.refs_4_.refs_1_.refs_2_, bf16[1024,1024]{1,0:T(8,128)(2,1)S(1)} %copy-done.3), custom_call_target="tpu_custom_call" | custom-call | flops 1258291200 | bytes 4194304 | tf_op jit(solution)/shard_map/pallas_call | solution.py:374
  186.3 0.0 collective-permute-done.6.refs_0_
  186.4 9.0 %collective-permute-done.7.refs_3_ = f32[7,32,8,128]{3,2,1,0:T(8,128)S(1)} collective-permute-done((f32[7,32,8,128]{3,2,1,0:T(8,128)S(1)}, f32[7,32,8,128]{3,2,1,0:T(8,128)S(1)}, u32[]{:S(2)}, u32[]{:S(2)}) %collective-permute-start.7) | collective-permute-done | bytes 917536 | tf_op jit(solution)/shard_map/ppermute | solution.py:397
  195.4 9.3 %shard_map.81 = f32[32,32,1024]{2,1,0:T(8,128)} custom-call(s32[32,32]{1,0:T(8,128)S(1)} %copy-done.4, bf16[200,80,256]{2,1,0:T(8,128)(2,1)S(1)} %bitcast.6, f32[7,32,8,128]{3,2,1,0:T(8,128)S(1)} %collective-permute-done.6.refs_0_, f32[16,32,8,128]{3,2,1,0:T(8,128)S(1)} %get-tuple-element.27.refs_0_.refs_1_, ...), custom_call_target="tpu_custom_call", output_to_operand_aliasing={{}: (7, {})} | custom-call | flops 1258291200 | bytes 4194304 | tf_op jit(solution)/shard_map/pallas_call | solution.py:374
  (3 shorter events, 0.0 us)
Async XLA Ops:
  111.1 15.5 %copy-start.4 = (s32[32,32]{1,0:T(8,128)S(1)}, s32[32,32]{1,0:T(8,128)}, u32[]{:S(2)}) copy-start(s32[32,32]{1,0:T(8,128)} %dip_ref.13) | copy-start | bytes 12292
  111.1 2.0 copy-start.1
  113.8 2.2 %copy-start.2 = (f32[32,264,128]{2,1,0:T(8,128)S(1)}, f32[32,264,128]{2,1,0:T(8,128)}, u32[]{:S(2)}) copy-start(f32[32,264,128]{2,1,0:T(8,128)} %copy-done.1) | copy-start | bytes 12976132
  122.0 17.8 %collective-permute-start = (f32[7,32,8,128]{3,2,1,0:T(8,128)S(1)}, f32[7,32,8,128]{3,2,1,0:T(8,128)S(1)}, u32[]{:S(2)}, u32[]{:S(2)}) collective-permute-start(f32[7,32,8,128]{3,2,1,0:T(8,128)S(1)} %bitcast.11), channel_id=1, source_target_pairs={{0,4},{4,8},{8,12},{12,16},{16,20},{20,24},{24,28},{1,5},{5,9},{9,... | collective-permute-start | bytes 2752520 | tf_op jit(solution)/shard_map/ppermute | solution.py:396
  124.7 21.9 %collective-permute-start.1 = (f32[7,32,8,128]{3,2,1,0:T(8,128)S(1)}, f32[7,32,8,128]{3,2,1,0:T(8,128)S(1)}, u32[]{:S(2)}, u32[]{:S(2)}) collective-permute-start(f32[7,32,8,128]{3,2,1,0:T(8,128)S(1)} %bitcast.10), channel_id=1, source_target_pairs={{4,0},{8,4},{12,8},{16,12},{20,16},{24,20},{28,24},{5,1},{9,5},{13... | collective-permute-start | bytes 2752520 | tf_op jit(solution)/shard_map/ppermute | solution.py:397
  126.6 3.3 %copy-start = (bf16[200,80,256]{2,1,0:T(8,128)(2,1)S(1)}, bf16[200,80,256]{2,1,0:T(8,128)(2,1)}, u32[]{:S(2)}) copy-start(bf16[200,80,256]{2,1,0:T(8,128)(2,1)} %constant.13.clone.taps_ref) | copy-start | bytes 24576004
  136.0 20.6 %collective-permute-start.4 = (f32[16,7,8,128]{3,2,1,0:T(8,128)S(1)}, f32[16,7,8,128]{3,2,1,0:T(8,128)S(1)}, u32[]{:S(2)}, u32[]{:S(2)}) collective-permute-start(f32[16,7,8,128]{3,2,1,0:T(8,128)S(1)} %get-tuple-element.24), channel_id=1, source_target_pairs={{0,1},{1,2},{2,3},{4,5},{5,6},{6,7},{8,9},{9,10},{10,11},{12,13},{... | collective-permute-start | bytes 1376264 | tf_op jit(solution)/shard_map/ppermute | solution.py:396
  138.4 18.2 %collective-permute-start.5 = (f32[16,7,8,128]{3,2,1,0:T(8,128)S(1)}, f32[16,7,8,128]{3,2,1,0:T(8,128)S(1)}, u32[]{:S(2)}, u32[]{:S(2)}) collective-permute-start(f32[16,7,8,128]{3,2,1,0:T(8,128)S(1)} %get-tuple-element.25), channel_id=1, source_target_pairs={{1,0},{2,1},{3,2},{5,4},{6,5},{7,6},{9,8},{10,9},{11,10},{13,12},{... | collective-permute-start | bytes 1376264 | tf_op jit(solution)/shard_map/ppermute | solution.py:397
  150.0 12.6 %collective-permute-start.2 = (f32[16,7,8,128]{3,2,1,0:T(8,128)S(1)}, f32[16,7,8,128]{3,2,1,0:T(8,128)S(1)}, u32[]{:S(2)}, u32[]{:S(2)}) collective-permute-start(f32[16,7,8,128]{3,2,1,0:T(8,128)S(1)} %get-tuple-element.21), channel_id=1, source_target_pairs={{0,1},{1,2},{2,3},{4,5},{5,6},{6,7},{8,9},{9,10},{10,11},{12,13},{... | collective-permute-start | bytes 1376264 | tf_op jit(solution)/shard_map/ppermute | solution.py:396
  152.0 10.7 %collective-permute-start.3 = (f32[16,7,8,128]{3,2,1,0:T(8,128)S(1)}, f32[16,7,8,128]{3,2,1,0:T(8,128)S(1)}, u32[]{:S(2)}, u32[]{:S(2)}) collective-permute-start(f32[16,7,8,128]{3,2,1,0:T(8,128)S(1)} %get-tuple-element.23), channel_id=1, source_target_pairs={{1,0},{2,1},{3,2},{5,4},{6,5},{7,6},{9,8},{10,9},{11,10},{13,12},{... | collective-permute-start | bytes 1376264 | tf_op jit(solution)/shard_map/ppermute | solution.py:397
  153.3 3.4 %slice-start = ((s8[8192000]{0:T(1024)(128)(4,1)}), s8[4194304]{0:T(1024)(128)(4,1)S(1)}, s32[]{:S(2)}) async-start(s8[8192000]{0:T(1024)(128)(4,1)} %bitcast.5), calls=%async_computation.1 | async-start | bytes 8388608
  153.3 3.4 %slice-start.1 = ((s8[8192000]{0:T(1024)(128)(4,1)}), s8[3997696]{0:T(1024)(128)(4,1)S(1)}, s32[]{:S(2)}) async-start(s8[8192000]{0:T(1024)(128)(4,1)} %bitcast.5), calls=%async_computation.2 | async-start | bytes 7995392
  153.3 3.4 %copy-start.5 = (s32[32,32]{1,0:T(8,128)S(1)}, s32[32,32]{1,0:T(8,128)}, u32[]{:S(2)}) copy-start(s32[32,32]{1,0:T(8,128)} %dip_ref.11) | copy-start | bytes 12292
  162.6 14.3 %copy-start.3 = (bf16[1024,1024]{1,0:T(8,128)(2,1)S(1)}, bf16[1024,1024]{1,0:T(8,128)(2,1)}, u32[]{:S(2)}) copy-start(bf16[1024,1024]{1,0:T(8,128)(2,1)} %constant.12.clone.refs_2_.refs_4_) | copy-start | bytes 6291460
  169.0 17.4 %collective-permute-start.6 = (f32[7,32,8,128]{3,2,1,0:T(8,128)S(1)}, f32[7,32,8,128]{3,2,1,0:T(8,128)S(1)}, u32[]{:S(2)}, u32[]{:S(2)}) collective-permute-start(f32[7,32,8,128]{3,2,1,0:T(8,128)S(1)} %get-tuple-element.26), channel_id=1, source_target_pairs={{0,4},{4,8},{8,12},{12,16},{16,20},{20,24},{24,28},{1,5},{5,9},{9,... | collective-permute-start | bytes 2752520 | tf_op jit(solution)/shard_map/ppermute | solution.py:396
  174.8 20.6 %collective-permute-start.7 = (f32[7,32,8,128]{3,2,1,0:T(8,128)S(1)}, f32[7,32,8,128]{3,2,1,0:T(8,128)S(1)}, u32[]{:S(2)}, u32[]{:S(2)}) collective-permute-start(f32[7,32,8,128]{3,2,1,0:T(8,128)S(1)} %get-tuple-element.28), channel_id=1, source_target_pairs={{4,0},{8,4},{12,8},{16,12},{20,16},{24,20},{28,24},{5,1},{9,5},{13... | collective-permute-start | bytes 2752520 | tf_op jit(solution)/shard_map/ppermute | solution.py:397

commit v8 on v6

--- a/solution.py
+++ b/solution.py
@@ -131,20 +131,15 @@
     )(target, bins, traces)
 
 
-def bin_kernel(bins_ref, scale_ref, blocks_ref, out_ref, head_ref, tail_ref, held_ref, even_ref, odd_ref, sems, in_sems, *, capacity, block_rows, edge):
-    parts = held_ref.shape[0]
-    senders = blocks_ref.shape[0] // parts
+def bin_kernel(blocks_ref, out_ref, head_ref, tail_ref, even_ref, odd_ref, listed_ref, places_ref, scale_ref, scales_ref, sems, *, capacity, block_rows, edge):
+    devices, rows, _ = blocks_ref.shape
+    room = listed_ref.shape[1]
     bin_total = out_ref.shape[0]
-    rows = held_ref.shape[2]
     unroll = 8
-    loads = [
-        pltpu.make_async_copy(
-            blocks_ref.at[pl.ds(part * senders, senders), pl.ds(0, rows), :], held_ref.at[part], in_sems.at[part]
-        )
-        for part in range(parts)
-    ]
-    for load in loads:
-        load.start()
+    listed = blocks_ref[:, rows - room :, :]
+    listed_ref[...] = jnp.where(listed < 0, float(bin_total), listed).astype(I32)
+    copy = pltpu.make_async_copy(listed_ref, places_ref, sems.at[0])
+    copy.start()
     nothing = jnp.zeros((PHASES, LANES), F32)
 
     def clear(i, _):
@@ -154,29 +149,42 @@
         return 0
 
     lax.fori_loop(0, bin_total // unroll, clear, 0)
-    for part in range(parts):
-        loads[part].wait()
-
-        def add_sender(sender, _):
-            first = (part * senders + sender) * (capacity * block_rows)
-            for i in range(capacity * block_rows):
-                total_ref = odd_ref if i % 2 else even_ref
-                total_ref[bins_ref[first + i]] += held_ref[part, sender, i * PHASES : (i + 1) * PHASES]
-            return 0
-
-        lax.fori_loop(0, senders, add_sender, 0)
+    copy.wait()
+    count_rows = scale_ref.shape[0]
+    numbers = lax.broadcasted_iota(I32, (count_rows, LANES), 0) * LANES + lax.broadcasted_iota(
+        I32, (count_rows, LANES), 1
+    )
+
+    def add_sender(sender, folds):
+        folds = list(folds)
+        for rank in range(capacity):
+            for j in range(block_rows):
+                total_ref = odd_ref if j % 2 else even_ref
+                place = places_ref[sender, rank, j]
+                row = (rank * block_rows + j) * PHASES
+                total_ref[place] += blocks_ref[sender, row : row + PHASES, :]
+                folds[j % 2] = folds[j % 2] + jnp.where(numbers == place, 1.0, 0.0)
+        return tuple(folds)
+
+    empty = jnp.zeros((count_rows, LANES), F32)
+    folds = lax.fori_loop(0, devices, add_sender, (empty, empty))
+    scale_ref[...] = 1.0 / jnp.maximum(folds[0] + folds[1], 1.0)
+    copy = pltpu.make_async_copy(scale_ref, scales_ref, sems.at[0])
+    copy.start()
+    copy.wait()
 
     def finish(i, _):
         for j in range(unroll):
             place = i * unroll + j
-            out_ref[place] = (even_ref[place] + odd_ref[place]) * scale_ref[place]
+            scale = scales_ref[place // LANES, place % LANES]
+            out_ref[place] = (even_ref[place] + odd_ref[place]) * scale
         return 0
 
     lax.fori_loop(0, edge // unroll, finish, 0)
-    head_copy = pltpu.make_async_copy(out_ref.at[pl.ds(0, edge)], head_ref, sems.at[0])
+    head_copy = pltpu.make_async_copy(out_ref.at[pl.ds(0, edge)], head_ref, sems.at[1])
     head_copy.start()
     lax.fori_loop((bin_total - edge) // unroll, bin_total // unroll, finish, 0)
-    tail_copy = pltpu.make_async_copy(out_ref.at[pl.ds(bin_total - edge, edge)], tail_ref, sems.at[1])
+    tail_copy = pltpu.make_async_copy(out_ref.at[pl.ds(bin_total - edge, edge)], tail_ref, sems.at[2])
     tail_copy.start()
     lax.fori_loop(edge // unroll, (bin_total - edge) // unroll, finish, 0)
     head_copy.wait()
@@ -187,14 +195,10 @@
     devices = blocks.shape[0]
     bin_total = tile_rows * tile_cols
     edge = HALF * tile_cols
-    rows = capacity * block_rows * PHASES
-    listed = blocks[:, rows : rows + capacity, :block_rows].astype(I32)
-    bins = jnp.where(listed < 0, bin_total, listed).reshape(-1)
-    fold = jnp.sum((jnp.arange(bin_total, dtype=I32)[:, None] == bins[None, :]).astype(F32), axis=1)
-    parts = 4
+    room = blocks.shape[1] - capacity * block_rows * PHASES
     stacked, head, tail = pl.pallas_call(
         functools.partial(bin_kernel, capacity=capacity, block_rows=block_rows, edge=edge),
-        in_specs=[SMEM, SMEM, ANY],
+        in_specs=[VMEM],
         out_specs=[VMEM, HBM, HBM],
         out_shape=[
             jax.ShapeDtypeStruct((bin_total, PHASES, LANES), F32),
@@ -202,14 +206,16 @@
             jax.ShapeDtypeStruct((edge, PHASES, LANES), F32),
         ],
         scratch_shapes=[
-            pltpu.VMEM((parts, devices // parts, rows, LANES), F32),
             pltpu.VMEM((bin_total + 8, PHASES, LANES), F32),
             pltpu.VMEM((bin_total + 8, PHASES, LANES), F32),
-            pltpu.SemaphoreType.DMA((2,)),
-            pltpu.SemaphoreType.DMA((parts,)),
+            pltpu.VMEM((devices, room, LANES), I32),
+            pltpu.SMEM((devices, room, LANES), I32),
+            pltpu.VMEM((bin_total // LANES, LANES), F32),
+            pltpu.SMEM((bin_total // LANES, LANES), F32),
+            pltpu.SemaphoreType.DMA((3,)),
         ],
-        compiler_params=pltpu.CompilerParams(vmem_limit_bytes=20 * MIB),
-    )(bins, 1.0 / jnp.maximum(fold, 1.0), blocks)
+        compiler_params=pltpu.CompilerParams(vmem_limit_bytes=14 * MIB),
+    )(blocks)
     shape = (tile_cols, PHASES, LANES)
     return stacked.reshape((tile_rows,) + shape), head.reshape((HALF,) + shape), tail.reshape((HALF,) + shape)
 
@@ -226,17 +232,19 @@
             weights_ref[block, :] = share.astype(BF16)
 
 
-def steer_window(dip_of, cells, first, count, put, halves_ref, spots_ref, weights_ref):
+def split_cells(cells, halves_ref):
     for pair in range(len(cells) // 2):
         both = jnp.concatenate([cells[2 * pair](), cells[2 * pair + 1]()], axis=0)
         upper = both.astype(BF16)
         halves_ref[pair * PAIR : (pair + 1) * PAIR, :LANES] = upper
         rest = (both - upper.astype(F32)).astype(BF16)
         halves_ref[pair * PAIR : (pair + 1) * PAIR, LANES:] = rest
+
+
+def apply_taps(dip_of, first, count, halves_ref, spots_ref, weights_ref):
     row = lax.broadcasted_iota(I32, (PAIR, LANES), 0)
     column = lax.broadcasted_iota(I32, (PAIR, LANES), 1)
     phase_gap = ((row & (PHASES - 1)) - (column & (PHASES - 1))).astype(F32).astype(BF16)
-    lane = lax.broadcasted_iota(I32, (PHASES, LANES), 1)
     none = jnp.zeros((PAIR, LANES), BF16)
     taps = []
     for pair in range(count // 2):
@@ -255,7 +263,11 @@
                     axis=1,
                 )
             )
-    sums = jnp.dot(jnp.concatenate(taps, axis=0), halves_ref[...], preferred_element_type=F32)
+    return jnp.dot(jnp.concatenate(taps, axis=0), halves_ref[...], preferred_element_type=F32)
+
+
+def move_lanes(sums, first, count, put):
+    lane = lax.broadcasted_iota(I32, (PHASES, LANES), 1)
     for pair in range(count // 2):
         for member in range(2):
             total = None
@@ -290,28 +302,34 @@
     def at(place, line):
         return (place, line) if along == 0 else (line, place)
 
-    def one_line(line, parity):
-        full = line_of(line)
-
-        def cell(index, local):
-            return lambda: pieces[index][at(local, full if whole[index] else line)]
-
-        def put(place, value):
-            if final:
-                staged_ref[pl.ds((local_of(place) * final + line % final) * PHASES, PHASES), :] = value
-            else:
-                out_ref[at(local_of(place), line)] = value
-
-        for i, (first, count, places) in enumerate(windows):
-            steer_window(
-                lambda place: dip_ref[at(place, full)],
-                [cell(*place) for place in places],
-                first, count, put, halves[parity * len(windows) + i], spots_ref, weights_ref,
+    def some_lines(step, _):
+        jobs = []
+        for parity in range(abreast):
+            line = abreast * step + parity
+            full = line_of(line)
+
+            def cell(index, local, line=line, full=full):
+                return lambda: pieces[index][at(local, full if whole[index] else line)]
+
+            def put(place, value, line=line):
+                if final:
+                    staged_ref[pl.ds((local_of(place) * final + line % final) * PHASES, PHASES), :] = value
+                else:
+                    out_ref[at(local_of(place), line)] = value
+
+            for i, (first, count, places) in enumerate(windows):
+                halves_ref = halves[parity * len(windows) + i]
+                split_cells([cell(*place) for place in places], halves_ref)
+                jobs.append((full, first, count, halves_ref, put))
+        waiting = None
+        for full, first, count, halves_ref, put in jobs:
+            sums = apply_taps(
+                lambda place: dip_ref[at(place, full)], first, count, halves_ref, spots_ref, weights_ref
             )
-
-    def some_lines(i, _):
-        for j in range(abreast):
-            one_line(abreast * i + j, j)
+            if waiting is not None:
+                move_lanes(*waiting)
+            waiting = (sums, first, count, put)
+        move_lanes(*waiting)
         return 0
 
     if not final:

time: 206 us -> 209 us (1.015)
  Pallas kernels: 56.7 us -> 64.2 us
  local copies, waits for them, and re-layouts: 4.32 us -> 0.02 us
    pallas_call x1, Pallas kernels: 6.57 us -> 14.1 us  [stack_bins(): pl.pallas_call(functools.partial(bin_kernel, capacity=capacity, block_row...]
    unnamed x10 -> x6, local copies, waits for them, and re-layouts: 4.21 us -> 0.02 us
  transfers between devices with their start and end apart: 8 -> 8, of which waited for: 2 -> 2; matrix products, arithmetic and copies ran while one was open for 0% -> 0% of each run, Pallas kernels for 14% -> 13%
where the time goes in v8:
time: 209 us
  blocking collectives  105 us (50%)
  Pallas kernels  64.2 us (31%)
  starting transfers between devices  20.6 us (10%)
  waiting for transfers between devices  19.3 us (9%)
    all_to_all x1, blocking collectives, on_device(): lax.all_to_all(outgoing, BOTH, split_axis=0, concat_axis=0, tiled=True)  105 us
    pallas_call x7, Pallas kernels, steer(): pl.pallas_call(functools.partial(steer_kernel, along=along, whole=[whole...  43.8 us
    ppermute x4, waiting for transfers between devices, swap_ends(): high = lax.ppermute(head, axis, [(i + 1, i) for i in range(count - 1)])  19.3 us
    pallas_call x1, Pallas kernels, stack_bins(): pl.pallas_call(functools.partial(bin_kernel, capacity=capacity, block_row...  14.1 us
    ppermute x4, starting transfers between devices, swap_ends(): low = lax.ppermute(tail, axis, [(i, i + 1) for i in range(count - 1)])  14 us
    ppermute x4, starting transfers between devices, swap_ends(): high = lax.ppermute(head, axis, [(i + 1, i) for i in range(count - 1)])  6.61 us
    pallas_call x1, Pallas kernels, pack(): pl.pallas_call(functools.partial(pack_kernel, capacity=capacity), in_spec...  6.37 us
  transfers between devices with their start and end apart: 8, of which 2 were waited for; matrix products, arithmetic and copies ran while one was open for 0% of the time, Pallas kernels for 13%

profile of v8, /device:TPU:1, one launch (start us, length us, event | category | flops | bytes accessed | tf_op | source)
XLA Modules:
  0.0 209.3 jit_solution(16138614321395330948)
XLA Ops:
  0.0 6.4 %shard_map.64 = f32[32,264,128]{2,1,0:T(8,128)} custom-call(s32[128]{0:T(128)} %bitcast.11, s32[4,128]{1,0:T(4,128)} %bitcast.10, f32[128,4,1024]{2,1,0:T(4,128)} %traces_ref.1), custom_call_target="tpu_custom_call" | custom-call | tf_op jit(solution)/shard_map/pallas_call | solution.py:115
  6.4 104.8 %all_to_all.5.blocks_ref = f32[32,264,128]{2,1,0:T(8,128)S(1)} all-to-all(f32[32,264,128]{2,1,0:T(8,128)} %shard_map.64), channel_id=1, replica_groups=mesh['inline'=8,'crosslin'=4] {'inline','crosslin'}, dimensions={0} | all-to-all | bytes 8650752 | tf_op jit(solution)/shard_map/all_to_all | solution.py:527
  111.1 0.0 copy-start.1
  111.1 14.1 %shard_map.65 = (f32[1024,8,128]{2,1,0:T(8,128)S(1)}, f32[224,8,128]{2,1,0:T(8,128)S(1)}, f32[224,8,128]{2,1,0:T(8,128)S(1)}) custom-call(f32[32,264,128]{2,1,0:T(8,128)S(1)} %all_to_all.5.blocks_ref), custom_call_target="tpu_custom_call" | custom-call | tf_op jit(solution)/shard_map/pallas_call | solution.py:199
  125.2 3.3 %collective-permute-start = (f32[7,32,8,128]{3,2,1,0:T(8,128)S(1)}, f32[7,32,8,128]{3,2,1,0:T(8,128)S(1)}, u32[]{:S(2)}, u32[]{:S(2)}) collective-permute-start(f32[7,32,8,128]{3,2,1,0:T(8,128)S(1)} %bitcast.9), channel_id=1, source_target_pairs={{0,4},{4,8},{8,12},{12,16},{16,20},{20,24},{24,28},{1,5},{5,9},{9,... | collective-permute-start | bytes 2752520 | tf_op jit(solution)/shard_map/ppermute | solution.py:445
  128.5 1.9 collective-permute-start.1
  130.5 0.0 copy-done.1
  130.5 6.0 %shard_map.66 = (f32[16,32,8,128]{3,2,1,0:T(8,128)S(1)}, f32[16,7,8,128]{3,2,1,0:T(8,128)S(1)}, f32[16,7,8,128]{3,2,1,0:T(8,128)S(1)}) custom-call(s32[32,32]{1,0:T(8,128)S(1)} %copy-done.1, f32[32,32,8,128]{3,2,1,0:T(8,128)S(1)} %bitcast.5), custom_call_target="tpu_custom_call" | custom-call | flops 1258291200 | bytes 4194304 | tf_op jit(solution)/shard_map/pallas_call | solution.py:423
  136.5 1.9 collective-permute-start.4
  138.4 1.3 collective-permute-start.5
  139.7 0.0 collective-permute-done.refs_0_
  139.8 10.7 %collective-permute-done.1.refs_2_ = f32[7,32,8,128]{3,2,1,0:T(8,128)S(1)} collective-permute-done((f32[7,32,8,128]{3,2,1,0:T(8,128)S(1)}, f32[7,32,8,128]{3,2,1,0:T(8,128)S(1)}, u32[]{:S(2)}, u32[]{:S(2)}) %collective-permute-start.1) | collective-permute-done | bytes 917536 | tf_op jit(solution)/shard_map/ppermute | solution.py:446
  150.4 3.4 %shard_map.67 = (f32[16,16,8,128]{3,2,1,0:T(8,128)S(1)}, f32[16,7,8,128]{3,2,1,0:T(8,128)S(1)}, f32[16,7,8,128]{3,2,1,0:T(8,128)S(1)}) custom-call(s32[32,32]{1,0:T(8,128)S(1)} %copy-done.1, f32[7,32,8,128]{3,2,1,0:T(8,128)S(1)} %collective-permute-done.refs_0_, f32[32,32,8,128]{3,2,1,0:T(8,128)S(1)} %bitcast.6, ...), custom_call_target="tpu_custom_call" | custom-call | flops 629145600 | bytes 2097152 | tf_op jit(solution)/shard_map/pallas_call | solution.py:423
  153.9 0.0 copy-start.2
  153.9 2.5 %collective-permute-start.2 = (f32[16,7,8,128]{3,2,1,0:T(8,128)S(1)}, f32[16,7,8,128]{3,2,1,0:T(8,128)S(1)}, u32[]{:S(2)}, u32[]{:S(2)}) collective-permute-start(f32[16,7,8,128]{3,2,1,0:T(8,128)S(1)} %get-tuple-element.21), channel_id=1, source_target_pairs={{0,1},{1,2},{2,3},{4,5},{5,6},{6,7},{8,9},{9,10},{10,11},{12,13},{... | collective-permute-start | bytes 1376264 | tf_op jit(solution)/shard_map/ppermute | solution.py:445
  156.3 1.3 collective-permute-start.3
  157.6 3.3 %shard_map.68.refs_3_.refs_2_ = f32[16,16,8,128]{3,2,1,0:T(8,128)S(1)} custom-call(s32[32,32]{1,0:T(8,128)S(1)} %copy-done.1, f32[7,32,8,128]{3,2,1,0:T(8,128)S(1)} %collective-permute-done.refs_0_, f32[32,32,8,128]{3,2,1,0:T(8,128)S(1)} %bitcast.7, f32[7,32,8,128]{3,2,1,0:T(8,128)S(1)} %collective-permute-done.1.refs_2_, ...), custom_call_target="tpu_custom_call" | custom-call | flops 629145600 | bytes 2097152 | tf_op jit(solution)/shard_map/pallas_call | solution.py:423
  160.9 0.0 copy-start
  160.9 0.0 collective-permute-done.4.refs_0_
  161.0 0.0 collective-permute-done.5.refs_2_
  161.0 0.0 copy-done.2
  161.0 5.9 %shard_map.69.refs_4_.refs_1_.refs_2_ = f32[16,32,8,128]{3,2,1,0:T(8,128)S(1)} custom-call(s32[32,32]{1,0:T(8,128)S(1)} %copy-done.2, f32[16,7,8,128]{3,2,1,0:T(8,128)S(1)} %collective-permute-done.4.refs_0_, f32[16,32,8,128]{3,2,1,0:T(8,128)S(1)} %get-tuple-element.20.refs_3_.refs_1_, f32[16,7,8,128]{3,2,1,0:T(8,128)S(1)} %collective-permute-done.5.refs_2_, ...), custom_call_target="tpu_custom_call" | custom-call | flops 1258291200 | bytes 4194304 | tf_op jit(solution)/shard_map/pallas_call | solution.py:423
  166.9 0.0 collective-permute-done.2.refs_0_
  166.9 0.0 collective-permute-done.3.refs_3_
  167.0 6.4 %shard_map.70 = (f32[16,32,8,128]{3,2,1,0:T(8,128)S(1)}, f32[7,32,8,128]{3,2,1,0:T(8,128)S(1)}, f32[7,32,8,128]{3,2,1,0:T(8,128)S(1)}) custom-call(s32[32,32]{1,0:T(8,128)S(1)} %copy-done.2, f32[16,7,8,128]{3,2,1,0:T(8,128)S(1)} %collective-permute-done.2.refs_0_, f32[16,16,8,128]{3,2,1,0:T(8,128)S(1)} %get-tuple-element.22.refs_3_.refs_1_, ...), custom_call_target="tpu_custom_call" | custom-call | flops 1258291200 | bytes 4194304 | tf_op jit(solution)/shard_map/pallas_call | solution.py:423
  173.3 6.3 %collective-permute-start.6 = (f32[7,32,8,128]{3,2,1,0:T(8,128)S(1)}, f32[7,32,8,128]{3,2,1,0:T(8,128)S(1)}, u32[]{:S(2)}, u32[]{:S(2)}) collective-permute-start(f32[7,32,8,128]{3,2,1,0:T(8,128)S(1)} %get-tuple-element.26), channel_id=1, source_target_pairs={{0,4},{4,8},{8,12},{12,16},{16,20},{20,24},{24,28},{1,5},{5,9},{9,... | collective-permute-start | bytes 2752520 | tf_op jit(solution)/shard_map/ppermute | solution.py:445
  179.7 2.1 %collective-permute-start.7 = (f32[7,32,8,128]{3,2,1,0:T(8,128)S(1)}, f32[7,32,8,128]{3,2,1,0:T(8,128)S(1)}, u32[]{:S(2)}, u32[]{:S(2)}) collective-permute-start(f32[7,32,8,128]{3,2,1,0:T(8,128)S(1)} %get-tuple-element.28), channel_id=1, source_target_pairs={{4,0},{8,4},{12,8},{16,12},{20,16},{24,20},{28,24},{5,1},{9,5},{13... | collective-permute-start | bytes 2752520 | tf_op jit(solution)/shard_map/ppermute | solution.py:446
  181.8 0.0 copy-done
  181.8 9.5 %shard_map.71.refs_5_ = f32[32,32,1024]{2,1,0:T(8,128)} custom-call(s32[32,32]{1,0:T(8,128)S(1)} %copy-done.1, f32[16,32,8,128]{3,2,1,0:T(8,128)S(1)} %get-tuple-element.27.refs_0_.refs_1_, f32[16,32,8,128]{3,2,1,0:T(8,128)S(1)} %shard_map.69.refs_4_.refs_1_.refs_2_, bf16[1024,1024]{1,0:T(8,128)(2,1)S(1)} %copy-done), custom_call_target="tpu_custom_call" | custom-call | flops 1258291200 | bytes 4194304 | tf_op jit(solution)/shard_map/pallas_call | solution.py:423
  191.2 0.0 collective-permute-done.6.refs_0_
  191.3 8.6 %collective-permute-done.7.refs_3_ = f32[7,32,8,128]{3,2,1,0:T(8,128)S(1)} collective-permute-done((f32[7,32,8,128]{3,2,1,0:T(8,128)S(1)}, f32[7,32,8,128]{3,2,1,0:T(8,128)S(1)}, u32[]{:S(2)}, u32[]{:S(2)}) %collective-permute-start.7) | collective-permute-done | bytes 917536 | tf_op jit(solution)/shard_map/ppermute | solution.py:446
  199.9 9.2 %shard_map.72 = f32[32,32,1024]{2,1,0:T(8,128)} custom-call(s32[32,32]{1,0:T(8,128)S(1)} %copy-done.1, f32[7,32,8,128]{3,2,1,0:T(8,128)S(1)} %collective-permute-done.6.refs_0_, f32[16,32,8,128]{3,2,1,0:T(8,128)S(1)} %get-tuple-element.27.refs_0_.refs_1_, f32[16,32,8,128]{3,2,1,0:T(8,128)S(1)} %shard_map.69.refs_4_.refs_1_.refs_2_, ...), custom_call_target="tpu_custom_call", output_to_operand_aliasing={{}: (6, {})} | custom-call | flops 1258291200 | bytes 4194304 | tf_op jit(solution)/shard_map/pallas_call | solution.py:423
Async XLA Ops:
  111.1 19.3 %copy-start.1 = (s32[32,32]{1,0:T(8,128)S(1)}, s32[32,32]{1,0:T(8,128)}, u32[]{:S(2)}) copy-start(s32[32,32]{1,0:T(8,128)} %dip_ref.13) | copy-start | bytes 12292
  125.2 14.5 %collective-permute-start = (f32[7,32,8,128]{3,2,1,0:T(8,128)S(1)}, f32[7,32,8,128]{3,2,1,0:T(8,128)S(1)}, u32[]{:S(2)}, u32[]{:S(2)}) collective-permute-start(f32[7,32,8,128]{3,2,1,0:T(8,128)S(1)} %bitcast.9), channel_id=1, source_target_pairs={{0,4},{4,8},{8,12},{12,16},{16,20},{20,24},{24,28},{1,5},{5,9},{9,... | collective-permute-start | bytes 2752520 | tf_op jit(solution)/shard_map/ppermute | solution.py:445
  128.5 21.9 %collective-permute-start.1 = (f32[7,32,8,128]{3,2,1,0:T(8,128)S(1)}, f32[7,32,8,128]{3,2,1,0:T(8,128)S(1)}, u32[]{:S(2)}, u32[]{:S(2)}) collective-permute-start(f32[7,32,8,128]{3,2,1,0:T(8,128)S(1)} %bitcast.8), channel_id=1, source_target_pairs={{4,0},{8,4},{12,8},{16,12},{20,16},{24,20},{28,24},{5,1},{9,5},{13... | collective-permute-start | bytes 2752520 | tf_op jit(solution)/shard_map/ppermute | solution.py:446
  136.5 24.4 %collective-permute-start.4 = (f32[16,7,8,128]{3,2,1,0:T(8,128)S(1)}, f32[16,7,8,128]{3,2,1,0:T(8,128)S(1)}, u32[]{:S(2)}, u32[]{:S(2)}) collective-permute-start(f32[16,7,8,128]{3,2,1,0:T(8,128)S(1)} %get-tuple-element.24), channel_id=1, source_target_pairs={{0,1},{1,2},{2,3},{4,5},{5,6},{6,7},{8,9},{9,10},{10,11},{12,13},{... | collective-permute-start | bytes 1376264 | tf_op jit(solution)/shard_map/ppermute | solution.py:445
  138.4 22.5 %collective-permute-start.5 = (f32[16,7,8,128]{3,2,1,0:T(8,128)S(1)}, f32[16,7,8,128]{3,2,1,0:T(8,128)S(1)}, u32[]{:S(2)}, u32[]{:S(2)}) collective-permute-start(f32[16,7,8,128]{3,2,1,0:T(8,128)S(1)} %get-tuple-element.25), channel_id=1, source_target_pairs={{1,0},{2,1},{3,2},{5,4},{6,5},{7,6},{9,8},{10,9},{11,10},{13,12},{... | collective-permute-start | bytes 1376264 | tf_op jit(solution)/shard_map/ppermute | solution.py:446
  153.9 7.1 %copy-start.2 = (s32[32,32]{1,0:T(8,128)S(1)}, s32[32,32]{1,0:T(8,128)}, u32[]{:S(2)}) copy-start(s32[32,32]{1,0:T(8,128)} %dip_ref.11) | copy-start | bytes 12292
  153.9 13.1 %collective-permute-start.2 = (f32[16,7,8,128]{3,2,1,0:T(8,128)S(1)}, f32[16,7,8,128]{3,2,1,0:T(8,128)S(1)}, u32[]{:S(2)}, u32[]{:S(2)}) collective-permute-start(f32[16,7,8,128]{3,2,1,0:T(8,128)S(1)} %get-tuple-element.21), channel_id=1, source_target_pairs={{0,1},{1,2},{2,3},{4,5},{5,6},{6,7},{8,9},{9,10},{10,11},{12,13},{... | collective-permute-start | bytes 1376264 | tf_op jit(solution)/shard_map/ppermute | solution.py:445
  156.3 10.6 %collective-permute-start.3 = (f32[16,7,8,128]{3,2,1,0:T(8,128)S(1)}, f32[16,7,8,128]{3,2,1,0:T(8,128)S(1)}, u32[]{:S(2)}, u32[]{:S(2)}) collective-permute-start(f32[16,7,8,128]{3,2,1,0:T(8,128)S(1)} %get-tuple-element.23), channel_id=1, source_target_pairs={{1,0},{2,1},{3,2},{5,4},{6,5},{7,6},{9,8},{10,9},{11,10},{13,12},{... | collective-permute-start | bytes 1376264 | tf_op jit(solution)/shard_map/ppermute | solution.py:446
  160.9 20.8 %copy-start = (bf16[1024,1024]{1,0:T(8,128)(2,1)S(1)}, bf16[1024,1024]{1,0:T(8,128)(2,1)}, u32[]{:S(2)}) copy-start(bf16[1024,1024]{1,0:T(8,128)(2,1)} %constant.2.clone.refs_2_.refs_4_) | copy-start | bytes 6291460
  173.3 17.9 %collective-permute-start.6 = (f32[7,32,8,128]{3,2,1,0:T(8,128)S(1)}, f32[7,32,8,128]{3,2,1,0:T(8,128)S(1)}, u32[]{:S(2)}, u32[]{:S(2)}) collective-permute-start(f32[7,32,8,128]{3,2,1,0:T(8,128)S(1)} %get-tuple-element.26), channel_id=1, source_target_pairs={{0,4},{4,8},{8,12},{12,16},{16,20},{20,24},{24,28},{1,5},{5,9},{9,... | collective-permute-start | bytes 2752520 | tf_op jit(solution)/shard_map/ppermute | solution.py:445
  179.7 20.2 %collective-permute-start.7 = (f32[7,32,8,128]{3,2,1,0:T(8,128)S(1)}, f32[7,32,8,128]{3,2,1,0:T(8,128)S(1)}, u32[]{:S(2)}, u32[]{:S(2)}) collective-permute-start(f32[7,32,8,128]{3,2,1,0:T(8,128)S(1)} %get-tuple-element.28), channel_id=1, source_target_pairs={{4,0},{8,4},{12,8},{16,12},{20,16},{24,20},{28,24},{5,1},{9,5},{13... | collective-permute-start | bytes 2752520 | tf_op jit(solution)/shard_map/ppermute | solution.py:446

commit v9 on v8

--- a/solution.py
+++ b/solution.py
@@ -14,6 +14,7 @@
 PHASES = 8
 PAIR = 2 * PHASES
 WIDE = 2 * LANES
+WINDOW = 16
 BORDER = 8
 REACH = -(-HALF * DMAX // PHASES)
 REACHES = range(-REACH, REACH + 1)
@@ -84,8 +85,9 @@
         ).start()
         row = jnp.zeros((1, LANES), I32)
         for j in range(block_rows):
-            row = jnp.where(lane == j, bins_ref[j, block], row)
-        listed_ref[device, pl.ds(rank, 1), :] = row.astype(F32)
+            row = jnp.where(lane == rank * block_rows + j, bins_ref[j, block], row)
+        own = (lane >= rank * block_rows) & (lane < (rank + 1) * block_rows)
+        listed_ref[device, 0:1, :] = jnp.where(own, row.astype(F32), listed_ref[device, 0:1, :])
         return 0
 
     for group in range(groups):
@@ -110,7 +112,7 @@
 def pack(traces, target, bins, devices, capacity):
     held, block_rows, samples = traces.shape
     span = block_rows * PHASES
-    room = -(-capacity // 8) * 8
+    room = 8
     groups = 2
     return pl.pallas_call(
         functools.partial(pack_kernel, capacity=capacity),
@@ -131,14 +133,21 @@
     )(target, bins, traces)
 
 
-def bin_kernel(blocks_ref, out_ref, head_ref, tail_ref, even_ref, odd_ref, listed_ref, places_ref, scale_ref, scales_ref, sems, *, capacity, block_rows, edge):
-    devices, rows, _ = blocks_ref.shape
-    room = listed_ref.shape[1]
-    bin_total = out_ref.shape[0]
+def bin_kernel(blocks_ref, out_ref, *refs, capacity, block_rows, edges):
+    edge_refs, refs = refs[: len(edges)], refs[len(edges) :]
+    even_ref, odd_ref, listed_ref, places_ref, scale_ref, scales_ref, sem, sems = refs
+    devices = blocks_ref.shape[0]
+    tile_rows, tile_cols = out_ref.shape[:2]
+    bin_total = tile_rows * tile_cols
     unroll = 8
-    listed = blocks_ref[:, rows - room :, :]
-    listed_ref[...] = jnp.where(listed < 0, float(bin_total), listed).astype(I32)
-    copy = pltpu.make_async_copy(listed_ref, places_ref, sems.at[0])
+
+    def read_list(sender, _):
+        listed = blocks_ref[sender, capacity * block_rows * PHASES : capacity * block_rows * PHASES + 1, :]
+        listed_ref[pl.ds(sender, 1), :] = jnp.where(listed < 0, float(bin_total), listed).astype(I32)
+        return 0
+
+    lax.fori_loop(0, devices, read_list, 0, unroll=8)
+    copy = pltpu.make_async_copy(listed_ref, places_ref, sem)
     copy.start()
     nothing = jnp.zeros((PHASES, LANES), F32)
 
@@ -160,7 +169,7 @@
         for rank in range(capacity):
             for j in range(block_rows):
                 total_ref = odd_ref if j % 2 else even_ref
-                place = places_ref[sender, rank, j]
+                place = places_ref[sender, rank * block_rows + j]
                 row = (rank * block_rows + j) * PHASES
                 total_ref[place] += blocks_ref[sender, row : row + PHASES, :]
                 folds[j % 2] = folds[j % 2] + jnp.where(numbers == place, 1.0, 0.0)
@@ -169,55 +178,62 @@
     empty = jnp.zeros((count_rows, LANES), F32)
     folds = lax.fori_loop(0, devices, add_sender, (empty, empty))
     scale_ref[...] = 1.0 / jnp.maximum(folds[0] + folds[1], 1.0)
-    copy = pltpu.make_async_copy(scale_ref, scales_ref, sems.at[0])
+    copy = pltpu.make_async_copy(scale_ref, scales_ref, sem)
     copy.start()
     copy.wait()
 
-    def finish(i, _):
-        for j in range(unroll):
-            place = i * unroll + j
+    def finish(row, _):
+        for col in range(tile_cols):
+            place = row * tile_cols + col
             scale = scales_ref[place // LANES, place % LANES]
-            out_ref[place] = (even_ref[place] + odd_ref[place]) * scale
+            out_ref[row, col] = (even_ref[place] + odd_ref[place]) * scale
         return 0
 
-    lax.fori_loop(0, edge // unroll, finish, 0)
-    head_copy = pltpu.make_async_copy(out_ref.at[pl.ds(0, edge)], head_ref, sems.at[1])
-    head_copy.start()
-    lax.fori_loop((bin_total - edge) // unroll, bin_total // unroll, finish, 0)
-    tail_copy = pltpu.make_async_copy(out_ref.at[pl.ds(bin_total - edge, edge)], tail_ref, sems.at[2])
-    tail_copy.start()
-    lax.fori_loop(edge // unroll, (bin_total - edge) // unroll, finish, 0)
-    head_copy.wait()
-    tail_copy.wait()
-
-
-def stack_bins(blocks, tile_rows, tile_cols, capacity, block_rows):
+    lax.fori_loop(0, HALF, finish, 0)
+    lax.fori_loop(tile_rows - HALF, tile_rows, finish, 0)
+    copies = edge_copies(out_ref, edges, edge_refs, sems)
+    for copy in copies:
+        copy.start()
+    lax.fori_loop(HALF, tile_rows - HALF, finish, 0)
+    for copy in copies:
+        copy.wait()
+
+
+def edge_copies(out_ref, edges, edge_refs, sems):
+    copies = []
+    for (_, moves), edge_ref in zip(edges, edge_refs):
+        for source, target in moves:
+            copies.append(pltpu.make_async_copy(out_ref.at[source], edge_ref.at[target], sems.at[len(copies)]))
+    return copies
+
+
+def edge_outputs(edges):
+    shapes = [jax.ShapeDtypeStruct(tuple(shape) + (PHASES, LANES), F32) for shape, _ in edges]
+    moves = sum(len(moves) for _, moves in edges)
+    return shapes, [HBM] * len(edges), pltpu.SemaphoreType.DMA((max(1, moves),))
+
+
+def stack_bins(blocks, tile_rows, tile_cols, capacity, block_rows, edges):
     devices = blocks.shape[0]
     bin_total = tile_rows * tile_cols
-    edge = HALF * tile_cols
-    room = blocks.shape[1] - capacity * block_rows * PHASES
-    stacked, head, tail = pl.pallas_call(
-        functools.partial(bin_kernel, capacity=capacity, block_rows=block_rows, edge=edge),
+    shapes, specs, sems = edge_outputs(edges)
+    return pl.pallas_call(
+        functools.partial(bin_kernel, capacity=capacity, block_rows=block_rows, edges=edges),
         in_specs=[VMEM],
-        out_specs=[VMEM, HBM, HBM],
-        out_shape=[
-            jax.ShapeDtypeStruct((bin_total, PHASES, LANES), F32),
-            jax.ShapeDtypeStruct((edge, PHASES, LANES), F32),
-            jax.ShapeDtypeStruct((edge, PHASES, LANES), F32),
-        ],
+        out_specs=[VMEM] + specs,
+        out_shape=[jax.ShapeDtypeStruct((tile_rows, tile_cols, PHASES, LANES), F32)] + shapes,
         scratch_shapes=[
             pltpu.VMEM((bin_total + 8, PHASES, LANES), F32),
             pltpu.VMEM((bin_total + 8, PHASES, LANES), F32),
-            pltpu.VMEM((devices, room, LANES), I32),
-            pltpu.SMEM((devices, room, LANES), I32),
+            pltpu.VMEM((devices, LANES), I32),
+            pltpu.SMEM((devices, LANES), I32),
             pltpu.VMEM((bin_total // LANES, LANES), F32),
             pltpu.SMEM((bin_total // LANES, LANES), F32),
-            pltpu.SemaphoreType.DMA((3,)),
+            pltpu.SemaphoreType.DMA,
+            sems,
         ],
         compiler_params=pltpu.CompilerParams(vmem_limit_bytes=14 * MIB),
     )(blocks)
-    shape = (tile_cols, PHASES, LANES)
-    return stacked.reshape((tile_rows,) + shape), head.reshape((HALF,) + shape), tail.reshape((HALF,) + shape)
 
 
 def fill_weights(spots_ref, weights_ref):
@@ -282,7 +298,7 @@
             put(first + 2 * pair + member, total)
 
 
-def steer_kernel(dip_ref, *refs, along, whole, lines, line_of, windows, local_of, edges, final, chained, pieces_count, abreast):
+def steer_kernel(dip_ref, *refs, along, whole, lines, line_of, windows, local_of, edges, final, batches, filled, chained, pieces_count, abreast):
     pieces, refs = refs[:pieces_count], refs[pieces_count:]
     if final:
         table_ref, refs = refs[0], refs[1:]
@@ -295,9 +311,9 @@
         staged_ref, result_ref = refs[abreast * len(windows) :]
     fill_weights(spots_ref, weights_ref)
     for i, halves_ref in enumerate(halves):
-        filled = len(windows[i % len(windows)][2]) * PHASES
-        if filled < WIDE:
-            halves_ref[filled:, :] = jnp.zeros((WIDE - filled, WIDE), BF16)
+        used = len(windows[i % len(windows)][2]) * PHASES
+        if used < WIDE:
+            halves_ref[used:, :] = jnp.zeros((WIDE - used, WIDE), BF16)
 
     def at(place, line):
         return (place, line) if along == 0 else (line, place)
@@ -333,11 +349,14 @@
         return 0
 
     if not final:
+        if filled is not None:
+            index, target = filled
+            fill = pltpu.make_async_copy(pieces[index], out_ref.at[target], sems.at[sems.shape[0] - 1])
+            fill.start()
         lax.fori_loop(0, lines // abreast, some_lines, 0)
-        copies = [
-            pltpu.make_async_copy(out_ref.at[pick], edge_ref, sems.at[i])
-            for i, (pick, edge_ref) in enumerate(zip(edges, edge_refs))
-        ]
+        if filled is not None:
+            fill.wait()
+        copies = edge_copies(out_ref, edges, edge_refs, sems)
         for copy in copies:
             copy.start()
         for copy in copies:
@@ -349,11 +368,12 @@
     def copies_of(batch, slot):
         return [
             pltpu.make_async_copy(
-                result_ref.at[slot, pl.ds(local_of(first), count)],
-                out_ref.at[pl.ds(first, count), pl.ds(pl.multiple_of(batch * final, 8), final), :],
-                sems.at[slot * len(windows) + i],
+                result_ref.at[slot, pl.ds(local_of(first), count), pl.ds(local, wide), :],
+                out_ref.at[pl.ds(first, count), pl.ds(full, wide), :],
+                sems.at[(slot * len(windows) + i) * len(batches[batch]) + j],
             )
             for i, (first, count, _) in enumerate(windows)
+            for j, (local, full, wide) in enumerate(batches[batch])
         ]
 
     for batch in range(lines // final):
@@ -383,11 +403,14 @@
             copy.wait()
 
 
-def steer(dip, pieces, along, lines, line_of, windows, local_of, edges=(), table=None, before=None, after=None):
-    abreast = 2 if along else 4
+def steer(
+    dip, pieces, along, lines, line_of, windows, local_of, edges=(), table=None, batches=None, before=None, after=None, filled=None
+):
     samples = PHASES * LANES
     outputs = sum(count for _, count, _ in windows)
     final = 16 if table is not None else 0
+    abreast = 4 * WINDOW // outputs
+    shapes, specs, sems = edge_outputs(edges)
     operands = [dip] + [array for array, _ in pieces]
     in_specs = [SMEM] + [VMEM] * len(pieces)
     aliases = {}
@@ -398,22 +421,22 @@
             aliases = {len(operands): 0}
             operands.append(before)
             in_specs.append(HBM)
-        out_shape = [jax.ShapeDtypeStruct((dip.shape[0], lines, samples), F32)]
+        out_shape = [jax.ShapeDtypeStruct(dip.shape + (samples,), F32)]
+        sems = pltpu.SemaphoreType.DMA((2 * len(windows) * len(batches[0]),))
         out_specs = [HBM]
     else:
-        shape = (outputs, lines) if along == 0 else (lines, outputs)
-        out_shape = [jax.ShapeDtypeStruct(shape + (PHASES, LANES), F32)]
-        out_specs = [VMEM]
-        for pick in edges:
-            size = [len(range(*s.indices(n))) for s, n in zip(pick, shape)]
-            out_shape.append(jax.ShapeDtypeStruct(tuple(size) + (PHASES, LANES), F32))
-            out_specs.append(HBM)
+        reach = outputs if filled is None else dip.shape[along]
+        shape = (reach, lines) if along == 0 else (lines, reach)
+        out_shape = [jax.ShapeDtypeStruct(shape + (PHASES, LANES), F32)] + shapes
+        out_specs = [VMEM] + specs
+        if filled is not None:
+            sems = pltpu.SemaphoreType.DMA((sems.shape[0] + 1,))
     if after is not None:
         operands.append(after)
         in_specs.append(ANY)
     most = max(count for _, count, _ in windows)
     constant = pltpu.VMEM((most * PAIR, LANES), BF16)
-    scratch = [constant, constant, pltpu.SemaphoreType.DMA((2 * len(windows) if final else max(1, len(edges)),))]
+    scratch = [constant, constant, sems]
     scratch += [pltpu.VMEM((WIDE, WIDE), BF16)] * (abreast * len(windows))
     if final:
         scratch += [
@@ -424,7 +447,7 @@
         functools.partial(
             steer_kernel,
             along=along, whole=[whole for _, whole in pieces], lines=lines, line_of=line_of, windows=windows,
-            local_of=local_of, edges=edges, final=final, chained=len(operands) - len(pieces) - 1 - bool(final), pieces_count=len(pieces), abreast=abreast,
+            local_of=local_of, edges=edges, final=final, batches=batches, filled=filled, chained=len(operands) - len(pieces) - 1 - bool(final), pieces_count=len(pieces), abreast=abreast,
         ),
         in_specs=in_specs,
         out_specs=out_specs,
@@ -451,9 +474,14 @@
     return [(index, first + i) for i in range(count)]
 
 
-def smooth(stacked, head, tail, along_rows, along_cols, table):
-    rows, cols = stacked.shape[:2]
+def rows_of(first, count):
+    return slice(first, first + count)
+
+
+def smooth(arrived, capacity, block_rows, dip_inline, dip_cross, table):
+    rows, cols = dip_inline.shape
     mid_rows, mid_cols = rows - 2 * BORDER, cols - 2 * BORDER
+    both = 2 * BORDER
     same = lambda line: line
     inner = lambda line: line + BORDER
     outer_col = lambda line: line + jnp.where(line < BORDER, 0, mid_cols)
@@ -461,60 +489,90 @@
     mid_place = lambda place: place - BORDER
     outer_place = lambda place: place if place < BORDER else place - mid_rows
     every = slice(None)
-    lead, last = slice(0, HALF), slice(2 * BORDER - HALF, 2 * BORDER)
-
-    def mid_windows(places):
-        return [(BORDER + i, 16, places[i : i + 16 + 2 * HALF]) for i in range(0, mid_rows, 16)]
-
-    low, high = swap_ends(head, tail, "inline")
-    middle, head_mid, tail_mid = steer(
-        along_rows, [(stacked, True)], 0, cols, same,
-        mid_windows(span_of(0, BORDER - HALF, mid_rows + 2 * HALF)), mid_place,
-        edges=[(every, lead), (every, slice(cols - HALF, cols))],
-    )
-    low_mid, high_mid = swap_ends(head_mid, tail_mid, "crosslin")
-    pieces = [(low, True), (stacked, True), (high, True)]
+    lead, last = rows_of(0, HALF), rows_of(both - HALF, HALF)
+    left, right, middle_cols = rows_of(0, BORDER), rows_of(cols - BORDER, BORDER), rows_of(BORDER, mid_cols)
+
+    def outer_edge(pick):
+        return ((HALF, both), [((pick, left), (every, rows_of(0, BORDER))), ((pick, right), (every, rows_of(BORDER, BORDER)))])
+
+    def whole_edge(shape, pick):
+        return (shape, [(pick, (every, every))])
+
+    def mid_windows(places, extent):
+        return [(i, WINDOW, places[i - BORDER : i - BORDER + WINDOW + 2 * HALF]) for i in range(BORDER, extent - BORDER, WINDOW)]
+
+    stacked, head_out, tail_out, head_mid, tail_mid = stack_bins(
+        arrived, rows, cols, capacity, block_rows,
+        [
+            outer_edge(rows_of(0, HALF)),
+            outer_edge(rows_of(rows - HALF, HALF)),
+            whole_edge((HALF, mid_cols), (rows_of(0, HALF), middle_cols)),
+            whole_edge((HALF, mid_cols), (rows_of(rows - HALF, HALF), middle_cols)),
+        ],
+    )
+    low_out, high_out = swap_ends(head_out, tail_out, "inline")
+    low_mid, high_mid = swap_ends(head_mid, tail_mid, "inline")
+
+    middle, head, tail = steer(
+        dip_inline, [(stacked, True)], 0, cols, same,
+        mid_windows(span_of(0, BORDER - HALF, mid_rows + 2 * HALF), rows), mid_place,
+        edges=[whole_edge((mid_rows, HALF), (every, lead)), whole_edge((mid_rows, HALF), (every, rows_of(cols - HALF, HALF)))],
+    )
+    left_mid, right_mid = swap_ends(head, tail, "crosslin")
     windows = [
         (0, BORDER, span_of(0, 0, HALF) + span_of(1, 0, BORDER + HALF)),
         (rows - BORDER, BORDER, span_of(1, rows - BORDER - HALF, BORDER + HALF) + span_of(2, 0, HALF)),
     ]
-    corners, head_out, tail_out = steer(
-        along_rows, pieces, 0, 2 * BORDER, outer_col, windows, outer_place, edges=[(every, lead), (every, last)],
-        after=middle,
-    )
-    low_out, high_out = swap_ends(head_out, tail_out, "crosslin")
-    (flanks,) = steer(along_rows, pieces, 0, mid_cols, inner, windows, outer_place, after=corners)
-
-    def cross_windows(places):
-        return [(i, 16, places[i : i + 16 + 2 * HALF]) for i in range(0, cols, 16)]
-
+    corners, head, tail = steer(
+        dip_inline, [(low_out, False), (stacked, True), (high_out, False)], 0, both, outer_col, windows, outer_place,
+        edges=[whole_edge((both, HALF), (every, lead)), whole_edge((both, HALF), (every, last))], after=middle,
+    )
+    left_out, right_out = swap_ends(head, tail, "crosslin")
+    (flanks,) = steer(
+        dip_inline, [(low_mid, False), (stacked, True), (high_mid, False)], 0, mid_cols, inner, windows, outer_place,
+        after=corners,
+    )
+
+    places = span_of(0, BORDER - HALF, HALF) + span_of(1, 0, mid_cols) + span_of(0, BORDER, HALF)
+    second_mid, head, tail = steer(
+        dip_cross, [(corners, False), (flanks, False)], 1, both, outer_row, mid_windows(places, cols), mid_place,
+        edges=[whole_edge((HALF, mid_cols), (lead, every)), whole_edge((HALF, mid_cols), (last, every))],
+    )
+    low_mid, high_mid = swap_ends(head, tail, "inline")
     places = span_of(0, 0, HALF) + span_of(1, 0, cols) + span_of(2, 0, HALF)
     (middle_second,) = steer(
-        along_cols, [(low_mid, False), (middle, False), (high_mid, False)], 1, mid_rows, inner,
-        cross_windows(places), same, after=flanks,
-    )
-    places = (
-        span_of(0, 0, HALF) + span_of(1, 0, BORDER) + span_of(2, 0, mid_cols) + span_of(1, BORDER, BORDER) + span_of(3, 0, HALF)
-    )
+        dip_cross, [(left_mid, False), (middle, False), (right_mid, False)], 1, mid_rows, inner,
+        [(i, WINDOW, places[i : i + WINDOW + 2 * HALF]) for i in range(0, cols, WINDOW)], same, after=second_mid,
+    )
+    windows = [
+        (0, BORDER, span_of(0, 0, HALF) + span_of(1, 0, BORDER) + span_of(2, 0, HALF)),
+        (cols - BORDER, BORDER, span_of(2, mid_cols - HALF, HALF) + span_of(1, BORDER, BORDER) + span_of(3, 0, HALF)),
+    ]
     border_second, head, tail = steer(
-        along_cols, [(low_out, False), (corners, False), (flanks, False), (high_out, False)], 1, 2 * BORDER,
-        outer_row, cross_windows(places), same, edges=[(lead, every), (last, every)], after=middle_second,
-    )
-
-    low, high = swap_ends(head, tail, "inline")
+        dip_cross,
+        [(left_out, False), (corners, False), (flanks, False), (right_out, False), (second_mid, False)],
+        1, both, outer_row, windows, same, filled=(4, (every, middle_cols)),
+        edges=[outer_edge(lead), outer_edge(last)], after=middle_second,
+    )
+    low_out, high_out = swap_ends(head, tail, "inline")
+
     places = span_of(0, BORDER - HALF, HALF) + span_of(1, 0, mid_rows) + span_of(0, BORDER, HALF)
     (result,) = steer(
-        along_rows, [(border_second, True), (middle_second, True)], 0, cols, same, mid_windows(places), mid_place,
-        table=table,
+        dip_inline, [(border_second, True), (middle_second, True)], 0, cols, same, mid_windows(places, rows), mid_place,
+        table=table, batches=[[(0, first, WINDOW)] for first in range(0, cols, WINDOW)],
     )
     windows = [
         (0, BORDER, span_of(0, 0, HALF) + span_of(1, 0, BORDER) + span_of(2, 0, HALF)),
         (rows - BORDER, BORDER, span_of(2, mid_rows - HALF, HALF) + span_of(1, BORDER, BORDER) + span_of(3, 0, HALF)),
     ]
-    (result,) = steer(
-        along_rows, [(low, True), (border_second, True), (middle_second, True), (high, True)], 0, cols, same,
-        windows, outer_place, table=table, before=result,
-    )
+    for low, high, lines, line_of, batches in (
+        (low_mid, high_mid, mid_cols, inner, [[(0, first, WINDOW)] for first in range(BORDER, cols - BORDER, WINDOW)]),
+        (low_out, high_out, both, outer_col, [[(0, 0, BORDER), (BORDER, cols - BORDER, BORDER)]]),
+    ):
+        (result,) = steer(
+            dip_inline, [(low, False), (border_second, True), (middle_second, True), (high, False)], 0, lines, line_of,
+            windows, outer_place, table=table, batches=batches, before=result,
+        )
     return result
 
 
@@ -522,12 +580,10 @@
     held, block_rows, samples = traces.shape
     devices = lax.axis_size("inline") * lax.axis_size("crosslin")
     capacity = 2 * held // devices
-    tile_rows, tile_cols = dip_inline.shape
     outgoing = pack(traces, destination.reshape(-1), bin_index.T, devices, capacity)
     arrived = lax.all_to_all(outgoing, BOTH, split_axis=0, concat_axis=0, tiled=True)
-    stacked, head, tail = stack_bins(arrived, tile_rows, tile_cols, capacity, block_rows)
     back = jnp.asarray(interleave_table(samples).T, BF16)
-    return smooth(stacked, head, tail, dip_inline, dip_cross, back)
+    return smooth(arrived, capacity, block_rows, dip_inline, dip_cross, back)
 
 
 def solution(mesh):

time: 209 us -> 205 us (0.981)
  the two profiles are of different devices: /device:TPU:1 before, /device:TPU:11 now
where the time goes in v9:
time: 205 us; the launch traced here: 204 us
  blocking collectives  102 us (50%)
  Pallas kernels  64.7 us (32%)
  starting transfers between devices  37.2 us (18%)
    all_to_all x1, blocking collectives, on_device(): lax.all_to_all(outgoing, BOTH, split_axis=0, concat_axis=0, tiled=True)  102 us
    pallas_call x9, Pallas kernels, steer(): pl.pallas_call(functools.partial(steer_kernel, along=along, whole=[whole...  46.8 us
    ppermute x6, starting transfers between devices, swap_ends(): low = lax.ppermute(tail, axis, [(i, i + 1) for i in range(count - 1)])  24.3 us
    ppermute x6, starting transfers between devices, swap_ends(): high = lax.ppermute(head, axis, [(i + 1, i) for i in range(count - 1)])  12.9 us
    pallas_call x1, Pallas kernels, stack_bins(): pl.pallas_call(functools.partial(bin_kernel, capacity=capacity, block_row...  11.4 us
    pallas_call x1, Pallas kernels, pack(): pl.pallas_call(functools.partial(pack_kernel, capacity=capacity), in_spec...  6.49 us
  transfers between devices with their start and end apart: 12, of which 0 were waited for; matrix products, arithmetic and copies ran while one was open for 0% of the time, Pallas kernels for 20%

profile of v9, /device:TPU:11, one launch (start us, length us, event | category | flops | bytes accessed | tf_op | source)
XLA Modules:
  0.0 204.1 jit_solution(14591179349925932364)
XLA Ops:
  0.0 6.5 %shard_map.64 = f32[32,264,128]{2,1,0:T(8,128)} custom-call(s32[128]{0:T(128)} %bitcast.3, s32[4,128]{1,0:T(4,128)} %bitcast.2, f32[128,4,1024]{2,1,0:T(4,128)} %traces_ref.1), custom_call_target="tpu_custom_call" | custom-call | tf_op jit(solution)/shard_map/pallas_call | solution.py:117
  6.5 101.7 %all_to_all.5.blocks_ref = f32[32,264,128]{2,1,0:T(8,128)S(1)} all-to-all(f32[32,264,128]{2,1,0:T(8,128)} %shard_map.64), channel_id=1, replica_groups=mesh['inline'=8,'crosslin'=4] {'inline','crosslin'}, dimensions={0} | all-to-all | bytes 8650752 | tf_op jit(solution)/shard_map/all_to_all | solution.py:584
  108.2 0.0 copy-start.1
  108.2 11.4 %shard_map.65 = (f32[32,32,8,128]{3,2,1,0:T(8,128)S(1)}, f32[7,16,8,128]{3,2,1,0:T(8,128)S(1)}, f32[7,16,8,128]{3,2,1,0:T(8,128)S(1)}, f32[7,16,8,128]{3,2,1,0:T(8,128)S(1)}, f32[7,16,8,128]{3,2,1,0:T(8,128)S(1)}) custom-call(f32[32,264,128]{2,1,0:T(8,128)S(1)} %all_to_all.5.blocks_ref), custom_call_target="tpu_custom_call" | custom-call | tf_op jit(solution)/shard_map/pallas_call | solution.py:220
  119.6 4.0 %collective-permute-start = (f32[7,16,8,128]{3,2,1,0:T(8,128)S(1)}, f32[7,16,8,128]{3,2,1,0:T(8,128)S(1)}, u32[]{:S(2)}, u32[]{:S(2)}) collective-permute-start(f32[7,16,8,128]{3,2,1,0:T(8,128)S(1)} %get-tuple-element.22), channel_id=1, source_target_pairs={{0,4},{4,8},{8,12},{12,16},{16,20},{20,24},{24,28},{1,5},{5,9},{9,... | collective-permute-start | bytes 1376264 | tf_op jit(solution)/shard_map/ppermute | solution.py:468
  123.6 1.9 collective-permute-start.1
  125.5 4.5 %collective-permute-start.3 = (f32[7,16,8,128]{3,2,1,0:T(8,128)S(1)}, f32[7,16,8,128]{3,2,1,0:T(8,128)S(1)}, u32[]{:S(2)}, u32[]{:S(2)}) collective-permute-start(f32[7,16,8,128]{3,2,1,0:T(8,128)S(1)} %get-tuple-element.28), channel_id=1, source_target_pairs={{0,4},{4,8},{8,12},{12,16},{16,20},{20,24},{24,28},{1,5},{5,9},{9,... | collective-permute-start | bytes 1376264 | tf_op jit(solution)/shard_map/ppermute | solution.py:468
  130.1 1.9 collective-permute-start.4
  132.0 0.0 copy-done.1
  132.0 6.0 %shard_map.66 = (f32[16,32,8,128]{3,2,1,0:T(8,128)S(1)}, f32[16,7,8,128]{3,2,1,0:T(8,128)S(1)}, f32[16,7,8,128]{3,2,1,0:T(8,128)S(1)}) custom-call(s32[32,32]{1,0:T(8,128)S(1)} %copy-done.1, f32[32,32,8,128]{3,2,1,0:T(8,128)S(1)} %get-tuple-element.23.refs_0_.refs_1_), custom_call_target="tpu_custom_call" | custom-call | flops 1258291200 | bytes 4194304 | tf_op jit(solution)/shard_map/pallas_call | solution.py:446
  138.0 2.8 %collective-permute-start.6 = (f32[16,7,8,128]{3,2,1,0:T(8,128)S(1)}, f32[16,7,8,128]{3,2,1,0:T(8,128)S(1)}, u32[]{:S(2)}, u32[]{:S(2)}) collective-permute-start(f32[16,7,8,128]{3,2,1,0:T(8,128)S(1)} %get-tuple-element.32), channel_id=1, source_target_pairs={{0,1},{1,2},{2,3},{4,5},{5,6},{6,7},{8,9},{9,10},{10,11},{12,13},{... | collective-permute-start | bytes 1376264 | tf_op jit(solution)/shard_map/ppermute | solution.py:468
  140.9 0.0 collective-permute-done.refs_0_
  140.9 2.5 %collective-permute-start.7 = (f32[16,7,8,128]{3,2,1,0:T(8,128)S(1)}, f32[16,7,8,128]{3,2,1,0:T(8,128)S(1)}, u32[]{:S(2)}, u32[]{:S(2)}) collective-permute-start(f32[16,7,8,128]{3,2,1,0:T(8,128)S(1)} %get-tuple-element.33), channel_id=1, source_target_pairs={{1,0},{2,1},{3,2},{5,4},{6,5},{7,6},{9,8},{10,9},{11,10},{13,12},{... | collective-permute-start | bytes 1376264 | tf_op jit(solution)/shard_map/ppermute | solution.py:469
  143.4 0.0 collective-permute-done.1.refs_2_
  143.4 3.4 %shard_map.67 = (f32[16,16,8,128]{3,2,1,0:T(8,128)S(1)}, f32[16,7,8,128]{3,2,1,0:T(8,128)S(1)}, f32[16,7,8,128]{3,2,1,0:T(8,128)S(1)}) custom-call(s32[32,32]{1,0:T(8,128)S(1)} %copy-done.1, f32[7,16,8,128]{3,2,1,0:T(8,128)S(1)} %collective-permute-done.refs_0_, f32[32,32,8,128]{3,2,1,0:T(8,128)S(1)} %get-tuple-element.23.refs_0_.refs_1_, ...), custom_call_target="tpu_custom_call" | custom-call | flops 629145600 | bytes 2097152 | tf_op jit(solution)/shard_map/pallas_call | solution.py:446
  146.8 0.0 copy-start.2
  146.8 2.8 %collective-permute-start.2 = (f32[16,7,8,128]{3,2,1,0:T(8,128)S(1)}, f32[16,7,8,128]{3,2,1,0:T(8,128)S(1)}, u32[]{:S(2)}, u32[]{:S(2)}) collective-permute-start(f32[16,7,8,128]{3,2,1,0:T(8,128)S(1)} %get-tuple-element.26), channel_id=1, source_target_pairs={{0,1},{1,2},{2,3},{4,5},{5,6},{6,7},{8,9},{9,10},{10,11},{12,13},{... | collective-permute-start | bytes 1376264 | tf_op jit(solution)/shard_map/ppermute | solution.py:468
  149.6 0.0 collective-permute-done.3.refs_0_
  149.6 2.5 %collective-permute-start.5 = (f32[16,7,8,128]{3,2,1,0:T(8,128)S(1)}, f32[16,7,8,128]{3,2,1,0:T(8,128)S(1)}, u32[]{:S(2)}, u32[]{:S(2)}) collective-permute-start(f32[16,7,8,128]{3,2,1,0:T(8,128)S(1)} %get-tuple-element.30), channel_id=1, source_target_pairs={{1,0},{2,1},{3,2},{5,4},{6,5},{7,6},{9,8},{10,9},{11,10},{13,12},{... | collective-permute-start | bytes 1376264 | tf_op jit(solution)/shard_map/ppermute | solution.py:469
  152.2 0.0 collective-permute-done.4.refs_2_
  152.2 3.3 %shard_map.68.refs_1_.refs_2_ = f32[16,16,8,128]{3,2,1,0:T(8,128)S(1)} custom-call(s32[32,32]{1,0:T(8,128)S(1)} %copy-done.1, f32[7,16,8,128]{3,2,1,0:T(8,128)S(1)} %collective-permute-done.3.refs_0_, f32[32,32,8,128]{3,2,1,0:T(8,128)S(1)} %get-tuple-element.23.refs_0_.refs_1_, f32[7,16,8,128]{3,2,1,0:T(8,128)S(1)} %collective-permute-done.4.refs_2_, ...), custom_call_target="tpu_custom_call" | custom-call | flops 629145600 | bytes 2097152 | tf_op jit(solution)/shard_map/pallas_call | solution.py:446
  155.5 0.0 copy-done.2
  155.5 4.0 %shard_map.69 = (f32[16,16,8,128]{3,2,1,0:T(8,128)S(1)}, f32[7,16,8,128]{3,2,1,0:T(8,128)S(1)}, f32[7,16,8,128]{3,2,1,0:T(8,128)S(1)}) custom-call(s32[32,32]{1,0:T(8,128)S(1)} %copy-done.2, f32[16,16,8,128]{3,2,1,0:T(8,128)S(1)} %get-tuple-element.27.refs_3_.refs_0_.refs_1_, f32[16,16,8,128]{3,2,1,0:T(8,128)S(1)} %shard_map.68.refs_1_.refs_2_), custom_call_target="tpu_custom_call" | custom-call | flops 629145600 | bytes 2097152 | tf_op jit(solution)/shard_map/pallas_call | solution.py:446
  159.5 5.7 %collective-permute-start.10 = (f32[7,16,8,128]{3,2,1,0:T(8,128)S(1)}, f32[7,16,8,128]{3,2,1,0:T(8,128)S(1)}, u32[]{:S(2)}, u32[]{:S(2)}) collective-permute-start(f32[7,16,8,128]{3,2,1,0:T(8,128)S(1)} %get-tuple-element.37), channel_id=1, source_target_pairs={{0,4},{4,8},{8,12},{12,16},{16,20},{20,24},{24,28},{1,5},{5,9},{9,... | collective-permute-start | bytes 1376264 | tf_op jit(solution)/shard_map/ppermute | solution.py:468
  165.1 0.0 collective-permute-done.6.refs_0_
  165.1 1.9 collective-permute-start.11
  167.1 0.0 collective-permute-done.7.refs_2_
  167.1 6.0 %shard_map.70.refs_5_.refs_1_.refs_2_ = f32[16,32,8,128]{3,2,1,0:T(8,128)S(1)} custom-call(s32[32,32]{1,0:T(8,128)S(1)} %copy-done.2, f32[16,7,8,128]{3,2,1,0:T(8,128)S(1)} %collective-permute-done.6.refs_0_, f32[16,32,8,128]{3,2,1,0:T(8,128)S(1)} %get-tuple-element.25.refs_3_.refs_1_, f32[16,7,8,128]{3,2,1,0:T(8,128)S(1)} %collective-permute-done.7.refs_2_, ...), custom_call_target="tpu_custom_call" | custom-call | flops 1258291200 | bytes 4194304 | tf_op jit(solution)/shard_map/pallas_call | solution.py:446
  173.0 0.0 copy-start
  173.1 0.0 collective-permute-done.2.refs_0_
  173.1 0.0 collective-permute-done.5.refs_3_
  173.1 3.6 %shard_map.71 = (f32[16,32,8,128]{3,2,1,0:T(8,128)S(1)}, f32[7,16,8,128]{3,2,1,0:T(8,128)S(1)}, f32[7,16,8,128]{3,2,1,0:T(8,128)S(1)}) custom-call(s32[32,32]{1,0:T(8,128)S(1)} %copy-done.2, f32[16,7,8,128]{3,2,1,0:T(8,128)S(1)} %collective-permute-done.2.refs_0_, f32[16,16,8,128]{3,2,1,0:T(8,128)S(1)} %get-tuple-element.27.refs_3_.refs_0_.refs_1_, ...), custom_call_target="tpu_custom_call" | custom-call | flops 629145600 | bytes 2097152 | tf_op jit(solution)/shard_map/pallas_call | solution.py:446
  176.7 4.5 %collective-permute-start.8 = (f32[7,16,8,128]{3,2,1,0:T(8,128)S(1)}, f32[7,16,8,128]{3,2,1,0:T(8,128)S(1)}, u32[]{:S(2)}, u32[]{:S(2)}) collective-permute-start(f32[7,16,8,128]{3,2,1,0:T(8,128)S(1)} %get-tuple-element.34), channel_id=1, source_target_pairs={{0,4},{4,8},{8,12},{12,16},{16,20},{20,24},{24,28},{1,5},{5,9},{9,... | collective-permute-start | bytes 1376264 | tf_op jit(solution)/shard_map/ppermute | solution.py:468
  181.2 2.1 %collective-permute-start.9 = (f32[7,16,8,128]{3,2,1,0:T(8,128)S(1)}, f32[7,16,8,128]{3,2,1,0:T(8,128)S(1)}, u32[]{:S(2)}, u32[]{:S(2)}) collective-permute-start(f32[7,16,8,128]{3,2,1,0:T(8,128)S(1)} %get-tuple-element.36), channel_id=1, source_target_pairs={{4,0},{8,4},{12,8},{16,12},{20,16},{24,20},{28,24},{5,1},{9,5},{13... | collective-permute-start | bytes 1376264 | tf_op jit(solution)/shard_map/ppermute | solution.py:469
  183.3 0.0 copy-done
  183.3 9.5 %shard_map.72.refs_5_ = f32[32,32,1024]{2,1,0:T(8,128)} custom-call(s32[32,32]{1,0:T(8,128)S(1)} %copy-done.1, f32[16,32,8,128]{3,2,1,0:T(8,128)S(1)} %get-tuple-element.35.refs_0_.refs_1_, f32[16,32,8,128]{3,2,1,0:T(8,128)S(1)} %shard_map.70.refs_5_.refs_1_.refs_2_, bf16[1024,1024]{1,0:T(8,128)(2,1)S(1)} %copy-done), custom_call_target="tpu_custom_call" | custom-call | flops 1258291200 | bytes 4194304 | tf_op jit(solution)/shard_map/pallas_call | solution.py:446
  192.8 0.0 collective-permute-done.10.refs_0_
  192.8 0.0 collective-permute-done.11.refs_3_
  192.8 5.5 %shard_map.73.refs_5_ = f32[32,32,1024]{2,1,0:T(8,128)} custom-call(s32[32,32]{1,0:T(8,128)S(1)} %copy-done.1, f32[7,16,8,128]{3,2,1,0:T(8,128)S(1)} %collective-permute-done.10.refs_0_, f32[16,32,8,128]{3,2,1,0:T(8,128)S(1)} %get-tuple-element.35.refs_0_.refs_1_, ...), custom_call_target="tpu_custom_call", output_to_operand_aliasing={{}: (6, {})} | custom-call | flops 629145600 | bytes 2097152 | tf_op jit(solution)/shard_map/pallas_call | solution.py:446
  198.4 0.0 collective-permute-done.8.refs_0_
  198.4 0.0 collective-permute-done.9.refs_3_
  198.4 5.5 %shard_map.74 = f32[32,32,1024]{2,1,0:T(8,128)} custom-call(s32[32,32]{1,0:T(8,128)S(1)} %copy-done.1, f32[7,16,8,128]{3,2,1,0:T(8,128)S(1)} %collective-permute-done.8.refs_0_, f32[16,32,8,128]{3,2,1,0:T(8,128)S(1)} %get-tuple-element.35.refs_0_.refs_1_, f32[16,32,8,128]{3,2,1,0:T(8,128)S(1)} %shard_map.70.refs_5_.refs_1_.refs_2_, ...), custom_call_target="tpu_custom_call", output_to_operand_aliasing={{}: (6, {})} | custom-call | flops 629145600 | bytes 2097152 | tf_op jit(solution)/shard_map/pallas_call | solution.py:446
Async XLA Ops:
  108.2 23.8 %copy-start.1 = (s32[32,32]{1,0:T(8,128)S(1)}, s32[32,32]{1,0:T(8,128)}, u32[]{:S(2)}) copy-start(s32[32,32]{1,0:T(8,128)} %dip_ref.17) | copy-start | bytes 12292
  119.6 21.3 %collective-permute-start = (f32[7,16,8,128]{3,2,1,0:T(8,128)S(1)}, f32[7,16,8,128]{3,2,1,0:T(8,128)S(1)}, u32[]{:S(2)}, u32[]{:S(2)}) collective-permute-start(f32[7,16,8,128]{3,2,1,0:T(8,128)S(1)} %get-tuple-element.22), channel_id=1, source_target_pairs={{0,4},{4,8},{8,12},{12,16},{16,20},{20,24},{24,28},{1,5},{5,9},{9,... | collective-permute-start | bytes 1376264 | tf_op jit(solution)/shard_map/ppermute | solution.py:468
  123.6 19.8 %collective-permute-start.1 = (f32[7,16,8,128]{3,2,1,0:T(8,128)S(1)}, f32[7,16,8,128]{3,2,1,0:T(8,128)S(1)}, u32[]{:S(2)}, u32[]{:S(2)}) collective-permute-start(f32[7,16,8,128]{3,2,1,0:T(8,128)S(1)} %get-tuple-element.24), channel_id=1, source_target_pairs={{4,0},{8,4},{12,8},{16,12},{20,16},{24,20},{28,24},{5,1},{9,5},{13... | collective-permute-start | bytes 1376264 | tf_op jit(solution)/shard_map/ppermute | solution.py:469
  125.5 24.1 %collective-permute-start.3 = (f32[7,16,8,128]{3,2,1,0:T(8,128)S(1)}, f32[7,16,8,128]{3,2,1,0:T(8,128)S(1)}, u32[]{:S(2)}, u32[]{:S(2)}) collective-permute-start(f32[7,16,8,128]{3,2,1,0:T(8,128)S(1)} %get-tuple-element.28), channel_id=1, source_target_pairs={{0,4},{4,8},{8,12},{12,16},{16,20},{20,24},{24,28},{1,5},{5,9},{9,... | collective-permute-start | bytes 1376264 | tf_op jit(solution)/shard_map/ppermute | solution.py:468
  130.1 22.1 %collective-permute-start.4 = (f32[7,16,8,128]{3,2,1,0:T(8,128)S(1)}, f32[7,16,8,128]{3,2,1,0:T(8,128)S(1)}, u32[]{:S(2)}, u32[]{:S(2)}) collective-permute-start(f32[7,16,8,128]{3,2,1,0:T(8,128)S(1)} %get-tuple-element.29), channel_id=1, source_target_pairs={{4,0},{8,4},{12,8},{16,12},{20,16},{24,20},{28,24},{5,1},{9,5},{13... | collective-permute-start | bytes 1376264 | tf_op jit(solution)/shard_map/ppermute | solution.py:469
  138.0 27.1 %collective-permute-start.6 = (f32[16,7,8,128]{3,2,1,0:T(8,128)S(1)}, f32[16,7,8,128]{3,2,1,0:T(8,128)S(1)}, u32[]{:S(2)}, u32[]{:S(2)}) collective-permute-start(f32[16,7,8,128]{3,2,1,0:T(8,128)S(1)} %get-tuple-element.32), channel_id=1, source_target_pairs={{0,1},{1,2},{2,3},{4,5},{5,6},{6,7},{8,9},{9,10},{10,11},{12,13},{... | collective-permute-start | bytes 1376264 | tf_op jit(solution)/shard_map/ppermute | solution.py:468
  140.9 26.2 %collective-permute-start.7 = (f32[16,7,8,128]{3,2,1,0:T(8,128)S(1)}, f32[16,7,8,128]{3,2,1,0:T(8,128)S(1)}, u32[]{:S(2)}, u32[]{:S(2)}) collective-permute-start(f32[16,7,8,128]{3,2,1,0:T(8,128)S(1)} %get-tuple-element.33), channel_id=1, source_target_pairs={{1,0},{2,1},{3,2},{5,4},{6,5},{7,6},{9,8},{10,9},{11,10},{13,12},{... | collective-permute-start | bytes 1376264 | tf_op jit(solution)/shard_map/ppermute | solution.py:469
  146.8 8.7 %copy-start.2 = (s32[32,32]{1,0:T(8,128)S(1)}, s32[32,32]{1,0:T(8,128)}, u32[]{:S(2)}) copy-start(s32[32,32]{1,0:T(8,128)} %dip_ref.14) | copy-start | bytes 12292
  146.8 26.2 %collective-permute-start.2 = (f32[16,7,8,128]{3,2,1,0:T(8,128)S(1)}, f32[16,7,8,128]{3,2,1,0:T(8,128)S(1)}, u32[]{:S(2)}, u32[]{:S(2)}) collective-permute-start(f32[16,7,8,128]{3,2,1,0:T(8,128)S(1)} %get-tuple-element.26), channel_id=1, source_target_pairs={{0,1},{1,2},{2,3},{4,5},{5,6},{6,7},{8,9},{9,10},{10,11},{12,13},{... | collective-permute-start | bytes 1376264 | tf_op jit(solution)/shard_map/ppermute | solution.py:468
  149.6 23.4 %collective-permute-start.5 = (f32[16,7,8,128]{3,2,1,0:T(8,128)S(1)}, f32[16,7,8,128]{3,2,1,0:T(8,128)S(1)}, u32[]{:S(2)}, u32[]{:S(2)}) collective-permute-start(f32[16,7,8,128]{3,2,1,0:T(8,128)S(1)} %get-tuple-element.30), channel_id=1, source_target_pairs={{1,0},{2,1},{3,2},{5,4},{6,5},{7,6},{9,8},{10,9},{11,10},{13,12},{... | collective-permute-start | bytes 1376264 | tf_op jit(solution)/shard_map/ppermute | solution.py:469
  159.5 33.3 %collective-permute-start.10 = (f32[7,16,8,128]{3,2,1,0:T(8,128)S(1)}, f32[7,16,8,128]{3,2,1,0:T(8,128)S(1)}, u32[]{:S(2)}, u32[]{:S(2)}) collective-permute-start(f32[7,16,8,128]{3,2,1,0:T(8,128)S(1)} %get-tuple-element.37), channel_id=1, source_target_pairs={{0,4},{4,8},{8,12},{12,16},{16,20},{20,24},{24,28},{1,5},{5,9},{9,... | collective-permute-start | bytes 1376264 | tf_op jit(solution)/shard_map/ppermute | solution.py:468
  165.1 27.7 %collective-permute-start.11 = (f32[7,16,8,128]{3,2,1,0:T(8,128)S(1)}, f32[7,16,8,128]{3,2,1,0:T(8,128)S(1)}, u32[]{:S(2)}, u32[]{:S(2)}) collective-permute-start(f32[7,16,8,128]{3,2,1,0:T(8,128)S(1)} %get-tuple-element.38), channel_id=1, source_target_pairs={{4,0},{8,4},{12,8},{16,12},{20,16},{24,20},{28,24},{5,1},{9,5},{13... | collective-permute-start | bytes 1376264 | tf_op jit(solution)/shard_map/ppermute | solution.py:469
  173.0 10.3 %copy-start = (bf16[1024,1024]{1,0:T(8,128)(2,1)S(1)}, bf16[1024,1024]{1,0:T(8,128)(2,1)}, u32[]{:S(2)}) copy-start(bf16[1024,1024]{1,0:T(8,128)(2,1)} %constant.2.clone.refs_2_.refs_4_) | copy-start | bytes 6291460
  176.7 21.7 %collective-permute-start.8 = (f32[7,16,8,128]{3,2,1,0:T(8,128)S(1)}, f32[7,16,8,128]{3,2,1,0:T(8,128)S(1)}, u32[]{:S(2)}, u32[]{:S(2)}) collective-permute-start(f32[7,16,8,128]{3,2,1,0:T(8,128)S(1)} %get-tuple-element.34), channel_id=1, source_target_pairs={{0,4},{4,8},{8,12},{12,16},{16,20},{20,24},{24,28},{1,5},{5,9},{9,... | collective-permute-start | bytes 1376264 | tf_op jit(solution)/shard_map/ppermute | solution.py:468
  181.2 17.2 %collective-permute-start.9 = (f32[7,16,8,128]{3,2,1,0:T(8,128)S(1)}, f32[7,16,8,128]{3,2,1,0:T(8,128)S(1)}, u32[]{:S(2)}, u32[]{:S(2)}) collective-permute-start(f32[7,16,8,128]{3,2,1,0:T(8,128)S(1)} %get-tuple-element.36), channel_id=1, source_target_pairs={{4,0},{8,4},{12,8},{16,12},{20,16},{24,20},{28,24},{5,1},{9,5},{13... | collective-permute-start | bytes 1376264 | tf_op jit(solution)/shard_map/ppermute | solution.py:469

commit v10 on v9

--- a/solution.py
+++ b/solution.py
@@ -2,7 +2,6 @@
 
 import jax
 import jax.numpy as jnp
-import numpy as np
 from jax import lax
 from jax.experimental import pallas as pl
 from jax.experimental.pallas import tpu as pltpu
@@ -14,6 +13,7 @@
 PHASES = 8
 PAIR = 2 * PHASES
 WIDE = 2 * LANES
+BLOCK = WIDE // PHASES
 WINDOW = 16
 BORDER = 8
 REACH = -(-HALF * DMAX // PHASES)
@@ -27,11 +27,11 @@
 F32, BF16, I32 = jnp.float32, jnp.bfloat16, jnp.int32
 
 
-def interleave_table(samples):
-    table = np.zeros((samples, samples), np.float32)
-    time = np.arange(samples)
-    table[time, time % PHASES * LANES + time // PHASES] = 1.0
-    return table
+def fill_interleave(table_ref, time_dim):
+    time = lax.broadcasted_iota(I32, (WIDE, WIDE), time_dim)
+    place = lax.broadcasted_iota(I32, (WIDE, WIDE), 1 - time_dim)
+    hit = time == place % BLOCK * PHASES + place // BLOCK
+    table_ref[...] = jnp.where(hit, 1.0, 0.0).astype(BF16)
 
 
 def move_samples(rows, table):
@@ -43,16 +43,20 @@
     return moved[:count] + moved[count:]
 
 
-def fill_interleave(table_ref):
-    size = table_ref.shape[0]
-    time = lax.broadcasted_iota(I32, (size, LANES), 0)
-    lane = lax.broadcasted_iota(I32, (size, LANES), 1)
-    gap = time - lane * PHASES
-    for phase in range(PHASES):
-        table_ref[:, phase * LANES : (phase + 1) * LANES] = jnp.where(gap == phase, 1.0, 0.0).astype(BF16)
-
-
-def pack_kernel(target_ref, bins_ref, traces_ref, out_ref, held_ref, table_ref, tiles_ref, used_ref, listed_ref, in_sems, sem, listed_sem, *, capacity):
+def swap_blocks(tiles):
+    count = LANES // BLOCK
+    block = lax.broadcasted_iota(I32, tiles[0].shape, 1) // BLOCK
+    swapped = []
+    for j in range(count):
+        total = tiles[j]
+        for m in range(count):
+            if m != j:
+                total = jnp.where(block == m, pltpu.roll(tiles[m], (m - j) * BLOCK % LANES, axis=1), total)
+        swapped.append(total)
+    return swapped
+
+
+def pack_kernel(mine_ref, target_ref, bins_ref, traces_ref, out_ref, held_ref, table_ref, tiles_ref, used_ref, listed_ref, in_sems, sem, listed_sem, *, capacity):
     held, block_rows, samples = traces_ref.shape
     devices, room, _ = listed_ref.shape
     span = block_rows * PHASES
@@ -64,9 +68,10 @@
     ]
     for load in loads:
         load.start()
-    fill_interleave(table_ref)
+    fill_interleave(table_ref, 0)
     lane = lax.broadcasted_iota(I32, (1, LANES), 1)
-    listed_ref[...] = jnp.full(listed_ref.shape, -1.0, F32)
+    listed_ref[...] = jnp.zeros(listed_ref.shape, F32)
+    own_lanes = mine_ref[0] % (LANES // (capacity * block_rows)) * (capacity * block_rows)
 
     def clear(device, _):
         used_ref[device] = 0
@@ -85,21 +90,25 @@
         ).start()
         row = jnp.zeros((1, LANES), I32)
         for j in range(block_rows):
-            row = jnp.where(lane == rank * block_rows + j, bins_ref[j, block], row)
-        own = (lane >= rank * block_rows) & (lane < (rank + 1) * block_rows)
-        listed_ref[device, 0:1, :] = jnp.where(own, row.astype(F32), listed_ref[device, 0:1, :])
+            row = jnp.where(lane == own_lanes + rank * block_rows + j, bins_ref[j, block] + 1, row)
+        listed_ref[device, 0:1, :] = listed_ref[device, 0:1, :] + row.astype(F32)
         return 0
 
     for group in range(groups):
         loads[group].wait()
         rows = held_ref[group].reshape(count * block_rows, samples)
-        moved = move_samples(rows, table_ref[...])
+        stretches = samples // WIDE
+        cut = jnp.concatenate([rows[:, i * WIDE : (i + 1) * WIDE] for i in range(stretches)], axis=0)
+        moved = move_samples(cut, table_ref[...])
         for eight in range(count * block_rows // 8):
-            for phase in range(PHASES):
-                first = (group * count * block_rows + eight * 8) * PHASES + phase
-                tiles_ref[pl.ds(first, 8, stride=PHASES), :] = moved[
-                    eight * 8 : eight * 8 + 8, phase * LANES : (phase + 1) * LANES
-                ]
+            for half in range(2):
+                parts = []
+                for i in range(stretches):
+                    begin = i * count * block_rows + eight * 8
+                    parts.append(moved[begin : begin + 8, half * LANES : (half + 1) * LANES])
+                for phase, part in enumerate(swap_blocks(parts)):
+                    first = (group * count * block_rows + eight * 8) * PHASES + half * 4 + phase
+                    tiles_ref[pl.ds(first, 8, stride=PHASES), :] = part
         lax.fori_loop(group * count, (group + 1) * count, send_block, 0, unroll=4)
     copy = pltpu.make_async_copy(
         listed_ref, out_ref.at[:, capacity * span : capacity * span + room, :], listed_sem
@@ -109,19 +118,19 @@
     pltpu.make_async_copy(tiles_ref, tiles_ref, sem).wait()
 
 
-def pack(traces, target, bins, devices, capacity):
+def pack(traces, mine, target, bins, devices, capacity):
     held, block_rows, samples = traces.shape
     span = block_rows * PHASES
     room = 8
     groups = 2
     return pl.pallas_call(
         functools.partial(pack_kernel, capacity=capacity),
-        in_specs=[SMEM, SMEM, HBM],
+        in_specs=[SMEM, SMEM, SMEM, HBM],
         out_specs=HBM,
         out_shape=jax.ShapeDtypeStruct((devices, capacity * span + room, LANES), F32),
         scratch_shapes=[
             pltpu.VMEM((groups, held // groups, block_rows, samples), F32),
-            pltpu.VMEM((samples, samples), BF16),
+            pltpu.VMEM((WIDE, WIDE), BF16),
             pltpu.VMEM((held * span, LANES), F32),
             pltpu.SMEM((devices,), I32),
             pltpu.VMEM((devices, room, LANES), F32),
@@ -130,7 +139,7 @@
             pltpu.SemaphoreType.DMA,
         ],
         compiler_params=pltpu.CompilerParams(vmem_limit_bytes=60 * MIB),
-    )(target, bins, traces)
+    )(mine, target, bins, traces)
 
 
 def bin_kernel(blocks_ref, out_ref, *refs, capacity, block_rows, edges):
@@ -140,13 +149,17 @@
     tile_rows, tile_cols = out_ref.shape[:2]
     bin_total = tile_rows * tile_cols
     unroll = 8
-
-    def read_list(sender, _):
-        listed = blocks_ref[sender, capacity * block_rows * PHASES : capacity * block_rows * PHASES + 1, :]
-        listed_ref[pl.ds(sender, 1), :] = jnp.where(listed < 0, float(bin_total), listed).astype(I32)
+    lanes = capacity * block_rows
+    shared = LANES // lanes
+
+    def read_lists(row, _):
+        total = jnp.zeros((1, LANES), F32)
+        for i in range(shared):
+            total = total + blocks_ref[row * shared + i, lanes * PHASES : lanes * PHASES + 1, :]
+        listed_ref[pl.ds(row, 1), :] = jnp.where(total > 0, total - 1.0, float(bin_total)).astype(I32)
         return 0
 
-    lax.fori_loop(0, devices, read_list, 0, unroll=8)
+    lax.fori_loop(0, devices // shared, read_lists, 0)
     copy = pltpu.make_async_copy(listed_ref, places_ref, sem)
     copy.start()
     nothing = jnp.zeros((PHASES, LANES), F32)
@@ -166,12 +179,13 @@
 
     def add_sender(sender, folds):
         folds = list(folds)
+        row, first = sender // shared, sender % shared * lanes
         for rank in range(capacity):
             for j in range(block_rows):
                 total_ref = odd_ref if j % 2 else even_ref
-                place = places_ref[sender, rank * block_rows + j]
-                row = (rank * block_rows + j) * PHASES
-                total_ref[place] += blocks_ref[sender, row : row + PHASES, :]
+                place = places_ref[row, first + rank * block_rows + j]
+                cell = (rank * block_rows + j) * PHASES
+                total_ref[place] += blocks_ref[sender, cell : cell + PHASES, :]
                 folds[j % 2] = folds[j % 2] + jnp.where(numbers == place, 1.0, 0.0)
         return tuple(folds)
 
@@ -183,9 +197,10 @@
     copy.wait()
 
     def finish(row, _):
+        high, low = row * tile_cols // LANES, row * tile_cols % LANES
         for col in range(tile_cols):
             place = row * tile_cols + col
-            scale = scales_ref[place // LANES, place % LANES]
+            scale = scales_ref[high, low + col]
             out_ref[row, col] = (even_ref[place] + odd_ref[place]) * scale
         return 0
 
@@ -225,8 +240,8 @@
         scratch_shapes=[
             pltpu.VMEM((bin_total + 8, PHASES, LANES), F32),
             pltpu.VMEM((bin_total + 8, PHASES, LANES), F32),
-            pltpu.VMEM((devices, LANES), I32),
-            pltpu.SMEM((devices, LANES), I32),
+            pltpu.VMEM((devices * capacity * block_rows // LANES, LANES), I32),
+            pltpu.SMEM((devices * capacity * block_rows // LANES, LANES), I32),
             pltpu.VMEM((bin_total // LANES, LANES), F32),
             pltpu.SMEM((bin_total // LANES, LANES), F32),
             pltpu.SemaphoreType.DMA,
@@ -279,7 +294,11 @@
                     axis=1,
                 )
             )
-    return jnp.dot(jnp.concatenate(taps, axis=0), halves_ref[...], preferred_element_type=F32)
+    half = len(taps) // 2
+    return [
+        jnp.dot(jnp.concatenate(part, axis=0), halves_ref[...], preferred_element_type=F32)
+        for part in (taps[:half], taps[half:])
+    ]
 
 
 def move_lanes(sums, first, count, put):
@@ -288,8 +307,8 @@
         for member in range(2):
             total = None
             for reach in REACHES:
-                begin = (pair * len(REACHES) + reach + REACH) * PAIR + member * PHASES
-                part = sums[begin : begin + PHASES, :LANES] + sums[begin : begin + PHASES, LANES:]
+                which, begin = divmod((pair * len(REACHES) + reach + REACH) * PAIR + member * PHASES, sums[0].shape[0])
+                part = sums[which][begin : begin + PHASES, :LANES] + sums[which][begin : begin + PHASES, LANES:]
                 if reach:
                     part = pltpu.roll(part, (-reach) % LANES, axis=1)
                     inside = lane < LANES - reach if reach > 0 else lane >= -reach
@@ -300,15 +319,14 @@
 
 def steer_kernel(dip_ref, *refs, along, whole, lines, line_of, windows, local_of, edges, final, batches, filled, chained, pieces_count, abreast):
     pieces, refs = refs[:pieces_count], refs[pieces_count:]
-    if final:
-        table_ref, refs = refs[0], refs[1:]
     refs = refs[chained:]
     out_ref, refs = refs[0], refs[1:]
     edge_refs, refs = refs[: len(edges)], refs[len(edges) :]
     spots_ref, weights_ref, sems, *refs = refs
     halves = refs[: abreast * len(windows)]
     if final:
-        staged_ref, result_ref = refs[abreast * len(windows) :]
+        staged_ref, result_ref, table_ref = refs[abreast * len(windows) :]
+        fill_interleave(table_ref, 1)
     fill_weights(spots_ref, weights_ref)
     for i, halves_ref in enumerate(halves):
         used = len(windows[i % len(windows)][2]) * PHASES
@@ -378,24 +396,30 @@
 
     for batch in range(lines // final):
         lax.fori_loop(batch * final // abreast, (batch + 1) * final // abreast, some_lines, 0)
-        rows = jnp.concatenate(
-            [
-                jnp.concatenate(
+        stretches = PHASES * LANES // WIDE
+        cuts = [[] for _ in range(stretches)]
+        for eight in range(outputs * final // 8):
+            sides = [
+                swap_blocks(
                     [
-                        staged_ref[pl.ds(eight * 8 * PHASES + phase, 8, stride=PHASES), :]
-                        for phase in range(PHASES)
-                    ],
-                    axis=1,
+                        staged_ref[pl.ds(eight * 8 * PHASES + half * 4 + phase, 8, stride=PHASES), :]
+                        for phase in range(PHASES // 2)
+                    ]
                 )
-                for eight in range(outputs * final // 8)
-            ],
-            axis=0,
-        )
+                for half in range(2)
+            ]
+            for i in range(stretches):
+                cuts[i].append(jnp.concatenate([sides[0][i], sides[1][i]], axis=1))
+        moved = move_samples(jnp.concatenate(sum(cuts, []), axis=0), table_ref[...])
         slot = batch % 2
         if batch >= 2:
             for copy in copies_of(batch - 2, slot):
                 copy.wait()
-        result_ref[slot] = move_samples(rows, table_ref[...]).reshape(result_ref.shape[1:])
+        count = outputs * final
+        for i in range(stretches):
+            result_ref[slot, :, :, i * WIDE : (i + 1) * WIDE] = moved[i * count : (i + 1) * count].reshape(
+                outputs, final, WIDE
+            )
         for copy in copies_of(batch, slot):
             copy.start()
     for batch in range(max(0, lines // final - 2), lines // final):
@@ -404,19 +428,17 @@
 
 
 def steer(
-    dip, pieces, along, lines, line_of, windows, local_of, edges=(), table=None, batches=None, before=None, after=None, filled=None
+    dip, pieces, along, lines, line_of, windows, local_of, edges=(), batches=None, before=None, after=None, filled=None
 ):
     samples = PHASES * LANES
     outputs = sum(count for _, count, _ in windows)
-    final = 16 if table is not None else 0
+    final = 16 if batches is not None else 0
     abreast = 4 * WINDOW // outputs
     shapes, specs, sems = edge_outputs(edges)
     operands = [dip] + [array for array, _ in pieces]
     in_specs = [SMEM] + [VMEM] * len(pieces)
     aliases = {}
     if final:
-        operands.append(table)
-        in_specs.append(VMEM)
         if before is not None:
             aliases = {len(operands): 0}
             operands.append(before)
@@ -442,12 +464,13 @@
         scratch += [
             pltpu.VMEM((outputs * final * PHASES, LANES), F32),
             pltpu.VMEM((2, outputs, final, samples), F32),
+            pltpu.VMEM((WIDE, WIDE), BF16),
         ]
     return pl.pallas_call(
         functools.partial(
             steer_kernel,
             along=along, whole=[whole for _, whole in pieces], lines=lines, line_of=line_of, windows=windows,
-            local_of=local_of, edges=edges, final=final, batches=batches, filled=filled, chained=len(operands) - len(pieces) - 1 - bool(final), pieces_count=len(pieces), abreast=abreast,
+            local_of=local_of, edges=edges, final=final, batches=batches, filled=filled, chained=len(operands) - len(pieces) - 1, pieces_count=len(pieces), abreast=abreast,
         ),
         in_specs=in_specs,
         out_specs=out_specs,
@@ -478,7 +501,7 @@
     return slice(first, first + count)
 
 
-def smooth(arrived, capacity, block_rows, dip_inline, dip_cross, table):
+def smooth(arrived, capacity, block_rows, dip_inline, dip_cross):
     rows, cols = dip_inline.shape
     mid_rows, mid_cols = rows - 2 * BORDER, cols - 2 * BORDER
     both = 2 * BORDER
@@ -559,7 +582,7 @@
     places = span_of(0, BORDER - HALF, HALF) + span_of(1, 0, mid_rows) + span_of(0, BORDER, HALF)
     (result,) = steer(
         dip_inline, [(border_second, True), (middle_second, True)], 0, cols, same, mid_windows(places, rows), mid_place,
-        table=table, batches=[[(0, first, WINDOW)] for first in range(0, cols, WINDOW)],
+        batches=[[(0, first, WINDOW)] for first in range(0, cols, WINDOW)],
     )
     windows = [
         (0, BORDER, span_of(0, 0, HALF) + span_of(1, 0, BORDER) + span_of(2, 0, HALF)),
@@ -571,19 +594,19 @@
     ):
         (result,) = steer(
             dip_inline, [(low, False), (border_second, True), (middle_second, True), (high, False)], 0, lines, line_of,
-            windows, outer_place, table=table, batches=batches, before=result,
+            windows, outer_place, batches=batches, before=result,
         )
     return result
 
 
 def on_device(traces, destination, bin_index, dip_inline, dip_cross):
-    held, block_rows, samples = traces.shape
+    held, block_rows, _ = traces.shape
     devices = lax.axis_size("inline") * lax.axis_size("crosslin")
     capacity = 2 * held // devices
-    outgoing = pack(traces, destination.reshape(-1), bin_index.T, devices, capacity)
+    mine = lax.axis_index("inline") * lax.axis_size("crosslin") + lax.axis_index("crosslin")
+    outgoing = pack(traces, mine.astype(I32).reshape(1), destination.reshape(-1), bin_index.T, devices, capacity)
     arrived = lax.all_to_all(outgoing, BOTH, split_axis=0, concat_axis=0, tiled=True)
-    back = jnp.asarray(interleave_table(samples).T, BF16)
-    return smooth(arrived, capacity, block_rows, dip_inline, dip_cross, back)
+    return smooth(arrived, capacity, block_rows, dip_inline, dip_cross)
 
 
 def solution(mesh):

time: 205 us -> 200 us (0.976)
  Pallas kernels: 64.7 us -> 59.2 us
    pallas_call x1, Pallas kernels: 11.4 us -> 6.97 us  [stack_bins(): pl.pallas_call(functools.partial(bin_kernel, capacity=capacity, block_row...]
where the time goes in v10:
time: 200 us; the launch traced here: 199 us
  blocking collectives  102 us (51%)
  Pallas kernels  59.2 us (30%)
  starting transfers between devices  37.5 us (19%)
    all_to_all x1, blocking collectives, on_device(): lax.all_to_all(outgoing, BOTH, split_axis=0, concat_axis=0, tiled=True)  102 us
    pallas_call x9, Pallas kernels, steer(): pl.pallas_call(functools.partial(steer_kernel, along=along, whole=[whole...  45.5 us
    ppermute x6, starting transfers between devices, swap_ends(): low = lax.ppermute(tail, axis, [(i, i + 1) for i in range(count - 1)])  23.3 us
    ppermute x6, starting transfers between devices, swap_ends(): high = lax.ppermute(head, axis, [(i + 1, i) for i in range(count - 1)])  14.2 us
    pallas_call x1, Pallas kernels, stack_bins(): pl.pallas_call(functools.partial(bin_kernel, capacity=capacity, block_row...  6.97 us
    pallas_call x1, Pallas kernels, pack(): pl.pallas_call(functools.partial(pack_kernel, capacity=capacity), in_spec...  6.69 us
  transfers between devices with their start and end apart: 12, of which 0 were waited for; matrix products, arithmetic and copies ran while one was open for 0% of the time, Pallas kernels for 20%

profile of v10, /device:TPU:11, one launch (start us, length us, event | category | flops | bytes accessed | tf_op | source)
XLA Modules:
  0.0 198.8 jit_solution(4635277360272916497)
XLA Ops:
  0.0 6.7 %shard_map.55 = f32[32,264,128]{2,1,0:T(8,128)} custom-call(s32[1]{0:T(128)} %bitcast.mine_ref, s32[128]{0:T(128)} %bitcast.4, s32[4,128]{1,0:T(4,128)} %bitcast.3, f32[128,4,1024]{2,1,0:T(4,128)} %traces_ref.1), custom_call_target="tpu_custom_call" | custom-call | tf_op jit(solution)/shard_map/pallas_call | solution.py:126
  6.7 101.7 %all_to_all.5.blocks_ref = f32[32,264,128]{2,1,0:T(8,128)S(1)} all-to-all(f32[32,264,128]{2,1,0:T(8,128)} %shard_map.55), channel_id=1, replica_groups=mesh['inline'=8,'crosslin'=4] {'inline','crosslin'}, dimensions={0} | all-to-all | bytes 8650752 | tf_op jit(solution)/shard_map/all_to_all | solution.py:608
  108.4 0.0 copy-start
  108.4 7.0 %shard_map.56 = (f32[32,32,8,128]{3,2,1,0:T(8,128)S(1)}, f32[7,16,8,128]{3,2,1,0:T(8,128)S(1)}, f32[7,16,8,128]{3,2,1,0:T(8,128)S(1)}, f32[7,16,8,128]{3,2,1,0:T(8,128)S(1)}, f32[7,16,8,128]{3,2,1,0:T(8,128)S(1)}) custom-call(f32[32,264,128]{2,1,0:T(8,128)S(1)} %all_to_all.5.blocks_ref), custom_call_target="tpu_custom_call" | custom-call | tf_op jit(solution)/shard_map/pallas_call | solution.py:235
  115.4 4.3 %collective-permute-start = (f32[7,16,8,128]{3,2,1,0:T(8,128)S(1)}, f32[7,16,8,128]{3,2,1,0:T(8,128)S(1)}, u32[]{:S(2)}, u32[]{:S(2)}) collective-permute-start(f32[7,16,8,128]{3,2,1,0:T(8,128)S(1)} %get-tuple-element.22), channel_id=1, source_target_pairs={{0,4},{4,8},{8,12},{12,16},{16,20},{20,24},{24,28},{1,5},{5,9},{9,... | collective-permute-start | bytes 1376264 | tf_op jit(solution)/shard_map/ppermute | solution.py:491
  119.6 1.9 collective-permute-start.1
  121.6 4.5 %collective-permute-start.3 = (f32[7,16,8,128]{3,2,1,0:T(8,128)S(1)}, f32[7,16,8,128]{3,2,1,0:T(8,128)S(1)}, u32[]{:S(2)}, u32[]{:S(2)}) collective-permute-start(f32[7,16,8,128]{3,2,1,0:T(8,128)S(1)} %get-tuple-element.28), channel_id=1, source_target_pairs={{0,4},{4,8},{8,12},{12,16},{16,20},{20,24},{24,28},{1,5},{5,9},{9,... | collective-permute-start | bytes 1376264 | tf_op jit(solution)/shard_map/ppermute | solution.py:491
  126.1 1.9 collective-permute-start.4
  128.1 0.0 copy-done
  128.1 6.0 %shard_map.57 = (f32[16,32,8,128]{3,2,1,0:T(8,128)S(1)}, f32[16,7,8,128]{3,2,1,0:T(8,128)S(1)}, f32[16,7,8,128]{3,2,1,0:T(8,128)S(1)}) custom-call(s32[32,32]{1,0:T(8,128)S(1)} %copy-done, f32[32,32,8,128]{3,2,1,0:T(8,128)S(1)} %get-tuple-element.23.refs_0_.refs_1_), custom_call_target="tpu_custom_call" | custom-call | flops 1258291200 | bytes 4194304 | tf_op jit(solution)/shard_map/pallas_call | solution.py:469
  134.0 2.2 %collective-permute-start.6 = (f32[16,7,8,128]{3,2,1,0:T(8,128)S(1)}, f32[16,7,8,128]{3,2,1,0:T(8,128)S(1)}, u32[]{:S(2)}, u32[]{:S(2)}) collective-permute-start(f32[16,7,8,128]{3,2,1,0:T(8,128)S(1)} %get-tuple-element.32), channel_id=1, source_target_pairs={{0,1},{1,2},{2,3},{4,5},{5,6},{6,7},{8,9},{9,10},{10,11},{12,13},{... | collective-permute-start | bytes 1376264 | tf_op jit(solution)/shard_map/ppermute | solution.py:491
  136.2 0.0 collective-permute-done.refs_0_
  136.2 3.1 %collective-permute-start.7 = (f32[16,7,8,128]{3,2,1,0:T(8,128)S(1)}, f32[16,7,8,128]{3,2,1,0:T(8,128)S(1)}, u32[]{:S(2)}, u32[]{:S(2)}) collective-permute-start(f32[16,7,8,128]{3,2,1,0:T(8,128)S(1)} %get-tuple-element.33), channel_id=1, source_target_pairs={{1,0},{2,1},{3,2},{5,4},{6,5},{7,6},{9,8},{10,9},{11,10},{13,12},{... | collective-permute-start | bytes 1376264 | tf_op jit(solution)/shard_map/ppermute | solution.py:492
  139.4 0.0 collective-permute-done.1.refs_2_
  139.4 3.4 %shard_map.58 = (f32[16,16,8,128]{3,2,1,0:T(8,128)S(1)}, f32[16,7,8,128]{3,2,1,0:T(8,128)S(1)}, f32[16,7,8,128]{3,2,1,0:T(8,128)S(1)}) custom-call(s32[32,32]{1,0:T(8,128)S(1)} %copy-done, f32[7,16,8,128]{3,2,1,0:T(8,128)S(1)} %collective-permute-done.refs_0_, f32[32,32,8,128]{3,2,1,0:T(8,128)S(1)} %get-tuple-element.23.refs_0_.refs_1_, ...), custom_call_target="tpu_custom_call" | custom-call | flops 629145600 | bytes 2097152 | tf_op jit(solution)/shard_map/pallas_call | solution.py:469
  142.8 0.0 copy-start.1
  142.8 2.1 %collective-permute-start.2 = (f32[16,7,8,128]{3,2,1,0:T(8,128)S(1)}, f32[16,7,8,128]{3,2,1,0:T(8,128)S(1)}, u32[]{:S(2)}, u32[]{:S(2)}) collective-permute-start(f32[16,7,8,128]{3,2,1,0:T(8,128)S(1)} %get-tuple-element.26), channel_id=1, source_target_pairs={{0,1},{1,2},{2,3},{4,5},{5,6},{6,7},{8,9},{9,10},{10,11},{12,13},{... | collective-permute-start | bytes 1376264 | tf_op jit(solution)/shard_map/ppermute | solution.py:491
  145.0 0.0 collective-permute-done.3.refs_0_
  145.0 3.2 %collective-permute-start.5 = (f32[16,7,8,128]{3,2,1,0:T(8,128)S(1)}, f32[16,7,8,128]{3,2,1,0:T(8,128)S(1)}, u32[]{:S(2)}, u32[]{:S(2)}) collective-permute-start(f32[16,7,8,128]{3,2,1,0:T(8,128)S(1)} %get-tuple-element.30), channel_id=1, source_target_pairs={{1,0},{2,1},{3,2},{5,4},{6,5},{7,6},{9,8},{10,9},{11,10},{13,12},{... | collective-permute-start | bytes 1376264 | tf_op jit(solution)/shard_map/ppermute | solution.py:492
  148.1 0.0 collective-permute-done.4.refs_2_
  148.2 3.3 %shard_map.59.refs_1_.refs_2_ = f32[16,16,8,128]{3,2,1,0:T(8,128)S(1)} custom-call(s32[32,32]{1,0:T(8,128)S(1)} %copy-done, f32[7,16,8,128]{3,2,1,0:T(8,128)S(1)} %collective-permute-done.3.refs_0_, f32[32,32,8,128]{3,2,1,0:T(8,128)S(1)} %get-tuple-element.23.refs_0_.refs_1_, f32[7,16,8,128]{3,2,1,0:T(8,128)S(1)} %collective-permute-done.4.refs_2_, ...), custom_call_target="tpu_custom_call" | custom-call | flops 629145600 | bytes 2097152 | tf_op jit(solution)/shard_map/pallas_call | solution.py:469
  151.5 0.0 copy-done.1
  151.5 3.8 %shard_map.60 = (f32[16,16,8,128]{3,2,1,0:T(8,128)S(1)}, f32[7,16,8,128]{3,2,1,0:T(8,128)S(1)}, f32[7,16,8,128]{3,2,1,0:T(8,128)S(1)}) custom-call(s32[32,32]{1,0:T(8,128)S(1)} %copy-done.1, f32[16,16,8,128]{3,2,1,0:T(8,128)S(1)} %get-tuple-element.27.refs_3_.refs_0_.refs_1_, f32[16,16,8,128]{3,2,1,0:T(8,128)S(1)} %shard_map.59.refs_1_.refs_2_), custom_call_target="tpu_custom_call" | custom-call | flops 629145600 | bytes 2097152 | tf_op jit(solution)/shard_map/pallas_call | solution.py:469
  155.3 5.7 %collective-permute-start.10 = (f32[7,16,8,128]{3,2,1,0:T(8,128)S(1)}, f32[7,16,8,128]{3,2,1,0:T(8,128)S(1)}, u32[]{:S(2)}, u32[]{:S(2)}) collective-permute-start(f32[7,16,8,128]{3,2,1,0:T(8,128)S(1)} %get-tuple-element.37), channel_id=1, source_target_pairs={{0,4},{4,8},{8,12},{12,16},{16,20},{20,24},{24,28},{1,5},{5,9},{9,... | collective-permute-start | bytes 1376264 | tf_op jit(solution)/shard_map/ppermute | solution.py:491
  161.0 0.0 collective-permute-done.6.refs_0_
  161.0 1.9 collective-permute-start.11
  162.9 0.0 collective-permute-done.7.refs_2_
  162.9 5.7 %shard_map.61.refs_5_.refs_1_.refs_2_ = f32[16,32,8,128]{3,2,1,0:T(8,128)S(1)} custom-call(s32[32,32]{1,0:T(8,128)S(1)} %copy-done.1, f32[16,7,8,128]{3,2,1,0:T(8,128)S(1)} %collective-permute-done.6.refs_0_, f32[16,32,8,128]{3,2,1,0:T(8,128)S(1)} %get-tuple-element.25.refs_3_.refs_1_, f32[16,7,8,128]{3,2,1,0:T(8,128)S(1)} %collective-permute-done.7.refs_2_, ...), custom_call_target="tpu_custom_call" | custom-call | flops 1258291200 | bytes 4194304 | tf_op jit(solution)/shard_map/pallas_call | solution.py:469
  168.7 0.0 collective-permute-done.2.refs_0_
  168.7 0.0 collective-permute-done.5.refs_3_
  168.7 3.6 %shard_map.62 = (f32[16,32,8,128]{3,2,1,0:T(8,128)S(1)}, f32[7,16,8,128]{3,2,1,0:T(8,128)S(1)}, f32[7,16,8,128]{3,2,1,0:T(8,128)S(1)}) custom-call(s32[32,32]{1,0:T(8,128)S(1)} %copy-done.1, f32[16,7,8,128]{3,2,1,0:T(8,128)S(1)} %collective-permute-done.2.refs_0_, f32[16,16,8,128]{3,2,1,0:T(8,128)S(1)} %get-tuple-element.27.refs_3_.refs_0_.refs_1_, ...), custom_call_target="tpu_custom_call" | custom-call | flops 629145600 | bytes 2097152 | tf_op jit(solution)/shard_map/pallas_call | solution.py:469
  172.3 4.5 %collective-permute-start.8 = (f32[7,16,8,128]{3,2,1,0:T(8,128)S(1)}, f32[7,16,8,128]{3,2,1,0:T(8,128)S(1)}, u32[]{:S(2)}, u32[]{:S(2)}) collective-permute-start(f32[7,16,8,128]{3,2,1,0:T(8,128)S(1)} %get-tuple-element.34), channel_id=1, source_target_pairs={{0,4},{4,8},{8,12},{12,16},{16,20},{20,24},{24,28},{1,5},{5,9},{9,... | collective-permute-start | bytes 1376264 | tf_op jit(solution)/shard_map/ppermute | solution.py:491
  176.8 2.1 %collective-permute-start.9 = (f32[7,16,8,128]{3,2,1,0:T(8,128)S(1)}, f32[7,16,8,128]{3,2,1,0:T(8,128)S(1)}, u32[]{:S(2)}, u32[]{:S(2)}) collective-permute-start(f32[7,16,8,128]{3,2,1,0:T(8,128)S(1)} %get-tuple-element.36), channel_id=1, source_target_pairs={{4,0},{8,4},{12,8},{16,12},{20,16},{24,20},{28,24},{5,1},{9,5},{13... | collective-permute-start | bytes 1376264 | tf_op jit(solution)/shard_map/ppermute | solution.py:492
  178.9 8.9 %shard_map.63.refs_4_ = f32[32,32,1024]{2,1,0:T(8,128)} custom-call(s32[32,32]{1,0:T(8,128)S(1)} %copy-done, f32[16,32,8,128]{3,2,1,0:T(8,128)S(1)} %get-tuple-element.35.refs_0_.refs_1_, f32[16,32,8,128]{3,2,1,0:T(8,128)S(1)} %shard_map.61.refs_5_.refs_1_.refs_2_), custom_call_target="tpu_custom_call" | custom-call | flops 1258291200 | bytes 4194304 | tf_op jit(solution)/shard_map/pallas_call | solution.py:469
  187.8 0.0 collective-permute-done.10.refs_0_
  187.8 0.0 collective-permute-done.11.refs_3_
  187.9 5.4 %shard_map.64.refs_4_ = f32[32,32,1024]{2,1,0:T(8,128)} custom-call(s32[32,32]{1,0:T(8,128)S(1)} %copy-done, f32[7,16,8,128]{3,2,1,0:T(8,128)S(1)} %collective-permute-done.10.refs_0_, f32[16,32,8,128]{3,2,1,0:T(8,128)S(1)} %get-tuple-element.35.refs_0_.refs_1_, ...), custom_call_target="tpu_custom_call", output_to_operand_aliasing={{}: (5, {})} | custom-call | flops 629145600 | bytes 2097152 | tf_op jit(solution)/shard_map/pallas_call | solution.py:469
  193.2 0.0 collective-permute-done.8.refs_0_
  193.3 0.0 collective-permute-done.9.refs_3_
  193.3 5.4 %shard_map.65 = f32[32,32,1024]{2,1,0:T(8,128)} custom-call(s32[32,32]{1,0:T(8,128)S(1)} %copy-done, f32[7,16,8,128]{3,2,1,0:T(8,128)S(1)} %collective-permute-done.8.refs_0_, f32[16,32,8,128]{3,2,1,0:T(8,128)S(1)} %get-tuple-element.35.refs_0_.refs_1_, f32[16,32,8,128]{3,2,1,0:T(8,128)S(1)} %shard_map.61.refs_5_.refs_1_.refs_2_, ...), custom_call_target="tpu_custom_call", output_to_operand_aliasing={{}: (5, {})} | custom-call | flops 629145600 | bytes 2097152 | tf_op jit(solution)/shard_map/pallas_call | solution.py:469
Async XLA Ops:
  108.4 19.7 %copy-start = (s32[32,32]{1,0:T(8,128)S(1)}, s32[32,32]{1,0:T(8,128)}, u32[]{:S(2)}) copy-start(s32[32,32]{1,0:T(8,128)} %dip_ref.17) | copy-start | bytes 12292
  115.4 20.8 %collective-permute-start = (f32[7,16,8,128]{3,2,1,0:T(8,128)S(1)}, f32[7,16,8,128]{3,2,1,0:T(8,128)S(1)}, u32[]{:S(2)}, u32[]{:S(2)}) collective-permute-start(f32[7,16,8,128]{3,2,1,0:T(8,128)S(1)} %get-tuple-element.22), channel_id=1, source_target_pairs={{0,4},{4,8},{8,12},{12,16},{16,20},{20,24},{24,28},{1,5},{5,9},{9,... | collective-permute-start | bytes 1376264 | tf_op jit(solution)/shard_map/ppermute | solution.py:491
  119.6 19.7 %collective-permute-start.1 = (f32[7,16,8,128]{3,2,1,0:T(8,128)S(1)}, f32[7,16,8,128]{3,2,1,0:T(8,128)S(1)}, u32[]{:S(2)}, u32[]{:S(2)}) collective-permute-start(f32[7,16,8,128]{3,2,1,0:T(8,128)S(1)} %get-tuple-element.24), channel_id=1, source_target_pairs={{4,0},{8,4},{12,8},{16,12},{20,16},{24,20},{28,24},{5,1},{9,5},{13... | collective-permute-start | bytes 1376264 | tf_op jit(solution)/shard_map/ppermute | solution.py:492
  121.6 23.4 %collective-permute-start.3 = (f32[7,16,8,128]{3,2,1,0:T(8,128)S(1)}, f32[7,16,8,128]{3,2,1,0:T(8,128)S(1)}, u32[]{:S(2)}, u32[]{:S(2)}) collective-permute-start(f32[7,16,8,128]{3,2,1,0:T(8,128)S(1)} %get-tuple-element.28), channel_id=1, source_target_pairs={{0,4},{4,8},{8,12},{12,16},{16,20},{20,24},{24,28},{1,5},{5,9},{9,... | collective-permute-start | bytes 1376264 | tf_op jit(solution)/shard_map/ppermute | solution.py:491
  126.1 22.0 %collective-permute-start.4 = (f32[7,16,8,128]{3,2,1,0:T(8,128)S(1)}, f32[7,16,8,128]{3,2,1,0:T(8,128)S(1)}, u32[]{:S(2)}, u32[]{:S(2)}) collective-permute-start(f32[7,16,8,128]{3,2,1,0:T(8,128)S(1)} %get-tuple-element.29), channel_id=1, source_target_pairs={{4,0},{8,4},{12,8},{16,12},{20,16},{24,20},{28,24},{5,1},{9,5},{13... | collective-permute-start | bytes 1376264 | tf_op jit(solution)/shard_map/ppermute | solution.py:492
  134.0 27.0 %collective-permute-start.6 = (f32[16,7,8,128]{3,2,1,0:T(8,128)S(1)}, f32[16,7,8,128]{3,2,1,0:T(8,128)S(1)}, u32[]{:S(2)}, u32[]{:S(2)}) collective-permute-start(f32[16,7,8,128]{3,2,1,0:T(8,128)S(1)} %get-tuple-element.32), channel_id=1, source_target_pairs={{0,1},{1,2},{2,3},{4,5},{5,6},{6,7},{8,9},{9,10},{10,11},{12,13},{... | collective-permute-start | bytes 1376264 | tf_op jit(solution)/shard_map/ppermute | solution.py:491
  136.2 26.7 %collective-permute-start.7 = (f32[16,7,8,128]{3,2,1,0:T(8,128)S(1)}, f32[16,7,8,128]{3,2,1,0:T(8,128)S(1)}, u32[]{:S(2)}, u32[]{:S(2)}) collective-permute-start(f32[16,7,8,128]{3,2,1,0:T(8,128)S(1)} %get-tuple-element.33), channel_id=1, source_target_pairs={{1,0},{2,1},{3,2},{5,4},{6,5},{7,6},{9,8},{10,9},{11,10},{13,12},{... | collective-permute-start | bytes 1376264 | tf_op jit(solution)/shard_map/ppermute | solution.py:492
  142.8 8.7 %copy-start.1 = (s32[32,32]{1,0:T(8,128)S(1)}, s32[32,32]{1,0:T(8,128)}, u32[]{:S(2)}) copy-start(s32[32,32]{1,0:T(8,128)} %dip_ref.14) | copy-start | bytes 12292
  142.8 25.8 %collective-permute-start.2 = (f32[16,7,8,128]{3,2,1,0:T(8,128)S(1)}, f32[16,7,8,128]{3,2,1,0:T(8,128)S(1)}, u32[]{:S(2)}, u32[]{:S(2)}) collective-permute-start(f32[16,7,8,128]{3,2,1,0:T(8,128)S(1)} %get-tuple-element.26), channel_id=1, source_target_pairs={{0,1},{1,2},{2,3},{4,5},{5,6},{6,7},{8,9},{9,10},{10,11},{12,13},{... | collective-permute-start | bytes 1376264 | tf_op jit(solution)/shard_map/ppermute | solution.py:491
  145.0 23.7 %collective-permute-start.5 = (f32[16,7,8,128]{3,2,1,0:T(8,128)S(1)}, f32[16,7,8,128]{3,2,1,0:T(8,128)S(1)}, u32[]{:S(2)}, u32[]{:S(2)}) collective-permute-start(f32[16,7,8,128]{3,2,1,0:T(8,128)S(1)} %get-tuple-element.30), channel_id=1, source_target_pairs={{1,0},{2,1},{3,2},{5,4},{6,5},{7,6},{9,8},{10,9},{11,10},{13,12},{... | collective-permute-start | bytes 1376264 | tf_op jit(solution)/shard_map/ppermute | solution.py:492
  155.3 32.5 %collective-permute-start.10 = (f32[7,16,8,128]{3,2,1,0:T(8,128)S(1)}, f32[7,16,8,128]{3,2,1,0:T(8,128)S(1)}, u32[]{:S(2)}, u32[]{:S(2)}) collective-permute-start(f32[7,16,8,128]{3,2,1,0:T(8,128)S(1)} %get-tuple-element.37), channel_id=1, source_target_pairs={{0,4},{4,8},{8,12},{12,16},{16,20},{20,24},{24,28},{1,5},{5,9},{9,... | collective-permute-start | bytes 1376264 | tf_op jit(solution)/shard_map/ppermute | solution.py:491
  161.0 26.9 %collective-permute-start.11 = (f32[7,16,8,128]{3,2,1,0:T(8,128)S(1)}, f32[7,16,8,128]{3,2,1,0:T(8,128)S(1)}, u32[]{:S(2)}, u32[]{:S(2)}) collective-permute-start(f32[7,16,8,128]{3,2,1,0:T(8,128)S(1)} %get-tuple-element.38), channel_id=1, source_target_pairs={{4,0},{8,4},{12,8},{16,12},{20,16},{24,20},{28,24},{5,1},{9,5},{13... | collective-permute-start | bytes 1376264 | tf_op jit(solution)/shard_map/ppermute | solution.py:492
  172.3 21.0 %collective-permute-start.8 = (f32[7,16,8,128]{3,2,1,0:T(8,128)S(1)}, f32[7,16,8,128]{3,2,1,0:T(8,128)S(1)}, u32[]{:S(2)}, u32[]{:S(2)}) collective-permute-start(f32[7,16,8,128]{3,2,1,0:T(8,128)S(1)} %get-tuple-element.34), channel_id=1, source_target_pairs={{0,4},{4,8},{8,12},{12,16},{16,20},{20,24},{24,28},{1,5},{5,9},{9,... | collective-permute-start | bytes 1376264 | tf_op jit(solution)/shard_map/ppermute | solution.py:491
  176.8 16.4 %collective-permute-start.9 = (f32[7,16,8,128]{3,2,1,0:T(8,128)S(1)}, f32[7,16,8,128]{3,2,1,0:T(8,128)S(1)}, u32[]{:S(2)}, u32[]{:S(2)}) collective-permute-start(f32[7,16,8,128]{3,2,1,0:T(8,128)S(1)} %get-tuple-element.36), channel_id=1, source_target_pairs={{4,0},{8,4},{12,8},{16,12},{20,16},{24,20},{28,24},{5,1},{9,5},{13... | collective-permute-start | bytes 1376264 | tf_op jit(solution)/shard_map/ppermute | solution.py:492

commit v11 on v10

--- a/solution.py
+++ b/solution.py
@@ -43,17 +43,23 @@
     return moved[:count] + moved[count:]
 
 
+def take_lanes(tile, index):
+    return jnp.take_along_axis(tile, index, axis=1, mode="promise_in_bounds")
+
+
 def swap_blocks(tiles):
-    count = LANES // BLOCK
-    block = lax.broadcasted_iota(I32, tiles[0].shape, 1) // BLOCK
-    swapped = []
-    for j in range(count):
-        total = tiles[j]
-        for m in range(count):
-            if m != j:
-                total = jnp.where(block == m, pltpu.roll(tiles[m], (m - j) * BLOCK % LANES, axis=1), total)
-        swapped.append(total)
-    return swapped
+    lane = lax.broadcasted_iota(I32, tiles[0].shape, 1)
+    tiles = list(tiles)
+    for step in (2, 1):
+        low = lane // BLOCK % (2 * step) < step
+        across = lane ^ (step * BLOCK)
+        for m in range(len(tiles)):
+            if m // step % 2 == 0:
+                first, second = tiles[m], tiles[m + step]
+                crossed = take_lanes(jnp.where(low, second, first), across)
+                tiles[m] = jnp.where(low, first, crossed)
+                tiles[m + step] = jnp.where(low, crossed, second)
+    return tiles
 
 
 def pack_kernel(mine_ref, target_ref, bins_ref, traces_ref, out_ref, held_ref, table_ref, tiles_ref, used_ref, listed_ref, in_sems, sem, listed_sem, *, capacity):
@@ -310,7 +316,7 @@
                 which, begin = divmod((pair * len(REACHES) + reach + REACH) * PAIR + member * PHASES, sums[0].shape[0])
                 part = sums[which][begin : begin + PHASES, :LANES] + sums[which][begin : begin + PHASES, LANES:]
                 if reach:
-                    part = pltpu.roll(part, (-reach) % LANES, axis=1)
+                    part = take_lanes(part, (lane + reach) & (LANES - 1))
                     inside = lane < LANES - reach if reach > 0 else lane >= -reach
                     part = jnp.where(inside, part, 0.0)
                 total = part if total is None else total + part

time: 200 us -> 209 us (1.045)
  Pallas kernels: 59.2 us -> 68.4 us
    pallas_call x9, Pallas kernels: 45.5 us -> 55 us  [steer(): pl.pallas_call(functools.partial(steer_kernel, along=along, whole=[whole...]
  transfers between devices with their start and end apart: 12 -> 12, of which waited for: 0 -> 0; matrix products, arithmetic and copies ran while one was open for 0% -> 0% of each run, Pallas kernels for 20% -> 24%
where the time goes in v11:
time: 209 us; the launch traced here: 207 us
  blocking collectives  102 us (49%)
  Pallas kernels  68.4 us (33%)
  starting transfers between devices  36.8 us (18%)
    all_to_all x1, blocking collectives, on_device(): lax.all_to_all(outgoing, BOTH, split_axis=0, concat_axis=0, tiled=True)  102 us
    pallas_call x9, Pallas kernels, steer(): pl.pallas_call(functools.partial(steer_kernel, along=along, whole=[whole...  55 us
    ppermute x6, starting transfers between devices, swap_ends(): low = lax.ppermute(tail, axis, [(i, i + 1) for i in range(count - 1)])  23.4 us
    ppermute x6, starting transfers between devices, swap_ends(): high = lax.ppermute(head, axis, [(i + 1, i) for i in range(count - 1)])  13.5 us
    pallas_call x1, Pallas kernels, stack_bins(): pl.pallas_call(functools.partial(bin_kernel, capacity=capacity, block_row...  7.36 us
    pallas_call x1, Pallas kernels, pack(): pl.pallas_call(functools.partial(pack_kernel, capacity=capacity), in_spec...  6.05 us
  transfers between devices with their start and end apart: 12, of which 0 were waited for; matrix products, arithmetic and copies ran while one was open for 0% of the time, Pallas kernels for 24%

profile of v11, /device:TPU:11, one launch (start us, length us, event | category | flops | bytes accessed | tf_op | source)
XLA Modules:
  0.0 207.5 jit_solution(8909005711260339695)
XLA Ops:
  0.0 6.1 %shard_map.55 = f32[32,264,128]{2,1,0:T(8,128)} custom-call(s32[1]{0:T(128)} %bitcast.mine_ref, s32[128]{0:T(128)} %bitcast.4, s32[4,128]{1,0:T(4,128)} %bitcast.3, f32[128,4,1024]{2,1,0:T(4,128)} %traces_ref.1), custom_call_target="tpu_custom_call" | custom-call | tf_op jit(solution)/shard_map/pallas_call | solution.py:132
  6.1 101.7 %all_to_all.5.blocks_ref = f32[32,264,128]{2,1,0:T(8,128)S(1)} all-to-all(f32[32,264,128]{2,1,0:T(8,128)} %shard_map.55), channel_id=1, replica_groups=mesh['inline'=8,'crosslin'=4] {'inline','crosslin'}, dimensions={0} | all-to-all | bytes 8650752 | tf_op jit(solution)/shard_map/all_to_all | solution.py:614
  107.8 0.0 copy-start
  107.8 7.4 %shard_map.56 = (f32[32,32,8,128]{3,2,1,0:T(8,128)S(1)}, f32[7,16,8,128]{3,2,1,0:T(8,128)S(1)}, f32[7,16,8,128]{3,2,1,0:T(8,128)S(1)}, f32[7,16,8,128]{3,2,1,0:T(8,128)S(1)}, f32[7,16,8,128]{3,2,1,0:T(8,128)S(1)}) custom-call(f32[32,264,128]{2,1,0:T(8,128)S(1)} %all_to_all.5.blocks_ref), custom_call_target="tpu_custom_call" | custom-call | tf_op jit(solution)/shard_map/pallas_call | solution.py:241
  115.1 3.6 %collective-permute-start = (f32[7,16,8,128]{3,2,1,0:T(8,128)S(1)}, f32[7,16,8,128]{3,2,1,0:T(8,128)S(1)}, u32[]{:S(2)}, u32[]{:S(2)}) collective-permute-start(f32[7,16,8,128]{3,2,1,0:T(8,128)S(1)} %get-tuple-element.22), channel_id=1, source_target_pairs={{0,4},{4,8},{8,12},{12,16},{16,20},{20,24},{24,28},{1,5},{5,9},{9,... | collective-permute-start | bytes 1376264 | tf_op jit(solution)/shard_map/ppermute | solution.py:497
  118.7 1.9 collective-permute-start.1
  120.7 4.5 %collective-permute-start.3 = (f32[7,16,8,128]{3,2,1,0:T(8,128)S(1)}, f32[7,16,8,128]{3,2,1,0:T(8,128)S(1)}, u32[]{:S(2)}, u32[]{:S(2)}) collective-permute-start(f32[7,16,8,128]{3,2,1,0:T(8,128)S(1)} %get-tuple-element.28), channel_id=1, source_target_pairs={{0,4},{4,8},{8,12},{12,16},{16,20},{20,24},{24,28},{1,5},{5,9},{9,... | collective-permute-start | bytes 1376264 | tf_op jit(solution)/shard_map/ppermute | solution.py:497
  125.2 1.9 collective-permute-start.4
  127.2 0.0 copy-done
  127.2 7.6 %shard_map.57 = (f32[16,32,8,128]{3,2,1,0:T(8,128)S(1)}, f32[16,7,8,128]{3,2,1,0:T(8,128)S(1)}, f32[16,7,8,128]{3,2,1,0:T(8,128)S(1)}) custom-call(s32[32,32]{1,0:T(8,128)S(1)} %copy-done, f32[32,32,8,128]{3,2,1,0:T(8,128)S(1)} %get-tuple-element.23.refs_0_.refs_1_), custom_call_target="tpu_custom_call" | custom-call | flops 1258291200 | bytes 4194304 | tf_op jit(solution)/shard_map/pallas_call | solution.py:475
  134.8 2.5 %collective-permute-start.6 = (f32[16,7,8,128]{3,2,1,0:T(8,128)S(1)}, f32[16,7,8,128]{3,2,1,0:T(8,128)S(1)}, u32[]{:S(2)}, u32[]{:S(2)}) collective-permute-start(f32[16,7,8,128]{3,2,1,0:T(8,128)S(1)} %get-tuple-element.32), channel_id=1, source_target_pairs={{0,1},{1,2},{2,3},{4,5},{5,6},{6,7},{8,9},{9,10},{10,11},{12,13},{... | collective-permute-start | bytes 1376264 | tf_op jit(solution)/shard_map/ppermute | solution.py:497
  137.3 0.0 collective-permute-done.refs_0_
  137.3 2.8 %collective-permute-start.7 = (f32[16,7,8,128]{3,2,1,0:T(8,128)S(1)}, f32[16,7,8,128]{3,2,1,0:T(8,128)S(1)}, u32[]{:S(2)}, u32[]{:S(2)}) collective-permute-start(f32[16,7,8,128]{3,2,1,0:T(8,128)S(1)} %get-tuple-element.33), channel_id=1, source_target_pairs={{1,0},{2,1},{3,2},{5,4},{6,5},{7,6},{9,8},{10,9},{11,10},{13,12},{... | collective-permute-start | bytes 1376264 | tf_op jit(solution)/shard_map/ppermute | solution.py:498
  140.1 0.0 collective-permute-done.1.refs_2_
  140.1 4.3 %shard_map.58 = (f32[16,16,8,128]{3,2,1,0:T(8,128)S(1)}, f32[16,7,8,128]{3,2,1,0:T(8,128)S(1)}, f32[16,7,8,128]{3,2,1,0:T(8,128)S(1)}) custom-call(s32[32,32]{1,0:T(8,128)S(1)} %copy-done, f32[7,16,8,128]{3,2,1,0:T(8,128)S(1)} %collective-permute-done.refs_0_, f32[32,32,8,128]{3,2,1,0:T(8,128)S(1)} %get-tuple-element.23.refs_0_.refs_1_, ...), custom_call_target="tpu_custom_call" | custom-call | flops 629145600 | bytes 2097152 | tf_op jit(solution)/shard_map/pallas_call | solution.py:475
  144.5 0.0 copy-start.1
  144.5 2.5 %collective-permute-start.2 = (f32[16,7,8,128]{3,2,1,0:T(8,128)S(1)}, f32[16,7,8,128]{3,2,1,0:T(8,128)S(1)}, u32[]{:S(2)}, u32[]{:S(2)}) collective-permute-start(f32[16,7,8,128]{3,2,1,0:T(8,128)S(1)} %get-tuple-element.26), channel_id=1, source_target_pairs={{0,1},{1,2},{2,3},{4,5},{5,6},{6,7},{8,9},{9,10},{10,11},{12,13},{... | collective-permute-start | bytes 1376264 | tf_op jit(solution)/shard_map/ppermute | solution.py:497
  147.0 0.0 collective-permute-done.3.refs_0_
  147.0 2.8 %collective-permute-start.5 = (f32[16,7,8,128]{3,2,1,0:T(8,128)S(1)}, f32[16,7,8,128]{3,2,1,0:T(8,128)S(1)}, u32[]{:S(2)}, u32[]{:S(2)}) collective-permute-start(f32[16,7,8,128]{3,2,1,0:T(8,128)S(1)} %get-tuple-element.30), channel_id=1, source_target_pairs={{1,0},{2,1},{3,2},{5,4},{6,5},{7,6},{9,8},{10,9},{11,10},{13,12},{... | collective-permute-start | bytes 1376264 | tf_op jit(solution)/shard_map/ppermute | solution.py:498
  149.8 0.0 collective-permute-done.4.refs_2_
  149.8 4.2 %shard_map.59.refs_1_.refs_2_ = f32[16,16,8,128]{3,2,1,0:T(8,128)S(1)} custom-call(s32[32,32]{1,0:T(8,128)S(1)} %copy-done, f32[7,16,8,128]{3,2,1,0:T(8,128)S(1)} %collective-permute-done.3.refs_0_, f32[32,32,8,128]{3,2,1,0:T(8,128)S(1)} %get-tuple-element.23.refs_0_.refs_1_, f32[7,16,8,128]{3,2,1,0:T(8,128)S(1)} %collective-permute-done.4.refs_2_, ...), custom_call_target="tpu_custom_call" | custom-call | flops 629145600 | bytes 2097152 | tf_op jit(solution)/shard_map/pallas_call | solution.py:475
  154.0 0.0 copy-done.1
  154.0 4.8 %shard_map.60 = (f32[16,16,8,128]{3,2,1,0:T(8,128)S(1)}, f32[7,16,8,128]{3,2,1,0:T(8,128)S(1)}, f32[7,16,8,128]{3,2,1,0:T(8,128)S(1)}) custom-call(s32[32,32]{1,0:T(8,128)S(1)} %copy-done.1, f32[16,16,8,128]{3,2,1,0:T(8,128)S(1)} %get-tuple-element.27.refs_3_.refs_0_.refs_1_, f32[16,16,8,128]{3,2,1,0:T(8,128)S(1)} %shard_map.59.refs_1_.refs_2_), custom_call_target="tpu_custom_call" | custom-call | flops 629145600 | bytes 2097152 | tf_op jit(solution)/shard_map/pallas_call | solution.py:475
  158.8 5.7 %collective-permute-start.10 = (f32[7,16,8,128]{3,2,1,0:T(8,128)S(1)}, f32[7,16,8,128]{3,2,1,0:T(8,128)S(1)}, u32[]{:S(2)}, u32[]{:S(2)}) collective-permute-start(f32[7,16,8,128]{3,2,1,0:T(8,128)S(1)} %get-tuple-element.37), channel_id=1, source_target_pairs={{0,4},{4,8},{8,12},{12,16},{16,20},{20,24},{24,28},{1,5},{5,9},{9,... | collective-permute-start | bytes 1376264 | tf_op jit(solution)/shard_map/ppermute | solution.py:497
  164.5 0.0 collective-permute-done.6.refs_0_
  164.5 1.9 collective-permute-start.11
  166.4 0.0 collective-permute-done.7.refs_2_
  166.4 7.6 %shard_map.61.refs_5_.refs_1_.refs_2_ = f32[16,32,8,128]{3,2,1,0:T(8,128)S(1)} custom-call(s32[32,32]{1,0:T(8,128)S(1)} %copy-done.1, f32[16,7,8,128]{3,2,1,0:T(8,128)S(1)} %collective-permute-done.6.refs_0_, f32[16,32,8,128]{3,2,1,0:T(8,128)S(1)} %get-tuple-element.25.refs_3_.refs_1_, f32[16,7,8,128]{3,2,1,0:T(8,128)S(1)} %collective-permute-done.7.refs_2_, ...), custom_call_target="tpu_custom_call" | custom-call | flops 1258291200 | bytes 4194304 | tf_op jit(solution)/shard_map/pallas_call | solution.py:475
  174.0 0.0 collective-permute-done.2.refs_0_
  174.0 0.0 collective-permute-done.5.refs_3_
  174.0 4.5 %shard_map.62 = (f32[16,32,8,128]{3,2,1,0:T(8,128)S(1)}, f32[7,16,8,128]{3,2,1,0:T(8,128)S(1)}, f32[7,16,8,128]{3,2,1,0:T(8,128)S(1)}) custom-call(s32[32,32]{1,0:T(8,128)S(1)} %copy-done.1, f32[16,7,8,128]{3,2,1,0:T(8,128)S(1)} %collective-permute-done.2.refs_0_, f32[16,16,8,128]{3,2,1,0:T(8,128)S(1)} %get-tuple-element.27.refs_3_.refs_0_.refs_1_, ...), custom_call_target="tpu_custom_call" | custom-call | flops 629145600 | bytes 2097152 | tf_op jit(solution)/shard_map/pallas_call | solution.py:475
  178.5 4.5 %collective-permute-start.8 = (f32[7,16,8,128]{3,2,1,0:T(8,128)S(1)}, f32[7,16,8,128]{3,2,1,0:T(8,128)S(1)}, u32[]{:S(2)}, u32[]{:S(2)}) collective-permute-start(f32[7,16,8,128]{3,2,1,0:T(8,128)S(1)} %get-tuple-element.34), channel_id=1, source_target_pairs={{0,4},{4,8},{8,12},{12,16},{16,20},{20,24},{24,28},{1,5},{5,9},{9,... | collective-permute-start | bytes 1376264 | tf_op jit(solution)/shard_map/ppermute | solution.py:497
  183.0 2.1 %collective-permute-start.9 = (f32[7,16,8,128]{3,2,1,0:T(8,128)S(1)}, f32[7,16,8,128]{3,2,1,0:T(8,128)S(1)}, u32[]{:S(2)}, u32[]{:S(2)}) collective-permute-start(f32[7,16,8,128]{3,2,1,0:T(8,128)S(1)} %get-tuple-element.36), channel_id=1, source_target_pairs={{4,0},{8,4},{12,8},{16,12},{20,16},{24,20},{28,24},{5,1},{9,5},{13... | collective-permute-start | bytes 1376264 | tf_op jit(solution)/shard_map/ppermute | solution.py:498
  185.1 10.1 %shard_map.63.refs_4_ = f32[32,32,1024]{2,1,0:T(8,128)} custom-call(s32[32,32]{1,0:T(8,128)S(1)} %copy-done, f32[16,32,8,128]{3,2,1,0:T(8,128)S(1)} %get-tuple-element.35.refs_0_.refs_1_, f32[16,32,8,128]{3,2,1,0:T(8,128)S(1)} %shard_map.61.refs_5_.refs_1_.refs_2_), custom_call_target="tpu_custom_call" | custom-call | flops 1258291200 | bytes 4194304 | tf_op jit(solution)/shard_map/pallas_call | solution.py:475
  195.2 0.0 collective-permute-done.10.refs_0_
  195.2 0.0 collective-permute-done.11.refs_3_
  195.2 6.0 %shard_map.64.refs_4_ = f32[32,32,1024]{2,1,0:T(8,128)} custom-call(s32[32,32]{1,0:T(8,128)S(1)} %copy-done, f32[7,16,8,128]{3,2,1,0:T(8,128)S(1)} %collective-permute-done.10.refs_0_, f32[16,32,8,128]{3,2,1,0:T(8,128)S(1)} %get-tuple-element.35.refs_0_.refs_1_, ...), custom_call_target="tpu_custom_call", output_to_operand_aliasing={{}: (5, {})} | custom-call | flops 629145600 | bytes 2097152 | tf_op jit(solution)/shard_map/pallas_call | solution.py:475
  201.2 0.0 collective-permute-done.8.refs_0_
  201.3 0.0 collective-permute-done.9.refs_3_
  201.3 6.0 %shard_map.65 = f32[32,32,1024]{2,1,0:T(8,128)} custom-call(s32[32,32]{1,0:T(8,128)S(1)} %copy-done, f32[7,16,8,128]{3,2,1,0:T(8,128)S(1)} %collective-permute-done.8.refs_0_, f32[16,32,8,128]{3,2,1,0:T(8,128)S(1)} %get-tuple-element.35.refs_0_.refs_1_, f32[16,32,8,128]{3,2,1,0:T(8,128)S(1)} %shard_map.61.refs_5_.refs_1_.refs_2_, ...), custom_call_target="tpu_custom_call", output_to_operand_aliasing={{}: (5, {})} | custom-call | flops 629145600 | bytes 2097152 | tf_op jit(solution)/shard_map/pallas_call | solution.py:475
Async XLA Ops:
  107.8 19.4 %copy-start = (s32[32,32]{1,0:T(8,128)S(1)}, s32[32,32]{1,0:T(8,128)}, u32[]{:S(2)}) copy-start(s32[32,32]{1,0:T(8,128)} %dip_ref.17) | copy-start | bytes 12292
  115.1 22.2 %collective-permute-start = (f32[7,16,8,128]{3,2,1,0:T(8,128)S(1)}, f32[7,16,8,128]{3,2,1,0:T(8,128)S(1)}, u32[]{:S(2)}, u32[]{:S(2)}) collective-permute-start(f32[7,16,8,128]{3,2,1,0:T(8,128)S(1)} %get-tuple-element.22), channel_id=1, source_target_pairs={{0,4},{4,8},{8,12},{12,16},{16,20},{20,24},{24,28},{1,5},{5,9},{9,... | collective-permute-start | bytes 1376264 | tf_op jit(solution)/shard_map/ppermute | solution.py:497
  118.7 21.4 %collective-permute-start.1 = (f32[7,16,8,128]{3,2,1,0:T(8,128)S(1)}, f32[7,16,8,128]{3,2,1,0:T(8,128)S(1)}, u32[]{:S(2)}, u32[]{:S(2)}) collective-permute-start(f32[7,16,8,128]{3,2,1,0:T(8,128)S(1)} %get-tuple-element.24), channel_id=1, source_target_pairs={{4,0},{8,4},{12,8},{16,12},{20,16},{24,20},{28,24},{5,1},{9,5},{13... | collective-permute-start | bytes 1376264 | tf_op jit(solution)/shard_map/ppermute | solution.py:498
  120.7 26.3 %collective-permute-start.3 = (f32[7,16,8,128]{3,2,1,0:T(8,128)S(1)}, f32[7,16,8,128]{3,2,1,0:T(8,128)S(1)}, u32[]{:S(2)}, u32[]{:S(2)}) collective-permute-start(f32[7,16,8,128]{3,2,1,0:T(8,128)S(1)} %get-tuple-element.28), channel_id=1, source_target_pairs={{0,4},{4,8},{8,12},{12,16},{16,20},{20,24},{24,28},{1,5},{5,9},{9,... | collective-permute-start | bytes 1376264 | tf_op jit(solution)/shard_map/ppermute | solution.py:497
  125.2 24.6 %collective-permute-start.4 = (f32[7,16,8,128]{3,2,1,0:T(8,128)S(1)}, f32[7,16,8,128]{3,2,1,0:T(8,128)S(1)}, u32[]{:S(2)}, u32[]{:S(2)}) collective-permute-start(f32[7,16,8,128]{3,2,1,0:T(8,128)S(1)} %get-tuple-element.29), channel_id=1, source_target_pairs={{4,0},{8,4},{12,8},{16,12},{20,16},{24,20},{28,24},{5,1},{9,5},{13... | collective-permute-start | bytes 1376264 | tf_op jit(solution)/shard_map/ppermute | solution.py:498
  134.8 29.7 %collective-permute-start.6 = (f32[16,7,8,128]{3,2,1,0:T(8,128)S(1)}, f32[16,7,8,128]{3,2,1,0:T(8,128)S(1)}, u32[]{:S(2)}, u32[]{:S(2)}) collective-permute-start(f32[16,7,8,128]{3,2,1,0:T(8,128)S(1)} %get-tuple-element.32), channel_id=1, source_target_pairs={{0,1},{1,2},{2,3},{4,5},{5,6},{6,7},{8,9},{9,10},{10,11},{12,13},{... | collective-permute-start | bytes 1376264 | tf_op jit(solution)/shard_map/ppermute | solution.py:497
  137.3 29.1 %collective-permute-start.7 = (f32[16,7,8,128]{3,2,1,0:T(8,128)S(1)}, f32[16,7,8,128]{3,2,1,0:T(8,128)S(1)}, u32[]{:S(2)}, u32[]{:S(2)}) collective-permute-start(f32[16,7,8,128]{3,2,1,0:T(8,128)S(1)} %get-tuple-element.33), channel_id=1, source_target_pairs={{1,0},{2,1},{3,2},{5,4},{6,5},{7,6},{9,8},{10,9},{11,10},{13,12},{... | collective-permute-start | bytes 1376264 | tf_op jit(solution)/shard_map/ppermute | solution.py:498
  144.5 9.6 %copy-start.1 = (s32[32,32]{1,0:T(8,128)S(1)}, s32[32,32]{1,0:T(8,128)}, u32[]{:S(2)}) copy-start(s32[32,32]{1,0:T(8,128)} %dip_ref.14) | copy-start | bytes 12292
  144.5 29.5 %collective-permute-start.2 = (f32[16,7,8,128]{3,2,1,0:T(8,128)S(1)}, f32[16,7,8,128]{3,2,1,0:T(8,128)S(1)}, u32[]{:S(2)}, u32[]{:S(2)}) collective-permute-start(f32[16,7,8,128]{3,2,1,0:T(8,128)S(1)} %get-tuple-element.26), channel_id=1, source_target_pairs={{0,1},{1,2},{2,3},{4,5},{5,6},{6,7},{8,9},{9,10},{10,11},{12,13},{... | collective-permute-start | bytes 1376264 | tf_op jit(solution)/shard_map/ppermute | solution.py:497
  147.0 27.0 %collective-permute-start.5 = (f32[16,7,8,128]{3,2,1,0:T(8,128)S(1)}, f32[16,7,8,128]{3,2,1,0:T(8,128)S(1)}, u32[]{:S(2)}, u32[]{:S(2)}) collective-permute-start(f32[16,7,8,128]{3,2,1,0:T(8,128)S(1)} %get-tuple-element.30), channel_id=1, source_target_pairs={{1,0},{2,1},{3,2},{5,4},{6,5},{7,6},{9,8},{10,9},{11,10},{13,12},{... | collective-permute-start | bytes 1376264 | tf_op jit(solution)/shard_map/ppermute | solution.py:498
  158.8 36.4 %collective-permute-start.10 = (f32[7,16,8,128]{3,2,1,0:T(8,128)S(1)}, f32[7,16,8,128]{3,2,1,0:T(8,128)S(1)}, u32[]{:S(2)}, u32[]{:S(2)}) collective-permute-start(f32[7,16,8,128]{3,2,1,0:T(8,128)S(1)} %get-tuple-element.37), channel_id=1, source_target_pairs={{0,4},{4,8},{8,12},{12,16},{16,20},{20,24},{24,28},{1,5},{5,9},{9,... | collective-permute-start | bytes 1376264 | tf_op jit(solution)/shard_map/ppermute | solution.py:497
  164.5 30.8 %collective-permute-start.11 = (f32[7,16,8,128]{3,2,1,0:T(8,128)S(1)}, f32[7,16,8,128]{3,2,1,0:T(8,128)S(1)}, u32[]{:S(2)}, u32[]{:S(2)}) collective-permute-start(f32[7,16,8,128]{3,2,1,0:T(8,128)S(1)} %get-tuple-element.38), channel_id=1, source_target_pairs={{4,0},{8,4},{12,8},{16,12},{20,16},{24,20},{28,24},{5,1},{9,5},{13... | collective-permute-start | bytes 1376264 | tf_op jit(solution)/shard_map/ppermute | solution.py:498
  178.5 22.7 %collective-permute-start.8 = (f32[7,16,8,128]{3,2,1,0:T(8,128)S(1)}, f32[7,16,8,128]{3,2,1,0:T(8,128)S(1)}, u32[]{:S(2)}, u32[]{:S(2)}) collective-permute-start(f32[7,16,8,128]{3,2,1,0:T(8,128)S(1)} %get-tuple-element.34), channel_id=1, source_target_pairs={{0,4},{4,8},{8,12},{12,16},{16,20},{20,24},{24,28},{1,5},{5,9},{9,... | collective-permute-start | bytes 1376264 | tf_op jit(solution)/shard_map/ppermute | solution.py:497
  183.0 18.2 %collective-permute-start.9 = (f32[7,16,8,128]{3,2,1,0:T(8,128)S(1)}, f32[7,16,8,128]{3,2,1,0:T(8,128)S(1)}, u32[]{:S(2)}, u32[]{:S(2)}) collective-permute-start(f32[7,16,8,128]{3,2,1,0:T(8,128)S(1)} %get-tuple-element.36), channel_id=1, source_target_pairs={{4,0},{8,4},{12,8},{16,12},{20,16},{24,20},{28,24},{5,1},{9,5},{13... | collective-permute-start | bytes 1376264 | tf_op jit(solution)/shard_map/ppermute | solution.py:498

commit v12 on v11

--- a/solution.py
+++ b/solution.py
@@ -18,6 +18,7 @@
 BORDER = 8
 REACH = -(-HALF * DMAX // PHASES)
 REACHES = range(-REACH, REACH + 1)
+FAR = [reach for reach in REACHES if abs(reach) > 1]
 BOTH = ("inline", "crosslin")
 MIB = 2**20
 VMEM = pl.BlockSpec(memory_space=pltpu.VMEM)
@@ -56,7 +57,8 @@
         for m in range(len(tiles)):
             if m // step % 2 == 0:
                 first, second = tiles[m], tiles[m + step]
-                crossed = take_lanes(jnp.where(low, second, first), across)
+                mixed = jnp.where(low, second, first)
+                crossed = pltpu.roll(mixed, LANES // 2, axis=1) if 2 * step * BLOCK == LANES else take_lanes(mixed, across)
                 tiles[m] = jnp.where(low, first, crossed)
                 tiles[m + step] = jnp.where(low, crossed, second)
     return tiles
@@ -300,27 +302,45 @@
                     axis=1,
                 )
             )
-    half = len(taps) // 2
-    return [
-        jnp.dot(jnp.concatenate(part, axis=0), halves_ref[...], preferred_element_type=F32)
-        for part in (taps[:half], taps[half:])
-    ]
-
-
-def move_lanes(sums, first, count, put):
-    lane = lax.broadcasted_iota(I32, (PHASES, LANES), 1)
+    return jnp.dot(jnp.concatenate(taps, axis=0), halves_ref[...], preferred_element_type=F32)
+
+
+def fill_shift(shift_ref):
+    size = shift_ref.shape[0]
+    source = lax.broadcasted_iota(I32, (size, LANES), 0)
+    lane = lax.broadcasted_iota(I32, (size, LANES), 1)
+    hit = jnp.zeros((size, LANES), jnp.bool_)
+    for i, reach in enumerate(FAR):
+        hit = hit | ((source // LANES == i) & (source % LANES == lane + reach))
+    shift_ref[...] = jnp.where(hit, 1.0, 0.0).astype(BF16)
+
+
+def move_lanes(sums, first, count, put, shift_ref):
+    lane = lax.broadcasted_iota(I32, (PAIR, LANES), 1)
+
+    def part(pair, reach):
+        begin = (pair * len(REACHES) + reach + REACH) * PAIR
+        return sums[begin : begin + PAIR, :LANES] + sums[begin : begin + PAIR, LANES:]
+
+    upper, rest = [], []
     for pair in range(count // 2):
+        far = jnp.concatenate([part(pair, reach) for reach in FAR], axis=1)
+        upper.append(far.astype(BF16))
+        rest.append((far - upper[-1].astype(F32)).astype(BF16))
+    far = jnp.dot(jnp.concatenate(upper + rest, axis=0), shift_ref[...], preferred_element_type=F32)
+    rows = count * PHASES
+    for pair in range(count // 2):
+        total = far[pair * PAIR : (pair + 1) * PAIR] + far[rows + pair * PAIR : rows + (pair + 1) * PAIR]
+        for reach in REACHES:
+            if reach not in FAR:
+                near = part(pair, reach)
+                if reach:
+                    near = pltpu.roll(near, (-reach) % LANES, axis=1)
+                    inside = lane < LANES - reach if reach > 0 else lane >= -reach
+                    near = jnp.where(inside, near, 0.0)
+                total = total + near
         for member in range(2):
-            total = None
-            for reach in REACHES:
-                which, begin = divmod((pair * len(REACHES) + reach + REACH) * PAIR + member * PHASES, sums[0].shape[0])
-                part = sums[which][begin : begin + PHASES, :LANES] + sums[which][begin : begin + PHASES, LANES:]
-                if reach:
-                    part = take_lanes(part, (lane + reach) & (LANES - 1))
-                    inside = lane < LANES - reach if reach > 0 else lane >= -reach
-                    part = jnp.where(inside, part, 0.0)
-                total = part if total is None else total + part
-            put(first + 2 * pair + member, total)
+            put(first + 2 * pair + member, total[member * PHASES : (member + 1) * PHASES])
 
 
 def steer_kernel(dip_ref, *refs, along, whole, lines, line_of, windows, local_of, edges, final, batches, filled, chained, pieces_count, abreast):
@@ -328,12 +348,13 @@
     refs = refs[chained:]
     out_ref, refs = refs[0], refs[1:]
     edge_refs, refs = refs[: len(edges)], refs[len(edges) :]
-    spots_ref, weights_ref, sems, *refs = refs
+    spots_ref, weights_ref, shift_ref, sems, *refs = refs
     halves = refs[: abreast * len(windows)]
     if final:
         staged_ref, result_ref, table_ref = refs[abreast * len(windows) :]
         fill_interleave(table_ref, 1)
     fill_weights(spots_ref, weights_ref)
+    fill_shift(shift_ref)
     for i, halves_ref in enumerate(halves):
         used = len(windows[i % len(windows)][2]) * PHASES
         if used < WIDE:
@@ -368,7 +389,7 @@
             )
             if waiting is not None:
                 move_lanes(*waiting)
-            waiting = (sums, first, count, put)
+            waiting = (sums, first, count, put, shift_ref)
         move_lanes(*waiting)
         return 0
 
@@ -464,7 +485,7 @@
         in_specs.append(ANY)
     most = max(count for _, count, _ in windows)
     constant = pltpu.VMEM((most * PAIR, LANES), BF16)
-    scratch = [constant, constant, sems]
+    scratch = [constant, constant, pltpu.VMEM((len(FAR) * LANES, LANES), BF16), sems]
     scratch += [pltpu.VMEM((WIDE, WIDE), BF16)] * (abreast * len(windows))
     if final:
         scratch += [

time: 209 us -> 218 us (1.043)
  Pallas kernels: 68.4 us -> 77.6 us
    pallas_call x9, Pallas kernels: 55 us -> 64 us  [steer(): pl.pallas_call(functools.partial(steer_kernel, along=along, whole=[whole...]
  transfers between devices with their start and end apart: 12 -> 12, of which waited for: 0 -> 0; matrix products, arithmetic and copies ran while one was open for 0% -> 0% of each run, Pallas kernels for 24% -> 26%
where the time goes in v12:
time: 218 us; the launch traced here: 217 us
  blocking collectives  102 us (47%)
  Pallas kernels  77.6 us (36%)
  starting transfers between devices  37.1 us (17%)
    all_to_all x1, blocking collectives, on_device(): lax.all_to_all(outgoing, BOTH, split_axis=0, concat_axis=0, tiled=True)  102 us
    pallas_call x9, Pallas kernels, steer(): pl.pallas_call(functools.partial(steer_kernel, along=along, whole=[whole...  64 us
    ppermute x6, starting transfers between devices, swap_ends(): low = lax.ppermute(tail, axis, [(i, i + 1) for i in range(count - 1)])  22.6 us
    ppermute x6, starting transfers between devices, swap_ends(): high = lax.ppermute(head, axis, [(i + 1, i) for i in range(count - 1)])  14.5 us
    pallas_call x1, Pallas kernels, stack_bins(): pl.pallas_call(functools.partial(bin_kernel, capacity=capacity, block_row...  7.47 us
    pallas_call x1, Pallas kernels, pack(): pl.pallas_call(functools.partial(pack_kernel, capacity=capacity), in_spec...  6.12 us
  transfers between devices with their start and end apart: 12, of which 0 were waited for; matrix products, arithmetic and copies ran while one was open for 0% of the time, Pallas kernels for 26%

profile of v12, /device:TPU:11, one launch (start us, length us, event | category | flops | bytes accessed | tf_op | source)
XLA Modules:
  0.0 216.8 jit_solution(17941406896178042578)
XLA Ops:
  0.0 6.1 %shard_map.55 = f32[32,264,128]{2,1,0:T(8,128)} custom-call(s32[1]{0:T(128)} %bitcast.mine_ref, s32[128]{0:T(128)} %bitcast.4, s32[4,128]{1,0:T(4,128)} %bitcast.3, f32[128,4,1024]{2,1,0:T(4,128)} %traces_ref.1), custom_call_target="tpu_custom_call" | custom-call | tf_op jit(solution)/shard_map/pallas_call | solution.py:134
  6.1 101.7 %all_to_all.5.blocks_ref = f32[32,264,128]{2,1,0:T(8,128)S(1)} all-to-all(f32[32,264,128]{2,1,0:T(8,128)} %shard_map.55), channel_id=1, replica_groups=mesh['inline'=8,'crosslin'=4] {'inline','crosslin'}, dimensions={0} | all-to-all | bytes 8650752 | tf_op jit(solution)/shard_map/all_to_all | solution.py:635
  107.8 0.0 copy-start
  107.8 7.5 %shard_map.56 = (f32[32,32,8,128]{3,2,1,0:T(8,128)S(1)}, f32[7,16,8,128]{3,2,1,0:T(8,128)S(1)}, f32[7,16,8,128]{3,2,1,0:T(8,128)S(1)}, f32[7,16,8,128]{3,2,1,0:T(8,128)S(1)}, f32[7,16,8,128]{3,2,1,0:T(8,128)S(1)}) custom-call(f32[32,264,128]{2,1,0:T(8,128)S(1)} %all_to_all.5.blocks_ref), custom_call_target="tpu_custom_call" | custom-call | tf_op jit(solution)/shard_map/pallas_call | solution.py:243
  115.3 3.9 %collective-permute-start = (f32[7,16,8,128]{3,2,1,0:T(8,128)S(1)}, f32[7,16,8,128]{3,2,1,0:T(8,128)S(1)}, u32[]{:S(2)}, u32[]{:S(2)}) collective-permute-start(f32[7,16,8,128]{3,2,1,0:T(8,128)S(1)} %get-tuple-element.22), channel_id=1, source_target_pairs={{0,4},{4,8},{8,12},{12,16},{16,20},{20,24},{24,28},{1,5},{5,9},{9,... | collective-permute-start | bytes 1376264 | tf_op jit(solution)/shard_map/ppermute | solution.py:518
  119.2 1.9 collective-permute-start.1
  121.1 4.5 %collective-permute-start.3 = (f32[7,16,8,128]{3,2,1,0:T(8,128)S(1)}, f32[7,16,8,128]{3,2,1,0:T(8,128)S(1)}, u32[]{:S(2)}, u32[]{:S(2)}) collective-permute-start(f32[7,16,8,128]{3,2,1,0:T(8,128)S(1)} %get-tuple-element.28), channel_id=1, source_target_pairs={{0,4},{4,8},{8,12},{12,16},{16,20},{20,24},{24,28},{1,5},{5,9},{9,... | collective-permute-start | bytes 1376264 | tf_op jit(solution)/shard_map/ppermute | solution.py:518
  125.7 1.9 collective-permute-start.4
  127.6 0.0 copy-done
  127.6 8.5 %shard_map.57 = (f32[16,32,8,128]{3,2,1,0:T(8,128)S(1)}, f32[16,7,8,128]{3,2,1,0:T(8,128)S(1)}, f32[16,7,8,128]{3,2,1,0:T(8,128)S(1)}) custom-call(s32[32,32]{1,0:T(8,128)S(1)} %copy-done, f32[32,32,8,128]{3,2,1,0:T(8,128)S(1)} %get-tuple-element.23.refs_0_.refs_1_), custom_call_target="tpu_custom_call" | custom-call | flops 1258291200 | bytes 4194304 | tf_op jit(solution)/shard_map/pallas_call | solution.py:496
  136.1 1.9 collective-permute-start.6
  138.1 0.0 collective-permute-done.refs_0_
  138.1 3.4 %collective-permute-start.7 = (f32[16,7,8,128]{3,2,1,0:T(8,128)S(1)}, f32[16,7,8,128]{3,2,1,0:T(8,128)S(1)}, u32[]{:S(2)}, u32[]{:S(2)}) collective-permute-start(f32[16,7,8,128]{3,2,1,0:T(8,128)S(1)} %get-tuple-element.33), channel_id=1, source_target_pairs={{1,0},{2,1},{3,2},{5,4},{6,5},{7,6},{9,8},{10,9},{11,10},{13,12},{... | collective-permute-start | bytes 1376264 | tf_op jit(solution)/shard_map/ppermute | solution.py:519
  141.5 0.0 collective-permute-done.1.refs_2_
  141.5 5.5 %shard_map.58 = (f32[16,16,8,128]{3,2,1,0:T(8,128)S(1)}, f32[16,7,8,128]{3,2,1,0:T(8,128)S(1)}, f32[16,7,8,128]{3,2,1,0:T(8,128)S(1)}) custom-call(s32[32,32]{1,0:T(8,128)S(1)} %copy-done, f32[7,16,8,128]{3,2,1,0:T(8,128)S(1)} %collective-permute-done.refs_0_, f32[32,32,8,128]{3,2,1,0:T(8,128)S(1)} %get-tuple-element.23.refs_0_.refs_1_, ...), custom_call_target="tpu_custom_call" | custom-call | flops 629145600 | bytes 2097152 | tf_op jit(solution)/shard_map/pallas_call | solution.py:496
  147.0 0.0 copy-start.1
  147.0 2.0 collective-permute-start.2
  149.0 0.0 collective-permute-done.3.refs_0_
  149.0 3.3 %collective-permute-start.5 = (f32[16,7,8,128]{3,2,1,0:T(8,128)S(1)}, f32[16,7,8,128]{3,2,1,0:T(8,128)S(1)}, u32[]{:S(2)}, u32[]{:S(2)}) collective-permute-start(f32[16,7,8,128]{3,2,1,0:T(8,128)S(1)} %get-tuple-element.30), channel_id=1, source_target_pairs={{1,0},{2,1},{3,2},{5,4},{6,5},{7,6},{9,8},{10,9},{11,10},{13,12},{... | collective-permute-start | bytes 1376264 | tf_op jit(solution)/shard_map/ppermute | solution.py:519
  152.3 0.0 collective-permute-done.4.refs_2_
  152.3 5.4 %shard_map.59.refs_1_.refs_2_ = f32[16,16,8,128]{3,2,1,0:T(8,128)S(1)} custom-call(s32[32,32]{1,0:T(8,128)S(1)} %copy-done, f32[7,16,8,128]{3,2,1,0:T(8,128)S(1)} %collective-permute-done.3.refs_0_, f32[32,32,8,128]{3,2,1,0:T(8,128)S(1)} %get-tuple-element.23.refs_0_.refs_1_, f32[7,16,8,128]{3,2,1,0:T(8,128)S(1)} %collective-permute-done.4.refs_2_, ...), custom_call_target="tpu_custom_call" | custom-call | flops 629145600 | bytes 2097152 | tf_op jit(solution)/shard_map/pallas_call | solution.py:496
  157.8 0.0 copy-done.1
  157.8 5.2 %shard_map.60 = (f32[16,16,8,128]{3,2,1,0:T(8,128)S(1)}, f32[7,16,8,128]{3,2,1,0:T(8,128)S(1)}, f32[7,16,8,128]{3,2,1,0:T(8,128)S(1)}) custom-call(s32[32,32]{1,0:T(8,128)S(1)} %copy-done.1, f32[16,16,8,128]{3,2,1,0:T(8,128)S(1)} %get-tuple-element.27.refs_3_.refs_0_.refs_1_, f32[16,16,8,128]{3,2,1,0:T(8,128)S(1)} %shard_map.59.refs_1_.refs_2_), custom_call_target="tpu_custom_call" | custom-call | flops 629145600 | bytes 2097152 | tf_op jit(solution)/shard_map/pallas_call | solution.py:496
  163.0 5.7 %collective-permute-start.10 = (f32[7,16,8,128]{3,2,1,0:T(8,128)S(1)}, f32[7,16,8,128]{3,2,1,0:T(8,128)S(1)}, u32[]{:S(2)}, u32[]{:S(2)}) collective-permute-start(f32[7,16,8,128]{3,2,1,0:T(8,128)S(1)} %get-tuple-element.37), channel_id=1, source_target_pairs={{0,4},{4,8},{8,12},{12,16},{16,20},{20,24},{24,28},{1,5},{5,9},{9,... | collective-permute-start | bytes 1376264 | tf_op jit(solution)/shard_map/ppermute | solution.py:518
  168.7 0.0 collective-permute-done.6.refs_0_
  168.7 1.9 collective-permute-start.11
  170.6 0.0 collective-permute-done.7.refs_2_
  170.6 8.4 %shard_map.61.refs_5_.refs_1_.refs_2_ = f32[16,32,8,128]{3,2,1,0:T(8,128)S(1)} custom-call(s32[32,32]{1,0:T(8,128)S(1)} %copy-done.1, f32[16,7,8,128]{3,2,1,0:T(8,128)S(1)} %collective-permute-done.6.refs_0_, f32[16,32,8,128]{3,2,1,0:T(8,128)S(1)} %get-tuple-element.25.refs_3_.refs_1_, f32[16,7,8,128]{3,2,1,0:T(8,128)S(1)} %collective-permute-done.7.refs_2_, ...), custom_call_target="tpu_custom_call" | custom-call | flops 1258291200 | bytes 4194304 | tf_op jit(solution)/shard_map/pallas_call | solution.py:496
  179.0 0.0 collective-permute-done.2.refs_0_
  179.0 0.0 collective-permute-done.5.refs_3_
  179.0 5.7 %shard_map.62 = (f32[16,32,8,128]{3,2,1,0:T(8,128)S(1)}, f32[7,16,8,128]{3,2,1,0:T(8,128)S(1)}, f32[7,16,8,128]{3,2,1,0:T(8,128)S(1)}) custom-call(s32[32,32]{1,0:T(8,128)S(1)} %copy-done.1, f32[16,7,8,128]{3,2,1,0:T(8,128)S(1)} %collective-permute-done.2.refs_0_, f32[16,16,8,128]{3,2,1,0:T(8,128)S(1)} %get-tuple-element.27.refs_3_.refs_0_.refs_1_, ...), custom_call_target="tpu_custom_call" | custom-call | flops 629145600 | bytes 2097152 | tf_op jit(solution)/shard_map/pallas_call | solution.py:496
  184.8 4.5 %collective-permute-start.8 = (f32[7,16,8,128]{3,2,1,0:T(8,128)S(1)}, f32[7,16,8,128]{3,2,1,0:T(8,128)S(1)}, u32[]{:S(2)}, u32[]{:S(2)}) collective-permute-start(f32[7,16,8,128]{3,2,1,0:T(8,128)S(1)} %get-tuple-element.34), channel_id=1, source_target_pairs={{0,4},{4,8},{8,12},{12,16},{16,20},{20,24},{24,28},{1,5},{5,9},{9,... | collective-permute-start | bytes 1376264 | tf_op jit(solution)/shard_map/ppermute | solution.py:518
  189.3 2.1 collective-permute-start.9
  191.4 10.8 %shard_map.63.refs_4_ = f32[32,32,1024]{2,1,0:T(8,128)} custom-call(s32[32,32]{1,0:T(8,128)S(1)} %copy-done, f32[16,32,8,128]{3,2,1,0:T(8,128)S(1)} %get-tuple-element.35.refs_0_.refs_1_, f32[16,32,8,128]{3,2,1,0:T(8,128)S(1)} %shard_map.61.refs_5_.refs_1_.refs_2_), custom_call_target="tpu_custom_call" | custom-call | flops 1258291200 | bytes 4194304 | tf_op jit(solution)/shard_map/pallas_call | solution.py:496
  202.2 0.0 collective-permute-done.10.refs_0_
  202.2 0.0 collective-permute-done.11.refs_3_
  202.3 7.2 %shard_map.64.refs_4_ = f32[32,32,1024]{2,1,0:T(8,128)} custom-call(s32[32,32]{1,0:T(8,128)S(1)} %copy-done, f32[7,16,8,128]{3,2,1,0:T(8,128)S(1)} %collective-permute-done.10.refs_0_, f32[16,32,8,128]{3,2,1,0:T(8,128)S(1)} %get-tuple-element.35.refs_0_.refs_1_, ...), custom_call_target="tpu_custom_call", output_to_operand_aliasing={{}: (5, {})} | custom-call | flops 629145600 | bytes 2097152 | tf_op jit(solution)/shard_map/pallas_call | solution.py:496
  209.5 0.0 collective-permute-done.8.refs_0_
  209.5 0.0 collective-permute-done.9.refs_3_
  209.5 7.2 %shard_map.65 = f32[32,32,1024]{2,1,0:T(8,128)} custom-call(s32[32,32]{1,0:T(8,128)S(1)} %copy-done, f32[7,16,8,128]{3,2,1,0:T(8,128)S(1)} %collective-permute-done.8.refs_0_, f32[16,32,8,128]{3,2,1,0:T(8,128)S(1)} %get-tuple-element.35.refs_0_.refs_1_, f32[16,32,8,128]{3,2,1,0:T(8,128)S(1)} %shard_map.61.refs_5_.refs_1_.refs_2_, ...), custom_call_target="tpu_custom_call", output_to_operand_aliasing={{}: (5, {})} | custom-call | flops 629145600 | bytes 2097152 | tf_op jit(solution)/shard_map/pallas_call | solution.py:496
Async XLA Ops:
  107.8 19.8 %copy-start = (s32[32,32]{1,0:T(8,128)S(1)}, s32[32,32]{1,0:T(8,128)}, u32[]{:S(2)}) copy-start(s32[32,32]{1,0:T(8,128)} %dip_ref.17) | copy-start | bytes 12292
  115.3 22.8 %collective-permute-start = (f32[7,16,8,128]{3,2,1,0:T(8,128)S(1)}, f32[7,16,8,128]{3,2,1,0:T(8,128)S(1)}, u32[]{:S(2)}, u32[]{:S(2)}) collective-permute-start(f32[7,16,8,128]{3,2,1,0:T(8,128)S(1)} %get-tuple-element.22), channel_id=1, source_target_pairs={{0,4},{4,8},{8,12},{12,16},{16,20},{20,24},{24,28},{1,5},{5,9},{9,... | collective-permute-start | bytes 1376264 | tf_op jit(solution)/shard_map/ppermute | solution.py:518
  119.2 22.3 %collective-permute-start.1 = (f32[7,16,8,128]{3,2,1,0:T(8,128)S(1)}, f32[7,16,8,128]{3,2,1,0:T(8,128)S(1)}, u32[]{:S(2)}, u32[]{:S(2)}) collective-permute-start(f32[7,16,8,128]{3,2,1,0:T(8,128)S(1)} %get-tuple-element.24), channel_id=1, source_target_pairs={{4,0},{8,4},{12,8},{16,12},{20,16},{24,20},{28,24},{5,1},{9,5},{13... | collective-permute-start | bytes 1376264 | tf_op jit(solution)/shard_map/ppermute | solution.py:519
  121.1 27.9 %collective-permute-start.3 = (f32[7,16,8,128]{3,2,1,0:T(8,128)S(1)}, f32[7,16,8,128]{3,2,1,0:T(8,128)S(1)}, u32[]{:S(2)}, u32[]{:S(2)}) collective-permute-start(f32[7,16,8,128]{3,2,1,0:T(8,128)S(1)} %get-tuple-element.28), channel_id=1, source_target_pairs={{0,4},{4,8},{8,12},{12,16},{16,20},{20,24},{24,28},{1,5},{5,9},{9,... | collective-permute-start | bytes 1376264 | tf_op jit(solution)/shard_map/ppermute | solution.py:518
  125.7 26.7 %collective-permute-start.4 = (f32[7,16,8,128]{3,2,1,0:T(8,128)S(1)}, f32[7,16,8,128]{3,2,1,0:T(8,128)S(1)}, u32[]{:S(2)}, u32[]{:S(2)}) collective-permute-start(f32[7,16,8,128]{3,2,1,0:T(8,128)S(1)} %get-tuple-element.29), channel_id=1, source_target_pairs={{4,0},{8,4},{12,8},{16,12},{20,16},{24,20},{28,24},{5,1},{9,5},{13... | collective-permute-start | bytes 1376264 | tf_op jit(solution)/shard_map/ppermute | solution.py:519
  136.1 32.6 %collective-permute-start.6 = (f32[16,7,8,128]{3,2,1,0:T(8,128)S(1)}, f32[16,7,8,128]{3,2,1,0:T(8,128)S(1)}, u32[]{:S(2)}, u32[]{:S(2)}) collective-permute-start(f32[16,7,8,128]{3,2,1,0:T(8,128)S(1)} %get-tuple-element.32), channel_id=1, source_target_pairs={{0,1},{1,2},{2,3},{4,5},{5,6},{6,7},{8,9},{9,10},{10,11},{12,13},{... | collective-permute-start | bytes 1376264 | tf_op jit(solution)/shard_map/ppermute | solution.py:518
  138.1 32.6 %collective-permute-start.7 = (f32[16,7,8,128]{3,2,1,0:T(8,128)S(1)}, f32[16,7,8,128]{3,2,1,0:T(8,128)S(1)}, u32[]{:S(2)}, u32[]{:S(2)}) collective-permute-start(f32[16,7,8,128]{3,2,1,0:T(8,128)S(1)} %get-tuple-element.33), channel_id=1, source_target_pairs={{1,0},{2,1},{3,2},{5,4},{6,5},{7,6},{9,8},{10,9},{11,10},{13,12},{... | collective-permute-start | bytes 1376264 | tf_op jit(solution)/shard_map/ppermute | solution.py:519
  147.0 10.8 %copy-start.1 = (s32[32,32]{1,0:T(8,128)S(1)}, s32[32,32]{1,0:T(8,128)}, u32[]{:S(2)}) copy-start(s32[32,32]{1,0:T(8,128)} %dip_ref.14) | copy-start | bytes 12292
  147.0 32.0 %collective-permute-start.2 = (f32[16,7,8,128]{3,2,1,0:T(8,128)S(1)}, f32[16,7,8,128]{3,2,1,0:T(8,128)S(1)}, u32[]{:S(2)}, u32[]{:S(2)}) collective-permute-start(f32[16,7,8,128]{3,2,1,0:T(8,128)S(1)} %get-tuple-element.26), channel_id=1, source_target_pairs={{0,1},{1,2},{2,3},{4,5},{5,6},{6,7},{8,9},{9,10},{10,11},{12,13},{... | collective-permute-start | bytes 1376264 | tf_op jit(solution)/shard_map/ppermute | solution.py:518
  149.0 30.0 %collective-permute-start.5 = (f32[16,7,8,128]{3,2,1,0:T(8,128)S(1)}, f32[16,7,8,128]{3,2,1,0:T(8,128)S(1)}, u32[]{:S(2)}, u32[]{:S(2)}) collective-permute-start(f32[16,7,8,128]{3,2,1,0:T(8,128)S(1)} %get-tuple-element.30), channel_id=1, source_target_pairs={{1,0},{2,1},{3,2},{5,4},{6,5},{7,6},{9,8},{10,9},{11,10},{13,12},{... | collective-permute-start | bytes 1376264 | tf_op jit(solution)/shard_map/ppermute | solution.py:519
  163.0 39.2 %collective-permute-start.10 = (f32[7,16,8,128]{3,2,1,0:T(8,128)S(1)}, f32[7,16,8,128]{3,2,1,0:T(8,128)S(1)}, u32[]{:S(2)}, u32[]{:S(2)}) collective-permute-start(f32[7,16,8,128]{3,2,1,0:T(8,128)S(1)} %get-tuple-element.37), channel_id=1, source_target_pairs={{0,4},{4,8},{8,12},{12,16},{16,20},{20,24},{24,28},{1,5},{5,9},{9,... | collective-permute-start | bytes 1376264 | tf_op jit(solution)/shard_map/ppermute | solution.py:518
  168.7 33.6 %collective-permute-start.11 = (f32[7,16,8,128]{3,2,1,0:T(8,128)S(1)}, f32[7,16,8,128]{3,2,1,0:T(8,128)S(1)}, u32[]{:S(2)}, u32[]{:S(2)}) collective-permute-start(f32[7,16,8,128]{3,2,1,0:T(8,128)S(1)} %get-tuple-element.38), channel_id=1, source_target_pairs={{4,0},{8,4},{12,8},{16,12},{20,16},{24,20},{28,24},{5,1},{9,5},{13... | collective-permute-start | bytes 1376264 | tf_op jit(solution)/shard_map/ppermute | solution.py:519
  184.8 24.7 %collective-permute-start.8 = (f32[7,16,8,128]{3,2,1,0:T(8,128)S(1)}, f32[7,16,8,128]{3,2,1,0:T(8,128)S(1)}, u32[]{:S(2)}, u32[]{:S(2)}) collective-permute-start(f32[7,16,8,128]{3,2,1,0:T(8,128)S(1)} %get-tuple-element.34), channel_id=1, source_target_pairs={{0,4},{4,8},{8,12},{12,16},{16,20},{20,24},{24,28},{1,5},{5,9},{9,... | collective-permute-start | bytes 1376264 | tf_op jit(solution)/shard_map/ppermute | solution.py:518
  189.3 20.2 %collective-permute-start.9 = (f32[7,16,8,128]{3,2,1,0:T(8,128)S(1)}, f32[7,16,8,128]{3,2,1,0:T(8,128)S(1)}, u32[]{:S(2)}, u32[]{:S(2)}) collective-permute-start(f32[7,16,8,128]{3,2,1,0:T(8,128)S(1)} %get-tuple-element.36), channel_id=1, source_target_pairs={{4,0},{8,4},{12,8},{16,12},{20,16},{24,20},{28,24},{5,1},{9,5},{13... | collective-permute-start | bytes 1376264 | tf_op jit(solution)/shard_map/ppermute | solution.py:519

commit v13 on v11

--- a/solution.py
+++ b/solution.py
@@ -62,7 +62,7 @@
     return tiles
 
 
-def pack_kernel(mine_ref, target_ref, bins_ref, traces_ref, out_ref, held_ref, table_ref, tiles_ref, used_ref, listed_ref, in_sems, sem, listed_sem, *, capacity):
+def pack_kernel(mine_ref, target_ref, bins_ref, traces_ref, out_ref, held_ref, table_ref, tiles_ref, used_ref, rank_ref, listed_ref, in_sems, sem, listed_sem, *, capacity):
     held, block_rows, samples = traces_ref.shape
     devices, room, _ = listed_ref.shape
     span = block_rows * PHASES
@@ -85,19 +85,29 @@
 
     lax.fori_loop(0, devices, clear, 0)
 
-    def send_block(block, _):
+    def choose_slot(block, _):
         device = target_ref[block]
         rank = used_ref[device]
         used_ref[device] = rank + 1
-        pltpu.make_async_copy(
-            tiles_ref.at[pl.ds(pl.multiple_of(block * span, 8), span), :],
-            out_ref.at[device, pl.ds(pl.multiple_of(rank * span, 8), span), :],
-            sem,
-        ).start()
+        rank_ref[block] = rank
         row = jnp.zeros((1, LANES), I32)
         for j in range(block_rows):
             row = jnp.where(lane == own_lanes + rank * block_rows + j, bins_ref[j, block] + 1, row)
         listed_ref[device, 0:1, :] = listed_ref[device, 0:1, :] + row.astype(F32)
+        return 0
+
+    lax.fori_loop(0, held, choose_slot, 0, unroll=4)
+    lists = pltpu.make_async_copy(
+        listed_ref, out_ref.at[:, capacity * span : capacity * span + room, :], listed_sem
+    )
+    lists.start()
+
+    def send_block(block, _):
+        pltpu.make_async_copy(
+            tiles_ref.at[pl.ds(pl.multiple_of(block * span, 8), span), :],
+            out_ref.at[target_ref[block], pl.ds(pl.multiple_of(rank_ref[block] * span, 8), span), :],
+            sem,
+        ).start()
         return 0
 
     for group in range(groups):
@@ -116,11 +126,7 @@
                     first = (group * count * block_rows + eight * 8) * PHASES + half * 4 + phase
                     tiles_ref[pl.ds(first, 8, stride=PHASES), :] = part
         lax.fori_loop(group * count, (group + 1) * count, send_block, 0, unroll=4)
-    copy = pltpu.make_async_copy(
-        listed_ref, out_ref.at[:, capacity * span : capacity * span + room, :], listed_sem
-    )
-    copy.start()
-    copy.wait()
+    lists.wait()
     pltpu.make_async_copy(tiles_ref, tiles_ref, sem).wait()
 
 
@@ -139,6 +145,7 @@
             pltpu.VMEM((WIDE, WIDE), BF16),
             pltpu.VMEM((held * span, LANES), F32),
             pltpu.SMEM((devices,), I32),
+            pltpu.SMEM((held,), I32),
             pltpu.VMEM((devices, room, LANES), F32),
             pltpu.SemaphoreType.DMA((groups,)),
             pltpu.SemaphoreType.DMA,
@@ -212,7 +219,7 @@
 
     lax.fori_loop(0, HALF, finish, 0)
     lax.fori_loop(tile_rows - HALF, tile_rows, finish, 0)
-    copies = edge_copies(out_ref, edges, edge_refs, sems)
+    copies = edge_copies(out_ref, (), edges, edge_refs, sems)
     for copy in copies:
         copy.start()
     lax.fori_loop(HALF, tile_rows - HALF, finish, 0)
@@ -220,11 +227,12 @@
         copy.wait()
 
 
-def edge_copies(out_ref, edges, edge_refs, sems):
+def edge_copies(out_ref, pieces, edges, edge_refs, sems):
     copies = []
     for (_, moves), edge_ref in zip(edges, edge_refs):
-        for source, target in moves:
-            copies.append(pltpu.make_async_copy(out_ref.at[source], edge_ref.at[target], sems.at[len(copies)]))
+        for source, target, *piece in moves:
+            from_ref = pieces[piece[0]] if piece else out_ref
+            copies.append(pltpu.make_async_copy(from_ref.at[source], edge_ref.at[target], sems.at[len(copies)]))
     return copies
 
 
@@ -300,11 +308,7 @@
                     axis=1,
                 )
             )
-    half = len(taps) // 2
-    return [
-        jnp.dot(jnp.concatenate(part, axis=0), halves_ref[...], preferred_element_type=F32)
-        for part in (taps[:half], taps[half:])
-    ]
+    return jnp.dot(jnp.concatenate(taps, axis=0), halves_ref[...], preferred_element_type=F32)
 
 
 def move_lanes(sums, first, count, put):
@@ -313,10 +317,10 @@
         for member in range(2):
             total = None
             for reach in REACHES:
-                which, begin = divmod((pair * len(REACHES) + reach + REACH) * PAIR + member * PHASES, sums[0].shape[0])
-                part = sums[which][begin : begin + PHASES, :LANES] + sums[which][begin : begin + PHASES, LANES:]
+                begin = (pair * len(REACHES) + reach + REACH) * PAIR + member * PHASES
+                part = sums[begin : begin + PHASES, :LANES] + sums[begin : begin + PHASES, LANES:]
                 if reach:
-                    part = take_lanes(part, (lane + reach) & (LANES - 1))
+                    part = pltpu.roll(part, (-reach) % LANES, axis=1)
                     inside = lane < LANES - reach if reach > 0 else lane >= -reach
                     part = jnp.where(inside, part, 0.0)
                 total = part if total is None else total + part
@@ -380,7 +384,7 @@
         lax.fori_loop(0, lines // abreast, some_lines, 0)
         if filled is not None:
             fill.wait()
-        copies = edge_copies(out_ref, edges, edge_refs, sems)
+        copies = edge_copies(out_ref, pieces, edges, edge_refs, sems)
         for copy in copies:
             copy.start()
         for copy in copies:
@@ -542,21 +546,31 @@
     low_out, high_out = swap_ends(head_out, tail_out, "inline")
     low_mid, high_mid = swap_ends(head_mid, tail_mid, "inline")
 
-    middle, head, tail = steer(
+    (middle,) = steer(
         dip_inline, [(stacked, True)], 0, cols, same,
         mid_windows(span_of(0, BORDER - HALF, mid_rows + 2 * HALF), rows), mid_place,
-        edges=[whole_edge((mid_rows, HALF), (every, lead)), whole_edge((mid_rows, HALF), (every, rows_of(cols - HALF, HALF)))],
-    )
-    left_mid, right_mid = swap_ends(head, tail, "crosslin")
+    )
     windows = [
         (0, BORDER, span_of(0, 0, HALF) + span_of(1, 0, BORDER + HALF)),
         (rows - BORDER, BORDER, span_of(1, rows - BORDER - HALF, BORDER + HALF) + span_of(2, 0, HALF)),
     ]
+    top, bottom, between = rows_of(0, BORDER), rows_of(rows - BORDER, BORDER), rows_of(BORDER, mid_rows)
+
+    def column_edge(outer, whole):
+        return (
+            (rows, HALF),
+            [
+                ((rows_of(0, BORDER), outer), (top, every)),
+                ((rows_of(BORDER, BORDER), outer), (bottom, every)),
+                ((every, whole), (between, every), 3),
+            ],
+        )
+
     corners, head, tail = steer(
-        dip_inline, [(low_out, False), (stacked, True), (high_out, False)], 0, both, outer_col, windows, outer_place,
-        edges=[whole_edge((both, HALF), (every, lead)), whole_edge((both, HALF), (every, last))], after=middle,
-    )
-    left_out, right_out = swap_ends(head, tail, "crosslin")
+        dip_inline, [(low_out, False), (stacked, True), (high_out, False), (middle, False)], 0, both, outer_col,
+        windows, outer_place, edges=[column_edge(lead, lead), column_edge(last, rows_of(cols - HALF, HALF))],
+    )
+    west, east = swap_ends(head, tail, "crosslin")
     (flanks,) = steer(
         dip_inline, [(low_mid, False), (stacked, True), (high_mid, False)], 0, mid_cols, inner, windows, outer_place,
         after=corners,
@@ -568,10 +582,9 @@
         edges=[whole_edge((HALF, mid_cols), (lead, every)), whole_edge((HALF, mid_cols), (last, every))],
     )
     low_mid, high_mid = swap_ends(head, tail, "inline")
-    places = span_of(0, 0, HALF) + span_of(1, 0, cols) + span_of(2, 0, HALF)
-    (middle_second,) = steer(
-        dip_cross, [(left_mid, False), (middle, False), (right_mid, False)], 1, mid_rows, inner,
-        [(i, WINDOW, places[i : i + WINDOW + 2 * HALF]) for i in range(0, cols, WINDOW)], same, after=second_mid,
+    (centre,) = steer(
+        dip_cross, [(middle, False)], 1, mid_rows, inner,
+        mid_windows(span_of(0, BORDER - HALF, mid_cols + 2 * HALF), cols), mid_place, after=second_mid,
     )
     windows = [
         (0, BORDER, span_of(0, 0, HALF) + span_of(1, 0, BORDER) + span_of(2, 0, HALF)),
@@ -579,11 +592,19 @@
     ]
     border_second, head, tail = steer(
         dip_cross,
-        [(left_out, False), (corners, False), (flanks, False), (right_out, False), (second_mid, False)],
+        [(west, True), (corners, False), (flanks, False), (east, True), (second_mid, False)],
         1, both, outer_row, windows, same, filled=(4, (every, middle_cols)),
-        edges=[outer_edge(lead), outer_edge(last)], after=middle_second,
+        edges=[outer_edge(lead), outer_edge(last)], after=centre,
     )
     low_out, high_out = swap_ends(head, tail, "inline")
+    windows = [
+        (0, BORDER, span_of(0, 0, HALF) + span_of(1, 0, BORDER + HALF)),
+        (cols - BORDER, BORDER, span_of(1, cols - BORDER - HALF, BORDER + HALF) + span_of(2, 0, HALF)),
+    ]
+    (middle_second,) = steer(
+        dip_cross, [(west, True), (middle, False), (east, True), (centre, False)], 1, mid_rows, inner, windows, same,
+        filled=(3, (every, middle_cols)), after=border_second,
+    )
 
     places = span_of(0, BORDER - HALF, HALF) + span_of(1, 0, mid_rows) + span_of(0, BORDER, HALF)
     (result,) = steer(

time: 209 us -> 200 us (0.957)
  waiting for transfers between devices: 0.03 us -> 12.1 us
  starting transfers between devices: 36.8 us -> 26.1 us
  Pallas kernels: 68.4 us -> 58.8 us
    pallas_call x9 -> x10, Pallas kernels: 55 us -> 46 us  [steer(): pl.pallas_call(functools.partial(steer_kernel, along=along, whole=[whole...]
    ppermute x6 -> x5, starting transfers between devices: 23.4 us -> 14.4 us  [swap_ends(): low = lax.ppermute(tail, axis, [(i, i + 1) for i in range(count - 1)])]
    ppermute x6 -> x5, waiting for transfers between devices: 0.02 us -> 7.09 us  [swap_ends(): high = lax.ppermute(head, axis, [(i + 1, i) for i in range(count - 1)])]
    ppermute x6 -> x5, waiting for transfers between devices: 0.02 us -> 5.04 us  [swap_ends(): low = lax.ppermute(tail, axis, [(i, i + 1) for i in range(count - 1)])]
    ppermute x6 -> x5, starting transfers between devices: 13.5 us -> 11.8 us  [swap_ends(): high = lax.ppermute(head, axis, [(i + 1, i) for i in range(count - 1)])]
  transfers between devices with their start and end apart: 12 -> 10, of which waited for: 0 -> 3; matrix products, arithmetic and copies ran while one was open for 0% -> 0% of each run, Pallas kernels for 24% -> 19%
where the time goes in v13:
time: 200 us; the launch traced here: 199 us
  blocking collectives  102 us (51%)
  Pallas kernels  58.8 us (29%)
  starting transfers between devices  26.1 us (13%)
  waiting for transfers between devices  12.1 us (6%)
    all_to_all x1, blocking collectives, on_device(): lax.all_to_all(outgoing, BOTH, split_axis=0, concat_axis=0, tiled=True)  102 us
    pallas_call x10, Pallas kernels, steer(): pl.pallas_call(functools.partial(steer_kernel, along=along, whole=[whole...  46 us
    ppermute x5, starting transfers between devices, swap_ends(): low = lax.ppermute(tail, axis, [(i, i + 1) for i in range(count - 1)])  14.4 us
    ppermute x5, starting transfers between devices, swap_ends(): high = lax.ppermute(head, axis, [(i + 1, i) for i in range(count - 1)])  11.8 us
    pallas_call x1, Pallas kernels, stack_bins(): pl.pallas_call(functools.partial(bin_kernel, capacity=capacity, block_row...  7.4 us
    ppermute x5, waiting for transfers between devices, swap_ends(): high = lax.ppermute(head, axis, [(i + 1, i) for i in range(count - 1)])  7.09 us
    pallas_call x1, Pallas kernels, pack(): pl.pallas_call(functools.partial(pack_kernel, capacity=capacity), in_spec...  5.44 us
    ppermute x5, waiting for transfers between devices, swap_ends(): low = lax.ppermute(tail, axis, [(i, i + 1) for i in range(count - 1)])  5.04 us
  transfers between devices with their start and end apart: 10, of which 3 were waited for; matrix products, arithmetic and copies ran while one was open for 0% of the time, Pallas kernels for 19%

profile of v13, /device:TPU:11, one launch (start us, length us, event | category | flops | bytes accessed | tf_op | source)
XLA Modules:
  0.0 199.2 jit_solution(9733893345982757772)
XLA Ops:
  0.0 5.4 %shard_map.55 = f32[32,264,128]{2,1,0:T(8,128)} custom-call(s32[1]{0:T(128)} %bitcast.mine_ref, s32[128]{0:T(128)} %bitcast.4, s32[4,128]{1,0:T(4,128)} %bitcast.3, f32[128,4,1024]{2,1,0:T(4,128)} %traces_ref.1), custom_call_target="tpu_custom_call" | custom-call | tf_op jit(solution)/shard_map/pallas_call | solution.py:138
  5.5 101.7 %all_to_all.5.blocks_ref = f32[32,264,128]{2,1,0:T(8,128)S(1)} all-to-all(f32[32,264,128]{2,1,0:T(8,128)} %shard_map.55), channel_id=1, replica_groups=mesh['inline'=8,'crosslin'=4] {'inline','crosslin'}, dimensions={0} | all-to-all | bytes 8650752 | tf_op jit(solution)/shard_map/all_to_all | solution.py:635
  107.1 0.0 copy-start
  107.1 7.4 %shard_map.56 = (f32[32,32,8,128]{3,2,1,0:T(8,128)S(1)}, f32[7,16,8,128]{3,2,1,0:T(8,128)S(1)}, f32[7,16,8,128]{3,2,1,0:T(8,128)S(1)}, f32[7,16,8,128]{3,2,1,0:T(8,128)S(1)}, f32[7,16,8,128]{3,2,1,0:T(8,128)S(1)}) custom-call(f32[32,264,128]{2,1,0:T(8,128)S(1)} %all_to_all.5.blocks_ref), custom_call_target="tpu_custom_call" | custom-call | tf_op jit(solution)/shard_map/pallas_call | solution.py:249
  114.5 4.0 %collective-permute-start = (f32[7,16,8,128]{3,2,1,0:T(8,128)S(1)}, f32[7,16,8,128]{3,2,1,0:T(8,128)S(1)}, u32[]{:S(2)}, u32[]{:S(2)}) collective-permute-start(f32[7,16,8,128]{3,2,1,0:T(8,128)S(1)} %get-tuple-element.19), channel_id=1, source_target_pairs={{0,4},{4,8},{8,12},{12,16},{16,20},{20,24},{24,28},{1,5},{5,9},{9,... | collective-permute-start | bytes 1376264 | tf_op jit(solution)/shard_map/ppermute | solution.py:501
  118.5 1.9 collective-permute-start.1
  120.5 0.0 copy-done
  120.5 5.9 %shard_map.57.refs_3_.refs_0_.refs_1_ = f32[16,32,8,128]{3,2,1,0:T(8,128)S(1)} custom-call(s32[32,32]{1,0:T(8,128)S(1)} %copy-done, f32[32,32,8,128]{3,2,1,0:T(8,128)S(1)} %get-tuple-element.20.refs_0_.refs_1_), custom_call_target="tpu_custom_call" | custom-call | flops 1258291200 | bytes 4194304 | tf_op jit(solution)/shard_map/pallas_call | solution.py:479
  126.4 0.0 collective-permute-done.refs_0_
  126.4 3.3 %collective-permute-done.1.refs_2_ = f32[7,16,8,128]{3,2,1,0:T(8,128)S(1)} collective-permute-done((f32[7,16,8,128]{3,2,1,0:T(8,128)S(1)}, f32[7,16,8,128]{3,2,1,0:T(8,128)S(1)}, u32[]{:S(2)}, u32[]{:S(2)}) %collective-permute-start.1) | collective-permute-done | bytes 458784 | tf_op jit(solution)/shard_map/ppermute | solution.py:502
  129.8 3.6 %shard_map.58 = (f32[16,16,8,128]{3,2,1,0:T(8,128)S(1)}, f32[32,7,8,128]{3,2,1,0:T(8,128)S(1)}, f32[32,7,8,128]{3,2,1,0:T(8,128)S(1)}) custom-call(s32[32,32]{1,0:T(8,128)S(1)} %copy-done, f32[7,16,8,128]{3,2,1,0:T(8,128)S(1)} %collective-permute-done.refs_0_, f32[32,32,8,128]{3,2,1,0:T(8,128)S(1)} %get-tuple-element.20.refs_0_.refs_1_, ...), custom_call_target="tpu_custom_call" | custom-call | flops 629145600 | bytes 2097152 | tf_op jit(solution)/shard_map/pallas_call | solution.py:479
  133.4 0.0 copy-start.1
  133.4 1.9 collective-permute-start.2
  135.3 3.4 %collective-permute-start.5 = (f32[32,7,8,128]{3,2,1,0:T(8,128)S(1)}, f32[32,7,8,128]{3,2,1,0:T(8,128)S(1)}, u32[]{:S(2)}, u32[]{:S(2)}) collective-permute-start(f32[32,7,8,128]{3,2,1,0:T(8,128)S(1)} %get-tuple-element.26), channel_id=1, source_target_pairs={{1,0},{2,1},{3,2},{5,4},{6,5},{7,6},{9,8},{10,9},{11,10},{13,12},{... | collective-permute-start | bytes 2752520 | tf_op jit(solution)/shard_map/ppermute | solution.py:502
  138.7 2.5 %collective-permute-start.3 = (f32[7,16,8,128]{3,2,1,0:T(8,128)S(1)}, f32[7,16,8,128]{3,2,1,0:T(8,128)S(1)}, u32[]{:S(2)}, u32[]{:S(2)}) collective-permute-start(f32[7,16,8,128]{3,2,1,0:T(8,128)S(1)} %get-tuple-element.24), channel_id=1, source_target_pairs={{0,4},{4,8},{8,12},{12,16},{16,20},{20,24},{24,28},{1,5},{5,9},{9,... | collective-permute-start | bytes 1376264 | tf_op jit(solution)/shard_map/ppermute | solution.py:501
  141.3 1.9 collective-permute-start.4
  143.2 5.0 %collective-permute-done.3.refs_0_ = f32[7,16,8,128]{3,2,1,0:T(8,128)S(1)} collective-permute-done((f32[7,16,8,128]{3,2,1,0:T(8,128)S(1)}, f32[7,16,8,128]{3,2,1,0:T(8,128)S(1)}, u32[]{:S(2)}, u32[]{:S(2)}) %collective-permute-start.3) | collective-permute-done | bytes 458784 | tf_op jit(solution)/shard_map/ppermute | solution.py:501
  148.2 3.7 %collective-permute-done.4.refs_2_ = f32[7,16,8,128]{3,2,1,0:T(8,128)S(1)} collective-permute-done((f32[7,16,8,128]{3,2,1,0:T(8,128)S(1)}, f32[7,16,8,128]{3,2,1,0:T(8,128)S(1)}, u32[]{:S(2)}, u32[]{:S(2)}) %collective-permute-start.4) | collective-permute-done | bytes 458784 | tf_op jit(solution)/shard_map/ppermute | solution.py:502
  151.9 3.3 %shard_map.59.refs_1_.refs_2_ = f32[16,16,8,128]{3,2,1,0:T(8,128)S(1)} custom-call(s32[32,32]{1,0:T(8,128)S(1)} %copy-done, f32[7,16,8,128]{3,2,1,0:T(8,128)S(1)} %collective-permute-done.3.refs_0_, f32[32,32,8,128]{3,2,1,0:T(8,128)S(1)} %get-tuple-element.20.refs_0_.refs_1_, f32[7,16,8,128]{3,2,1,0:T(8,128)S(1)} %collective-permute-done.4.refs_2_, ...), custom_call_target="tpu_custom_call" | custom-call | flops 629145600 | bytes 2097152 | tf_op jit(solution)/shard_map/pallas_call | solution.py:479
  155.3 0.0 copy-done.1
  155.3 4.0 %shard_map.60 = (f32[16,16,8,128]{3,2,1,0:T(8,128)S(1)}, f32[7,16,8,128]{3,2,1,0:T(8,128)S(1)}, f32[7,16,8,128]{3,2,1,0:T(8,128)S(1)}) custom-call(s32[32,32]{1,0:T(8,128)S(1)} %copy-done.1, f32[16,16,8,128]{3,2,1,0:T(8,128)S(1)} %get-tuple-element.23.refs_3_.refs_0_.refs_1_, f32[16,16,8,128]{3,2,1,0:T(8,128)S(1)} %shard_map.59.refs_1_.refs_2_), custom_call_target="tpu_custom_call" | custom-call | flops 629145600 | bytes 2097152 | tf_op jit(solution)/shard_map/pallas_call | solution.py:479
  159.2 1.9 collective-permute-start.8
  161.2 2.4 %collective-permute-start.9 = (f32[7,16,8,128]{3,2,1,0:T(8,128)S(1)}, f32[7,16,8,128]{3,2,1,0:T(8,128)S(1)}, u32[]{:S(2)}, u32[]{:S(2)}) collective-permute-start(f32[7,16,8,128]{3,2,1,0:T(8,128)S(1)} %get-tuple-element.32), channel_id=1, source_target_pairs={{4,0},{8,4},{12,8},{16,12},{20,16},{24,20},{28,24},{5,1},{9,5},{13... | collective-permute-start | bytes 1376264 | tf_op jit(solution)/shard_map/ppermute | solution.py:502
  163.6 3.4 %shard_map.61.refs_5_.refs_3_ = f32[16,16,8,128]{3,2,1,0:T(8,128)S(1)} custom-call(s32[32,32]{1,0:T(8,128)S(1)} %copy-done.1, f32[16,32,8,128]{3,2,1,0:T(8,128)S(1)} %shard_map.57.refs_3_.refs_0_.refs_1_, f32[16,16,8,128]{3,2,1,0:T(8,128)S(1)} %get-tuple-element.27.refs_1_.refs_4_), custom_call_target="tpu_custom_call" | custom-call | flops 629145600 | bytes 2097152 | tf_op jit(solution)/shard_map/pallas_call | solution.py:479
  167.0 0.0 collective-permute-done.2.refs_0_
  167.0 0.0 collective-permute-done.5.refs_3_.refs_2_
  167.0 3.6 %shard_map.62 = (f32[16,32,8,128]{3,2,1,0:T(8,128)S(1)}, f32[7,16,8,128]{3,2,1,0:T(8,128)S(1)}, f32[7,16,8,128]{3,2,1,0:T(8,128)S(1)}) custom-call(s32[32,32]{1,0:T(8,128)S(1)} %copy-done.1, f32[32,7,8,128]{3,2,1,0:T(8,128)S(1)} %collective-permute-done.2.refs_0_, f32[16,16,8,128]{3,2,1,0:T(8,128)S(1)} %get-tuple-element.23.refs_3_.refs_0_.refs_1_, ...), custom_call_target="tpu_custom_call" | custom-call | flops 629145600 | bytes 2097152 | tf_op jit(solution)/shard_map/pallas_call | solution.py:479
  170.6 4.1 %collective-permute-start.6 = (f32[7,16,8,128]{3,2,1,0:T(8,128)S(1)}, f32[7,16,8,128]{3,2,1,0:T(8,128)S(1)}, u32[]{:S(2)}, u32[]{:S(2)}) collective-permute-start(f32[7,16,8,128]{3,2,1,0:T(8,128)S(1)} %get-tuple-element.28), channel_id=1, source_target_pairs={{0,4},{4,8},{8,12},{12,16},{16,20},{20,24},{24,28},{1,5},{5,9},{9,... | collective-permute-start | bytes 1376264 | tf_op jit(solution)/shard_map/ppermute | solution.py:501
  174.7 2.1 %collective-permute-start.7 = (f32[7,16,8,128]{3,2,1,0:T(8,128)S(1)}, f32[7,16,8,128]{3,2,1,0:T(8,128)S(1)}, u32[]{:S(2)}, u32[]{:S(2)}) collective-permute-start(f32[7,16,8,128]{3,2,1,0:T(8,128)S(1)} %get-tuple-element.30), channel_id=1, source_target_pairs={{4,0},{8,4},{12,8},{16,12},{20,16},{24,20},{28,24},{5,1},{9,5},{13... | collective-permute-start | bytes 1376264 | tf_op jit(solution)/shard_map/ppermute | solution.py:502
  176.8 3.4 %shard_map.63.refs_1_.refs_2_ = f32[16,32,8,128]{3,2,1,0:T(8,128)S(1)} custom-call(s32[32,32]{1,0:T(8,128)S(1)} %copy-done.1, f32[32,7,8,128]{3,2,1,0:T(8,128)S(1)} %collective-permute-done.2.refs_0_, f32[16,32,8,128]{3,2,1,0:T(8,128)S(1)} %shard_map.57.refs_3_.refs_0_.refs_1_, f32[32,7,8,128]{3,2,1,0:T(8,128)S(1)} %collective-permute-done.5.refs_3_.refs_2_, ...), custom_call_target="tpu_custom_call" | custom-call | flops 629145600 | bytes 2097152 | tf_op jit(solution)/shard_map/pallas_call | solution.py:479
  180.2 8.5 %shard_map.64.refs_4_ = f32[32,32,1024]{2,1,0:T(8,128)} custom-call(s32[32,32]{1,0:T(8,128)S(1)} %copy-done, f32[16,32,8,128]{3,2,1,0:T(8,128)S(1)} %get-tuple-element.29.refs_4_.refs_0_.refs_1_, f32[16,32,8,128]{3,2,1,0:T(8,128)S(1)} %shard_map.63.refs_1_.refs_2_), custom_call_target="tpu_custom_call" | custom-call | flops 1258291200 | bytes 4194304 | tf_op jit(solution)/shard_map/pallas_call | solution.py:479
  188.8 0.0 collective-permute-done.8.refs_0_
  188.8 0.0 collective-permute-done.9.refs_3_
  188.8 5.1 %shard_map.65.refs_4_ = f32[32,32,1024]{2,1,0:T(8,128)} custom-call(s32[32,32]{1,0:T(8,128)S(1)} %copy-done, f32[7,16,8,128]{3,2,1,0:T(8,128)S(1)} %collective-permute-done.8.refs_0_, f32[16,32,8,128]{3,2,1,0:T(8,128)S(1)} %get-tuple-element.29.refs_4_.refs_0_.refs_1_, ...), custom_call_target="tpu_custom_call", output_to_operand_aliasing={{}: (5, {})} | custom-call | flops 629145600 | bytes 2097152 | tf_op jit(solution)/shard_map/pallas_call | solution.py:479
  193.9 0.0 collective-permute-done.6.refs_0_
  193.9 0.0 collective-permute-done.7.refs_3_
  193.9 5.1 %shard_map.66 = f32[32,32,1024]{2,1,0:T(8,128)} custom-call(s32[32,32]{1,0:T(8,128)S(1)} %copy-done, f32[7,16,8,128]{3,2,1,0:T(8,128)S(1)} %collective-permute-done.6.refs_0_, f32[16,32,8,128]{3,2,1,0:T(8,128)S(1)} %get-tuple-element.29.refs_4_.refs_0_.refs_1_, f32[16,32,8,128]{3,2,1,0:T(8,128)S(1)} %shard_map.63.refs_1_.refs_2_, ...), custom_call_target="tpu_custom_call", output_to_operand_aliasing={{}: (5, {})} | custom-call | flops 629145600 | bytes 2097152 | tf_op jit(solution)/shard_map/pallas_call | solution.py:479
Async XLA Ops:
  107.1 13.3 %copy-start = (s32[32,32]{1,0:T(8,128)S(1)}, s32[32,32]{1,0:T(8,128)}, u32[]{:S(2)}) copy-start(s32[32,32]{1,0:T(8,128)} %dip_ref.19) | copy-start | bytes 12292
  114.5 11.9 %collective-permute-start = (f32[7,16,8,128]{3,2,1,0:T(8,128)S(1)}, f32[7,16,8,128]{3,2,1,0:T(8,128)S(1)}, u32[]{:S(2)}, u32[]{:S(2)}) collective-permute-start(f32[7,16,8,128]{3,2,1,0:T(8,128)S(1)} %get-tuple-element.19), channel_id=1, source_target_pairs={{0,4},{4,8},{8,12},{12,16},{16,20},{20,24},{24,28},{1,5},{5,9},{9,... | collective-permute-start | bytes 1376264 | tf_op jit(solution)/shard_map/ppermute | solution.py:501
  118.5 11.2 %collective-permute-start.1 = (f32[7,16,8,128]{3,2,1,0:T(8,128)S(1)}, f32[7,16,8,128]{3,2,1,0:T(8,128)S(1)}, u32[]{:S(2)}, u32[]{:S(2)}) collective-permute-start(f32[7,16,8,128]{3,2,1,0:T(8,128)S(1)} %get-tuple-element.21), channel_id=1, source_target_pairs={{4,0},{8,4},{12,8},{16,12},{20,16},{24,20},{28,24},{5,1},{9,5},{13... | collective-permute-start | bytes 1376264 | tf_op jit(solution)/shard_map/ppermute | solution.py:502
  133.4 21.9 %copy-start.1 = (s32[32,32]{1,0:T(8,128)S(1)}, s32[32,32]{1,0:T(8,128)}, u32[]{:S(2)}) copy-start(s32[32,32]{1,0:T(8,128)} %dip_ref.16) | copy-start | bytes 12292
  133.4 33.6 %collective-permute-start.2 = (f32[32,7,8,128]{3,2,1,0:T(8,128)S(1)}, f32[32,7,8,128]{3,2,1,0:T(8,128)S(1)}, u32[]{:S(2)}, u32[]{:S(2)}) collective-permute-start(f32[32,7,8,128]{3,2,1,0:T(8,128)S(1)} %get-tuple-element.22), channel_id=1, source_target_pairs={{0,1},{1,2},{2,3},{4,5},{5,6},{6,7},{8,9},{9,10},{10,11},{12,13},{... | collective-permute-start | bytes 2752520 | tf_op jit(solution)/shard_map/ppermute | solution.py:501
  135.3 31.7 %collective-permute-start.5 = (f32[32,7,8,128]{3,2,1,0:T(8,128)S(1)}, f32[32,7,8,128]{3,2,1,0:T(8,128)S(1)}, u32[]{:S(2)}, u32[]{:S(2)}) collective-permute-start(f32[32,7,8,128]{3,2,1,0:T(8,128)S(1)} %get-tuple-element.26), channel_id=1, source_target_pairs={{1,0},{2,1},{3,2},{5,4},{6,5},{7,6},{9,8},{10,9},{11,10},{13,12},{... | collective-permute-start | bytes 2752520 | tf_op jit(solution)/shard_map/ppermute | solution.py:502
  138.7 9.5 %collective-permute-start.3 = (f32[7,16,8,128]{3,2,1,0:T(8,128)S(1)}, f32[7,16,8,128]{3,2,1,0:T(8,128)S(1)}, u32[]{:S(2)}, u32[]{:S(2)}) collective-permute-start(f32[7,16,8,128]{3,2,1,0:T(8,128)S(1)} %get-tuple-element.24), channel_id=1, source_target_pairs={{0,4},{4,8},{8,12},{12,16},{16,20},{20,24},{24,28},{1,5},{5,9},{9,... | collective-permute-start | bytes 1376264 | tf_op jit(solution)/shard_map/ppermute | solution.py:501
  141.3 10.7 %collective-permute-start.4 = (f32[7,16,8,128]{3,2,1,0:T(8,128)S(1)}, f32[7,16,8,128]{3,2,1,0:T(8,128)S(1)}, u32[]{:S(2)}, u32[]{:S(2)}) collective-permute-start(f32[7,16,8,128]{3,2,1,0:T(8,128)S(1)} %get-tuple-element.25), channel_id=1, source_target_pairs={{4,0},{8,4},{12,8},{16,12},{20,16},{24,20},{28,24},{5,1},{9,5},{13... | collective-permute-start | bytes 1376264 | tf_op jit(solution)/shard_map/ppermute | solution.py:502
  159.2 29.5 %collective-permute-start.8 = (f32[7,16,8,128]{3,2,1,0:T(8,128)S(1)}, f32[7,16,8,128]{3,2,1,0:T(8,128)S(1)}, u32[]{:S(2)}, u32[]{:S(2)}) collective-permute-start(f32[7,16,8,128]{3,2,1,0:T(8,128)S(1)} %get-tuple-element.31), channel_id=1, source_target_pairs={{0,4},{4,8},{8,12},{12,16},{16,20},{20,24},{24,28},{1,5},{5,9},{9,... | collective-permute-start | bytes 1376264 | tf_op jit(solution)/shard_map/ppermute | solution.py:501
  161.2 27.6 %collective-permute-start.9 = (f32[7,16,8,128]{3,2,1,0:T(8,128)S(1)}, f32[7,16,8,128]{3,2,1,0:T(8,128)S(1)}, u32[]{:S(2)}, u32[]{:S(2)}) collective-permute-start(f32[7,16,8,128]{3,2,1,0:T(8,128)S(1)} %get-tuple-element.32), channel_id=1, source_target_pairs={{4,0},{8,4},{12,8},{16,12},{20,16},{24,20},{28,24},{5,1},{9,5},{13... | collective-permute-start | bytes 1376264 | tf_op jit(solution)/shard_map/ppermute | solution.py:502
  170.6 23.2 %collective-permute-start.6 = (f32[7,16,8,128]{3,2,1,0:T(8,128)S(1)}, f32[7,16,8,128]{3,2,1,0:T(8,128)S(1)}, u32[]{:S(2)}, u32[]{:S(2)}) collective-permute-start(f32[7,16,8,128]{3,2,1,0:T(8,128)S(1)} %get-tuple-element.28), channel_id=1, source_target_pairs={{0,4},{4,8},{8,12},{12,16},{16,20},{20,24},{24,28},{1,5},{5,9},{9,... | collective-permute-start | bytes 1376264 | tf_op jit(solution)/shard_map/ppermute | solution.py:501
  174.7 19.2 %collective-permute-start.7 = (f32[7,16,8,128]{3,2,1,0:T(8,128)S(1)}, f32[7,16,8,128]{3,2,1,0:T(8,128)S(1)}, u32[]{:S(2)}, u32[]{:S(2)}) collective-permute-start(f32[7,16,8,128]{3,2,1,0:T(8,128)S(1)} %get-tuple-element.30), channel_id=1, source_target_pairs={{4,0},{8,4},{12,8},{16,12},{20,16},{24,20},{28,24},{5,1},{9,5},{13... | collective-permute-start | bytes 1376264 | tf_op jit(solution)/shard_map/ppermute | solution.py:502

commit v14 on v13

--- a/solution.py
+++ b/solution.py
@@ -534,17 +534,11 @@
     def mid_windows(places, extent):
         return [(i, WINDOW, places[i - BORDER : i - BORDER + WINDOW + 2 * HALF]) for i in range(BORDER, extent - BORDER, WINDOW)]
 
-    stacked, head_out, tail_out, head_mid, tail_mid = stack_bins(
+    stacked, head, tail = stack_bins(
         arrived, rows, cols, capacity, block_rows,
-        [
-            outer_edge(rows_of(0, HALF)),
-            outer_edge(rows_of(rows - HALF, HALF)),
-            whole_edge((HALF, mid_cols), (rows_of(0, HALF), middle_cols)),
-            whole_edge((HALF, mid_cols), (rows_of(rows - HALF, HALF), middle_cols)),
-        ],
-    )
-    low_out, high_out = swap_ends(head_out, tail_out, "inline")
-    low_mid, high_mid = swap_ends(head_mid, tail_mid, "inline")
+        [whole_edge((HALF, cols), (rows_of(0, HALF), every)), whole_edge((HALF, cols), (rows_of(rows - HALF, HALF), every))],
+    )
+    low, high = swap_ends(head, tail, "inline")
 
     (middle,) = steer(
         dip_inline, [(stacked, True)], 0, cols, same,
@@ -567,12 +561,12 @@
         )
 
     corners, head, tail = steer(
-        dip_inline, [(low_out, False), (stacked, True), (high_out, False), (middle, False)], 0, both, outer_col,
+        dip_inline, [(low, True), (stacked, True), (high, True), (middle, False)], 0, both, outer_col,
         windows, outer_place, edges=[column_edge(lead, lead), column_edge(last, rows_of(cols - HALF, HALF))],
     )
     west, east = swap_ends(head, tail, "crosslin")
     (flanks,) = steer(
-        dip_inline, [(low_mid, False), (stacked, True), (high_mid, False)], 0, mid_cols, inner, windows, outer_place,
+        dip_inline, [(low, True), (stacked, True), (high, True)], 0, mid_cols, inner, windows, outer_place,
         after=corners,
     )
 

time: 200 us -> 203 us (1.015); the launches traced: 199 us -> 200 us
  waiting for transfers between devices: 12.1 us -> 18.5 us
  starting transfers between devices: 26.1 us -> 20.8 us
    ppermute x5 -> x4, waiting for transfers between devices: 5.04 us -> 13.1 us  [swap_ends(): low = lax.ppermute(tail, axis, [(i, i + 1) for i in range(count - 1)])]
    ppermute x5 -> x4, starting transfers between devices: 14.4 us -> 10.6 us  [swap_ends(): low = lax.ppermute(tail, axis, [(i, i + 1) for i in range(count - 1)])]
    ppermute x5 -> x4, waiting for transfers between devices: 7.09 us -> 5.34 us  [swap_ends(): high = lax.ppermute(head, axis, [(i + 1, i) for i in range(count - 1)])]
    ppermute x5 -> x4, starting transfers between devices: 11.8 us -> 10.2 us  [swap_ends(): high = lax.ppermute(head, axis, [(i + 1, i) for i in range(count - 1)])]
  transfers between devices with their start and end apart: 10 -> 8, of which waited for: 3 -> 4; matrix products, arithmetic and copies ran while one was open for 0% -> 0% of each run, Pallas kernels for 19% -> 19%
where the time goes in v14:
time: 203 us; the launch traced here: 200 us
  blocking collectives  102 us (50%)
  Pallas kernels  58.6 us (29%)
  starting transfers between devices  20.8 us (10%)
  waiting for transfers between devices  18.5 us (9%)
    all_to_all x1, blocking collectives, on_device(): lax.all_to_all(outgoing, BOTH, split_axis=0, concat_axis=0, tiled=True)  102 us
    pallas_call x10, Pallas kernels, steer(): pl.pallas_call(functools.partial(steer_kernel, along=along, whole=[whole...  46 us
    ppermute x4, waiting for transfers between devices, swap_ends(): low = lax.ppermute(tail, axis, [(i, i + 1) for i in range(count - 1)])  13.1 us
    ppermute x4, starting transfers between devices, swap_ends(): low = lax.ppermute(tail, axis, [(i, i + 1) for i in range(count - 1)])  10.6 us
    ppermute x4, starting transfers between devices, swap_ends(): high = lax.ppermute(head, axis, [(i + 1, i) for i in range(count - 1)])  10.2 us
    pallas_call x1, Pallas kernels, stack_bins(): pl.pallas_call(functools.partial(bin_kernel, capacity=capacity, block_row...  7.14 us
    pallas_call x1, Pallas kernels, pack(): pl.pallas_call(functools.partial(pack_kernel, capacity=capacity), in_spec...  5.43 us
    ppermute x4, waiting for transfers between devices, swap_ends(): high = lax.ppermute(head, axis, [(i + 1, i) for i in range(count - 1)])  5.34 us
  transfers between devices with their start and end apart: 8, of which 4 were waited for; matrix products, arithmetic and copies ran while one was open for 0% of the time, Pallas kernels for 19%

profile of v14, /device:TPU:11, one launch (start us, length us, event | category | flops | bytes accessed | tf_op | source)
XLA Modules:
  0.0 199.8 jit_solution(4713310436640562904)
XLA Ops:
  0.0 5.4 %shard_map.55 = f32[32,264,128]{2,1,0:T(8,128)} custom-call(s32[1]{0:T(128)} %bitcast.mine_ref, s32[128]{0:T(128)} %bitcast.4, s32[4,128]{1,0:T(4,128)} %bitcast.3, f32[128,4,1024]{2,1,0:T(4,128)} %traces_ref.1), custom_call_target="tpu_custom_call" | custom-call | tf_op jit(solution)/shard_map/pallas_call | solution.py:138
  5.4 101.7 %all_to_all.5.blocks_ref = f32[32,264,128]{2,1,0:T(8,128)S(1)} all-to-all(f32[32,264,128]{2,1,0:T(8,128)} %shard_map.55), channel_id=1, replica_groups=mesh['inline'=8,'crosslin'=4] {'inline','crosslin'}, dimensions={0} | all-to-all | bytes 8650752 | tf_op jit(solution)/shard_map/all_to_all | solution.py:629
  107.1 0.0 copy-start
  107.1 7.1 %shard_map.56 = (f32[32,32,8,128]{3,2,1,0:T(8,128)S(1)}, f32[7,32,8,128]{3,2,1,0:T(8,128)S(1)}, f32[7,32,8,128]{3,2,1,0:T(8,128)S(1)}) custom-call(f32[32,264,128]{2,1,0:T(8,128)S(1)} %all_to_all.5.blocks_ref), custom_call_target="tpu_custom_call" | custom-call | tf_op jit(solution)/shard_map/pallas_call | solution.py:249
  114.3 4.4 %collective-permute-start = (f32[7,32,8,128]{3,2,1,0:T(8,128)S(1)}, f32[7,32,8,128]{3,2,1,0:T(8,128)S(1)}, u32[]{:S(2)}, u32[]{:S(2)}) collective-permute-start(f32[7,32,8,128]{3,2,1,0:T(8,128)S(1)} %get-tuple-element.17), channel_id=1, source_target_pairs={{0,4},{4,8},{8,12},{12,16},{16,20},{20,24},{24,28},{1,5},{5,9},{9,... | collective-permute-start | bytes 2752520 | tf_op jit(solution)/shard_map/ppermute | solution.py:501
  118.6 1.9 collective-permute-start.1
  120.6 0.0 copy-done
  120.6 5.9 %shard_map.57.refs_3_.refs_0_.refs_1_ = f32[16,32,8,128]{3,2,1,0:T(8,128)S(1)} custom-call(s32[32,32]{1,0:T(8,128)S(1)} %copy-done, f32[32,32,8,128]{3,2,1,0:T(8,128)S(1)} %get-tuple-element.18.refs_0_.refs_1_), custom_call_target="tpu_custom_call" | custom-call | flops 1258291200 | bytes 4194304 | tf_op jit(solution)/shard_map/pallas_call | solution.py:479
  126.5 9.3 %collective-permute-done.refs_0_ = f32[7,32,8,128]{3,2,1,0:T(8,128)S(1)} collective-permute-done((f32[7,32,8,128]{3,2,1,0:T(8,128)S(1)}, f32[7,32,8,128]{3,2,1,0:T(8,128)S(1)}, u32[]{:S(2)}, u32[]{:S(2)}) %collective-permute-start) | collective-permute-done | bytes 917536 | tf_op jit(solution)/shard_map/ppermute | solution.py:501
  135.9 3.7 %collective-permute-done.1.refs_2_ = f32[7,32,8,128]{3,2,1,0:T(8,128)S(1)} collective-permute-done((f32[7,32,8,128]{3,2,1,0:T(8,128)S(1)}, f32[7,32,8,128]{3,2,1,0:T(8,128)S(1)}, u32[]{:S(2)}, u32[]{:S(2)}) %collective-permute-start.1) | collective-permute-done | bytes 917536 | tf_op jit(solution)/shard_map/ppermute | solution.py:502
  139.6 3.6 %shard_map.58 = (f32[16,16,8,128]{3,2,1,0:T(8,128)S(1)}, f32[32,7,8,128]{3,2,1,0:T(8,128)S(1)}, f32[32,7,8,128]{3,2,1,0:T(8,128)S(1)}) custom-call(s32[32,32]{1,0:T(8,128)S(1)} %copy-done, f32[7,32,8,128]{3,2,1,0:T(8,128)S(1)} %collective-permute-done.refs_0_, f32[32,32,8,128]{3,2,1,0:T(8,128)S(1)} %get-tuple-element.18.refs_0_.refs_1_, ...), custom_call_target="tpu_custom_call" | custom-call | flops 629145600 | bytes 2097152 | tf_op jit(solution)/shard_map/pallas_call | solution.py:479
  143.2 0.0 copy-start.1
  143.2 2.0 collective-permute-start.2
  145.2 3.4 %collective-permute-start.3 = (f32[32,7,8,128]{3,2,1,0:T(8,128)S(1)}, f32[32,7,8,128]{3,2,1,0:T(8,128)S(1)}, u32[]{:S(2)}, u32[]{:S(2)}) collective-permute-start(f32[32,7,8,128]{3,2,1,0:T(8,128)S(1)} %get-tuple-element.22), channel_id=1, source_target_pairs={{1,0},{2,1},{3,2},{5,4},{6,5},{7,6},{9,8},{10,9},{11,10},{13,12},{... | collective-permute-start | bytes 2752520 | tf_op jit(solution)/shard_map/ppermute | solution.py:502
  148.6 3.3 %shard_map.59.refs_1_.refs_2_ = f32[16,16,8,128]{3,2,1,0:T(8,128)S(1)} custom-call(s32[32,32]{1,0:T(8,128)S(1)} %copy-done, f32[7,32,8,128]{3,2,1,0:T(8,128)S(1)} %collective-permute-done.refs_0_, f32[32,32,8,128]{3,2,1,0:T(8,128)S(1)} %get-tuple-element.18.refs_0_.refs_1_, f32[7,32,8,128]{3,2,1,0:T(8,128)S(1)} %collective-permute-done.1.refs_2_, ...), custom_call_target="tpu_custom_call" | custom-call | flops 629145600 | bytes 2097152 | tf_op jit(solution)/shard_map/pallas_call | solution.py:479
  151.9 0.0 copy-done.1
  151.9 4.0 %shard_map.60 = (f32[16,16,8,128]{3,2,1,0:T(8,128)S(1)}, f32[7,16,8,128]{3,2,1,0:T(8,128)S(1)}, f32[7,16,8,128]{3,2,1,0:T(8,128)S(1)}) custom-call(s32[32,32]{1,0:T(8,128)S(1)} %copy-done.1, f32[16,16,8,128]{3,2,1,0:T(8,128)S(1)} %get-tuple-element.21.refs_3_.refs_0_.refs_1_, f32[16,16,8,128]{3,2,1,0:T(8,128)S(1)} %shard_map.59.refs_1_.refs_2_), custom_call_target="tpu_custom_call" | custom-call | flops 629145600 | bytes 2097152 | tf_op jit(solution)/shard_map/pallas_call | solution.py:479
  155.9 2.3 %collective-permute-start.6 = (f32[7,16,8,128]{3,2,1,0:T(8,128)S(1)}, f32[7,16,8,128]{3,2,1,0:T(8,128)S(1)}, u32[]{:S(2)}, u32[]{:S(2)}) collective-permute-start(f32[7,16,8,128]{3,2,1,0:T(8,128)S(1)} %get-tuple-element.27), channel_id=1, source_target_pairs={{0,4},{4,8},{8,12},{12,16},{16,20},{20,24},{24,28},{1,5},{5,9},{9,... | collective-permute-start | bytes 1376264 | tf_op jit(solution)/shard_map/ppermute | solution.py:501
  158.2 2.0 %collective-permute-start.7 = (f32[7,16,8,128]{3,2,1,0:T(8,128)S(1)}, f32[7,16,8,128]{3,2,1,0:T(8,128)S(1)}, u32[]{:S(2)}, u32[]{:S(2)}) collective-permute-start(f32[7,16,8,128]{3,2,1,0:T(8,128)S(1)} %get-tuple-element.28), channel_id=1, source_target_pairs={{4,0},{8,4},{12,8},{16,12},{20,16},{24,20},{28,24},{5,1},{9,5},{13... | collective-permute-start | bytes 1376264 | tf_op jit(solution)/shard_map/ppermute | solution.py:502
  160.2 3.4 %shard_map.61.refs_5_.refs_3_ = f32[16,16,8,128]{3,2,1,0:T(8,128)S(1)} custom-call(s32[32,32]{1,0:T(8,128)S(1)} %copy-done.1, f32[16,32,8,128]{3,2,1,0:T(8,128)S(1)} %shard_map.57.refs_3_.refs_0_.refs_1_, f32[16,16,8,128]{3,2,1,0:T(8,128)S(1)} %get-tuple-element.23.refs_1_.refs_4_), custom_call_target="tpu_custom_call" | custom-call | flops 629145600 | bytes 2097152 | tf_op jit(solution)/shard_map/pallas_call | solution.py:479
  163.6 3.8 %collective-permute-done.2.refs_0_ = f32[32,7,8,128]{3,2,1,0:T(8,128)S(1)} collective-permute-done((f32[32,7,8,128]{3,2,1,0:T(8,128)S(1)}, f32[32,7,8,128]{3,2,1,0:T(8,128)S(1)}, u32[]{:S(2)}, u32[]{:S(2)}) %collective-permute-start.2) | collective-permute-done | bytes 917536 | tf_op jit(solution)/shard_map/ppermute | solution.py:501
  167.4 1.6 collective-permute-done.3.refs_3_.refs_2_
  169.0 3.6 %shard_map.62 = (f32[16,32,8,128]{3,2,1,0:T(8,128)S(1)}, f32[7,16,8,128]{3,2,1,0:T(8,128)S(1)}, f32[7,16,8,128]{3,2,1,0:T(8,128)S(1)}) custom-call(s32[32,32]{1,0:T(8,128)S(1)} %copy-done.1, f32[32,7,8,128]{3,2,1,0:T(8,128)S(1)} %collective-permute-done.2.refs_0_, f32[16,16,8,128]{3,2,1,0:T(8,128)S(1)} %get-tuple-element.21.refs_3_.refs_0_.refs_1_, ...), custom_call_target="tpu_custom_call" | custom-call | flops 629145600 | bytes 2097152 | tf_op jit(solution)/shard_map/pallas_call | solution.py:479
  172.6 1.9 collective-permute-start.4
  174.6 2.9 %collective-permute-start.5 = (f32[7,16,8,128]{3,2,1,0:T(8,128)S(1)}, f32[7,16,8,128]{3,2,1,0:T(8,128)S(1)}, u32[]{:S(2)}, u32[]{:S(2)}) collective-permute-start(f32[7,16,8,128]{3,2,1,0:T(8,128)S(1)} %get-tuple-element.26), channel_id=1, source_target_pairs={{4,0},{8,4},{12,8},{16,12},{20,16},{24,20},{28,24},{5,1},{9,5},{13... | collective-permute-start | bytes 1376264 | tf_op jit(solution)/shard_map/ppermute | solution.py:502
  177.5 3.4 %shard_map.63.refs_1_.refs_2_ = f32[16,32,8,128]{3,2,1,0:T(8,128)S(1)} custom-call(s32[32,32]{1,0:T(8,128)S(1)} %copy-done.1, f32[32,7,8,128]{3,2,1,0:T(8,128)S(1)} %collective-permute-done.2.refs_0_, f32[16,32,8,128]{3,2,1,0:T(8,128)S(1)} %shard_map.57.refs_3_.refs_0_.refs_1_, f32[32,7,8,128]{3,2,1,0:T(8,128)S(1)} %collective-permute-done.3.refs_3_.refs_2_, ...), custom_call_target="tpu_custom_call" | custom-call | flops 629145600 | bytes 2097152 | tf_op jit(solution)/shard_map/pallas_call | solution.py:479
  180.9 8.5 %shard_map.64.refs_4_ = f32[32,32,1024]{2,1,0:T(8,128)} custom-call(s32[32,32]{1,0:T(8,128)S(1)} %copy-done, f32[16,32,8,128]{3,2,1,0:T(8,128)S(1)} %get-tuple-element.25.refs_4_.refs_0_.refs_1_, f32[16,32,8,128]{3,2,1,0:T(8,128)S(1)} %shard_map.63.refs_1_.refs_2_), custom_call_target="tpu_custom_call" | custom-call | flops 1258291200 | bytes 4194304 | tf_op jit(solution)/shard_map/pallas_call | solution.py:479
  189.4 0.0 collective-permute-done.6.refs_0_
  189.4 0.0 collective-permute-done.7.refs_3_
  189.4 5.1 %shard_map.65.refs_4_ = f32[32,32,1024]{2,1,0:T(8,128)} custom-call(s32[32,32]{1,0:T(8,128)S(1)} %copy-done, f32[7,16,8,128]{3,2,1,0:T(8,128)S(1)} %collective-permute-done.6.refs_0_, f32[16,32,8,128]{3,2,1,0:T(8,128)S(1)} %get-tuple-element.25.refs_4_.refs_0_.refs_1_, ...), custom_call_target="tpu_custom_call", output_to_operand_aliasing={{}: (5, {})} | custom-call | flops 629145600 | bytes 2097152 | tf_op jit(solution)/shard_map/pallas_call | solution.py:479
  194.6 0.0 collective-permute-done.4.refs_0_
  194.6 0.0 collective-permute-done.5.refs_3_
  194.6 5.1 %shard_map.66 = f32[32,32,1024]{2,1,0:T(8,128)} custom-call(s32[32,32]{1,0:T(8,128)S(1)} %copy-done, f32[7,16,8,128]{3,2,1,0:T(8,128)S(1)} %collective-permute-done.4.refs_0_, f32[16,32,8,128]{3,2,1,0:T(8,128)S(1)} %get-tuple-element.25.refs_4_.refs_0_.refs_1_, f32[16,32,8,128]{3,2,1,0:T(8,128)S(1)} %shard_map.63.refs_1_.refs_2_, ...), custom_call_target="tpu_custom_call", output_to_operand_aliasing={{}: (5, {})} | custom-call | flops 629145600 | bytes 2097152 | tf_op jit(solution)/shard_map/pallas_call | solution.py:479
Async XLA Ops:
  107.1 13.5 %copy-start = (s32[32,32]{1,0:T(8,128)S(1)}, s32[32,32]{1,0:T(8,128)}, u32[]{:S(2)}) copy-start(s32[32,32]{1,0:T(8,128)} %dip_ref.19) | copy-start | bytes 12292
  114.3 21.6 %collective-permute-start = (f32[7,32,8,128]{3,2,1,0:T(8,128)S(1)}, f32[7,32,8,128]{3,2,1,0:T(8,128)S(1)}, u32[]{:S(2)}, u32[]{:S(2)}) collective-permute-start(f32[7,32,8,128]{3,2,1,0:T(8,128)S(1)} %get-tuple-element.17), channel_id=1, source_target_pairs={{0,4},{4,8},{8,12},{12,16},{16,20},{20,24},{24,28},{1,5},{5,9},{9,... | collective-permute-start | bytes 2752520 | tf_op jit(solution)/shard_map/ppermute | solution.py:501
  118.6 20.9 %collective-permute-start.1 = (f32[7,32,8,128]{3,2,1,0:T(8,128)S(1)}, f32[7,32,8,128]{3,2,1,0:T(8,128)S(1)}, u32[]{:S(2)}, u32[]{:S(2)}) collective-permute-start(f32[7,32,8,128]{3,2,1,0:T(8,128)S(1)} %get-tuple-element.19), channel_id=1, source_target_pairs={{4,0},{8,4},{12,8},{16,12},{20,16},{24,20},{28,24},{5,1},{9,5},{13... | collective-permute-start | bytes 2752520 | tf_op jit(solution)/shard_map/ppermute | solution.py:502
  143.2 8.7 %copy-start.1 = (s32[32,32]{1,0:T(8,128)S(1)}, s32[32,32]{1,0:T(8,128)}, u32[]{:S(2)}) copy-start(s32[32,32]{1,0:T(8,128)} %dip_ref.16) | copy-start | bytes 12292
  143.2 24.2 %collective-permute-start.2 = (f32[32,7,8,128]{3,2,1,0:T(8,128)S(1)}, f32[32,7,8,128]{3,2,1,0:T(8,128)S(1)}, u32[]{:S(2)}, u32[]{:S(2)}) collective-permute-start(f32[32,7,8,128]{3,2,1,0:T(8,128)S(1)} %get-tuple-element.20), channel_id=1, source_target_pairs={{0,1},{1,2},{2,3},{4,5},{5,6},{6,7},{8,9},{9,10},{10,11},{12,13},{... | collective-permute-start | bytes 2752520 | tf_op jit(solution)/shard_map/ppermute | solution.py:501
  145.2 23.8 %collective-permute-start.3 = (f32[32,7,8,128]{3,2,1,0:T(8,128)S(1)}, f32[32,7,8,128]{3,2,1,0:T(8,128)S(1)}, u32[]{:S(2)}, u32[]{:S(2)}) collective-permute-start(f32[32,7,8,128]{3,2,1,0:T(8,128)S(1)} %get-tuple-element.22), channel_id=1, source_target_pairs={{1,0},{2,1},{3,2},{5,4},{6,5},{7,6},{9,8},{10,9},{11,10},{13,12},{... | collective-permute-start | bytes 2752520 | tf_op jit(solution)/shard_map/ppermute | solution.py:502
  155.9 33.6 %collective-permute-start.6 = (f32[7,16,8,128]{3,2,1,0:T(8,128)S(1)}, f32[7,16,8,128]{3,2,1,0:T(8,128)S(1)}, u32[]{:S(2)}, u32[]{:S(2)}) collective-permute-start(f32[7,16,8,128]{3,2,1,0:T(8,128)S(1)} %get-tuple-element.27), channel_id=1, source_target_pairs={{0,4},{4,8},{8,12},{12,16},{16,20},{20,24},{24,28},{1,5},{5,9},{9,... | collective-permute-start | bytes 1376264 | tf_op jit(solution)/shard_map/ppermute | solution.py:501
  158.2 31.3 %collective-permute-start.7 = (f32[7,16,8,128]{3,2,1,0:T(8,128)S(1)}, f32[7,16,8,128]{3,2,1,0:T(8,128)S(1)}, u32[]{:S(2)}, u32[]{:S(2)}) collective-permute-start(f32[7,16,8,128]{3,2,1,0:T(8,128)S(1)} %get-tuple-element.28), channel_id=1, source_target_pairs={{4,0},{8,4},{12,8},{16,12},{20,16},{24,20},{28,24},{5,1},{9,5},{13... | collective-permute-start | bytes 1376264 | tf_op jit(solution)/shard_map/ppermute | solution.py:502
  172.6 21.9 %collective-permute-start.4 = (f32[7,16,8,128]{3,2,1,0:T(8,128)S(1)}, f32[7,16,8,128]{3,2,1,0:T(8,128)S(1)}, u32[]{:S(2)}, u32[]{:S(2)}) collective-permute-start(f32[7,16,8,128]{3,2,1,0:T(8,128)S(1)} %get-tuple-element.24), channel_id=1, source_target_pairs={{0,4},{4,8},{8,12},{12,16},{16,20},{20,24},{24,28},{1,5},{5,9},{9,... | collective-permute-start | bytes 1376264 | tf_op jit(solution)/shard_map/ppermute | solution.py:501
  174.6 20.0 %collective-permute-start.5 = (f32[7,16,8,128]{3,2,1,0:T(8,128)S(1)}, f32[7,16,8,128]{3,2,1,0:T(8,128)S(1)}, u32[]{:S(2)}, u32[]{:S(2)}) collective-permute-start(f32[7,16,8,128]{3,2,1,0:T(8,128)S(1)} %get-tuple-element.26), channel_id=1, source_target_pairs={{4,0},{8,4},{12,8},{16,12},{20,16},{24,20},{28,24},{5,1},{9,5},{13... | collective-permute-start | bytes 1376264 | tf_op jit(solution)/shard_map/ppermute | solution.py:502

commit v15 on v13

--- a/solution.py
+++ b/solution.py
@@ -489,7 +489,7 @@
         input_output_aliases=aliases,
         compiler_params=pltpu.CompilerParams(vmem_limit_bytes=16 * MIB),
         cost_estimate=pl.CostEstimate(
-            flops=2400 * outputs * lines * samples,
+            flops=40000 * outputs * lines * samples,
             bytes_accessed=8 * outputs * lines * samples,
             transcendentals=0,
         ),

time: 200 us -> 196 us (0.980)
  waiting for transfers between devices: 12.1 us -> 4.49 us
    ppermute x5, waiting for transfers between devices: 7.09 us -> 2.95 us  [swap_ends(): high = lax.ppermute(head, axis, [(i + 1, i) for i in range(count - 1)])]
    ppermute x5, waiting for transfers between devices: 5.04 us -> 1.55 us  [swap_ends(): low = lax.ppermute(tail, axis, [(i, i + 1) for i in range(count - 1)])]
    ppermute x5, starting transfers between devices: 14.4 us -> 16.7 us  [swap_ends(): low = lax.ppermute(tail, axis, [(i, i + 1) for i in range(count - 1)])]
  transfers between devices with their start and end apart: 10 -> 10, of which waited for: 3 -> 3; matrix products, arithmetic and copies ran while one was open for 0% -> 0% of each run, Pallas kernels for 19% -> 21%
where the time goes in v15:
time: 196 us; the launch traced here: 193 us
  blocking collectives  102 us (52%)
  Pallas kernels  58.9 us (30%)
  starting transfers between devices  27.9 us (14%)
  waiting for transfers between devices  4.49 us (2%)
    all_to_all x1, blocking collectives, on_device(): lax.all_to_all(outgoing, BOTH, split_axis=0, concat_axis=0, tiled=True)  102 us
    pallas_call x10, Pallas kernels, steer(): pl.pallas_call(functools.partial(steer_kernel, along=along, whole=[whole...  46 us
    ppermute x5, starting transfers between devices, swap_ends(): low = lax.ppermute(tail, axis, [(i, i + 1) for i in range(count - 1)])  16.7 us
    ppermute x5, starting transfers between devices, swap_ends(): high = lax.ppermute(head, axis, [(i + 1, i) for i in range(count - 1)])  11.2 us
    pallas_call x1, Pallas kernels, stack_bins(): pl.pallas_call(functools.partial(bin_kernel, capacity=capacity, block_row...  7.46 us
    pallas_call x1, Pallas kernels, pack(): pl.pallas_call(functools.partial(pack_kernel, capacity=capacity), in_spec...  5.42 us
  transfers between devices with their start and end apart: 10, of which 3 were waited for; matrix products, arithmetic and copies ran while one was open for 0% of the time, Pallas kernels for 21%

profile of v15, /device:TPU:11, one launch (start us, length us, event | category | flops | bytes accessed | tf_op | source)
XLA Modules:
  0.0 193.4 jit_solution(3563983752208820390)
XLA Ops:
  0.0 5.4 %shard_map.55 = f32[32,264,128]{2,1,0:T(8,128)} custom-call(s32[1]{0:T(128)} %bitcast.mine_ref, s32[128]{0:T(128)} %bitcast.4, s32[4,128]{1,0:T(4,128)} %bitcast.3, f32[128,4,1024]{2,1,0:T(4,128)} %traces_ref.1), custom_call_target="tpu_custom_call" | custom-call | tf_op jit(solution)/shard_map/pallas_call | solution.py:138
  5.4 101.7 %all_to_all.5.blocks_ref = f32[32,264,128]{2,1,0:T(8,128)S(1)} all-to-all(f32[32,264,128]{2,1,0:T(8,128)} %shard_map.55), channel_id=1, replica_groups=mesh['inline'=8,'crosslin'=4] {'inline','crosslin'}, dimensions={0} | all-to-all | bytes 8650752 | tf_op jit(solution)/shard_map/all_to_all | solution.py:635
  107.1 0.0 copy-start.1
  107.1 7.5 %shard_map.56 = (f32[32,32,8,128]{3,2,1,0:T(8,128)S(1)}, f32[7,16,8,128]{3,2,1,0:T(8,128)S(1)}, f32[7,16,8,128]{3,2,1,0:T(8,128)S(1)}, f32[7,16,8,128]{3,2,1,0:T(8,128)S(1)}, f32[7,16,8,128]{3,2,1,0:T(8,128)S(1)}) custom-call(f32[32,264,128]{2,1,0:T(8,128)S(1)} %all_to_all.5.blocks_ref), custom_call_target="tpu_custom_call" | custom-call | tf_op jit(solution)/shard_map/pallas_call | solution.py:249
  114.6 3.8 %collective-permute-start = (f32[7,16,8,128]{3,2,1,0:T(8,128)S(1)}, f32[7,16,8,128]{3,2,1,0:T(8,128)S(1)}, u32[]{:S(2)}, u32[]{:S(2)}) collective-permute-start(f32[7,16,8,128]{3,2,1,0:T(8,128)S(1)} %get-tuple-element.19), channel_id=1, source_target_pairs={{0,4},{4,8},{8,12},{12,16},{16,20},{20,24},{24,28},{1,5},{5,9},{9,... | collective-permute-start | bytes 1376264 | tf_op jit(solution)/shard_map/ppermute | solution.py:501
  118.3 1.9 collective-permute-start.1
  120.3 4.5 %collective-permute-start.3 = (f32[7,16,8,128]{3,2,1,0:T(8,128)S(1)}, f32[7,16,8,128]{3,2,1,0:T(8,128)S(1)}, u32[]{:S(2)}, u32[]{:S(2)}) collective-permute-start(f32[7,16,8,128]{3,2,1,0:T(8,128)S(1)} %get-tuple-element.24), channel_id=1, source_target_pairs={{0,4},{4,8},{8,12},{12,16},{16,20},{20,24},{24,28},{1,5},{5,9},{9,... | collective-permute-start | bytes 1376264 | tf_op jit(solution)/shard_map/ppermute | solution.py:501
  124.8 1.9 collective-permute-start.4
  126.8 0.0 copy-done.1
  126.8 5.9 %shard_map.57.refs_3_.refs_0_.refs_1_ = f32[16,32,8,128]{3,2,1,0:T(8,128)S(1)} custom-call(s32[32,32]{1,0:T(8,128)S(1)} %copy-done.1, f32[32,32,8,128]{3,2,1,0:T(8,128)S(1)} %get-tuple-element.20.refs_0_.refs_1_), custom_call_target="tpu_custom_call" | custom-call | flops 20971520000 | bytes 4194304 | tf_op jit(solution)/shard_map/pallas_call | solution.py:479
  132.7 0.0 collective-permute-done.refs_0_
  132.7 1.1 collective-permute-done.1.refs_2_
  133.8 3.6 %shard_map.58 = (f32[16,16,8,128]{3,2,1,0:T(8,128)S(1)}, f32[32,7,8,128]{3,2,1,0:T(8,128)S(1)}, f32[32,7,8,128]{3,2,1,0:T(8,128)S(1)}) custom-call(s32[32,32]{1,0:T(8,128)S(1)} %copy-done.1, f32[7,16,8,128]{3,2,1,0:T(8,128)S(1)} %collective-permute-done.refs_0_, f32[32,32,8,128]{3,2,1,0:T(8,128)S(1)} %get-tuple-element.20.refs_0_.refs_1_, ...), custom_call_target="tpu_custom_call" | custom-call | flops 10485760000 | bytes 2097152 | tf_op jit(solution)/shard_map/pallas_call | solution.py:479
  137.5 2.1 %collective-permute-start.2 = (f32[32,7,8,128]{3,2,1,0:T(8,128)S(1)}, f32[32,7,8,128]{3,2,1,0:T(8,128)S(1)}, u32[]{:S(2)}, u32[]{:S(2)}) collective-permute-start(f32[32,7,8,128]{3,2,1,0:T(8,128)S(1)} %get-tuple-element.22), channel_id=1, source_target_pairs={{0,1},{1,2},{2,3},{4,5},{5,6},{6,7},{8,9},{9,10},{10,11},{12,13},{... | collective-permute-start | bytes 2752520 | tf_op jit(solution)/shard_map/ppermute | solution.py:501
  139.6 3.2 %collective-permute-start.5 = (f32[32,7,8,128]{3,2,1,0:T(8,128)S(1)}, f32[32,7,8,128]{3,2,1,0:T(8,128)S(1)}, u32[]{:S(2)}, u32[]{:S(2)}) collective-permute-start(f32[32,7,8,128]{3,2,1,0:T(8,128)S(1)} %get-tuple-element.26), channel_id=1, source_target_pairs={{1,0},{2,1},{3,2},{5,4},{6,5},{7,6},{9,8},{10,9},{11,10},{13,12},{... | collective-permute-start | bytes 2752520 | tf_op jit(solution)/shard_map/ppermute | solution.py:502
  142.8 0.0 collective-permute-done.3.refs_0_
  142.8 0.0 collective-permute-done.4.refs_2_
  142.8 0.0 copy-start
  142.8 3.3 %shard_map.59.refs_1_.refs_2_ = f32[16,16,8,128]{3,2,1,0:T(8,128)S(1)} custom-call(s32[32,32]{1,0:T(8,128)S(1)} %copy-done.1, f32[7,16,8,128]{3,2,1,0:T(8,128)S(1)} %collective-permute-done.3.refs_0_, f32[32,32,8,128]{3,2,1,0:T(8,128)S(1)} %get-tuple-element.20.refs_0_.refs_1_, f32[7,16,8,128]{3,2,1,0:T(8,128)S(1)} %collective-permute-done.4.refs_2_, ...), custom_call_target="tpu_custom_call" | custom-call | flops 10485760000 | bytes 2097152 | tf_op jit(solution)/shard_map/pallas_call | solution.py:479
  146.1 0.0 copy-done
  146.2 4.0 %shard_map.60 = (f32[16,16,8,128]{3,2,1,0:T(8,128)S(1)}, f32[7,16,8,128]{3,2,1,0:T(8,128)S(1)}, f32[7,16,8,128]{3,2,1,0:T(8,128)S(1)}) custom-call(s32[32,32]{1,0:T(8,128)S(1)} %copy-done, f32[16,16,8,128]{3,2,1,0:T(8,128)S(1)} %get-tuple-element.23.refs_3_.refs_0_.refs_1_, f32[16,16,8,128]{3,2,1,0:T(8,128)S(1)} %shard_map.59.refs_1_.refs_2_), custom_call_target="tpu_custom_call" | custom-call | flops 10485760000 | bytes 2097152 | tf_op jit(solution)/shard_map/pallas_call | solution.py:479
  150.1 4.0 %collective-permute-start.8 = (f32[7,16,8,128]{3,2,1,0:T(8,128)S(1)}, f32[7,16,8,128]{3,2,1,0:T(8,128)S(1)}, u32[]{:S(2)}, u32[]{:S(2)}) collective-permute-start(f32[7,16,8,128]{3,2,1,0:T(8,128)S(1)} %get-tuple-element.31), channel_id=1, source_target_pairs={{0,4},{4,8},{8,12},{12,16},{16,20},{20,24},{24,28},{1,5},{5,9},{9,... | collective-permute-start | bytes 1376264 | tf_op jit(solution)/shard_map/ppermute | solution.py:501
  154.1 1.9 collective-permute-start.9
  156.1 3.4 %shard_map.61.refs_5_.refs_3_ = f32[16,16,8,128]{3,2,1,0:T(8,128)S(1)} custom-call(s32[32,32]{1,0:T(8,128)S(1)} %copy-done, f32[16,32,8,128]{3,2,1,0:T(8,128)S(1)} %shard_map.57.refs_3_.refs_0_.refs_1_, f32[16,16,8,128]{3,2,1,0:T(8,128)S(1)} %get-tuple-element.27.refs_1_.refs_4_), custom_call_target="tpu_custom_call" | custom-call | flops 10485760000 | bytes 2097152 | tf_op jit(solution)/shard_map/pallas_call | solution.py:479
  159.5 1.5 collective-permute-done.2.refs_0_
  161.0 1.8 collective-permute-done.5.refs_3_.refs_2_
  162.9 3.6 %shard_map.62 = (f32[16,32,8,128]{3,2,1,0:T(8,128)S(1)}, f32[7,16,8,128]{3,2,1,0:T(8,128)S(1)}, f32[7,16,8,128]{3,2,1,0:T(8,128)S(1)}) custom-call(s32[32,32]{1,0:T(8,128)S(1)} %copy-done, f32[32,7,8,128]{3,2,1,0:T(8,128)S(1)} %collective-permute-done.2.refs_0_, f32[16,16,8,128]{3,2,1,0:T(8,128)S(1)} %get-tuple-element.23.refs_3_.refs_0_.refs_1_, ...), custom_call_target="tpu_custom_call" | custom-call | flops 10485760000 | bytes 2097152 | tf_op jit(solution)/shard_map/pallas_call | solution.py:479
  166.5 2.3 %collective-permute-start.6 = (f32[7,16,8,128]{3,2,1,0:T(8,128)S(1)}, f32[7,16,8,128]{3,2,1,0:T(8,128)S(1)}, u32[]{:S(2)}, u32[]{:S(2)}) collective-permute-start(f32[7,16,8,128]{3,2,1,0:T(8,128)S(1)} %get-tuple-element.28), channel_id=1, source_target_pairs={{0,4},{4,8},{8,12},{12,16},{16,20},{20,24},{24,28},{1,5},{5,9},{9,... | collective-permute-start | bytes 1376264 | tf_op jit(solution)/shard_map/ppermute | solution.py:501
  168.8 2.2 %collective-permute-start.7 = (f32[7,16,8,128]{3,2,1,0:T(8,128)S(1)}, f32[7,16,8,128]{3,2,1,0:T(8,128)S(1)}, u32[]{:S(2)}, u32[]{:S(2)}) collective-permute-start(f32[7,16,8,128]{3,2,1,0:T(8,128)S(1)} %get-tuple-element.30), channel_id=1, source_target_pairs={{4,0},{8,4},{12,8},{16,12},{20,16},{24,20},{28,24},{5,1},{9,5},{13... | collective-permute-start | bytes 1376264 | tf_op jit(solution)/shard_map/ppermute | solution.py:502
  171.0 3.4 %shard_map.63.refs_1_.refs_2_ = f32[16,32,8,128]{3,2,1,0:T(8,128)S(1)} custom-call(s32[32,32]{1,0:T(8,128)S(1)} %copy-done, f32[32,7,8,128]{3,2,1,0:T(8,128)S(1)} %collective-permute-done.2.refs_0_, f32[16,32,8,128]{3,2,1,0:T(8,128)S(1)} %shard_map.57.refs_3_.refs_0_.refs_1_, f32[32,7,8,128]{3,2,1,0:T(8,128)S(1)} %collective-permute-done.5.refs_3_.refs_2_, ...), custom_call_target="tpu_custom_call" | custom-call | flops 10485760000 | bytes 2097152 | tf_op jit(solution)/shard_map/pallas_call | solution.py:479
  174.4 8.5 %shard_map.64.refs_4_ = f32[32,32,1024]{2,1,0:T(8,128)} custom-call(s32[32,32]{1,0:T(8,128)S(1)} %copy-done.1, f32[16,32,8,128]{3,2,1,0:T(8,128)S(1)} %get-tuple-element.29.refs_4_.refs_0_.refs_1_, f32[16,32,8,128]{3,2,1,0:T(8,128)S(1)} %shard_map.63.refs_1_.refs_2_), custom_call_target="tpu_custom_call" | custom-call | flops 20971520000 | bytes 4194304 | tf_op jit(solution)/shard_map/pallas_call | solution.py:479
  182.9 0.0 collective-permute-done.8.refs_0_
  182.9 0.0 collective-permute-done.9.refs_3_
  183.0 5.1 %shard_map.65.refs_4_ = f32[32,32,1024]{2,1,0:T(8,128)} custom-call(s32[32,32]{1,0:T(8,128)S(1)} %copy-done.1, f32[7,16,8,128]{3,2,1,0:T(8,128)S(1)} %collective-permute-done.8.refs_0_, f32[16,32,8,128]{3,2,1,0:T(8,128)S(1)} %get-tuple-element.29.refs_4_.refs_0_.refs_1_, ...), custom_call_target="tpu_custom_call", output_to_operand_aliasing={{}: (5, {})} | custom-call | flops 10485760000 | bytes 2097152 | tf_op jit(solution)/shard_map/pallas_call | solution.py:479
  188.1 0.0 collective-permute-done.6.refs_0_
  188.1 0.0 collective-permute-done.7.refs_3_
  188.1 5.1 %shard_map.66 = f32[32,32,1024]{2,1,0:T(8,128)} custom-call(s32[32,32]{1,0:T(8,128)S(1)} %copy-done.1, f32[7,16,8,128]{3,2,1,0:T(8,128)S(1)} %collective-permute-done.6.refs_0_, f32[16,32,8,128]{3,2,1,0:T(8,128)S(1)} %get-tuple-element.29.refs_4_.refs_0_.refs_1_, f32[16,32,8,128]{3,2,1,0:T(8,128)S(1)} %shard_map.63.refs_1_.refs_2_, ...), custom_call_target="tpu_custom_call", output_to_operand_aliasing={{}: (5, {})} | custom-call | flops 10485760000 | bytes 2097152 | tf_op jit(solution)/shard_map/pallas_call | solution.py:479
Async XLA Ops:
  107.1 19.7 %copy-start.1 = (s32[32,32]{1,0:T(8,128)S(1)}, s32[32,32]{1,0:T(8,128)}, u32[]{:S(2)}) copy-start(s32[32,32]{1,0:T(8,128)} %dip_ref.19) | copy-start | bytes 12292
  114.6 18.1 %collective-permute-start = (f32[7,16,8,128]{3,2,1,0:T(8,128)S(1)}, f32[7,16,8,128]{3,2,1,0:T(8,128)S(1)}, u32[]{:S(2)}, u32[]{:S(2)}) collective-permute-start(f32[7,16,8,128]{3,2,1,0:T(8,128)S(1)} %get-tuple-element.19), channel_id=1, source_target_pairs={{0,4},{4,8},{8,12},{12,16},{16,20},{20,24},{24,28},{1,5},{5,9},{9,... | collective-permute-start | bytes 1376264 | tf_op jit(solution)/shard_map/ppermute | solution.py:501
  118.3 15.5 %collective-permute-start.1 = (f32[7,16,8,128]{3,2,1,0:T(8,128)S(1)}, f32[7,16,8,128]{3,2,1,0:T(8,128)S(1)}, u32[]{:S(2)}, u32[]{:S(2)}) collective-permute-start(f32[7,16,8,128]{3,2,1,0:T(8,128)S(1)} %get-tuple-element.21), channel_id=1, source_target_pairs={{4,0},{8,4},{12,8},{16,12},{20,16},{24,20},{28,24},{5,1},{9,5},{13... | collective-permute-start | bytes 1376264 | tf_op jit(solution)/shard_map/ppermute | solution.py:502
  120.3 22.5 %collective-permute-start.3 = (f32[7,16,8,128]{3,2,1,0:T(8,128)S(1)}, f32[7,16,8,128]{3,2,1,0:T(8,128)S(1)}, u32[]{:S(2)}, u32[]{:S(2)}) collective-permute-start(f32[7,16,8,128]{3,2,1,0:T(8,128)S(1)} %get-tuple-element.24), channel_id=1, source_target_pairs={{0,4},{4,8},{8,12},{12,16},{16,20},{20,24},{24,28},{1,5},{5,9},{9,... | collective-permute-start | bytes 1376264 | tf_op jit(solution)/shard_map/ppermute | solution.py:501
  124.8 18.0 %collective-permute-start.4 = (f32[7,16,8,128]{3,2,1,0:T(8,128)S(1)}, f32[7,16,8,128]{3,2,1,0:T(8,128)S(1)}, u32[]{:S(2)}, u32[]{:S(2)}) collective-permute-start(f32[7,16,8,128]{3,2,1,0:T(8,128)S(1)} %get-tuple-element.25), channel_id=1, source_target_pairs={{4,0},{8,4},{12,8},{16,12},{20,16},{24,20},{28,24},{5,1},{9,5},{13... | collective-permute-start | bytes 1376264 | tf_op jit(solution)/shard_map/ppermute | solution.py:502
  137.5 23.6 %collective-permute-start.2 = (f32[32,7,8,128]{3,2,1,0:T(8,128)S(1)}, f32[32,7,8,128]{3,2,1,0:T(8,128)S(1)}, u32[]{:S(2)}, u32[]{:S(2)}) collective-permute-start(f32[32,7,8,128]{3,2,1,0:T(8,128)S(1)} %get-tuple-element.22), channel_id=1, source_target_pairs={{0,1},{1,2},{2,3},{4,5},{5,6},{6,7},{8,9},{9,10},{10,11},{12,13},{... | collective-permute-start | bytes 2752520 | tf_op jit(solution)/shard_map/ppermute | solution.py:501
  139.6 23.3 %collective-permute-start.5 = (f32[32,7,8,128]{3,2,1,0:T(8,128)S(1)}, f32[32,7,8,128]{3,2,1,0:T(8,128)S(1)}, u32[]{:S(2)}, u32[]{:S(2)}) collective-permute-start(f32[32,7,8,128]{3,2,1,0:T(8,128)S(1)} %get-tuple-element.26), channel_id=1, source_target_pairs={{1,0},{2,1},{3,2},{5,4},{6,5},{7,6},{9,8},{10,9},{11,10},{13,12},{... | collective-permute-start | bytes 2752520 | tf_op jit(solution)/shard_map/ppermute | solution.py:502
  142.8 3.3 %copy-start = (s32[32,32]{1,0:T(8,128)S(1)}, s32[32,32]{1,0:T(8,128)}, u32[]{:S(2)}) copy-start(s32[32,32]{1,0:T(8,128)} %dip_ref.16) | copy-start | bytes 12292
  150.1 32.8 %collective-permute-start.8 = (f32[7,16,8,128]{3,2,1,0:T(8,128)S(1)}, f32[7,16,8,128]{3,2,1,0:T(8,128)S(1)}, u32[]{:S(2)}, u32[]{:S(2)}) collective-permute-start(f32[7,16,8,128]{3,2,1,0:T(8,128)S(1)} %get-tuple-element.31), channel_id=1, source_target_pairs={{0,4},{4,8},{8,12},{12,16},{16,20},{20,24},{24,28},{1,5},{5,9},{9,... | collective-permute-start | bytes 1376264 | tf_op jit(solution)/shard_map/ppermute | solution.py:501
  154.1 28.8 %collective-permute-start.9 = (f32[7,16,8,128]{3,2,1,0:T(8,128)S(1)}, f32[7,16,8,128]{3,2,1,0:T(8,128)S(1)}, u32[]{:S(2)}, u32[]{:S(2)}) collective-permute-start(f32[7,16,8,128]{3,2,1,0:T(8,128)S(1)} %get-tuple-element.32), channel_id=1, source_target_pairs={{4,0},{8,4},{12,8},{16,12},{20,16},{24,20},{28,24},{5,1},{9,5},{13... | collective-permute-start | bytes 1376264 | tf_op jit(solution)/shard_map/ppermute | solution.py:502
  166.5 21.6 %collective-permute-start.6 = (f32[7,16,8,128]{3,2,1,0:T(8,128)S(1)}, f32[7,16,8,128]{3,2,1,0:T(8,128)S(1)}, u32[]{:S(2)}, u32[]{:S(2)}) collective-permute-start(f32[7,16,8,128]{3,2,1,0:T(8,128)S(1)} %get-tuple-element.28), channel_id=1, source_target_pairs={{0,4},{4,8},{8,12},{12,16},{16,20},{20,24},{24,28},{1,5},{5,9},{9,... | collective-permute-start | bytes 1376264 | tf_op jit(solution)/shard_map/ppermute | solution.py:501
  168.8 19.3 %collective-permute-start.7 = (f32[7,16,8,128]{3,2,1,0:T(8,128)S(1)}, f32[7,16,8,128]{3,2,1,0:T(8,128)S(1)}, u32[]{:S(2)}, u32[]{:S(2)}) collective-permute-start(f32[7,16,8,128]{3,2,1,0:T(8,128)S(1)} %get-tuple-element.30), channel_id=1, source_target_pairs={{4,0},{8,4},{12,8},{16,12},{20,16},{24,20},{28,24},{5,1},{9,5},{13... | collective-permute-start | bytes 1376264 | tf_op jit(solution)/shard_map/ppermute | solution.py:502

commit v16 on v15

--- a/solution.py
+++ b/solution.py
@@ -489,7 +489,7 @@
         input_output_aliases=aliases,
         compiler_params=pltpu.CompilerParams(vmem_limit_bytes=16 * MIB),
         cost_estimate=pl.CostEstimate(
-            flops=40000 * outputs * lines * samples,
+            flops=16000 * outputs * lines * samples,
             bytes_accessed=8 * outputs * lines * samples,
             transcendentals=0,
         ),
@@ -586,6 +586,14 @@
         dip_cross, [(middle, False)], 1, mid_rows, inner,
         mid_windows(span_of(0, BORDER - HALF, mid_cols + 2 * HALF), cols), mid_place, after=second_mid,
     )
+    places = span_of(0, BORDER - HALF, HALF) + span_of(1, 0, mid_rows) + span_of(0, BORDER, HALF)
+    middle_windows = mid_windows(places, rows)
+    middle_batches = [[(0, first, WINDOW)] for first in range(BORDER, cols - BORDER, WINDOW)]
+    outer_batches = [[(0, 0, BORDER), (BORDER, cols - BORDER, BORDER)]]
+    (result,) = steer(
+        dip_inline, [(second_mid, False), (centre, False)], 0, mid_cols, inner, middle_windows, mid_place,
+        batches=middle_batches,
+    )
     windows = [
         (0, BORDER, span_of(0, 0, HALF) + span_of(1, 0, BORDER) + span_of(2, 0, HALF)),
         (cols - BORDER, BORDER, span_of(2, mid_cols - HALF, HALF) + span_of(1, BORDER, BORDER) + span_of(3, 0, HALF)),
@@ -606,18 +614,17 @@
         filled=(3, (every, middle_cols)), after=border_second,
     )
 
-    places = span_of(0, BORDER - HALF, HALF) + span_of(1, 0, mid_rows) + span_of(0, BORDER, HALF)
     (result,) = steer(
-        dip_inline, [(border_second, True), (middle_second, True)], 0, cols, same, mid_windows(places, rows), mid_place,
-        batches=[[(0, first, WINDOW)] for first in range(0, cols, WINDOW)],
+        dip_inline, [(border_second, True), (middle_second, True)], 0, both, outer_col, middle_windows, mid_place,
+        batches=outer_batches, before=result,
     )
     windows = [
         (0, BORDER, span_of(0, 0, HALF) + span_of(1, 0, BORDER) + span_of(2, 0, HALF)),
         (rows - BORDER, BORDER, span_of(2, mid_rows - HALF, HALF) + span_of(1, BORDER, BORDER) + span_of(3, 0, HALF)),
     ]
     for low, high, lines, line_of, batches in (
-        (low_mid, high_mid, mid_cols, inner, [[(0, first, WINDOW)] for first in range(BORDER, cols - BORDER, WINDOW)]),
-        (low_out, high_out, both, outer_col, [[(0, 0, BORDER), (BORDER, cols - BORDER, BORDER)]]),
+        (low_mid, high_mid, mid_cols, inner, middle_batches),
+        (low_out, high_out, both, outer_col, outer_batches),
     ):
         (result,) = steer(
             dip_inline, [(low, False), (border_second, True), (middle_second, True), (high, False)], 0, lines, line_of,

time: 196 us -> 196 us (level)
  waiting for transfers between devices: 4.49 us -> 0.94 us
  starting transfers between devices: 27.9 us -> 30.7 us
    ppermute x5, starting transfers between devices: 16.7 us -> 19.4 us  [swap_ends(): low = lax.ppermute(tail, axis, [(i, i + 1) for i in range(count - 1)])]
    ppermute x5, waiting for transfers between devices: 2.95 us -> 0.93 us  [swap_ends(): high = lax.ppermute(head, axis, [(i + 1, i) for i in range(count - 1)])]
    pallas_call x10 -> x11, Pallas kernels: 46 us -> 47.9 us  [steer(): pl.pallas_call(functools.partial(steer_kernel, along=along, whole=[whole...]
  transfers between devices with their start and end apart: 10 -> 10, of which waited for: 3 -> 1; matrix products, arithmetic and copies ran while one was open for 0% -> 0% of each run, Pallas kernels for 21% -> 22%
where the time goes in v16:
time: 196 us; the launch traced here: 194 us
  blocking collectives  102 us (52%)
  Pallas kernels  60.6 us (31%)
  starting transfers between devices  30.7 us (16%)
    all_to_all x1, blocking collectives, on_device(): lax.all_to_all(outgoing, BOTH, split_axis=0, concat_axis=0, tiled=True)  102 us
    pallas_call x11, Pallas kernels, steer(): pl.pallas_call(functools.partial(steer_kernel, along=along, whole=[whole...  47.9 us
    ppermute x5, starting transfers between devices, swap_ends(): low = lax.ppermute(tail, axis, [(i, i + 1) for i in range(count - 1)])  19.4 us
    ppermute x5, starting transfers between devices, swap_ends(): high = lax.ppermute(head, axis, [(i + 1, i) for i in range(count - 1)])  11.3 us
    pallas_call x1, Pallas kernels, stack_bins(): pl.pallas_call(functools.partial(bin_kernel, capacity=capacity, block_row...  7.23 us
    pallas_call x1, Pallas kernels, pack(): pl.pallas_call(functools.partial(pack_kernel, capacity=capacity), in_spec...  5.45 us
  transfers between devices with their start and end apart: 10, of which 1 were waited for; matrix products, arithmetic and copies ran while one was open for 0% of the time, Pallas kernels for 22%

profile of v16, /device:TPU:11, one launch (start us, length us, event | category | flops | bytes accessed | tf_op | source)
XLA Modules:
  0.0 194.4 jit_solution(6849960467457444158)
XLA Ops:
  0.0 5.5 %shard_map.55 = f32[32,264,128]{2,1,0:T(8,128)} custom-call(s32[1]{0:T(128)} %bitcast.mine_ref, s32[128]{0:T(128)} %bitcast.4, s32[4,128]{1,0:T(4,128)} %bitcast.3, f32[128,4,1024]{2,1,0:T(4,128)} %traces_ref.1), custom_call_target="tpu_custom_call" | custom-call | tf_op jit(solution)/shard_map/pallas_call | solution.py:138
  5.5 101.7 %all_to_all.5.blocks_ref = f32[32,264,128]{2,1,0:T(8,128)S(1)} all-to-all(f32[32,264,128]{2,1,0:T(8,128)} %shard_map.55), channel_id=1, replica_groups=mesh['inline'=8,'crosslin'=4] {'inline','crosslin'}, dimensions={0} | all-to-all | bytes 8650752 | tf_op jit(solution)/shard_map/all_to_all | solution.py:642
  107.2 0.0 copy-start.1
  107.2 7.2 %shard_map.56 = (f32[32,32,8,128]{3,2,1,0:T(8,128)S(1)}, f32[7,16,8,128]{3,2,1,0:T(8,128)S(1)}, f32[7,16,8,128]{3,2,1,0:T(8,128)S(1)}, f32[7,16,8,128]{3,2,1,0:T(8,128)S(1)}, f32[7,16,8,128]{3,2,1,0:T(8,128)S(1)}) custom-call(f32[32,264,128]{2,1,0:T(8,128)S(1)} %all_to_all.5.blocks_ref), custom_call_target="tpu_custom_call" | custom-call | tf_op jit(solution)/shard_map/pallas_call | solution.py:249
  114.4 4.2 %collective-permute-start = (f32[7,16,8,128]{3,2,1,0:T(8,128)S(1)}, f32[7,16,8,128]{3,2,1,0:T(8,128)S(1)}, u32[]{:S(2)}, u32[]{:S(2)}) collective-permute-start(f32[7,16,8,128]{3,2,1,0:T(8,128)S(1)} %get-tuple-element.19), channel_id=1, source_target_pairs={{0,4},{4,8},{8,12},{12,16},{16,20},{20,24},{24,28},{1,5},{5,9},{9,... | collective-permute-start | bytes 1376264 | tf_op jit(solution)/shard_map/ppermute | solution.py:501
  118.6 1.9 collective-permute-start.1
  120.6 4.5 %collective-permute-start.3 = (f32[7,16,8,128]{3,2,1,0:T(8,128)S(1)}, f32[7,16,8,128]{3,2,1,0:T(8,128)S(1)}, u32[]{:S(2)}, u32[]{:S(2)}) collective-permute-start(f32[7,16,8,128]{3,2,1,0:T(8,128)S(1)} %get-tuple-element.24), channel_id=1, source_target_pairs={{0,4},{4,8},{8,12},{12,16},{16,20},{20,24},{24,28},{1,5},{5,9},{9,... | collective-permute-start | bytes 1376264 | tf_op jit(solution)/shard_map/ppermute | solution.py:501
  125.1 1.9 collective-permute-start.4
  127.0 0.0 copy-done.1
  127.1 5.9 %shard_map.57.refs_3_.refs_0_.refs_1_ = f32[16,32,8,128]{3,2,1,0:T(8,128)S(1)} custom-call(s32[32,32]{1,0:T(8,128)S(1)} %copy-done.1, f32[32,32,8,128]{3,2,1,0:T(8,128)S(1)} %get-tuple-element.20.refs_0_.refs_1_), custom_call_target="tpu_custom_call" | custom-call | flops 8388608000 | bytes 4194304 | tf_op jit(solution)/shard_map/pallas_call | solution.py:479
  133.0 0.0 collective-permute-done.refs_0_
  133.0 0.9 collective-permute-done.1.refs_2_
  133.9 3.6 %shard_map.58 = (f32[16,16,8,128]{3,2,1,0:T(8,128)S(1)}, f32[32,7,8,128]{3,2,1,0:T(8,128)S(1)}, f32[32,7,8,128]{3,2,1,0:T(8,128)S(1)}) custom-call(s32[32,32]{1,0:T(8,128)S(1)} %copy-done.1, f32[7,16,8,128]{3,2,1,0:T(8,128)S(1)} %collective-permute-done.refs_0_, f32[32,32,8,128]{3,2,1,0:T(8,128)S(1)} %get-tuple-element.20.refs_0_.refs_1_, ...), custom_call_target="tpu_custom_call" | custom-call | flops 4194304000 | bytes 2097152 | tf_op jit(solution)/shard_map/pallas_call | solution.py:479
  137.6 1.9 collective-permute-start.2
  139.5 3.4 %collective-permute-start.5 = (f32[32,7,8,128]{3,2,1,0:T(8,128)S(1)}, f32[32,7,8,128]{3,2,1,0:T(8,128)S(1)}, u32[]{:S(2)}, u32[]{:S(2)}) collective-permute-start(f32[32,7,8,128]{3,2,1,0:T(8,128)S(1)} %get-tuple-element.26), channel_id=1, source_target_pairs={{1,0},{2,1},{3,2},{5,4},{6,5},{7,6},{9,8},{10,9},{11,10},{13,12},{... | collective-permute-start | bytes 2752520 | tf_op jit(solution)/shard_map/ppermute | solution.py:502
  142.9 0.0 collective-permute-done.3.refs_0_
  142.9 0.0 collective-permute-done.4.refs_2_
  142.9 0.0 copy-start
  142.9 3.3 %shard_map.59.refs_1_.refs_2_ = f32[16,16,8,128]{3,2,1,0:T(8,128)S(1)} custom-call(s32[32,32]{1,0:T(8,128)S(1)} %copy-done.1, f32[7,16,8,128]{3,2,1,0:T(8,128)S(1)} %collective-permute-done.3.refs_0_, f32[32,32,8,128]{3,2,1,0:T(8,128)S(1)} %get-tuple-element.20.refs_0_.refs_1_, f32[7,16,8,128]{3,2,1,0:T(8,128)S(1)} %collective-permute-done.4.refs_2_, ...), custom_call_target="tpu_custom_call" | custom-call | flops 4194304000 | bytes 2097152 | tf_op jit(solution)/shard_map/pallas_call | solution.py:479
  146.3 0.0 copy-done
  146.3 4.0 %shard_map.60 = (f32[16,16,8,128]{3,2,1,0:T(8,128)S(1)}, f32[7,16,8,128]{3,2,1,0:T(8,128)S(1)}, f32[7,16,8,128]{3,2,1,0:T(8,128)S(1)}) custom-call(s32[32,32]{1,0:T(8,128)S(1)} %copy-done, f32[16,16,8,128]{3,2,1,0:T(8,128)S(1)} %get-tuple-element.23.refs_3_.refs_0_.refs_1_, f32[16,16,8,128]{3,2,1,0:T(8,128)S(1)} %shard_map.59.refs_1_.refs_2_), custom_call_target="tpu_custom_call" | custom-call | flops 4194304000 | bytes 2097152 | tf_op jit(solution)/shard_map/pallas_call | solution.py:479
  150.3 4.2 %collective-permute-start.8 = (f32[7,16,8,128]{3,2,1,0:T(8,128)S(1)}, f32[7,16,8,128]{3,2,1,0:T(8,128)S(1)}, u32[]{:S(2)}, u32[]{:S(2)}) collective-permute-start(f32[7,16,8,128]{3,2,1,0:T(8,128)S(1)} %get-tuple-element.31), channel_id=1, source_target_pairs={{0,4},{4,8},{8,12},{12,16},{16,20},{20,24},{24,28},{1,5},{5,9},{9,... | collective-permute-start | bytes 1376264 | tf_op jit(solution)/shard_map/ppermute | solution.py:501
  154.4 1.9 collective-permute-start.9
  156.4 3.4 %shard_map.61.refs_5_.refs_3_.refs_1_ = f32[16,16,8,128]{3,2,1,0:T(8,128)S(1)} custom-call(s32[32,32]{1,0:T(8,128)S(1)} %copy-done, f32[16,32,8,128]{3,2,1,0:T(8,128)S(1)} %shard_map.57.refs_3_.refs_0_.refs_1_, f32[16,16,8,128]{3,2,1,0:T(8,128)S(1)} %get-tuple-element.27.refs_1_.refs_4_.refs_0_), custom_call_target="tpu_custom_call" | custom-call | flops 4194304000 | bytes 2097152 | tf_op jit(solution)/shard_map/pallas_call | solution.py:479
  159.8 5.2 %shard_map.64.refs_2_ = f32[32,32,1024]{2,1,0:T(8,128)} custom-call(s32[32,32]{1,0:T(8,128)S(1)} %copy-done.1, f32[16,16,8,128]{3,2,1,0:T(8,128)S(1)} %get-tuple-element.27.refs_1_.refs_4_.refs_0_, f32[16,16,8,128]{3,2,1,0:T(8,128)S(1)} %shard_map.61.refs_5_.refs_3_.refs_1_), custom_call_target="tpu_custom_call" | custom-call | flops 4194304000 | bytes 2097152 | tf_op jit(solution)/shard_map/pallas_call | solution.py:479
  165.0 0.0 collective-permute-done.2.refs_0_
  165.0 0.0 collective-permute-done.5.refs_3_.refs_2_
  165.1 3.6 %shard_map.62 = (f32[16,32,8,128]{3,2,1,0:T(8,128)S(1)}, f32[7,16,8,128]{3,2,1,0:T(8,128)S(1)}, f32[7,16,8,128]{3,2,1,0:T(8,128)S(1)}) custom-call(s32[32,32]{1,0:T(8,128)S(1)} %copy-done, f32[32,7,8,128]{3,2,1,0:T(8,128)S(1)} %collective-permute-done.2.refs_0_, f32[16,16,8,128]{3,2,1,0:T(8,128)S(1)} %get-tuple-element.23.refs_3_.refs_0_.refs_1_, ...), custom_call_target="tpu_custom_call" | custom-call | flops 4194304000 | bytes 2097152 | tf_op jit(solution)/shard_map/pallas_call | solution.py:479
  168.7 4.5 %collective-permute-start.6 = (f32[7,16,8,128]{3,2,1,0:T(8,128)S(1)}, f32[7,16,8,128]{3,2,1,0:T(8,128)S(1)}, u32[]{:S(2)}, u32[]{:S(2)}) collective-permute-start(f32[7,16,8,128]{3,2,1,0:T(8,128)S(1)} %get-tuple-element.28), channel_id=1, source_target_pairs={{0,4},{4,8},{8,12},{12,16},{16,20},{20,24},{24,28},{1,5},{5,9},{9,... | collective-permute-start | bytes 1376264 | tf_op jit(solution)/shard_map/ppermute | solution.py:501
  173.2 2.1 %collective-permute-start.7 = (f32[7,16,8,128]{3,2,1,0:T(8,128)S(1)}, f32[7,16,8,128]{3,2,1,0:T(8,128)S(1)}, u32[]{:S(2)}, u32[]{:S(2)}) collective-permute-start(f32[7,16,8,128]{3,2,1,0:T(8,128)S(1)} %get-tuple-element.30), channel_id=1, source_target_pairs={{4,0},{8,4},{12,8},{16,12},{20,16},{24,20},{28,24},{5,1},{9,5},{13... | collective-permute-start | bytes 1376264 | tf_op jit(solution)/shard_map/ppermute | solution.py:502
  175.3 3.4 %shard_map.63.refs_1_.refs_2_ = f32[16,32,8,128]{3,2,1,0:T(8,128)S(1)} custom-call(s32[32,32]{1,0:T(8,128)S(1)} %copy-done, f32[32,7,8,128]{3,2,1,0:T(8,128)S(1)} %collective-permute-done.2.refs_0_, f32[16,32,8,128]{3,2,1,0:T(8,128)S(1)} %shard_map.57.refs_3_.refs_0_.refs_1_, f32[32,7,8,128]{3,2,1,0:T(8,128)S(1)} %collective-permute-done.5.refs_3_.refs_2_, ...), custom_call_target="tpu_custom_call" | custom-call | flops 4194304000 | bytes 2097152 | tf_op jit(solution)/shard_map/pallas_call | solution.py:479
  178.7 5.3 %shard_map.65.refs_4_ = f32[32,32,1024]{2,1,0:T(8,128)} custom-call(s32[32,32]{1,0:T(8,128)S(1)} %copy-done.1, f32[16,32,8,128]{3,2,1,0:T(8,128)S(1)} %get-tuple-element.29.refs_4_.refs_0_.refs_1_, f32[16,32,8,128]{3,2,1,0:T(8,128)S(1)} %shard_map.63.refs_1_.refs_2_, f32[32,32,1024]{2,1,0:T(8,128)} %shard_map.64.refs_2_), custom_call_target="tpu_custom_call", output_to_operand_aliasing={{}: (3, {})} | custom-call | flops 4194304000 | bytes 2097152 | tf_op jit(solution)/shard_map/pallas_call | solution.py:479
  184.0 0.0 collective-permute-done.8.refs_0_
  184.0 0.0 collective-permute-done.9.refs_3_
  184.0 5.1 %shard_map.66.refs_4_ = f32[32,32,1024]{2,1,0:T(8,128)} custom-call(s32[32,32]{1,0:T(8,128)S(1)} %copy-done.1, f32[7,16,8,128]{3,2,1,0:T(8,128)S(1)} %collective-permute-done.8.refs_0_, f32[16,32,8,128]{3,2,1,0:T(8,128)S(1)} %get-tuple-element.29.refs_4_.refs_0_.refs_1_, ...), custom_call_target="tpu_custom_call", output_to_operand_aliasing={{}: (5, {})} | custom-call | flops 4194304000 | bytes 2097152 | tf_op jit(solution)/shard_map/pallas_call | solution.py:479
  189.1 0.0 collective-permute-done.6.refs_0_
  189.1 0.0 collective-permute-done.7.refs_3_
  189.1 5.1 %shard_map.67 = f32[32,32,1024]{2,1,0:T(8,128)} custom-call(s32[32,32]{1,0:T(8,128)S(1)} %copy-done.1, f32[7,16,8,128]{3,2,1,0:T(8,128)S(1)} %collective-permute-done.6.refs_0_, f32[16,32,8,128]{3,2,1,0:T(8,128)S(1)} %get-tuple-element.29.refs_4_.refs_0_.refs_1_, f32[16,32,8,128]{3,2,1,0:T(8,128)S(1)} %shard_map.63.refs_1_.refs_2_, ...), custom_call_target="tpu_custom_call", output_to_operand_aliasing={{}: (5, {})} | custom-call | flops 4194304000 | bytes 2097152 | tf_op jit(solution)/shard_map/pallas_call | solution.py:479
Async XLA Ops:
  107.2 19.9 %copy-start.1 = (s32[32,32]{1,0:T(8,128)S(1)}, s32[32,32]{1,0:T(8,128)}, u32[]{:S(2)}) copy-start(s32[32,32]{1,0:T(8,128)} %dip_ref.21) | copy-start | bytes 12292
  114.4 18.6 %collective-permute-start = (f32[7,16,8,128]{3,2,1,0:T(8,128)S(1)}, f32[7,16,8,128]{3,2,1,0:T(8,128)S(1)}, u32[]{:S(2)}, u32[]{:S(2)}) collective-permute-start(f32[7,16,8,128]{3,2,1,0:T(8,128)S(1)} %get-tuple-element.19), channel_id=1, source_target_pairs={{0,4},{4,8},{8,12},{12,16},{16,20},{20,24},{24,28},{1,5},{5,9},{9,... | collective-permute-start | bytes 1376264 | tf_op jit(solution)/shard_map/ppermute | solution.py:501
  118.6 15.3 %collective-permute-start.1 = (f32[7,16,8,128]{3,2,1,0:T(8,128)S(1)}, f32[7,16,8,128]{3,2,1,0:T(8,128)S(1)}, u32[]{:S(2)}, u32[]{:S(2)}) collective-permute-start(f32[7,16,8,128]{3,2,1,0:T(8,128)S(1)} %get-tuple-element.21), channel_id=1, source_target_pairs={{4,0},{8,4},{12,8},{16,12},{20,16},{24,20},{28,24},{5,1},{9,5},{13... | collective-permute-start | bytes 1376264 | tf_op jit(solution)/shard_map/ppermute | solution.py:502
  120.6 22.3 %collective-permute-start.3 = (f32[7,16,8,128]{3,2,1,0:T(8,128)S(1)}, f32[7,16,8,128]{3,2,1,0:T(8,128)S(1)}, u32[]{:S(2)}, u32[]{:S(2)}) collective-permute-start(f32[7,16,8,128]{3,2,1,0:T(8,128)S(1)} %get-tuple-element.24), channel_id=1, source_target_pairs={{0,4},{4,8},{8,12},{12,16},{16,20},{20,24},{24,28},{1,5},{5,9},{9,... | collective-permute-start | bytes 1376264 | tf_op jit(solution)/shard_map/ppermute | solution.py:501
  125.1 17.8 %collective-permute-start.4 = (f32[7,16,8,128]{3,2,1,0:T(8,128)S(1)}, f32[7,16,8,128]{3,2,1,0:T(8,128)S(1)}, u32[]{:S(2)}, u32[]{:S(2)}) collective-permute-start(f32[7,16,8,128]{3,2,1,0:T(8,128)S(1)} %get-tuple-element.25), channel_id=1, source_target_pairs={{4,0},{8,4},{12,8},{16,12},{20,16},{24,20},{28,24},{5,1},{9,5},{13... | collective-permute-start | bytes 1376264 | tf_op jit(solution)/shard_map/ppermute | solution.py:502
  137.6 27.5 %collective-permute-start.2 = (f32[32,7,8,128]{3,2,1,0:T(8,128)S(1)}, f32[32,7,8,128]{3,2,1,0:T(8,128)S(1)}, u32[]{:S(2)}, u32[]{:S(2)}) collective-permute-start(f32[32,7,8,128]{3,2,1,0:T(8,128)S(1)} %get-tuple-element.22), channel_id=1, source_target_pairs={{0,1},{1,2},{2,3},{4,5},{5,6},{6,7},{8,9},{9,10},{10,11},{12,13},{... | collective-permute-start | bytes 2752520 | tf_op jit(solution)/shard_map/ppermute | solution.py:501
  139.5 25.6 %collective-permute-start.5 = (f32[32,7,8,128]{3,2,1,0:T(8,128)S(1)}, f32[32,7,8,128]{3,2,1,0:T(8,128)S(1)}, u32[]{:S(2)}, u32[]{:S(2)}) collective-permute-start(f32[32,7,8,128]{3,2,1,0:T(8,128)S(1)} %get-tuple-element.26), channel_id=1, source_target_pairs={{1,0},{2,1},{3,2},{5,4},{6,5},{7,6},{9,8},{10,9},{11,10},{13,12},{... | collective-permute-start | bytes 2752520 | tf_op jit(solution)/shard_map/ppermute | solution.py:502
  142.9 3.3 %copy-start = (s32[32,32]{1,0:T(8,128)S(1)}, s32[32,32]{1,0:T(8,128)}, u32[]{:S(2)}) copy-start(s32[32,32]{1,0:T(8,128)} %dip_ref.17) | copy-start | bytes 12292
  150.3 33.7 %collective-permute-start.8 = (f32[7,16,8,128]{3,2,1,0:T(8,128)S(1)}, f32[7,16,8,128]{3,2,1,0:T(8,128)S(1)}, u32[]{:S(2)}, u32[]{:S(2)}) collective-permute-start(f32[7,16,8,128]{3,2,1,0:T(8,128)S(1)} %get-tuple-element.31), channel_id=1, source_target_pairs={{0,4},{4,8},{8,12},{12,16},{16,20},{20,24},{24,28},{1,5},{5,9},{9,... | collective-permute-start | bytes 1376264 | tf_op jit(solution)/shard_map/ppermute | solution.py:501
  154.4 29.5 %collective-permute-start.9 = (f32[7,16,8,128]{3,2,1,0:T(8,128)S(1)}, f32[7,16,8,128]{3,2,1,0:T(8,128)S(1)}, u32[]{:S(2)}, u32[]{:S(2)}) collective-permute-start(f32[7,16,8,128]{3,2,1,0:T(8,128)S(1)} %get-tuple-element.32), channel_id=1, source_target_pairs={{4,0},{8,4},{12,8},{16,12},{20,16},{24,20},{28,24},{5,1},{9,5},{13... | collective-permute-start | bytes 1376264 | tf_op jit(solution)/shard_map/ppermute | solution.py:502
  168.7 20.5 %collective-permute-start.6 = (f32[7,16,8,128]{3,2,1,0:T(8,128)S(1)}, f32[7,16,8,128]{3,2,1,0:T(8,128)S(1)}, u32[]{:S(2)}, u32[]{:S(2)}) collective-permute-start(f32[7,16,8,128]{3,2,1,0:T(8,128)S(1)} %get-tuple-element.28), channel_id=1, source_target_pairs={{0,4},{4,8},{8,12},{12,16},{16,20},{20,24},{24,28},{1,5},{5,9},{9,... | collective-permute-start | bytes 1376264 | tf_op jit(solution)/shard_map/ppermute | solution.py:501
  173.2 15.9 %collective-permute-start.7 = (f32[7,16,8,128]{3,2,1,0:T(8,128)S(1)}, f32[7,16,8,128]{3,2,1,0:T(8,128)S(1)}, u32[]{:S(2)}, u32[]{:S(2)}) collective-permute-start(f32[7,16,8,128]{3,2,1,0:T(8,128)S(1)} %get-tuple-element.30), channel_id=1, source_target_pairs={{4,0},{8,4},{12,8},{16,12},{20,16},{24,20},{28,24},{5,1},{9,5},{13... | collective-permute-start | bytes 1376264 | tf_op jit(solution)/shard_map/ppermute | solution.py:502

commit v17 on v16

--- a/solution.py
+++ b/solution.py
@@ -442,7 +442,7 @@
 ):
     samples = PHASES * LANES
     outputs = sum(count for _, count, _ in windows)
-    final = 16 if batches is not None else 0
+    final = BORDER if batches is not None else 0
     abreast = 4 * WINDOW // outputs
     shapes, specs, sems = edge_outputs(edges)
     operands = [dip] + [array for array, _ in pieces]
@@ -588,8 +588,8 @@
     )
     places = span_of(0, BORDER - HALF, HALF) + span_of(1, 0, mid_rows) + span_of(0, BORDER, HALF)
     middle_windows = mid_windows(places, rows)
-    middle_batches = [[(0, first, WINDOW)] for first in range(BORDER, cols - BORDER, WINDOW)]
-    outer_batches = [[(0, 0, BORDER), (BORDER, cols - BORDER, BORDER)]]
+    middle_batches = [[(0, first, BORDER)] for first in range(BORDER, cols - BORDER, BORDER)]
+    outer_batches = [[(0, 0, BORDER)], [(0, cols - BORDER, BORDER)]]
     (result,) = steer(
         dip_inline, [(second_mid, False), (centre, False)], 0, mid_cols, inner, middle_windows, mid_place,
         batches=middle_batches,

time: 196 us -> 196 us (level)
  no operation moved by 1% of the time
where the time goes in v17:
time: 196 us; the launch traced here: 194 us
  blocking collectives  102 us (52%)
  Pallas kernels  60.7 us (31%)
  starting transfers between devices  30.4 us (16%)
    all_to_all x1, blocking collectives, on_device(): lax.all_to_all(outgoing, BOTH, split_axis=0, concat_axis=0, tiled=True)  102 us
    pallas_call x11, Pallas kernels, steer(): pl.pallas_call(functools.partial(steer_kernel, along=along, whole=[whole...  47.8 us
    ppermute x5, starting transfers between devices, swap_ends(): low = lax.ppermute(tail, axis, [(i, i + 1) for i in range(count - 1)])  19.1 us
    ppermute x5, starting transfers between devices, swap_ends(): high = lax.ppermute(head, axis, [(i + 1, i) for i in range(count - 1)])  11.3 us
    pallas_call x1, Pallas kernels, stack_bins(): pl.pallas_call(functools.partial(bin_kernel, capacity=capacity, block_row...  7.49 us
    pallas_call x1, Pallas kernels, pack(): pl.pallas_call(functools.partial(pack_kernel, capacity=capacity), in_spec...  5.43 us
  transfers between devices with their start and end apart: 10, of which 1 were waited for; matrix products, arithmetic and copies ran while one was open for 0% of the time, Pallas kernels for 22%

profile of v17, /device:TPU:11, one launch (start us, length us, event | category | flops | bytes accessed | tf_op | source)
XLA Modules:
  0.0 194.3 jit_solution(17720880117518109816)
XLA Ops:
  0.0 5.4 %shard_map.55 = f32[32,264,128]{2,1,0:T(8,128)} custom-call(s32[1]{0:T(128)} %bitcast.mine_ref, s32[128]{0:T(128)} %bitcast.4, s32[4,128]{1,0:T(4,128)} %bitcast.3, f32[128,4,1024]{2,1,0:T(4,128)} %traces_ref.1), custom_call_target="tpu_custom_call" | custom-call | tf_op jit(solution)/shard_map/pallas_call | solution.py:138
  5.4 101.7 %all_to_all.5.blocks_ref = f32[32,264,128]{2,1,0:T(8,128)S(1)} all-to-all(f32[32,264,128]{2,1,0:T(8,128)} %shard_map.55), channel_id=1, replica_groups=mesh['inline'=8,'crosslin'=4] {'inline','crosslin'}, dimensions={0} | all-to-all | bytes 8650752 | tf_op jit(solution)/shard_map/all_to_all | solution.py:642
  107.1 0.0 copy-start.1
  107.1 7.5 %shard_map.56 = (f32[32,32,8,128]{3,2,1,0:T(8,128)S(1)}, f32[7,16,8,128]{3,2,1,0:T(8,128)S(1)}, f32[7,16,8,128]{3,2,1,0:T(8,128)S(1)}, f32[7,16,8,128]{3,2,1,0:T(8,128)S(1)}, f32[7,16,8,128]{3,2,1,0:T(8,128)S(1)}) custom-call(f32[32,264,128]{2,1,0:T(8,128)S(1)} %all_to_all.5.blocks_ref), custom_call_target="tpu_custom_call" | custom-call | tf_op jit(solution)/shard_map/pallas_call | solution.py:249
  114.6 4.0 %collective-permute-start = (f32[7,16,8,128]{3,2,1,0:T(8,128)S(1)}, f32[7,16,8,128]{3,2,1,0:T(8,128)S(1)}, u32[]{:S(2)}, u32[]{:S(2)}) collective-permute-start(f32[7,16,8,128]{3,2,1,0:T(8,128)S(1)} %get-tuple-element.19), channel_id=1, source_target_pairs={{0,4},{4,8},{8,12},{12,16},{16,20},{20,24},{24,28},{1,5},{5,9},{9,... | collective-permute-start | bytes 1376264 | tf_op jit(solution)/shard_map/ppermute | solution.py:501
  118.6 1.9 collective-permute-start.1
  120.6 4.5 %collective-permute-start.3 = (f32[7,16,8,128]{3,2,1,0:T(8,128)S(1)}, f32[7,16,8,128]{3,2,1,0:T(8,128)S(1)}, u32[]{:S(2)}, u32[]{:S(2)}) collective-permute-start(f32[7,16,8,128]{3,2,1,0:T(8,128)S(1)} %get-tuple-element.24), channel_id=1, source_target_pairs={{0,4},{4,8},{8,12},{12,16},{16,20},{20,24},{24,28},{1,5},{5,9},{9,... | collective-permute-start | bytes 1376264 | tf_op jit(solution)/shard_map/ppermute | solution.py:501
  125.1 1.9 collective-permute-start.4
  127.0 0.0 copy-done.1
  127.0 5.9 %shard_map.57.refs_3_.refs_0_.refs_1_ = f32[16,32,8,128]{3,2,1,0:T(8,128)S(1)} custom-call(s32[32,32]{1,0:T(8,128)S(1)} %copy-done.1, f32[32,32,8,128]{3,2,1,0:T(8,128)S(1)} %get-tuple-element.20.refs_0_.refs_1_), custom_call_target="tpu_custom_call" | custom-call | flops 8388608000 | bytes 4194304 | tf_op jit(solution)/shard_map/pallas_call | solution.py:479
  133.0 0.0 collective-permute-done.refs_0_
  133.0 1.0 collective-permute-done.1.refs_2_
  134.0 3.6 %shard_map.58 = (f32[16,16,8,128]{3,2,1,0:T(8,128)S(1)}, f32[32,7,8,128]{3,2,1,0:T(8,128)S(1)}, f32[32,7,8,128]{3,2,1,0:T(8,128)S(1)}) custom-call(s32[32,32]{1,0:T(8,128)S(1)} %copy-done.1, f32[7,16,8,128]{3,2,1,0:T(8,128)S(1)} %collective-permute-done.refs_0_, f32[32,32,8,128]{3,2,1,0:T(8,128)S(1)} %get-tuple-element.20.refs_0_.refs_1_, ...), custom_call_target="tpu_custom_call" | custom-call | flops 4194304000 | bytes 2097152 | tf_op jit(solution)/shard_map/pallas_call | solution.py:479
  137.6 1.9 collective-permute-start.2
  139.5 3.4 %collective-permute-start.5 = (f32[32,7,8,128]{3,2,1,0:T(8,128)S(1)}, f32[32,7,8,128]{3,2,1,0:T(8,128)S(1)}, u32[]{:S(2)}, u32[]{:S(2)}) collective-permute-start(f32[32,7,8,128]{3,2,1,0:T(8,128)S(1)} %get-tuple-element.26), channel_id=1, source_target_pairs={{1,0},{2,1},{3,2},{5,4},{6,5},{7,6},{9,8},{10,9},{11,10},{13,12},{... | collective-permute-start | bytes 2752520 | tf_op jit(solution)/shard_map/ppermute | solution.py:502
  143.0 0.0 collective-permute-done.3.refs_0_
  143.0 0.0 collective-permute-done.4.refs_2_
  143.0 0.0 copy-start
  143.0 3.3 %shard_map.59.refs_1_.refs_2_ = f32[16,16,8,128]{3,2,1,0:T(8,128)S(1)} custom-call(s32[32,32]{1,0:T(8,128)S(1)} %copy-done.1, f32[7,16,8,128]{3,2,1,0:T(8,128)S(1)} %collective-permute-done.3.refs_0_, f32[32,32,8,128]{3,2,1,0:T(8,128)S(1)} %get-tuple-element.20.refs_0_.refs_1_, f32[7,16,8,128]{3,2,1,0:T(8,128)S(1)} %collective-permute-done.4.refs_2_, ...), custom_call_target="tpu_custom_call" | custom-call | flops 4194304000 | bytes 2097152 | tf_op jit(solution)/shard_map/pallas_call | solution.py:479
  146.3 0.0 copy-done
  146.3 4.0 %shard_map.60 = (f32[16,16,8,128]{3,2,1,0:T(8,128)S(1)}, f32[7,16,8,128]{3,2,1,0:T(8,128)S(1)}, f32[7,16,8,128]{3,2,1,0:T(8,128)S(1)}) custom-call(s32[32,32]{1,0:T(8,128)S(1)} %copy-done, f32[16,16,8,128]{3,2,1,0:T(8,128)S(1)} %get-tuple-element.23.refs_3_.refs_0_.refs_1_, f32[16,16,8,128]{3,2,1,0:T(8,128)S(1)} %shard_map.59.refs_1_.refs_2_), custom_call_target="tpu_custom_call" | custom-call | flops 4194304000 | bytes 2097152 | tf_op jit(solution)/shard_map/pallas_call | solution.py:479
  150.3 4.1 %collective-permute-start.8 = (f32[7,16,8,128]{3,2,1,0:T(8,128)S(1)}, f32[7,16,8,128]{3,2,1,0:T(8,128)S(1)}, u32[]{:S(2)}, u32[]{:S(2)}) collective-permute-start(f32[7,16,8,128]{3,2,1,0:T(8,128)S(1)} %get-tuple-element.31), channel_id=1, source_target_pairs={{0,4},{4,8},{8,12},{12,16},{16,20},{20,24},{24,28},{1,5},{5,9},{9,... | collective-permute-start | bytes 1376264 | tf_op jit(solution)/shard_map/ppermute | solution.py:501
  154.4 1.9 collective-permute-start.9
  156.4 3.4 %shard_map.61.refs_5_.refs_3_.refs_1_ = f32[16,16,8,128]{3,2,1,0:T(8,128)S(1)} custom-call(s32[32,32]{1,0:T(8,128)S(1)} %copy-done, f32[16,32,8,128]{3,2,1,0:T(8,128)S(1)} %shard_map.57.refs_3_.refs_0_.refs_1_, f32[16,16,8,128]{3,2,1,0:T(8,128)S(1)} %get-tuple-element.27.refs_1_.refs_4_.refs_0_), custom_call_target="tpu_custom_call" | custom-call | flops 4194304000 | bytes 2097152 | tf_op jit(solution)/shard_map/pallas_call | solution.py:479
  159.8 5.2 %shard_map.64.refs_2_ = f32[32,32,1024]{2,1,0:T(8,128)} custom-call(s32[32,32]{1,0:T(8,128)S(1)} %copy-done.1, f32[16,16,8,128]{3,2,1,0:T(8,128)S(1)} %get-tuple-element.27.refs_1_.refs_4_.refs_0_, f32[16,16,8,128]{3,2,1,0:T(8,128)S(1)} %shard_map.61.refs_5_.refs_3_.refs_1_), custom_call_target="tpu_custom_call" | custom-call | flops 4194304000 | bytes 2097152 | tf_op jit(solution)/shard_map/pallas_call | solution.py:479
  165.0 0.0 collective-permute-done.2.refs_0_
  165.0 0.0 collective-permute-done.5.refs_3_.refs_2_
  165.0 3.6 %shard_map.62 = (f32[16,32,8,128]{3,2,1,0:T(8,128)S(1)}, f32[7,16,8,128]{3,2,1,0:T(8,128)S(1)}, f32[7,16,8,128]{3,2,1,0:T(8,128)S(1)}) custom-call(s32[32,32]{1,0:T(8,128)S(1)} %copy-done, f32[32,7,8,128]{3,2,1,0:T(8,128)S(1)} %collective-permute-done.2.refs_0_, f32[16,16,8,128]{3,2,1,0:T(8,128)S(1)} %get-tuple-element.23.refs_3_.refs_0_.refs_1_, ...), custom_call_target="tpu_custom_call" | custom-call | flops 4194304000 | bytes 2097152 | tf_op jit(solution)/shard_map/pallas_call | solution.py:479
  168.6 4.5 %collective-permute-start.6 = (f32[7,16,8,128]{3,2,1,0:T(8,128)S(1)}, f32[7,16,8,128]{3,2,1,0:T(8,128)S(1)}, u32[]{:S(2)}, u32[]{:S(2)}) collective-permute-start(f32[7,16,8,128]{3,2,1,0:T(8,128)S(1)} %get-tuple-element.28), channel_id=1, source_target_pairs={{0,4},{4,8},{8,12},{12,16},{16,20},{20,24},{24,28},{1,5},{5,9},{9,... | collective-permute-start | bytes 1376264 | tf_op jit(solution)/shard_map/ppermute | solution.py:501
  173.2 2.1 %collective-permute-start.7 = (f32[7,16,8,128]{3,2,1,0:T(8,128)S(1)}, f32[7,16,8,128]{3,2,1,0:T(8,128)S(1)}, u32[]{:S(2)}, u32[]{:S(2)}) collective-permute-start(f32[7,16,8,128]{3,2,1,0:T(8,128)S(1)} %get-tuple-element.30), channel_id=1, source_target_pairs={{4,0},{8,4},{12,8},{16,12},{20,16},{24,20},{28,24},{5,1},{9,5},{13... | collective-permute-start | bytes 1376264 | tf_op jit(solution)/shard_map/ppermute | solution.py:502
  175.3 3.4 %shard_map.63.refs_1_.refs_2_ = f32[16,32,8,128]{3,2,1,0:T(8,128)S(1)} custom-call(s32[32,32]{1,0:T(8,128)S(1)} %copy-done, f32[32,7,8,128]{3,2,1,0:T(8,128)S(1)} %collective-permute-done.2.refs_0_, f32[16,32,8,128]{3,2,1,0:T(8,128)S(1)} %shard_map.57.refs_3_.refs_0_.refs_1_, f32[32,7,8,128]{3,2,1,0:T(8,128)S(1)} %collective-permute-done.5.refs_3_.refs_2_, ...), custom_call_target="tpu_custom_call" | custom-call | flops 4194304000 | bytes 2097152 | tf_op jit(solution)/shard_map/pallas_call | solution.py:479
  178.7 5.2 %shard_map.65.refs_4_ = f32[32,32,1024]{2,1,0:T(8,128)} custom-call(s32[32,32]{1,0:T(8,128)S(1)} %copy-done.1, f32[16,32,8,128]{3,2,1,0:T(8,128)S(1)} %get-tuple-element.29.refs_4_.refs_0_.refs_1_, f32[16,32,8,128]{3,2,1,0:T(8,128)S(1)} %shard_map.63.refs_1_.refs_2_, f32[32,32,1024]{2,1,0:T(8,128)} %shard_map.64.refs_2_), custom_call_target="tpu_custom_call", output_to_operand_aliasing={{}: (3, {})} | custom-call | flops 4194304000 | bytes 2097152 | tf_op jit(solution)/shard_map/pallas_call | solution.py:479
  183.9 0.0 collective-permute-done.8.refs_0_
  183.9 0.0 collective-permute-done.9.refs_3_
  183.9 5.1 %shard_map.66.refs_4_ = f32[32,32,1024]{2,1,0:T(8,128)} custom-call(s32[32,32]{1,0:T(8,128)S(1)} %copy-done.1, f32[7,16,8,128]{3,2,1,0:T(8,128)S(1)} %collective-permute-done.8.refs_0_, f32[16,32,8,128]{3,2,1,0:T(8,128)S(1)} %get-tuple-element.29.refs_4_.refs_0_.refs_1_, ...), custom_call_target="tpu_custom_call", output_to_operand_aliasing={{}: (5, {})} | custom-call | flops 4194304000 | bytes 2097152 | tf_op jit(solution)/shard_map/pallas_call | solution.py:479
  189.0 0.0 collective-permute-done.6.refs_0_
  189.0 0.0 collective-permute-done.7.refs_3_
  189.0 5.1 %shard_map.67 = f32[32,32,1024]{2,1,0:T(8,128)} custom-call(s32[32,32]{1,0:T(8,128)S(1)} %copy-done.1, f32[7,16,8,128]{3,2,1,0:T(8,128)S(1)} %collective-permute-done.6.refs_0_, f32[16,32,8,128]{3,2,1,0:T(8,128)S(1)} %get-tuple-element.29.refs_4_.refs_0_.refs_1_, f32[16,32,8,128]{3,2,1,0:T(8,128)S(1)} %shard_map.63.refs_1_.refs_2_, ...), custom_call_target="tpu_custom_call", output_to_operand_aliasing={{}: (5, {})} | custom-call | flops 4194304000 | bytes 2097152 | tf_op jit(solution)/shard_map/pallas_call | solution.py:479
Async XLA Ops:
  107.1 19.9 %copy-start.1 = (s32[32,32]{1,0:T(8,128)S(1)}, s32[32,32]{1,0:T(8,128)}, u32[]{:S(2)}) copy-start(s32[32,32]{1,0:T(8,128)} %dip_ref.21) | copy-start | bytes 12292
  114.6 18.4 %collective-permute-start = (f32[7,16,8,128]{3,2,1,0:T(8,128)S(1)}, f32[7,16,8,128]{3,2,1,0:T(8,128)S(1)}, u32[]{:S(2)}, u32[]{:S(2)}) collective-permute-start(f32[7,16,8,128]{3,2,1,0:T(8,128)S(1)} %get-tuple-element.19), channel_id=1, source_target_pairs={{0,4},{4,8},{8,12},{12,16},{16,20},{20,24},{24,28},{1,5},{5,9},{9,... | collective-permute-start | bytes 1376264 | tf_op jit(solution)/shard_map/ppermute | solution.py:501
  118.6 15.3 %collective-permute-start.1 = (f32[7,16,8,128]{3,2,1,0:T(8,128)S(1)}, f32[7,16,8,128]{3,2,1,0:T(8,128)S(1)}, u32[]{:S(2)}, u32[]{:S(2)}) collective-permute-start(f32[7,16,8,128]{3,2,1,0:T(8,128)S(1)} %get-tuple-element.21), channel_id=1, source_target_pairs={{4,0},{8,4},{12,8},{16,12},{20,16},{24,20},{28,24},{5,1},{9,5},{13... | collective-permute-start | bytes 1376264 | tf_op jit(solution)/shard_map/ppermute | solution.py:502
  120.6 22.4 %collective-permute-start.3 = (f32[7,16,8,128]{3,2,1,0:T(8,128)S(1)}, f32[7,16,8,128]{3,2,1,0:T(8,128)S(1)}, u32[]{:S(2)}, u32[]{:S(2)}) collective-permute-start(f32[7,16,8,128]{3,2,1,0:T(8,128)S(1)} %get-tuple-element.24), channel_id=1, source_target_pairs={{0,4},{4,8},{8,12},{12,16},{16,20},{20,24},{24,28},{1,5},{5,9},{9,... | collective-permute-start | bytes 1376264 | tf_op jit(solution)/shard_map/ppermute | solution.py:501
  125.1 17.9 %collective-permute-start.4 = (f32[7,16,8,128]{3,2,1,0:T(8,128)S(1)}, f32[7,16,8,128]{3,2,1,0:T(8,128)S(1)}, u32[]{:S(2)}, u32[]{:S(2)}) collective-permute-start(f32[7,16,8,128]{3,2,1,0:T(8,128)S(1)} %get-tuple-element.25), channel_id=1, source_target_pairs={{4,0},{8,4},{12,8},{16,12},{20,16},{24,20},{28,24},{5,1},{9,5},{13... | collective-permute-start | bytes 1376264 | tf_op jit(solution)/shard_map/ppermute | solution.py:502
  137.6 27.4 %collective-permute-start.2 = (f32[32,7,8,128]{3,2,1,0:T(8,128)S(1)}, f32[32,7,8,128]{3,2,1,0:T(8,128)S(1)}, u32[]{:S(2)}, u32[]{:S(2)}) collective-permute-start(f32[32,7,8,128]{3,2,1,0:T(8,128)S(1)} %get-tuple-element.22), channel_id=1, source_target_pairs={{0,1},{1,2},{2,3},{4,5},{5,6},{6,7},{8,9},{9,10},{10,11},{12,13},{... | collective-permute-start | bytes 2752520 | tf_op jit(solution)/shard_map/ppermute | solution.py:501
  139.5 25.5 %collective-permute-start.5 = (f32[32,7,8,128]{3,2,1,0:T(8,128)S(1)}, f32[32,7,8,128]{3,2,1,0:T(8,128)S(1)}, u32[]{:S(2)}, u32[]{:S(2)}) collective-permute-start(f32[32,7,8,128]{3,2,1,0:T(8,128)S(1)} %get-tuple-element.26), channel_id=1, source_target_pairs={{1,0},{2,1},{3,2},{5,4},{6,5},{7,6},{9,8},{10,9},{11,10},{13,12},{... | collective-permute-start | bytes 2752520 | tf_op jit(solution)/shard_map/ppermute | solution.py:502
  143.0 3.3 %copy-start = (s32[32,32]{1,0:T(8,128)S(1)}, s32[32,32]{1,0:T(8,128)}, u32[]{:S(2)}) copy-start(s32[32,32]{1,0:T(8,128)} %dip_ref.17) | copy-start | bytes 12292
  150.3 33.6 %collective-permute-start.8 = (f32[7,16,8,128]{3,2,1,0:T(8,128)S(1)}, f32[7,16,8,128]{3,2,1,0:T(8,128)S(1)}, u32[]{:S(2)}, u32[]{:S(2)}) collective-permute-start(f32[7,16,8,128]{3,2,1,0:T(8,128)S(1)} %get-tuple-element.31), channel_id=1, source_target_pairs={{0,4},{4,8},{8,12},{12,16},{16,20},{20,24},{24,28},{1,5},{5,9},{9,... | collective-permute-start | bytes 1376264 | tf_op jit(solution)/shard_map/ppermute | solution.py:501
  154.4 29.5 %collective-permute-start.9 = (f32[7,16,8,128]{3,2,1,0:T(8,128)S(1)}, f32[7,16,8,128]{3,2,1,0:T(8,128)S(1)}, u32[]{:S(2)}, u32[]{:S(2)}) collective-permute-start(f32[7,16,8,128]{3,2,1,0:T(8,128)S(1)} %get-tuple-element.32), channel_id=1, source_target_pairs={{4,0},{8,4},{12,8},{16,12},{20,16},{24,20},{28,24},{5,1},{9,5},{13... | collective-permute-start | bytes 1376264 | tf_op jit(solution)/shard_map/ppermute | solution.py:502
  168.6 20.4 %collective-permute-start.6 = (f32[7,16,8,128]{3,2,1,0:T(8,128)S(1)}, f32[7,16,8,128]{3,2,1,0:T(8,128)S(1)}, u32[]{:S(2)}, u32[]{:S(2)}) collective-permute-start(f32[7,16,8,128]{3,2,1,0:T(8,128)S(1)} %get-tuple-element.28), channel_id=1, source_target_pairs={{0,4},{4,8},{8,12},{12,16},{16,20},{20,24},{24,28},{1,5},{5,9},{9,... | collective-permute-start | bytes 1376264 | tf_op jit(solution)/shard_map/ppermute | solution.py:501
  173.2 15.9 %collective-permute-start.7 = (f32[7,16,8,128]{3,2,1,0:T(8,128)S(1)}, f32[7,16,8,128]{3,2,1,0:T(8,128)S(1)}, u32[]{:S(2)}, u32[]{:S(2)}) collective-permute-start(f32[7,16,8,128]{3,2,1,0:T(8,128)S(1)} %get-tuple-element.30), channel_id=1, source_target_pairs={{4,0},{8,4},{12,8},{16,12},{20,16},{24,20},{28,24},{5,1},{9,5},{13... | collective-permute-start | bytes 1376264 | tf_op jit(solution)/shard_map/ppermute | solution.py:502
